TPU v7x, 32 devices: a whole 2x2x4 slice. The times are simulated.
32 devices in a mesh: boot: 2 (over x), space: 16 (over z, y, core).
Axes of the slice: x: 2, y: 2, z: 4, core: 2. Of those that a mesh axis runs over, the one named last changes fastest.
Arguments:
- background_states: bfloat16 [512, 32768], P('space'), may hold values from -6 to 6
- measurement_anomaly_matrix: bfloat16 [6144, 512], P('space'), may hold values from -6 to 6
- departure_vector: bfloat16 [6144], P('space'), may hold values from -6 to 6
- measurement_precision: float32 [6144], P('space'), may hold values from 0.25 to 4
- measurement_region_targets: int32 [6144, 2], P('space'), may hold values from 0 to 15, all different within a row; in each aligned block of 384 rows (0 to 383, 384 to 767, ...) at most 96 rows name the same one
- localization_factor_scaled: int32 [6144, 2], P('space'), may hold values from 16 to 1024
- bootstrap_multiplicity: int32 [12288], P(('boot', 'space')), parts along dimension 0, may hold values from 0 to 3
Outputs:
- analysis: bfloat16 [1024, 32768], P(('boot', 'space')), parts along dimension 0
There are 2 independent parts, one for each index of `boot`. A program takes and returns all parts, laid end to end along the dimension named above; an argument that names none is the same for every part. Nothing has to cross between parts.
Inputs may be any that keep to these rules, and one draw needn't show every extreme that they name: `measurement_region_targets`: each row names 2 different patches. Among the rows of one device (aligned blocks of 384 rows) no patch is named more than 96 times, a bound that some block reaches.
All inputs are finite; a program needn't handle non-finite values.
Results may differ from a plain program's by a relative error of at most 0.0075.
Values may be sent and summed in bfloat16 or wider, within the bound.
No kernel may reach another device: no remote copies, remote signals or barrier semaphores. Data moves between devices by JAX's collectives and lax.ppermute only.
A program may use at most 64 MiB of HBM per device.

v0:
```python
import functools

import jax
import jax.numpy as jnp
from jax import lax
from jax.experimental import pallas as pl
from jax.experimental.pallas import tpu as pltpu
from jax.sharding import PartitionSpec as P

NS_STEPS = 6
LANES = 128
VMEM_BYTES = 48 * 1024 * 1024
F32 = jnp.float32
BF16 = jnp.bfloat16


def pack_kernel(targets_ref, local_ref, mult_ref, prec_ref, dep_ref, rows_ref, slots_ref, info_ref):
    patches, cap, _ = slots_ref.shape
    count = rows_ref.shape[0]
    weight = local_ref[...].astype(F32) / 1024.0 * (mult_ref[...].astype(F32) * prec_ref[...])
    weight = weight.astype(BF16).astype(F32)
    dep = dep_ref[...].astype(F32)
    patch_id = lax.broadcasted_iota(jnp.int32, (patches, count), 0)
    first = patch_id == targets_ref[0:1, :]
    second = patch_id == targets_ref[1:2, :]
    named = jnp.logical_or(first, second)
    earlier = lax.broadcasted_iota(jnp.int32, (count, count), 0) < lax.broadcasted_iota(
        jnp.int32, (count, count), 1
    )
    rank = jnp.dot(
        named.astype(F32).astype(BF16), earlier.astype(F32).astype(BF16), preferred_element_type=F32
    )
    rank = jnp.where(named, rank, -1.0)
    by_patch = jnp.where(first, weight[0:1, :], jnp.where(second, weight[1:2, :], 0.0))
    slot_id = lax.broadcasted_iota(jnp.int32, (cap, count), 0).astype(F32)
    lane = lax.broadcasted_iota(jnp.int32, (cap, LANES), 1)
    info = jnp.zeros((cap, LANES), F32)
    rows = rows_ref[...]
    for patch in range(patches):
        pick = jnp.where(slot_id == rank[patch : patch + 1, :], 1.0, 0.0)
        slots_ref[patch] = jnp.dot(pick.astype(BF16), rows, preferred_element_type=F32).astype(BF16)
        weight_col = jnp.sum(pick * by_patch[patch : patch + 1, :], axis=1, keepdims=True)
        dep_col = jnp.sum(pick * dep, axis=1, keepdims=True)
        info = jnp.where(lane == patch, weight_col, info)
        info = jnp.where(lane == patches + patch, dep_col, info)
    info_ref[...] = info.astype(BF16)


def pack(targets, local, mult, prec, dep, rows, patches, cap):
    members = rows.shape[1]
    count = rows.shape[0]
    return pl.pallas_call(
        pack_kernel,
        out_shape=(
            jax.ShapeDtypeStruct((patches, cap, members), BF16),
            jax.ShapeDtypeStruct((cap, LANES), BF16),
        ),
        compiler_params=pltpu.CompilerParams(vmem_limit_bytes=VMEM_BYTES),
        cost_estimate=pl.CostEstimate(
            flops=2 * patches * cap * count * members,
            bytes_accessed=2 * (patches * cap + count) * members,
            transcendentals=0,
        ),
        name="pack_rows",
    )(targets.T, local.T, mult[None, :], prec[None, :], dep[None, :], rows)


def halves(value):
    high = value.astype(BF16)
    return high, (value - high.astype(F32)).astype(BF16)


def product(left_high, left_low, right_high, right_low):
    dot = functools.partial(jnp.dot, preferred_element_type=F32)
    return dot(left_high, right_high) + (dot(left_high, right_low) + dot(left_low, right_high))


def weights_kernel(rows_ref, info_ref, blended_ref, y_high, y_low, z_high, z_low, f_high, f_low):
    sources, cap, members = rows_ref.shape
    patch = lax.axis_index("space")
    lane = lax.broadcasted_iota(jnp.int32, (cap, LANES), 1)
    gram = jnp.zeros((members, members), F32)
    drive = jnp.zeros((1, members), F32)
    for source in range(sources):
        info = info_ref[source].astype(F32)
        weight_col = jnp.sum(jnp.where(lane == patch, info, 0.0), axis=1, keepdims=True)
        dep_col = jnp.sum(jnp.where(lane == sources + patch, info, 0.0), axis=1, keepdims=True)
        rows = rows_ref[source]
        scaled = (weight_col * rows.astype(F32)).astype(BF16)
        gram += lax.dot_general(rows, scaled, (((0,), (0,)), ((), ())), preferred_element_type=F32)
        drive += jnp.sum(dep_col * scaled.astype(F32), axis=0, keepdims=True)

    row_id = lax.broadcasted_iota(jnp.int32, (members, members), 0)
    col_id = lax.broadcasted_iota(jnp.int32, (members, members), 1)
    diagonal = row_id == col_id
    identity = jnp.where(diagonal, 1.0, 0.0)
    shifted = identity + gram / (members - 1.0)
    squares = jnp.sum(jnp.sum(shifted * shifted, axis=0, keepdims=True), axis=1, keepdims=True)
    frobenius = jnp.sqrt(squares)
    current = shifted / frobenius

    def put(high_ref, low_ref, value):
        high_ref[...], low_ref[...] = halves(value)

    def factor_of(zy):
        return 1.5 * identity - 0.5 * zy

    first = factor_of(current)
    put(y_high, y_low, current)
    put(f_high, f_low, first)
    put(z_high, z_low, first)
    put(y_high, y_low, product(y_high[...], y_low[...], f_high[...], f_low[...]))

    def step(_, carry):
        zy = product(z_high[...], z_low[...], y_high[...], y_low[...])
        put(f_high, f_low, factor_of(zy))
        put(y_high, y_low, product(y_high[...], y_low[...], f_high[...], f_low[...]))
        put(z_high, z_low, product(f_high[...], f_low[...], z_high[...], z_low[...]))
        return carry

    lax.fori_loop(1, NS_STEPS - 1, step, 0)
    zy = product(z_high[...], z_low[...], y_high[...], y_low[...])
    put(f_high, f_low, factor_of(zy))
    root = product(f_high[...], f_low[...], z_high[...], z_low[...]) / jnp.sqrt(frobenius)

    drive_col = jnp.sum(jnp.where(diagonal, drive, 0.0), axis=1, keepdims=True)
    inner = jnp.sum(root * drive_col, axis=0, keepdims=True)
    mean_weight = jnp.sum(root * inner, axis=1, keepdims=True) / (members - 1.0)
    blended_ref[...] = (root + mean_weight).astype(BF16)


def patch_weights(rows, info):
    sources, cap, members = rows.shape
    half = pltpu.VMEM((members, members), BF16)
    return pl.pallas_call(
        weights_kernel,
        out_shape=jax.ShapeDtypeStruct((members, members), BF16),
        scratch_shapes=[half] * 6,
        compiler_params=pltpu.CompilerParams(vmem_limit_bytes=VMEM_BYTES),
        cost_estimate=pl.CostEstimate(
            flops=2 * members * members * (sources * cap + 45 * members),
            bytes_accessed=2 * sources * cap * members,
            transcendentals=0,
        ),
        name="patch_weights",
    )(rows, info)


def local(
    background_states,
    measurement_anomaly_matrix,
    departure_vector,
    measurement_precision,
    measurement_region_targets,
    localization_factor_scaled,
    bootstrap_multiplicity,
):
    device_count = lax.axis_size("space")
    local_rows = measurement_anomaly_matrix.shape[0]
    targets_per = measurement_region_targets.shape[1]
    slot_cap = 2 * targets_per * local_rows // device_count
    slots, info = pack(
        measurement_region_targets,
        localization_factor_scaled,
        bootstrap_multiplicity,
        measurement_precision,
        departure_vector,
        measurement_anomaly_matrix,
        device_count,
        slot_cap,
    )
    info_got = lax.all_gather(info, "space", axis=0, tiled=False)
    rows_got = lax.all_to_all(slots, "space", split_axis=0, concat_axis=0, tiled=True)
    background = lax.all_to_all(
        background_states, "space", split_axis=1, concat_axis=0, tiled=True
    )
    blended = patch_weights(rows_got, info_got)
    centre = jnp.mean(background.astype(F32), axis=0)
    perturb = (background.astype(F32) - centre[None, :]).astype(BF16)
    update = lax.dot_general(
        blended, perturb, (((0,), (0,)), ((), ())), preferred_element_type=F32
    )
    analysis = (centre[None, :] + update).astype(BF16)
    return lax.all_to_all(analysis, "space", split_axis=0, concat_axis=1, tiled=True)


def solution(mesh):
    in_specs = (
        P("space", None),
        P("space", None),
        P("space"),
        P("space"),
        P("space", None),
        P("space", None),
        P(("boot", "space")),
    )
    out_specs = P(("boot", "space"), None)
    return jax.shard_map(local, mesh=mesh, in_specs=in_specs, out_specs=out_specs, check_vma=False)
```

profile of v0, /device:TPU:0, one launch (start us, length us, event | category | flops | bytes accessed | tf_op | source)
XLA Modules:
  0.0 190.0 jit_solution(6740938634025910653)
XLA Ops:
  0.0 0.7 broadcast_in_dim.13.dep_ref
  0.7 0.7 broadcast_in_dim.12.prec_ref
  1.4 0.7 broadcast_in_dim.11.mult_ref
  2.0 0.0 copy-start
  2.1 1.0 copy-done
  3.0 0.0 copy-start.1
  3.0 0.7 copy-done.1
  3.7 0.0 copy-start.2
  3.7 0.7 copy-done.2
  4.4 2.8 %pack_rows.1 = (bf16[16,96,512]{2,1,0:T(8,128)(2,1)}, bf16[96,128]{1,0:T(8,128)(2,1)S(1)}) custom-call(s32[2,384]{1,0:T(2,128)S(1)} %bitcast.20, s32[2,384]{1,0:T(2,128)S(1)} %bitcast.21, s32[1,384]{1,0:T(1,128)S(1)} %broadcast_in_dim.11.mult_ref, f32[1,384]{1,0:T(1,128)S(1)} %broadcast_in_dim.12.prec_ref, bf16[1,384]{1,0:T(2,128)(2,1)S(1)} %broadcast_in_dim.13.dep_ref, ...), custom_call_target="tpu_custom_call" | custom-call | flops 603979776 | bytes 1966080 | tf_op jit(solution)/shard_map/pack_rows/pallas_call | solution.py:52
  7.3 7.4 %all-to-all-start.1 = ((bf16[16,96,512]{2,1,0:T(8,128)(2,1)}), bf16[16,96,512]{2,1,0:T(8,128)(2,1)S(1)}, u32[]{:S(2)}, u32[]{:S(2)}) async-start(bf16[16,96,512]{2,1,0:T(8,128)(2,1)} %get-tuple-element.7), calls=%async_computation.1 | async-start | bytes 3145728 | tf_op jit(solution)/shard_map/all_to_all | solution.py:173
  14.6 3.2 %copy.13 = bf16[4,16,8,2048]{3,2,0,1:T(8,128)(2,1)} copy(bf16[4,16,8,2048]{3,2,1,0:T(8,128)(2,1)} %bitcast.24) | data formatting | bytes 4194304 | tf_op jit(solution)/shard_map/all_to_all | solution.py:174
  17.8 28.8 %all-to-all-done.1.rows_ref = bf16[16,96,512]{2,1,0:T(8,128)(2,1)S(1)} async-done(((bf16[16,96,512]{2,1,0:T(8,128)(2,1)}), bf16[16,96,512]{2,1,0:T(8,128)(2,1)S(1)}, u32[]{:S(2)}, u32[]{:S(2)}) %all-to-all-start.1) | async-done | bytes 1572896 | tf_op jit(solution)/shard_map/all_to_all | solution.py:173
  46.6 9.2 %all-to-all-start = ((bf16[32,16,2048]{2,0,1:T(8,128)(2,1)}), bf16[32,16,2048]{2,0,1:T(8,128)(2,1)}, u32[]{:S(2)}, u32[]{:S(2)}) async-start(bf16[32,16,2048]{2,0,1:T(8,128)(2,1)} %bitcast.22), calls=%async_computation | async-start | bytes 4194304 | tf_op jit(solution)/shard_map/all_to_all | solution.py:174
  55.8 55.9 %all-gather = bf16[1536,128]{1,0:T(8,128)(2,1)S(1)} all-gather(bf16[96,128]{1,0:T(8,128)(2,1)S(1)} %get-tuple-element.8), channel_id=2, replica_groups=mesh['boot'=2,'space'=16] {'space'}, dimensions={0}, use_global_device_ids=true | all-gather | bytes 417792 | tf_op jit(solution)/shard_map/all_gather | solution.py:172
  111.7 17.3 %patch_weights.1 = bf16[512,512]{1,0:T(8,128)(2,1)S(1)} custom-call(bf16[16,96,512]{2,1,0:T(8,128)(2,1)S(1)} %all-to-all-done.1.rows_ref, bf16[16,96,128]{2,1,0:T(8,128)(2,1)S(1)} %bitcast.19), custom_call_target="tpu_custom_call" | custom-call | flops 12884901888 | bytes 1572864 | tf_op jit(solution)/shard_map/patch_weights/pallas_call | solution.py:135
  129.0 0.0 all-to-all-done
  129.0 2.0 %convert_reduce_fusion = f32[2048]{0:T(1024)S(1)} fusion(bf16[32,16,2048]{2,0,1:T(8,128)(2,1)} %all-to-all-done), kind=kLoop, calls=%fused_computation.4 | loop fusion | flops 2095104 | bytes 2105344 | tf_op jit(solution)/shard_map/reduce_sum | solution.py:178
  130.9 2.0 %fusion = bf16[512,2048]{1,0:T(8,128)(2,1)S(1)} fusion(f32[2048]{0:T(1024)S(1)} %broadcast_multiply_fusion, bf16[32,16,2048]{2,0,1:T(8,128)(2,1)} %all-to-all-done), kind=kLoop, calls=%fused_computation.1 | loop fusion | flops 3145728 | bytes 4202496 | tf_op jit(solution)/shard_map/convert_element_type | solution.py:179
  133.0 1.3 add_convert_fusion
  134.3 54.3 %all_to_all.37 = bf16[16,32,2048]{2,1,0:T(8,128)(2,1)S(1)} all-to-all(bf16[16,32,2048]{2,1,0:T(8,128)(2,1)S(1)} %bitcast.25), channel_id=1, replica_groups=mesh['boot'=2,'space'=16] {'space'}, dimensions={0} | all-to-all | bytes 4194304 | tf_op jit(solution)/shard_map/all_to_all | solution.py:184
  188.6 1.5 copy.11
  (1 shorter events, 0.0 us)
Async XLA Ops:
  2.0 1.0 copy-start
  3.0 0.7 copy-start.1
  3.7 0.7 copy-start.2
  7.3 39.4 %all-to-all-start.1 = ((bf16[16,96,512]{2,1,0:T(8,128)(2,1)}), bf16[16,96,512]{2,1,0:T(8,128)(2,1)S(1)}, u32[]{:S(2)}, u32[]{:S(2)}) async-start(bf16[16,96,512]{2,1,0:T(8,128)(2,1)} %get-tuple-element.7), calls=%async_computation.1 | async-start | bytes 3145728 | tf_op jit(solution)/shard_map/all_to_all | solution.py:173
  46.6 82.3 %all-to-all-start = ((bf16[32,16,2048]{2,0,1:T(8,128)(2,1)}), bf16[32,16,2048]{2,0,1:T(8,128)(2,1)}, u32[]{:S(2)}, u32[]{:S(2)}) async-start(bf16[32,16,2048]{2,0,1:T(8,128)(2,1)} %bitcast.22), calls=%async_computation | async-start | bytes 4194304 | tf_op jit(solution)/shard_map/all_to_all | solution.py:174
where the time goes:
time: 191 us; the launch traced here: 190 us
  blocking collectives  110 us (58%)
  waiting for transfers between devices  28.8 us (15%)
  Pallas kernels  20.1 us (11%)
  starting transfers between devices  16.5 us (9%)
  local copies, waits for them, and re-layouts  9.03 us (5%)
  other arithmetic  4 us (2%)
    all_gather x1, blocking collectives, local(): info_got = lax.all_gather(info, 'space', axis=0, tiled=False)  55.9 us
    all_to_all x1, blocking collectives, local(): lax.all_to_all(analysis, 'space', split_axis=0, concat_axis=1, tiled=True)  54.3 us
    all_to_all x1, waiting for transfers between devices, local(): lax.all_to_all(slots, 'space', split_axis=0, concat_axis=0, tiled=True)  28.8 us
    pallas_call x1, Pallas kernels, patch_weights(): pl.pallas_call(weights_kernel, out_shape=jax.ShapeDtypeStruct((members, m...  17.3 us
    all_to_all x1, starting transfers between devices, local(): lax.all_to_all(background_states, 'space', split_axis=1, concat_axis=0, t...  9.16 us
    all_to_all x1, starting transfers between devices, local(): lax.all_to_all(slots, 'space', split_axis=0, concat_axis=0, tiled=True)  7.39 us
  transfers between devices with their start and end apart: 2, of which 1 were waited for; matrix products, arithmetic and copies ran while one was open for 2% of the time, Pallas kernels for 9%

commit v1 on v0

--- a/solution.py
+++ b/solution.py
@@ -9,17 +9,31 @@
 
 NS_STEPS = 6
 LANES = 128
+TAIL = 8
 VMEM_BYTES = 48 * 1024 * 1024
 F32 = jnp.float32
 BF16 = jnp.bfloat16
 
 
-def pack_kernel(targets_ref, local_ref, mult_ref, prec_ref, dep_ref, rows_ref, slots_ref, info_ref):
-    patches, cap, _ = slots_ref.shape
-    count = rows_ref.shape[0]
-    weight = local_ref[...].astype(F32) / 1024.0 * (mult_ref[...].astype(F32) * prec_ref[...])
+def pack_kernel(*refs):
+    sources, slots_ref, fetched, info_ref, sems = refs[:6], refs[6], refs[7:13], refs[13], refs[14]
+    copies = [
+        pltpu.make_async_copy(source, target, sems.at[i])
+        for i, (source, target) in enumerate(zip(sources, fetched))
+    ]
+    for copy in copies:
+        copy.start()
+    for copy in copies:
+        copy.wait()
+    targets_ref, local_ref, mult_ref, prec_ref, dep_ref, rows_ref = fetched
+    patches = slots_ref.shape[0]
+    cap = slots_ref.shape[1] - TAIL
+    count, members = rows_ref.shape
+    mult = mult_ref[...].reshape(1, count).astype(F32)
+    prec = prec_ref[...].reshape(1, count)
+    weight = local_ref[...].astype(F32) / 1024.0 * (mult * prec)
     weight = weight.astype(BF16).astype(F32)
-    dep = dep_ref[...].astype(F32)
+    dep = dep_ref[...].astype(F32).reshape(1, count)
     patch_id = lax.broadcasted_iota(jnp.int32, (patches, count), 0)
     first = patch_id == targets_ref[0:1, :]
     second = patch_id == targets_ref[1:2, :]
@@ -36,25 +50,39 @@
     lane = lax.broadcasted_iota(jnp.int32, (cap, LANES), 1)
     info = jnp.zeros((cap, LANES), F32)
     rows = rows_ref[...]
+    filled = []
     for patch in range(patches):
         pick = jnp.where(slot_id == rank[patch : patch + 1, :], 1.0, 0.0)
-        slots_ref[patch] = jnp.dot(pick.astype(BF16), rows, preferred_element_type=F32).astype(BF16)
         weight_col = jnp.sum(pick * by_patch[patch : patch + 1, :], axis=1, keepdims=True)
         dep_col = jnp.sum(pick * dep, axis=1, keepdims=True)
         info = jnp.where(lane == patch, weight_col, info)
         info = jnp.where(lane == patches + patch, dep_col, info)
-    info_ref[...] = info.astype(BF16)
+    info_ref[...] = jnp.zeros((LANES, LANES), F32)
+    info_ref[0:cap, :] = info
+    info = info_ref[...].T
+    tail_id = lax.broadcasted_iota(jnp.int32, (TAIL, LANES), 0)
+    blank = jnp.zeros((TAIL, members - LANES), F32)
+    for patch in range(patches):
+        pick = jnp.where(slot_id == rank[patch : patch + 1, :], 1.0, 0.0)
+        block = jnp.dot(pick.astype(BF16), rows, preferred_element_type=F32)
+        tail = jnp.where(
+            tail_id == 0,
+            info[patch : patch + 1, :],
+            jnp.where(tail_id == 1, info[patches + patch : patches + patch + 1, :], 0.0),
+        )
+        tail = jnp.concatenate([tail, blank], axis=1)
+        slots_ref[patch] = jnp.concatenate([block, tail], axis=0).astype(BF16)
 
 
 def pack(targets, local, mult, prec, dep, rows, patches, cap):
-    members = rows.shape[1]
-    count = rows.shape[0]
+    count, members = rows.shape
+    operands = (targets.T, local.T, mult, prec, dep, rows)
     return pl.pallas_call(
         pack_kernel,
-        out_shape=(
-            jax.ShapeDtypeStruct((patches, cap, members), BF16),
-            jax.ShapeDtypeStruct((cap, LANES), BF16),
-        ),
+        out_shape=jax.ShapeDtypeStruct((patches, cap + TAIL, members), BF16),
+        in_specs=[pl.BlockSpec(memory_space=pltpu.HBM)] * len(operands),
+        scratch_shapes=[pltpu.VMEM(operand.shape, operand.dtype) for operand in operands]
+        + [pltpu.VMEM((LANES, LANES), F32), pltpu.SemaphoreType.DMA((len(operands),))],
         compiler_params=pltpu.CompilerParams(vmem_limit_bytes=VMEM_BYTES),
         cost_estimate=pl.CostEstimate(
             flops=2 * patches * cap * count * members,
@@ -62,7 +90,7 @@
             transcendentals=0,
         ),
         name="pack_rows",
-    )(targets.T, local.T, mult[None, :], prec[None, :], dep[None, :], rows)
+    )(*operands)
 
 
 def halves(value):
@@ -75,16 +103,21 @@
     return dot(left_high, right_high) + (dot(left_high, right_low) + dot(left_low, right_high))
 
 
-def weights_kernel(rows_ref, info_ref, blended_ref, y_high, y_low, z_high, z_low, f_high, f_low):
-    sources, cap, members = rows_ref.shape
-    patch = lax.axis_index("space")
-    lane = lax.broadcasted_iota(jnp.int32, (cap, LANES), 1)
+def weights_kernel(rows_ref, blended_ref, info_ref, y_high, y_low, z_high, z_low, f_high, f_low):
+    sources, depth, members = rows_ref.shape
+    cap = depth - TAIL
+    for source in range(sources):
+        tail = rows_ref[source].astype(F32)[cap:depth, 0:LANES]
+        info_ref[source : source + 1, :] = tail[0:1, :]
+        info_ref[sources + source : sources + source + 1, :] = tail[1:2, :]
+    info = info_ref[...].T[0:depth, :]
+    real = lax.broadcasted_iota(jnp.int32, (depth, LANES), 0) < cap
+    info = jnp.where(real, info, 0.0)
     gram = jnp.zeros((members, members), F32)
     drive = jnp.zeros((1, members), F32)
     for source in range(sources):
-        info = info_ref[source].astype(F32)
-        weight_col = jnp.sum(jnp.where(lane == patch, info, 0.0), axis=1, keepdims=True)
-        dep_col = jnp.sum(jnp.where(lane == sources + patch, info, 0.0), axis=1, keepdims=True)
+        weight_col = info[:, source : source + 1]
+        dep_col = info[:, sources + source : sources + source + 1]
         rows = rows_ref[source]
         scaled = (weight_col * rows.astype(F32)).astype(BF16)
         gram += lax.dot_general(rows, scaled, (((0,), (0,)), ((), ())), preferred_element_type=F32)
@@ -125,25 +158,133 @@
 
     drive_col = jnp.sum(jnp.where(diagonal, drive, 0.0), axis=1, keepdims=True)
     inner = jnp.sum(root * drive_col, axis=0, keepdims=True)
-    mean_weight = jnp.sum(root * inner, axis=1, keepdims=True) / (members - 1.0)
+    inner_col = jnp.sum(jnp.where(diagonal, inner, 0.0), axis=1, keepdims=True)
+    mean_weight = jnp.sum(root * inner_col, axis=0, keepdims=True) / (members - 1.0)
     blended_ref[...] = (root + mean_weight).astype(BF16)
 
 
-def patch_weights(rows, info):
-    sources, cap, members = rows.shape
+def patch_weights(rows):
+    sources, depth, members = rows.shape
     half = pltpu.VMEM((members, members), BF16)
     return pl.pallas_call(
         weights_kernel,
         out_shape=jax.ShapeDtypeStruct((members, members), BF16),
-        scratch_shapes=[half] * 6,
+        scratch_shapes=[pltpu.VMEM((LANES, LANES), F32)] + [half] * 6,
         compiler_params=pltpu.CompilerParams(vmem_limit_bytes=VMEM_BYTES),
         cost_estimate=pl.CostEstimate(
-            flops=2 * members * members * (sources * cap + 45 * members),
-            bytes_accessed=2 * sources * cap * members,
+            flops=2 * members * members * (sources * depth + 45 * members),
+            bytes_accessed=2 * sources * depth * members,
             transcendentals=0,
         ),
         name="patch_weights",
-    )(rows, info)
+    )(rows)
+
+
+def update_kernel(blended_ref, background_ref, analysis_ref):
+    background = background_ref[...].astype(F32)
+    centre = jnp.sum(background, axis=0, keepdims=True) / background.shape[0]
+    perturb = (background - centre).astype(BF16)
+    update = jnp.dot(blended_ref[...], perturb, preferred_element_type=F32)
+    analysis_ref[...] = (centre + update).astype(BF16)
+
+
+def update_points(blended, background):
+    members, points = background.shape
+    tile = min(points, 256)
+    return pl.pallas_call(
+        update_kernel,
+        grid=(points // tile,),
+        in_specs=[
+            pl.BlockSpec((members, members), lambda i: (0, 0)),
+            pl.BlockSpec((members, tile), lambda i: (0, i)),
+        ],
+        out_specs=pl.BlockSpec((members, tile), lambda i: (0, i)),
+        out_shape=jax.ShapeDtypeStruct((members, points), BF16),
+        compiler_params=pltpu.CompilerParams(vmem_limit_bytes=VMEM_BYTES),
+        cost_estimate=pl.CostEstimate(
+            flops=2 * members * members * points,
+            bytes_accessed=4 * members * points + 2 * members * members,
+            transcendentals=0,
+        ),
+        name="update_points",
+    )(blended, background)
+
+
+def share_columns(turn, share):
+    groups = lax.axis_size("boot")
+    return lax.rem(lax.axis_index("boot") + turn, groups) * share
+
+
+def run_copies(copies):
+    for copy in copies:
+        copy.start()
+    for copy in copies:
+        copy.wait()
+
+
+def cut_kernel(states_ref, cut_ref, sems):
+    patches, _, share = cut_ref.shape
+    region = states_ref.shape[1] // patches
+    begin = share_columns(0, share)
+    run_copies(
+        [
+            pltpu.make_async_copy(
+                states_ref.at[:, pl.ds(pl.multiple_of(patch * region + begin, LANES), share)],
+                cut_ref.at[patch],
+                sems.at[patch],
+            )
+            for patch in range(patches)
+        ]
+    )
+
+
+def cut_share(states, patches, share):
+    own_members = states.shape[0]
+    return pl.pallas_call(
+        cut_kernel,
+        in_specs=[pl.BlockSpec(memory_space=pltpu.HBM)],
+        out_specs=pl.BlockSpec(memory_space=pl.ANY),
+        out_shape=jax.ShapeDtypeStruct((patches, own_members, share), BF16),
+        scratch_shapes=[pltpu.SemaphoreType.DMA((patches,))],
+        cost_estimate=pl.CostEstimate(
+            flops=0, bytes_accessed=4 * patches * own_members * share, transcendentals=0
+        ),
+        name="cut_share",
+    )(states)
+
+
+def place_kernel(turn, piece_ref, *refs):
+    whole_ref, sems = refs[-2:]
+    patches, _, share = piece_ref.shape
+    region = whole_ref.shape[1] // patches
+    begin = share_columns(turn, share)
+    run_copies(
+        [
+            pltpu.make_async_copy(
+                piece_ref.at[patch],
+                whole_ref.at[:, pl.ds(pl.multiple_of(patch * region + begin, LANES), share)],
+                sems.at[patch],
+            )
+            for patch in range(patches)
+        ]
+    )
+
+
+def place_piece(turn, piece, whole, points):
+    patches, own_members, share = piece.shape
+    operands = (piece,) if whole is None else (piece, whole)
+    return pl.pallas_call(
+        functools.partial(place_kernel, turn),
+        in_specs=[pl.BlockSpec(memory_space=pl.ANY)] * len(operands),
+        out_specs=pl.BlockSpec(memory_space=pl.ANY),
+        out_shape=jax.ShapeDtypeStruct((own_members, points), BF16),
+        input_output_aliases={} if whole is None else {1: 0},
+        scratch_shapes=[pltpu.SemaphoreType.DMA((patches,))],
+        cost_estimate=pl.CostEstimate(
+            flops=0, bytes_accessed=4 * patches * own_members * share, transcendentals=0
+        ),
+        name="place_piece",
+    )(*operands)
 
 
 def local(
@@ -156,10 +297,15 @@
     bootstrap_multiplicity,
 ):
     device_count = lax.axis_size("space")
+    groups = lax.axis_size("boot")
     local_rows = measurement_anomaly_matrix.shape[0]
     targets_per = measurement_region_targets.shape[1]
     slot_cap = 2 * targets_per * local_rows // device_count
-    slots, info = pack(
+    own_members, points = background_states.shape
+    members = own_members * device_count
+    region = points // device_count
+    share = region // groups
+    slots = pack(
         measurement_region_targets,
         localization_factor_scaled,
         bootstrap_multiplicity,
@@ -169,19 +315,25 @@
         device_count,
         slot_cap,
     )
-    info_got = lax.all_gather(info, "space", axis=0, tiled=False)
     rows_got = lax.all_to_all(slots, "space", split_axis=0, concat_axis=0, tiled=True)
-    background = lax.all_to_all(
-        background_states, "space", split_axis=1, concat_axis=0, tiled=True
-    )
-    blended = patch_weights(rows_got, info_got)
-    centre = jnp.mean(background.astype(F32), axis=0)
-    perturb = (background.astype(F32) - centre[None, :]).astype(BF16)
-    update = lax.dot_general(
-        blended, perturb, (((0,), (0,)), ((), ())), preferred_element_type=F32
-    )
-    analysis = (centre[None, :] + update).astype(BF16)
-    return lax.all_to_all(analysis, "space", split_axis=0, concat_axis=1, tiled=True)
+
+    own_share = cut_share(background_states, device_count, share)
+    rows_got, own_share = lax.optimization_barrier((rows_got, own_share))
+    own_share = lax.all_to_all(own_share, "space", split_axis=0, concat_axis=0, tiled=True)
+    own_share = own_share.reshape(members, share)
+    shares = [own_share]
+    for turn in range(1, groups):
+        shares.append(
+            lax.ppermute(own_share, "boot", [(g, (g - turn) % groups) for g in range(groups)])
+        )
+
+    blended = patch_weights(rows_got)
+    whole = None
+    for turn, part in enumerate(shares):
+        analysis = update_points(blended, part).reshape(device_count, own_members, share)
+        piece = lax.all_to_all(analysis, "space", split_axis=0, concat_axis=0, tiled=True)
+        whole = place_piece(turn, piece, whole, points)
+    return whole
 
 
 def solution(mesh):

time: 191 us -> 193 us (1.010)
  blocking collectives: 110 us -> 0 us
  Pallas kernels: 20.1 us -> 124 us
  starting transfers between devices: 16.5 us -> 31.2 us
  other arithmetic: 4 us -> 0 us
  local copies, waits for them, and re-layouts: 9.03 us -> 6.57 us
    pallas_call x1 -> x6, Pallas kernels: 2.84 us -> 106 us  [the longest x2 66 us: place_piece(): pl.pallas_call(functools.partial(place_kernel, turn), in_specs=[pl.BlockS...]
    all_gather x1 -> x0, blocking collectives: 55.9 us -> none  [local(): info_got = lax.all_gather(info, 'space', axis=0, tiled=False)]
    all_to_all x1 -> x0, blocking collectives: 54.3 us -> none  [local(): lax.all_to_all(analysis, 'space', split_axis=0, concat_axis=1, tiled=True)]
    all_to_all x1, waiting for transfers between devices: 28.8 us -> 1.23 us  [local(): lax.all_to_all(slots, 'space', split_axis=0, concat_axis=0, tiled=True)]
    ppermute x0 -> x1, waiting for transfers between devices: none -> 23.9 us  [local(): lax.ppermute(own_share, 'boot', [(g, (g - turn) % groups) for g in range(...]
    all_to_all x1 -> x3, starting transfers between devices: 9.16 us -> 22.2 us  [the longest x2 12.6 us: local(): lax.all_to_all(analysis, 'space', split_axis=0, concat_axis=0, tiled=True)]
    all_to_all x1 -> x3, waiting for transfers between devices: 0.01 us -> 5.39 us  [the longest x1 5.38 us: local(): lax.all_to_all(own_share, 'space', split_axis=0, concat_axis=0, tiled=True)]
    all_to_all x2 -> x0, local copies, waits for them, and re-layouts: 4.62 us -> none  [the longest x1 3.16 us: local(): lax.all_to_all(background_states, 'space', split_axis=1, concat_axis=0, t...]
  transfers between devices with their start and end apart: 2 -> 5, of which waited for: 1 -> 3; matrix products, arithmetic and copies ran while one was open for 2% -> 0% of each run, Pallas kernels for 9% -> 45%
where the time goes in v1:
time: 193 us; the launch traced here: 192 us
  Pallas kernels  124 us (64%)
  starting transfers between devices  31.2 us (16%)
  waiting for transfers between devices  30.5 us (16%)
  local copies, waits for them, and re-layouts  6.57 us (3%)
    pallas_call x2, Pallas kernels, place_piece(): pl.pallas_call(functools.partial(place_kernel, turn), in_specs=[pl.BlockS...  66 us
    pallas_call x1, Pallas kernels, cut_share(): pl.pallas_call(cut_kernel, in_specs=[pl.BlockSpec(memory_space=pltpu.HBM)...  33 us
    ppermute x1, waiting for transfers between devices, local(): lax.ppermute(own_share, 'boot', [(g, (g - turn) % groups) for g in range(...  23.9 us
    pallas_call x1, Pallas kernels, patch_weights(): pl.pallas_call(weights_kernel, out_shape=jax.ShapeDtypeStruct((members, m...  17.5 us
    all_to_all x2, starting transfers between devices, local(): lax.all_to_all(analysis, 'space', split_axis=0, concat_axis=0, tiled=True)  12.6 us
    all_to_all x1, starting transfers between devices, local(): lax.all_to_all(own_share, 'space', split_axis=0, concat_axis=0, tiled=True)  9.63 us
    all_to_all x1, starting transfers between devices, local(): lax.all_to_all(slots, 'space', split_axis=0, concat_axis=0, tiled=True)  7.38 us
    unnamed x18, local copies, waits for them, and re-layouts  6.57 us
  transfers between devices with their start and end apart: 5, of which 3 were waited for; matrix products, arithmetic and copies ran while one was open for 0% of the time, Pallas kernels for 45%

profile of v1, /device:TPU:0, one launch (start us, length us, event | category | flops | bytes accessed | tf_op | source)
XLA Modules:
  0.0 192.4 jit_solution(5641058310742678086)
XLA Ops:
  0.0 0.0 copy-start.1
  0.0 1.0 copy-done.1
  1.0 0.0 copy-start.2
  1.0 0.7 copy-done.2
  1.7 0.0 copy-start.3
  1.7 0.7 copy-done.3
  2.4 0.0 copy-start.4
  2.4 0.7 copy-done.4
  3.0 0.0 copy-start.5
  3.1 0.7 copy-done.5
  3.7 0.0 copy-start.6
  3.7 0.7 copy-done.6
  4.4 1.8 pack_rows.1
  6.3 0.0 copy-start
  6.3 1.2 copy-done
  7.4 7.4 %all-to-all-start = ((bf16[16,104,512]{2,1,0:T(8,128)(2,1)}), bf16[16,104,512]{2,1,0:T(8,128)(2,1)S(1)}, u32[]{:S(2)}, u32[]{:S(2)}) async-start(bf16[16,104,512]{2,1,0:T(8,128)(2,1)} %copy-done), calls=%async_computation | async-start | bytes 3407872 | tf_op jit(solution)/shard_map/all_to_all | solution.py:318
  14.8 33.0 %cut_share.1 = bf16[16,32,1024]{2,1,0:T(8,128)(2,1)} custom-call(bf16[32,32768]{1,0:T(8,128)(2,1)} %states_ref.1), custom_call_target="tpu_custom_call" | custom-call | bytes 2097152 | tf_op jit(solution)/shard_map/cut_share/pallas_call | solution.py:243
  47.9 1.2 all-to-all-done.rows_ref
  49.1 9.6 %all-to-all-start.1 = ((bf16[16,32,1024]{2,1,0:T(8,128)(2,1)}), bf16[16,32,1024]{2,1,0:T(8,128)(2,1)S(1)}, u32[]{:S(2)}, u32[]{:S(2)}) async-start(bf16[16,32,1024]{2,1,0:T(8,128)(2,1)} %cut_share.1), calls=%async_computation.1 | async-start | bytes 2097152 | tf_op jit(solution)/shard_map/all_to_all | solution.py:322
  58.7 17.5 %patch_weights.1.blended_ref = bf16[512,512]{1,0:T(8,128)(2,1)S(1)} custom-call(bf16[16,104,512]{2,1,0:T(8,128)(2,1)S(1)} %all-to-all-done.rows_ref), custom_call_target="tpu_custom_call" | custom-call | flops 12952010752 | bytes 1703936 | tf_op jit(solution)/shard_map/patch_weights/pallas_call | solution.py:169
  76.3 5.4 %all-to-all-done.1 = bf16[16,32,1024]{2,1,0:T(8,128)(2,1)S(1)} async-done(((bf16[16,32,1024]{2,1,0:T(8,128)(2,1)}), bf16[16,32,1024]{2,1,0:T(8,128)(2,1)S(1)}, u32[]{:S(2)}, u32[]{:S(2)}) %all-to-all-start.1) | async-done | bytes 1048608 | tf_op jit(solution)/shard_map/all_to_all | solution.py:322
  81.7 2.8 %update_points.3 = bf16[512,1024]{1,0:T(8,128)(2,1)} custom-call(bf16[512,512]{1,0:T(8,128)(2,1)S(1)} %patch_weights.1.blended_ref, bf16[512,1024]{1,0:T(8,128)(2,1)S(1)} %bitcast.5), custom_call_target="tpu_custom_call" | custom-call | flops 536870912 | bytes 2621440 | tf_op jit(solution)/shard_map/update_points/pallas_call | solution.py:194
  84.4 6.9 %all-to-all-start.3 = ((bf16[16,32,1024]{2,1,0:T(8,128)(2,1)}), bf16[16,32,1024]{2,1,0:T(8,128)(2,1)S(1)}, u32[]{:S(2)}, u32[]{:S(2)}) async-start(bf16[16,32,1024]{2,1,0:T(8,128)(2,1)} %bitcast.4), calls=%async_computation.3 | async-start | bytes 2097152 | tf_op jit(solution)/shard_map/all_to_all | solution.py:334
  91.3 1.6 collective-permute-start
  92.9 23.9 %collective-permute-done.background_ref = bf16[512,1024]{1,0:T(8,128)(2,1)S(1)} collective-permute-done((bf16[512,1024]{1,0:T(8,128)(2,1)S(1)}, bf16[512,1024]{1,0:T(8,128)(2,1)S(1)}, u32[]{:S(2)}, u32[]{:S(2)}) %collective-permute-start) | collective-permute-done | bytes 1048608 | tf_op jit(solution)/shard_map/ppermute | solution.py:327
  116.8 2.8 %update_points.2 = bf16[512,1024]{1,0:T(8,128)(2,1)} custom-call(bf16[512,512]{1,0:T(8,128)(2,1)S(1)} %patch_weights.1.blended_ref, bf16[512,1024]{1,0:T(8,128)(2,1)S(1)} %collective-permute-done.background_ref), custom_call_target="tpu_custom_call" | custom-call | flops 536870912 | bytes 2621440 | tf_op jit(solution)/shard_map/update_points/pallas_call | solution.py:194
  119.6 0.0 all-to-all-done.3.piece_ref
  119.6 0.0 copy-start.7
  119.6 5.7 %all-to-all-start.2 = ((bf16[16,32,1024]{2,1,0:T(8,128)(2,1)}), bf16[16,32,1024]{2,1,0:T(8,128)(2,1)S(1)}, u32[]{:S(2)}, u32[]{:S(2)}) async-start(bf16[16,32,1024]{2,1,0:T(8,128)(2,1)} %bitcast.3), calls=%async_computation.2 | async-start | bytes 2097152 | tf_op jit(solution)/shard_map/all_to_all | solution.py:334
  125.4 0.0 copy-done.7
  125.4 33.0 %place_piece.2.refs_0_ = bf16[32,32768]{1,0:T(8,128)(2,1)} custom-call(bf16[16,32,1024]{2,1,0:T(8,128)(2,1)} %copy-done.7), custom_call_target="tpu_custom_call" | custom-call | bytes 2097152 | tf_op jit(solution)/shard_map/place_piece/pallas_call | solution.py:276
  158.4 0.0 all-to-all-done.2.piece_ref
  158.4 0.0 copy-start.8
  158.4 1.0 copy-done.8
  159.4 33.0 %place_piece.3 = bf16[32,32768]{1,0:T(8,128)(2,1)} custom-call(bf16[16,32,1024]{2,1,0:T(8,128)(2,1)} %copy-done.8, bf16[32,32768]{1,0:T(8,128)(2,1)} %place_piece.2.refs_0_), custom_call_target="tpu_custom_call", output_to_operand_aliasing={{}: (1, {})} | custom-call | bytes 2097152 | tf_op jit(solution)/shard_map/place_piece/pallas_call | solution.py:276
Async XLA Ops:
  0.0 1.0 copy-start.1
  1.0 0.7 copy-start.2
  1.7 0.7 copy-start.3
  2.4 0.7 copy-start.4
  3.0 0.7 copy-start.5
  3.7 0.7 copy-start.6
  6.3 1.2 copy-start
  7.4 41.6 %all-to-all-start = ((bf16[16,104,512]{2,1,0:T(8,128)(2,1)}), bf16[16,104,512]{2,1,0:T(8,128)(2,1)S(1)}, u32[]{:S(2)}, u32[]{:S(2)}) async-start(bf16[16,104,512]{2,1,0:T(8,128)(2,1)} %copy-done), calls=%async_computation | async-start | bytes 3407872 | tf_op jit(solution)/shard_map/all_to_all | solution.py:318
  49.1 32.6 %all-to-all-start.1 = ((bf16[16,32,1024]{2,1,0:T(8,128)(2,1)}), bf16[16,32,1024]{2,1,0:T(8,128)(2,1)S(1)}, u32[]{:S(2)}, u32[]{:S(2)}) async-start(bf16[16,32,1024]{2,1,0:T(8,128)(2,1)} %cut_share.1), calls=%async_computation.1 | async-start | bytes 2097152 | tf_op jit(solution)/shard_map/all_to_all | solution.py:322
  84.4 35.2 %all-to-all-start.3 = ((bf16[16,32,1024]{2,1,0:T(8,128)(2,1)}), bf16[16,32,1024]{2,1,0:T(8,128)(2,1)S(1)}, u32[]{:S(2)}, u32[]{:S(2)}) async-start(bf16[16,32,1024]{2,1,0:T(8,128)(2,1)} %bitcast.4), calls=%async_computation.3 | async-start | bytes 2097152 | tf_op jit(solution)/shard_map/all_to_all | solution.py:334
  91.3 25.5 %collective-permute-start = (bf16[512,1024]{1,0:T(8,128)(2,1)S(1)}, bf16[512,1024]{1,0:T(8,128)(2,1)S(1)}, u32[]{:S(2)}, u32[]{:S(2)}) collective-permute-start(bf16[512,1024]{1,0:T(8,128)(2,1)S(1)} %bitcast.6), channel_id=1, source_target_pairs={{0,16},{16,0},{1,17},{17,1},{2,18},{18,2},{3,19},{19,3},{4,20},{20... | collective-permute-start | bytes 3145736 | tf_op jit(solution)/shard_map/ppermute | solution.py:327
  119.6 5.8 %copy-start.7 = (bf16[16,32,1024]{2,1,0:T(8,128)(2,1)}, bf16[16,32,1024]{2,1,0:T(8,128)(2,1)S(1)}, u32[]{:S(2)}) copy-start(bf16[16,32,1024]{2,1,0:T(8,128)(2,1)S(1)} %all-to-all-done.3.piece_ref) | copy-start | bytes 3145732
  119.6 38.8 %all-to-all-start.2 = ((bf16[16,32,1024]{2,1,0:T(8,128)(2,1)}), bf16[16,32,1024]{2,1,0:T(8,128)(2,1)S(1)}, u32[]{:S(2)}, u32[]{:S(2)}) async-start(bf16[16,32,1024]{2,1,0:T(8,128)(2,1)} %bitcast.3), calls=%async_computation.2 | async-start | bytes 2097152 | tf_op jit(solution)/shard_map/all_to_all | solution.py:334
  158.4 1.0 copy-start.8

commit v2 on v1

v2 whole, which is shorter than its diff:
```python
import functools

import jax
import jax.numpy as jnp
from jax import lax
from jax.experimental import pallas as pl
from jax.experimental.pallas import tpu as pltpu
from jax.sharding import PartitionSpec as P

NS_STEPS = 6
LANES = 128
TAIL = 8
MOST_PERMUTES = 16
VMEM_BYTES = 48 * 1024 * 1024
F32 = jnp.float32
BF16 = jnp.bfloat16


def pack_kernel(*refs):
    sources, refs = refs[:6], refs[6:]
    fetched, info_ref, rank_ref, sems = refs[-9:-3], refs[-3], refs[-2], refs[-1]
    slots_refs = refs[:-9]
    copies = [
        pltpu.make_async_copy(source, target, sems.at[i])
        for i, (source, target) in enumerate(zip(sources, fetched))
    ]
    for copy in copies:
        copy.start()
    for copy in copies:
        copy.wait()
    targets_ref, local_ref, mult_ref, prec_ref, dep_ref, rows_ref = fetched
    patches = len(slots_refs)
    cap = slots_refs[0].shape[0] - TAIL
    count, members = rows_ref.shape
    me = lax.axis_index("space")
    mult = mult_ref[...].reshape(1, count).astype(F32)
    prec = prec_ref[...].reshape(1, count)
    weight = local_ref[...].astype(F32) / 1024.0 * (mult * prec)
    weight = weight.astype(BF16).astype(F32)
    dep = dep_ref[...].astype(F32).reshape(1, count)
    patch_id = lax.broadcasted_iota(jnp.int32, (patches, count), 0)
    first = patch_id == targets_ref[0:1, :]
    second = patch_id == targets_ref[1:2, :]
    named = jnp.logical_or(first, second)
    earlier = lax.broadcasted_iota(jnp.int32, (count, count), 0) < lax.broadcasted_iota(
        jnp.int32, (count, count), 1
    )
    rank = jnp.dot(
        named.astype(F32).astype(BF16), earlier.astype(F32).astype(BF16), preferred_element_type=F32
    )
    rank = jnp.where(named, rank, -1.0)
    by_patch = jnp.where(first, weight[0:1, :], jnp.where(second, weight[1:2, :], 0.0))
    slot_id = lax.broadcasted_iota(jnp.int32, (cap, count), 0).astype(F32)
    lane = lax.broadcasted_iota(jnp.int32, (cap, LANES), 1)
    info = jnp.zeros((cap, LANES), F32)
    rows = rows_ref[...]
    for patch in range(patches):
        pick = jnp.where(slot_id == rank[patch : patch + 1, :], 1.0, 0.0)
        weight_col = jnp.sum(pick * by_patch[patch : patch + 1, :], axis=1, keepdims=True)
        dep_col = jnp.sum(pick * dep, axis=1, keepdims=True)
        info = jnp.where(lane == patch, weight_col, info)
        info = jnp.where(lane == patches + patch, dep_col, info)
    info_ref[...] = jnp.zeros((LANES, LANES), F32)
    info_ref[0:cap, :] = info
    info_ref[...] = info_ref[...].T
    rank_ref[...] = rank
    tail_id = lax.broadcasted_iota(jnp.int32, (TAIL, LANES), 0)
    blank = jnp.zeros((TAIL, members - LANES), F32)
    for turn, slots_ref in enumerate(slots_refs):
        patch = me ^ turn
        pick = jnp.where(slot_id == rank_ref[pl.ds(patch, 1), :], 1.0, 0.0)
        block = jnp.dot(pick.astype(BF16), rows, preferred_element_type=F32)
        tail = jnp.where(
            tail_id == 0,
            info_ref[pl.ds(patch, 1), :],
            jnp.where(tail_id == 1, info_ref[pl.ds(patches + patch, 1), :], 0.0),
        )
        tail = jnp.concatenate([tail, blank], axis=1)
        slots_ref[...] = jnp.concatenate([block, tail], axis=0).astype(BF16)


def pack(targets, local, mult, prec, dep, rows, patches, cap):
    count, members = rows.shape
    operands = (targets.T, local.T, mult, prec, dep, rows)
    return pl.pallas_call(
        pack_kernel,
        out_shape=[jax.ShapeDtypeStruct((cap + TAIL, members), BF16)] * patches,
        in_specs=[pl.BlockSpec(memory_space=pltpu.HBM)] * len(operands),
        scratch_shapes=[pltpu.VMEM(operand.shape, operand.dtype) for operand in operands]
        + [
            pltpu.VMEM((LANES, LANES), F32),
            pltpu.VMEM((patches, count), F32),
            pltpu.SemaphoreType.DMA((len(operands),)),
        ],
        compiler_params=pltpu.CompilerParams(vmem_limit_bytes=VMEM_BYTES),
        cost_estimate=pl.CostEstimate(
            flops=2 * patches * cap * count * members,
            bytes_accessed=2 * (patches * cap + count) * members,
            transcendentals=0,
        ),
        name="pack_rows",
    )(*operands)


def halves(value):
    high = value.astype(BF16)
    return high, (value - high.astype(F32)).astype(BF16)


def product(left_high, left_low, right_high, right_low):
    dot = functools.partial(jnp.dot, preferred_element_type=F32)
    return dot(left_high, right_high) + (dot(left_high, right_low) + dot(left_low, right_high))


def weights_kernel(*refs):
    rows_refs, blended_ref, info_ref = refs[:-8], refs[-8], refs[-7]
    y_high, y_low, z_high, z_low, f_high, f_low = refs[-6:]
    sources = len(rows_refs)
    depth, members = rows_refs[0].shape
    cap = depth - TAIL
    for source in range(sources):
        tail = rows_refs[source][...].astype(F32)[cap:depth, 0:LANES]
        info_ref[source : source + 1, :] = tail[0:1, :]
        info_ref[sources + source : sources + source + 1, :] = tail[1:2, :]
    info = info_ref[...].T[0:depth, :]
    real = lax.broadcasted_iota(jnp.int32, (depth, LANES), 0) < cap
    info = jnp.where(real, info, 0.0)
    gram = jnp.zeros((members, members), F32)
    drive = jnp.zeros((1, members), F32)
    for source in range(sources):
        weight_col = info[:, source : source + 1]
        dep_col = info[:, sources + source : sources + source + 1]
        rows = rows_refs[source][...]
        scaled = (weight_col * rows.astype(F32)).astype(BF16)
        gram += lax.dot_general(rows, scaled, (((0,), (0,)), ((), ())), preferred_element_type=F32)
        drive += jnp.sum(dep_col * scaled.astype(F32), axis=0, keepdims=True)

    row_id = lax.broadcasted_iota(jnp.int32, (members, members), 0)
    col_id = lax.broadcasted_iota(jnp.int32, (members, members), 1)
    diagonal = row_id == col_id
    identity = jnp.where(diagonal, 1.0, 0.0)
    shifted = identity + gram / (members - 1.0)
    squares = jnp.sum(jnp.sum(shifted * shifted, axis=0, keepdims=True), axis=1, keepdims=True)
    frobenius = jnp.sqrt(squares)
    current = shifted / frobenius

    def put(high_ref, low_ref, value):
        high_ref[...], low_ref[...] = halves(value)

    def factor_of(zy):
        return 1.5 * identity - 0.5 * zy

    first = factor_of(current)
    put(y_high, y_low, current)
    put(f_high, f_low, first)
    put(z_high, z_low, first)
    put(y_high, y_low, product(y_high[...], y_low[...], f_high[...], f_low[...]))

    def step(_, carry):
        zy = product(z_high[...], z_low[...], y_high[...], y_low[...])
        put(f_high, f_low, factor_of(zy))
        put(y_high, y_low, product(y_high[...], y_low[...], f_high[...], f_low[...]))
        put(z_high, z_low, product(f_high[...], f_low[...], z_high[...], z_low[...]))
        return carry

    lax.fori_loop(1, NS_STEPS - 1, step, 0)
    zy = product(z_high[...], z_low[...], y_high[...], y_low[...])
    put(f_high, f_low, factor_of(zy))
    root = product(f_high[...], f_low[...], z_high[...], z_low[...]) / jnp.sqrt(frobenius)

    drive_col = jnp.sum(jnp.where(diagonal, drive, 0.0), axis=1, keepdims=True)
    inner = jnp.sum(root * drive_col, axis=0, keepdims=True)
    inner_col = jnp.sum(jnp.where(diagonal, inner, 0.0), axis=1, keepdims=True)
    mean_weight = jnp.sum(root * inner_col, axis=0, keepdims=True) / (members - 1.0)
    blended_ref[...] = (root + mean_weight).astype(BF16)


def patch_weights(rows):
    sources = len(rows)
    depth, members = rows[0].shape
    half = pltpu.VMEM((members, members), BF16)
    return pl.pallas_call(
        weights_kernel,
        out_shape=jax.ShapeDtypeStruct((members, members), BF16),
        scratch_shapes=[pltpu.VMEM((LANES, LANES), F32)] + [half] * 6,
        compiler_params=pltpu.CompilerParams(vmem_limit_bytes=VMEM_BYTES),
        cost_estimate=pl.CostEstimate(
            flops=2 * members * members * (sources * depth + 45 * members),
            bytes_accessed=2 * sources * depth * members,
            transcendentals=0,
        ),
        name="patch_weights",
    )(*rows)


def update_kernel(blended_ref, background_ref, *refs):
    analysis_refs, whole_ref = refs[:-1], refs[-1]
    me = lax.axis_index("space")
    rows = analysis_refs[0].shape[0]
    members, points = background_ref.shape
    tile = min(points, 256)
    for begin in range(0, points, tile):
        columns = slice(begin, begin + tile)
        background = background_ref[:, columns].astype(F32)
        centre = jnp.sum(background, axis=0, keepdims=True) / members
        perturb = (background - centre).astype(BF16)
        update = jnp.dot(blended_ref[...], perturb, preferred_element_type=F32)
        whole_ref[:, columns] = centre + update
    for turn, analysis_ref in enumerate(analysis_refs):
        begin = pl.multiple_of((me ^ turn) * rows, rows)
        analysis_ref[...] = whole_ref[pl.ds(begin, rows), :].astype(BF16)


def update_points(blended, background, holders):
    members, points = background.shape
    return pl.pallas_call(
        update_kernel,
        out_shape=[jax.ShapeDtypeStruct((members // holders, points), BF16)] * holders,
        scratch_shapes=[pltpu.VMEM((members, points), F32)],
        compiler_params=pltpu.CompilerParams(vmem_limit_bytes=VMEM_BYTES),
        cost_estimate=pl.CostEstimate(
            flops=2 * members * members * points,
            bytes_accessed=4 * members * points + 2 * members * members,
            transcendentals=0,
        ),
        name="update_points",
    )(blended, background)


def cut_kernel(states_ref, *cut_refs):
    me = lax.axis_index("space")
    share = cut_refs[0].shape[1]
    region = states_ref.shape[1] // len(cut_refs)
    offset = lax.axis_index("boot") * share
    for turn, cut_ref in enumerate(cut_refs):
        begin = pl.multiple_of((me ^ turn) * region + offset, LANES)
        cut_ref[...] = states_ref[:, pl.ds(begin, share)]


def cut_share(states, patches, share):
    own_members = states.shape[0]
    return pl.pallas_call(
        cut_kernel,
        out_shape=[jax.ShapeDtypeStruct((own_members, share), BF16)] * patches,
        compiler_params=pltpu.CompilerParams(vmem_limit_bytes=VMEM_BYTES),
        cost_estimate=pl.CostEstimate(
            flops=0, bytes_accessed=4 * patches * own_members * share, transcendentals=0
        ),
        name="cut_share",
    )(states)


def join_kernel(*refs):
    piece_refs, joined_ref, whole_ref = refs[:-2], refs[-2], refs[-1]
    me = lax.axis_index("space")
    rows = piece_refs[0].shape[0]
    for turn, piece_ref in enumerate(piece_refs):
        begin = pl.multiple_of((me ^ turn) * rows, rows)
        whole_ref[pl.ds(begin, rows), :] = piece_ref[...].astype(F32)
    joined_ref[...] = whole_ref[...].astype(BF16)


def join_members(pieces):
    rows, share = pieces[0].shape
    members = rows * len(pieces)
    return pl.pallas_call(
        join_kernel,
        out_shape=jax.ShapeDtypeStruct((members, share), BF16),
        scratch_shapes=[pltpu.VMEM((members, share), F32)],
        compiler_params=pltpu.CompilerParams(vmem_limit_bytes=VMEM_BYTES),
        cost_estimate=pl.CostEstimate(
            flops=0, bytes_accessed=4 * members * share, transcendentals=0
        ),
        name="join_members",
    )(*pieces)


def place_kernel(groups, *refs):
    piece_refs, whole_ref = refs[:-1], refs[-1]
    patches = len(piece_refs) // groups
    share = piece_refs[0].shape[1]
    me, group = lax.axis_index("space"), lax.axis_index("boot")
    for place, piece_ref in enumerate(piece_refs):
        shift, turn = divmod(place, patches)
        offset = lax.rem(group + shift, groups) * share
        begin = pl.multiple_of((me ^ turn) * groups * share + offset, LANES)
        whole_ref[:, pl.ds(begin, share)] = piece_ref[...]


def place_pieces(pieces, groups):
    own_members, share = pieces[0].shape
    points = share * len(pieces)
    return pl.pallas_call(
        functools.partial(place_kernel, groups),
        out_shape=jax.ShapeDtypeStruct((own_members, points), BF16),
        compiler_params=pltpu.CompilerParams(vmem_limit_bytes=VMEM_BYTES),
        cost_estimate=pl.CostEstimate(
            flops=0, bytes_accessed=4 * own_members * points, transcendentals=0
        ),
        name="place_pieces",
    )(*pieces)


def swap(pieces):
    devices = len(pieces)
    if devices > MOST_PERMUTES:
        order = lax.axis_index("space") ^ jnp.arange(devices, dtype=jnp.int32)
        stacked = jnp.stack(pieces)[order]
        stacked = lax.all_to_all(stacked, "space", split_axis=0, concat_axis=0, tiled=True)[order]
        return [stacked[turn] for turn in range(devices)]
    return [pieces[0]] + [
        lax.ppermute(pieces[turn], "space", [(d, d ^ turn) for d in range(devices)])
        for turn in range(1, devices)
    ]


def local(
    background_states,
    measurement_anomaly_matrix,
    departure_vector,
    measurement_precision,
    measurement_region_targets,
    localization_factor_scaled,
    bootstrap_multiplicity,
):
    device_count = lax.axis_size("space")
    groups = lax.axis_size("boot")
    local_rows = measurement_anomaly_matrix.shape[0]
    targets_per = measurement_region_targets.shape[1]
    slot_cap = 2 * targets_per * local_rows // device_count
    own_members, points = background_states.shape
    region = points // device_count
    share = region // groups
    slots = pack(
        measurement_region_targets,
        localization_factor_scaled,
        bootstrap_multiplicity,
        measurement_precision,
        departure_vector,
        measurement_anomaly_matrix,
        device_count,
        slot_cap,
    )
    cuts = cut_share(background_states, device_count, share)
    rows_got = swap(slots)
    middle = 5 * device_count // 8
    rows_got[middle], cuts = lax.optimization_barrier((rows_got[middle], cuts))
    own_share = join_members(swap(cuts))
    shares = [own_share]
    for turn in range(1, groups):
        shares.append(
            lax.ppermute(own_share, "boot", [(g, (g - turn) % groups) for g in range(groups)])
        )

    blended = patch_weights(rows_got)
    pieces = []
    for part in shares:
        pieces += swap(update_points(blended, part, device_count))
    return place_pieces(pieces, groups)


def solution(mesh):
    in_specs = (
        P("space", None),
        P("space", None),
        P("space"),
        P("space"),
        P("space", None),
        P("space", None),
        P(("boot", "space")),
    )
    out_specs = P(("boot", "space"), None)
    return jax.shard_map(local, mesh=mesh, in_specs=in_specs, out_specs=out_specs, check_vma=False)
```

time: 193 us -> 165 us (0.85)
  Pallas kernels: 124 us -> 23.4 us
  starting transfers between devices: 31.2 us -> 104 us
  local copies, waits for them, and re-layouts: 6.57 us -> 4.56 us
    ppermute x0 -> x60, starting transfers between devices: none -> 102 us  [swap(): lax.ppermute(pieces[turn], 'space', [(d, d ^ turn) for d in range(devices)])]
    pallas_call x6, Pallas kernels: 106 us -> 5.64 us  [the longest x2 1.92 us: update_points(): pl.pallas_call(update_kernel, out_shape=[jax.ShapeDtypeStruct((members //...]
    ppermute x0 -> x60, waiting for transfers between devices: none -> 32.1 us  [swap(): lax.ppermute(pieces[turn], 'space', [(d, d ^ turn) for d in range(devices)])]
    all_to_all x4 -> x0, starting transfers between devices: 29.6 us -> none  [the longest x2 12.6 us: local(): lax.all_to_all(analysis, 'space', split_axis=0, concat_axis=0, tiled=True)]
    ppermute x1, waiting for transfers between devices: 23.9 us -> 0.01 us  [local(): lax.ppermute(own_share, 'boot', [(g, (g - turn) % groups) for g in range(...]
    all_to_all x4 -> x0, waiting for transfers between devices: 6.62 us -> none  [the longest x1 5.38 us: local(): lax.all_to_all(own_share, 'space', split_axis=0, concat_axis=0, tiled=True)]
    unnamed x18 -> x14, local copies, waits for them, and re-layouts: 6.57 us -> 4.56 us
  transfers between devices with their start and end apart: 5 -> 61, of which waited for: 3 -> 9; matrix products, arithmetic and copies ran while one was open for 0% -> 0% of each run, Pallas kernels for 45% -> 12%
where the time goes in v2:
time: 165 us; the launch traced here: 164 us
  starting transfers between devices  104 us (63%)
  waiting for transfers between devices  32.1 us (19%)
  Pallas kernels  23.4 us (14%)
  local copies, waits for them, and re-layouts  4.56 us (3%)
    ppermute x60, starting transfers between devices, swap(): lax.ppermute(pieces[turn], 'space', [(d, d ^ turn) for d in range(devices)])  102 us
    ppermute x60, waiting for transfers between devices, swap(): lax.ppermute(pieces[turn], 'space', [(d, d ^ turn) for d in range(devices)])  32.1 us
    pallas_call x1, Pallas kernels, patch_weights(): pl.pallas_call(weights_kernel, out_shape=jax.ShapeDtypeStruct((members, m...  17.7 us
    unnamed x14, local copies, waits for them, and re-layouts  4.56 us
  transfers between devices with their start and end apart: 61, of which 9 were waited for; matrix products, arithmetic and copies ran while one was open for 0% of the time, Pallas kernels for 12%

profile of v2, /device:TPU:0, one launch (start us, length us, event | category | flops | bytes accessed | tf_op | source)
XLA Modules:
  0.0 163.7 jit_solution(5983192442232136089)
XLA Ops:
  0.0 1.1 copy-done.1
  4.6 1.9 %pack_rows.1 = (bf16[104,512]{1,0:T(8,128)(2,1)S(1)}, bf16[104,512]{1,0:T(8,128)(2,1)S(1)}, bf16[104,512]{1,0:T(8,128)(2,1)S(1)}, bf16[104,512]{1,0:T(8,128)(2,1...) custom-call(s32[2,384]{1,0:T(2,128)S(1)} %bitcast.2, ...), custom_call_target="tpu_custom_call" | custom-call | flops 603979776 | bytes 1966080 | tf_op jit(solution)/shard_map/pack_rows/pallas_call | solution.py:85
  7.0 2.6 %collective-permute-start.1 = (bf16[104,512]{1,0:T(8,128)(2,1)S(1)}, bf16[104,512]{1,0:T(8,128)(2,1)S(1)}, u32[]{:S(2)}, u32[]{:S(2)}) collective-permute-start(bf16[104,512]{1,0:T(8,128)(2,1)S(1)} %get-tuple-element.88), channel_id=1, source_target_pairs={{0,2},{1,3},{2,0},{3,1},{4,6},{5,7},{6,4},{7,5},{8,10},{9,11},{10,... | collective-permute-start | bytes 319496 | tf_op jit(solution)/shard_map/ppermute | solution.py:312
  9.6 1.8 %collective-permute-start.3 = (bf16[104,512]{1,0:T(8,128)(2,1)S(1)}, bf16[104,512]{1,0:T(8,128)(2,1)S(1)}, u32[]{:S(2)}, u32[]{:S(2)}) collective-permute-start(bf16[104,512]{1,0:T(8,128)(2,1)S(1)} %get-tuple-element.90), channel_id=1, source_target_pairs={{0,4},{1,5},{2,6},{3,7},{4,0},{5,1},{6,2},{7,3},{8,12},{9,13},{10,... | collective-permute-start | bytes 319496 | tf_op jit(solution)/shard_map/ppermute | solution.py:312
  11.4 3.5 %collective-permute-start.9 = (bf16[104,512]{1,0:T(8,128)(2,1)S(1)}, bf16[104,512]{1,0:T(8,128)(2,1)S(1)}, u32[]{:S(2)}, u32[]{:S(2)}) collective-permute-start(bf16[104,512]{1,0:T(8,128)(2,1)S(1)} %get-tuple-element.96), channel_id=1, source_target_pairs={{0,10},{1,11},{2,8},{3,9},{4,14},{5,15},{6,12},{7,13},{8,2},{9,3},... | collective-permute-start | bytes 319496 | tf_op jit(solution)/shard_map/ppermute | solution.py:312
  15.0 1.4 collective-permute-start.5
  16.4 1.5 collective-permute-start.6
  17.8 3.7 %collective-permute-start.7 = (bf16[104,512]{1,0:T(8,128)(2,1)S(1)}, bf16[104,512]{1,0:T(8,128)(2,1)S(1)}, u32[]{:S(2)}, u32[]{:S(2)}) collective-permute-start(bf16[104,512]{1,0:T(8,128)(2,1)S(1)} %get-tuple-element.94), channel_id=1, source_target_pairs={{0,8},{1,9},{2,10},{3,11},{4,12},{5,13},{6,14},{7,15},{8,0},{9,1},... | collective-permute-start | bytes 319496 | tf_op jit(solution)/shard_map/ppermute | solution.py:312
  21.9 3.3 %collective-permute-done.5.refs_6_ = bf16[104,512]{1,0:T(8,128)(2,1)S(1)} collective-permute-done((bf16[104,512]{1,0:T(8,128)(2,1)S(1)}, bf16[104,512]{1,0:T(8,128)(2,1)S(1)}, u32[]{:S(2)}, u32[]{:S(2)}) %collective-permute-start.5) | collective-permute-done | bytes 106528 | tf_op jit(solution)/shard_map/ppermute | solution.py:312
  25.2 2.9 %collective-permute-start.16 = (bf16[32,1024]{1,0:T(8,128)(2,1)S(1)}, bf16[32,1024]{1,0:T(8,128)(2,1)S(1)}, u32[]{:S(2)}, u32[]{:S(2)}) collective-permute-start(bf16[32,1024]{1,0:T(8,128)(2,1)S(1)} %get-tuple-element.121), channel_id=1, source_target_pairs={{0,2},{1,3},{2,0},{3,1},{4,6},{5,7},{6,4},{7,5},{8,10},{9,11},{10,... | collective-permute-start | bytes 196616 | tf_op jit(solution)/shard_map/ppermute | solution.py:312
  28.1 1.5 collective-permute-done.6.refs_7_
  30.3 1.8 %collective-permute-done.8.refs_9_ = bf16[104,512]{1,0:T(8,128)(2,1)S(1)} collective-permute-done((bf16[104,512]{1,0:T(8,128)(2,1)S(1)}, bf16[104,512]{1,0:T(8,128)(2,1)S(1)}, u32[]{:S(2)}, u32[]{:S(2)}) %collective-permute-start.8) | collective-permute-done | bytes 106528 | tf_op jit(solution)/shard_map/ppermute | solution.py:312
  32.1 1.6 collective-permute-start.20
  34.7 1.8 %collective-permute-start.22 = (bf16[32,1024]{1,0:T(8,128)(2,1)S(1)}, bf16[32,1024]{1,0:T(8,128)(2,1)S(1)}, u32[]{:S(2)}, u32[]{:S(2)}) collective-permute-start(bf16[32,1024]{1,0:T(8,128)(2,1)S(1)} %get-tuple-element.127), channel_id=1, source_target_pairs={{0,8},{1,9},{2,10},{3,11},{4,12},{5,13},{6,14},{7,15},{8,0},{9,1},... | collective-permute-start | bytes 196616 | tf_op jit(solution)/shard_map/ppermute | solution.py:312
  37.4 1.9 %collective-permute-start.24 = (bf16[32,1024]{1,0:T(8,128)(2,1)S(1)}, bf16[32,1024]{1,0:T(8,128)(2,1)S(1)}, u32[]{:S(2)}, u32[]{:S(2)}) collective-permute-start(bf16[32,1024]{1,0:T(8,128)(2,1)S(1)} %get-tuple-element.129), channel_id=1, source_target_pairs={{0,10},{1,11},{2,8},{3,9},{4,14},{5,15},{6,12},{7,13},{8,2},{9,3},... | collective-permute-start | bytes 196616 | tf_op jit(solution)/shard_map/ppermute | solution.py:312
  39.3 1.6 collective-permute-start.25
  40.9 3.2 %collective-permute-start.26 = (bf16[32,1024]{1,0:T(8,128)(2,1)S(1)}, bf16[32,1024]{1,0:T(8,128)(2,1)S(1)}, u32[]{:S(2)}, u32[]{:S(2)}) collective-permute-start(bf16[32,1024]{1,0:T(8,128)(2,1)S(1)} %get-tuple-element.131), channel_id=1, source_target_pairs={{0,12},{1,13},{2,14},{3,15},{4,8},{5,9},{6,10},{7,11},{8,4},{9,5},... | collective-permute-start | bytes 196616 | tf_op jit(solution)/shard_map/ppermute | solution.py:312
  44.2 3.6 %collective-permute-start.27 = (bf16[32,1024]{1,0:T(8,128)(2,1)S(1)}, bf16[32,1024]{1,0:T(8,128)(2,1)S(1)}, u32[]{:S(2)}, u32[]{:S(2)}) collective-permute-start(bf16[32,1024]{1,0:T(8,128)(2,1)S(1)} %get-tuple-element.132), channel_id=1, source_target_pairs={{0,13},{1,12},{2,15},{3,14},{4,9},{5,8},{6,11},{7,10},{8,5},{9,4},... | collective-permute-start | bytes 196616 | tf_op jit(solution)/shard_map/ppermute | solution.py:312
  48.5 3.1 %collective-permute-start.28 = (bf16[32,1024]{1,0:T(8,128)(2,1)S(1)}, bf16[32,1024]{1,0:T(8,128)(2,1)S(1)}, u32[]{:S(2)}, u32[]{:S(2)}) collective-permute-start(bf16[32,1024]{1,0:T(8,128)(2,1)S(1)} %get-tuple-element.133), channel_id=1, source_target_pairs={{0,14},{1,15},{2,12},{3,13},{4,10},{5,11},{6,8},{7,9},{8,6},{9,7},... | collective-permute-start | bytes 196616 | tf_op jit(solution)/shard_map/ppermute | solution.py:312
  51.6 2.0 %collective-permute-start.29 = (bf16[32,1024]{1,0:T(8,128)(2,1)S(1)}, bf16[32,1024]{1,0:T(8,128)(2,1)S(1)}, u32[]{:S(2)}, u32[]{:S(2)}) collective-permute-start(bf16[32,1024]{1,0:T(8,128)(2,1)S(1)} %get-tuple-element.134), channel_id=1, source_target_pairs={{0,15},{1,14},{2,13},{3,12},{4,11},{5,10},{6,9},{7,8},{8,7},{9,6},... | collective-permute-start | bytes 196616 | tf_op jit(solution)/shard_map/ppermute | solution.py:312
  53.6 1.9 %collective-permute-start.11 = (bf16[104,512]{1,0:T(8,128)(2,1)S(1)}, bf16[104,512]{1,0:T(8,128)(2,1)S(1)}, u32[]{:S(2)}, u32[]{:S(2)}) collective-permute-start(bf16[104,512]{1,0:T(8,128)(2,1)S(1)} %get-tuple-element.115), channel_id=1, source_target_pairs={{0,12},{1,13},{2,14},{3,15},{4,8},{5,9},{6,10},{7,11},{8,4},{9,5},... | collective-permute-start | bytes 319496 | tf_op jit(solution)/shard_map/ppermute | solution.py:312
  55.5 1.7 %collective-permute-start.12 = (bf16[104,512]{1,0:T(8,128)(2,1)S(1)}, bf16[104,512]{1,0:T(8,128)(2,1)S(1)}, u32[]{:S(2)}, u32[]{:S(2)}) collective-permute-start(bf16[104,512]{1,0:T(8,128)(2,1)S(1)} %get-tuple-element.116), channel_id=1, source_target_pairs={{0,13},{1,12},{2,15},{3,14},{4,9},{5,8},{6,11},{7,10},{8,5},{9,4},... | collective-permute-start | bytes 319496 | tf_op jit(solution)/shard_map/ppermute | solution.py:312
  57.2 2.5 %collective-permute-start.13 = (bf16[104,512]{1,0:T(8,128)(2,1)S(1)}, bf16[104,512]{1,0:T(8,128)(2,1)S(1)}, u32[]{:S(2)}, u32[]{:S(2)}) collective-permute-start(bf16[104,512]{1,0:T(8,128)(2,1)S(1)} %get-tuple-element.117), channel_id=1, source_target_pairs={{0,14},{1,15},{2,12},{3,13},{4,10},{5,11},{6,8},{7,9},{8,6},{9,7},... | collective-permute-start | bytes 319496 | tf_op jit(solution)/shard_map/ppermute | solution.py:312
  59.7 2.0 %collective-permute-start.14 = (bf16[104,512]{1,0:T(8,128)(2,1)S(1)}, bf16[104,512]{1,0:T(8,128)(2,1)S(1)}, u32[]{:S(2)}, u32[]{:S(2)}) collective-permute-start(bf16[104,512]{1,0:T(8,128)(2,1)S(1)} %get-tuple-element.118), channel_id=1, source_target_pairs={{0,15},{1,14},{2,13},{3,12},{4,11},{5,10},{6,9},{7,8},{8,7},{9,6},... | collective-permute-start | bytes 319496 | tf_op jit(solution)/shard_map/ppermute | solution.py:312
  61.9 13.4 %collective-permute-done.10.refs_11_ = bf16[104,512]{1,0:T(8,128)(2,1)S(1)} collective-permute-done((bf16[104,512]{1,0:T(8,128)(2,1)S(1)}, bf16[104,512]{1,0:T(8,128)(2,1)S(1)}, u32[]{:S(2)}, u32[]{:S(2)}) %collective-permute-start.10) | collective-permute-done | bytes 106528 | tf_op jit(solution)/shard_map/ppermute | solution.py:312
  75.3 1.5 collective-permute-start.45
  76.9 17.7 %patch_weights.1.blended_ref = bf16[512,512]{1,0:T(8,128)(2,1)S(1)} custom-call(bf16[104,512]{1,0:T(8,128)(2,1)S(1)} %get-tuple-element.86.refs_0_, bf16[104,512]{1,0:T(8,128)(2,1)S(1)} %collective-permute-done.refs_1_, bf16[104,512]{1,0:T(8,128)(2,1)S(1)} %collective-permute-done.1.refs_2_, bf16[104,512]{1,0:T(8,128)(2,1)S(1)} %collective-permute-done.2.refs_3_, ...), custom_call_target="tpu_custom_call" | custom-call | flops 12952010752 | bytes 1703936 | tf_op jit(solution)/shard_map/patch_weights/pallas_call | solution.py:182
  97.5 8.1 %collective-permute-start.33 = (bf16[32,1024]{1,0:T(8,128)(2,1)S(1)}, bf16[32,1024]{1,0:T(8,128)(2,1)S(1)}, u32[]{:S(2)}, u32[]{:S(2)}) collective-permute-start(bf16[32,1024]{1,0:T(8,128)(2,1)S(1)} %get-tuple-element.139), channel_id=1, source_target_pairs={{0,4},{1,5},{2,6},{3,7},{4,0},{5,1},{6,2},{7,3},{8,12},{9,13},{10,... | collective-permute-start | bytes 196616 | tf_op jit(solution)/shard_map/ppermute | solution.py:312
  105.7 3.4 %collective-permute-start.35 = (bf16[32,1024]{1,0:T(8,128)(2,1)S(1)}, bf16[32,1024]{1,0:T(8,128)(2,1)S(1)}, u32[]{:S(2)}, u32[]{:S(2)}) collective-permute-start(bf16[32,1024]{1,0:T(8,128)(2,1)S(1)} %get-tuple-element.141), channel_id=1, source_target_pairs={{0,6},{1,7},{2,4},{3,5},{4,2},{5,3},{6,0},{7,1},{8,14},{9,15},{10,... | collective-permute-start | bytes 196616 | tf_op jit(solution)/shard_map/ppermute | solution.py:312
  109.8 1.2 collective-permute-start.37
  111.0 1.1 collective-permute-start.38
  112.1 3.7 %collective-permute-start.39 = (bf16[32,1024]{1,0:T(8,128)(2,1)S(1)}, bf16[32,1024]{1,0:T(8,128)(2,1)S(1)}, u32[]{:S(2)}, u32[]{:S(2)}) collective-permute-start(bf16[32,1024]{1,0:T(8,128)(2,1)S(1)} %get-tuple-element.145), channel_id=1, source_target_pairs={{0,10},{1,11},{2,8},{3,9},{4,14},{5,15},{6,12},{7,13},{8,2},{9,3},... | collective-permute-start | bytes 196616 | tf_op jit(solution)/shard_map/ppermute | solution.py:312
  116.4 2.3 %collective-permute-done.37.refs_8_ = bf16[32,1024]{1,0:T(8,128)(2,1)S(1)} collective-permute-done((bf16[32,1024]{1,0:T(8,128)(2,1)S(1)}, bf16[32,1024]{1,0:T(8,128)(2,1)S(1)}, u32[]{:S(2)}, u32[]{:S(2)}) %collective-permute-start.37) | collective-permute-done | bytes 65568 | tf_op jit(solution)/shard_map/ppermute | solution.py:312
  118.7 5.4 %collective-permute-start.41 = (bf16[32,1024]{1,0:T(8,128)(2,1)S(1)}, bf16[32,1024]{1,0:T(8,128)(2,1)S(1)}, u32[]{:S(2)}, u32[]{:S(2)}) collective-permute-start(bf16[32,1024]{1,0:T(8,128)(2,1)S(1)} %get-tuple-element.147), channel_id=1, source_target_pairs={{0,12},{1,13},{2,14},{3,15},{4,8},{5,9},{6,10},{7,11},{8,4},{9,5},... | collective-permute-start | bytes 196616 | tf_op jit(solution)/shard_map/ppermute | solution.py:312
  124.9 2.9 %collective-permute-start.43 = (bf16[32,1024]{1,0:T(8,128)(2,1)S(1)}, bf16[32,1024]{1,0:T(8,128)(2,1)S(1)}, u32[]{:S(2)}, u32[]{:S(2)}) collective-permute-start(bf16[32,1024]{1,0:T(8,128)(2,1)S(1)} %get-tuple-element.149), channel_id=1, source_target_pairs={{0,14},{1,15},{2,12},{3,13},{4,10},{5,11},{6,8},{7,9},{8,6},{9,7},... | collective-permute-start | bytes 196616 | tf_op jit(solution)/shard_map/ppermute | solution.py:312
  129.4 1.4 collective-permute-start.46
  132.3 3.8 %collective-permute-start.49 = (bf16[32,1024]{1,0:T(8,128)(2,1)S(1)}, bf16[32,1024]{1,0:T(8,128)(2,1)S(1)}, u32[]{:S(2)}, u32[]{:S(2)}) collective-permute-start(bf16[32,1024]{1,0:T(8,128)(2,1)S(1)} %get-tuple-element.155), channel_id=1, source_target_pairs={{0,4},{1,5},{2,6},{3,7},{4,0},{5,1},{6,2},{7,3},{8,12},{9,13},{10,... | collective-permute-start | bytes 196616 | tf_op jit(solution)/shard_map/ppermute | solution.py:312
  137.4 1.9 %collective-permute-start.52 = (bf16[32,1024]{1,0:T(8,128)(2,1)S(1)}, bf16[32,1024]{1,0:T(8,128)(2,1)S(1)}, u32[]{:S(2)}, u32[]{:S(2)}) collective-permute-start(bf16[32,1024]{1,0:T(8,128)(2,1)S(1)} %get-tuple-element.158), channel_id=1, source_target_pairs={{0,7},{1,6},{2,5},{3,4},{4,3},{5,2},{6,1},{7,0},{8,15},{9,14},{10,... | collective-permute-start | bytes 196616 | tf_op jit(solution)/shard_map/ppermute | solution.py:312
  139.3 1.9 %collective-permute-start.53 = (bf16[32,1024]{1,0:T(8,128)(2,1)S(1)}, bf16[32,1024]{1,0:T(8,128)(2,1)S(1)}, u32[]{:S(2)}, u32[]{:S(2)}) collective-permute-start(bf16[32,1024]{1,0:T(8,128)(2,1)S(1)} %get-tuple-element.159), channel_id=1, source_target_pairs={{0,8},{1,9},{2,10},{3,11},{4,12},{5,13},{6,14},{7,15},{8,0},{9,1},... | collective-permute-start | bytes 196616 | tf_op jit(solution)/shard_map/ppermute | solution.py:312
  143.0 2.5 %collective-permute-start.56 = (bf16[32,1024]{1,0:T(8,128)(2,1)S(1)}, bf16[32,1024]{1,0:T(8,128)(2,1)S(1)}, u32[]{:S(2)}, u32[]{:S(2)}) collective-permute-start(bf16[32,1024]{1,0:T(8,128)(2,1)S(1)} %get-tuple-element.162), channel_id=1, source_target_pairs={{0,11},{1,10},{2,9},{3,8},{4,15},{5,14},{6,13},{7,12},{8,3},{9,2},... | collective-permute-start | bytes 196616 | tf_op jit(solution)/shard_map/ppermute | solution.py:312
  145.5 1.9 %collective-permute-start.57 = (bf16[32,1024]{1,0:T(8,128)(2,1)S(1)}, bf16[32,1024]{1,0:T(8,128)(2,1)S(1)}, u32[]{:S(2)}, u32[]{:S(2)}) collective-permute-start(bf16[32,1024]{1,0:T(8,128)(2,1)S(1)} %get-tuple-element.163), channel_id=1, source_target_pairs={{0,12},{1,13},{2,14},{3,15},{4,8},{5,9},{6,10},{7,11},{8,4},{9,5},... | collective-permute-start | bytes 196616 | tf_op jit(solution)/shard_map/ppermute | solution.py:312
  147.4 1.7 %collective-permute-start.58 = (bf16[32,1024]{1,0:T(8,128)(2,1)S(1)}, bf16[32,1024]{1,0:T(8,128)(2,1)S(1)}, u32[]{:S(2)}, u32[]{:S(2)}) collective-permute-start(bf16[32,1024]{1,0:T(8,128)(2,1)S(1)} %get-tuple-element.164), channel_id=1, source_target_pairs={{0,13},{1,12},{2,15},{3,14},{4,9},{5,8},{6,11},{7,10},{8,5},{9,4},... | collective-permute-start | bytes 196616 | tf_op jit(solution)/shard_map/ppermute | solution.py:312
  149.1 4.8 %collective-permute-done.54.refs_25_ = bf16[32,1024]{1,0:T(8,128)(2,1)S(1)} collective-permute-done((bf16[32,1024]{1,0:T(8,128)(2,1)S(1)}, bf16[32,1024]{1,0:T(8,128)(2,1)S(1)}, u32[]{:S(2)}, u32[]{:S(2)}) %collective-permute-start.54) | collective-permute-done | bytes 65568 | tf_op jit(solution)/shard_map/ppermute | solution.py:312
  153.9 1.4 collective-permute-start.59
  155.4 2.7 %collective-permute-start.60 = (bf16[32,1024]{1,0:T(8,128)(2,1)S(1)}, bf16[32,1024]{1,0:T(8,128)(2,1)S(1)}, u32[]{:S(2)}, u32[]{:S(2)}) collective-permute-start(bf16[32,1024]{1,0:T(8,128)(2,1)S(1)} %get-tuple-element.166), channel_id=1, source_target_pairs={{0,15},{1,14},{2,13},{3,12},{4,11},{5,10},{6,9},{7,8},{8,7},{9,6},... | collective-permute-start | bytes 196616 | tf_op jit(solution)/shard_map/ppermute | solution.py:312
  158.1 2.9 %collective-permute-done.59.refs_30_ = bf16[32,1024]{1,0:T(8,128)(2,1)S(1)} collective-permute-done((bf16[32,1024]{1,0:T(8,128)(2,1)S(1)}, bf16[32,1024]{1,0:T(8,128)(2,1)S(1)}, u32[]{:S(2)}, u32[]{:S(2)}) %collective-permute-start.59) | collective-permute-done | bytes 65568 | tf_op jit(solution)/shard_map/ppermute | solution.py:312
  160.9 1.3 collective-permute-done.60.refs_31_
  162.2 1.5 place_pieces.1
  (95 shorter events, 19.4 us)
Async XLA Ops:
  6.5 8.5 %collective-permute-start = (bf16[104,512]{1,0:T(8,128)(2,1)S(1)}, bf16[104,512]{1,0:T(8,128)(2,1)S(1)}, u32[]{:S(2)}, u32[]{:S(2)}) collective-permute-start(bf16[104,512]{1,0:T(8,128)(2,1)S(1)} %get-tuple-element.87), channel_id=1, source_target_pairs={{0,1},{1,0},{2,3},{3,2},{4,5},{5,4},{6,7},{7,6},{8,9},{9,8},{10,11... | collective-permute-start | bytes 319496 | tf_op jit(solution)/shard_map/ppermute | solution.py:312
  7.0 8.0 %collective-permute-start.1 = (bf16[104,512]{1,0:T(8,128)(2,1)S(1)}, bf16[104,512]{1,0:T(8,128)(2,1)S(1)}, u32[]{:S(2)}, u32[]{:S(2)}) collective-permute-start(bf16[104,512]{1,0:T(8,128)(2,1)S(1)} %get-tuple-element.88), channel_id=1, source_target_pairs={{0,2},{1,3},{2,0},{3,1},{4,6},{5,7},{6,4},{7,5},{8,10},{9,11},{10,... | collective-permute-start | bytes 319496 | tf_op jit(solution)/shard_map/ppermute | solution.py:312
  9.6 8.2 %collective-permute-start.3 = (bf16[104,512]{1,0:T(8,128)(2,1)S(1)}, bf16[104,512]{1,0:T(8,128)(2,1)S(1)}, u32[]{:S(2)}, u32[]{:S(2)}) collective-permute-start(bf16[104,512]{1,0:T(8,128)(2,1)S(1)} %get-tuple-element.90), channel_id=1, source_target_pairs={{0,4},{1,5},{2,6},{3,7},{4,0},{5,1},{6,2},{7,3},{8,12},{9,13},{10,... | collective-permute-start | bytes 319496 | tf_op jit(solution)/shard_map/ppermute | solution.py:312
  11.4 10.1 %collective-permute-start.9 = (bf16[104,512]{1,0:T(8,128)(2,1)S(1)}, bf16[104,512]{1,0:T(8,128)(2,1)S(1)}, u32[]{:S(2)}, u32[]{:S(2)}) collective-permute-start(bf16[104,512]{1,0:T(8,128)(2,1)S(1)} %get-tuple-element.96), channel_id=1, source_target_pairs={{0,10},{1,11},{2,8},{3,9},{4,14},{5,15},{6,12},{7,13},{8,2},{9,3},... | collective-permute-start | bytes 319496 | tf_op jit(solution)/shard_map/ppermute | solution.py:312
  15.0 10.2 %collective-permute-start.5 = (bf16[104,512]{1,0:T(8,128)(2,1)S(1)}, bf16[104,512]{1,0:T(8,128)(2,1)S(1)}, u32[]{:S(2)}, u32[]{:S(2)}) collective-permute-start(bf16[104,512]{1,0:T(8,128)(2,1)S(1)} %get-tuple-element.92), channel_id=1, source_target_pairs={{0,6},{1,7},{2,4},{3,5},{4,2},{5,3},{6,0},{7,1},{8,14},{9,15},{10,... | collective-permute-start | bytes 319496 | tf_op jit(solution)/shard_map/ppermute | solution.py:312
  16.4 13.2 %collective-permute-start.6 = (bf16[104,512]{1,0:T(8,128)(2,1)S(1)}, bf16[104,512]{1,0:T(8,128)(2,1)S(1)}, u32[]{:S(2)}, u32[]{:S(2)}) collective-permute-start(bf16[104,512]{1,0:T(8,128)(2,1)S(1)} %get-tuple-element.93), channel_id=1, source_target_pairs={{0,7},{1,6},{2,5},{3,4},{4,3},{5,2},{6,1},{7,0},{8,15},{9,14},{10,... | collective-permute-start | bytes 319496 | tf_op jit(solution)/shard_map/ppermute | solution.py:312
  17.8 12.5 %collective-permute-start.7 = (bf16[104,512]{1,0:T(8,128)(2,1)S(1)}, bf16[104,512]{1,0:T(8,128)(2,1)S(1)}, u32[]{:S(2)}, u32[]{:S(2)}) collective-permute-start(bf16[104,512]{1,0:T(8,128)(2,1)S(1)} %get-tuple-element.94), channel_id=1, source_target_pairs={{0,8},{1,9},{2,10},{3,11},{4,12},{5,13},{6,14},{7,15},{8,0},{9,1},... | collective-permute-start | bytes 319496 | tf_op jit(solution)/shard_map/ppermute | solution.py:312
  21.6 10.6 %collective-permute-start.8 = (bf16[104,512]{1,0:T(8,128)(2,1)S(1)}, bf16[104,512]{1,0:T(8,128)(2,1)S(1)}, u32[]{:S(2)}, u32[]{:S(2)}) collective-permute-start(bf16[104,512]{1,0:T(8,128)(2,1)S(1)} %get-tuple-element.95), channel_id=1, source_target_pairs={{0,9},{1,8},{2,11},{3,10},{4,13},{5,12},{6,15},{7,14},{8,1},{9,0},... | collective-permute-start | bytes 319496 | tf_op jit(solution)/shard_map/ppermute | solution.py:312
  21.7 10.5 %collective-permute-start.15 = (bf16[32,1024]{1,0:T(8,128)(2,1)S(1)}, bf16[32,1024]{1,0:T(8,128)(2,1)S(1)}, u32[]{:S(2)}, u32[]{:S(2)}) collective-permute-start(bf16[32,1024]{1,0:T(8,128)(2,1)S(1)} %get-tuple-element.120), channel_id=1, source_target_pairs={{0,1},{1,0},{2,3},{3,2},{4,5},{5,4},{6,7},{7,6},{8,9},{9,8},{10,11... | collective-permute-start | bytes 196616 | tf_op jit(solution)/shard_map/ppermute | solution.py:312
  25.2 8.5 %collective-permute-start.16 = (bf16[32,1024]{1,0:T(8,128)(2,1)S(1)}, bf16[32,1024]{1,0:T(8,128)(2,1)S(1)}, u32[]{:S(2)}, u32[]{:S(2)}) collective-permute-start(bf16[32,1024]{1,0:T(8,128)(2,1)S(1)} %get-tuple-element.121), channel_id=1, source_target_pairs={{0,2},{1,3},{2,0},{3,1},{4,6},{5,7},{6,4},{7,5},{8,10},{9,11},{10,... | collective-permute-start | bytes 196616 | tf_op jit(solution)/shard_map/ppermute | solution.py:312
  32.1 7.2 %collective-permute-start.20 = (bf16[32,1024]{1,0:T(8,128)(2,1)S(1)}, bf16[32,1024]{1,0:T(8,128)(2,1)S(1)}, u32[]{:S(2)}, u32[]{:S(2)}) collective-permute-start(bf16[32,1024]{1,0:T(8,128)(2,1)S(1)} %get-tuple-element.125), channel_id=1, source_target_pairs={{0,6},{1,7},{2,4},{3,5},{4,2},{5,3},{6,0},{7,1},{8,14},{9,15},{10,... | collective-permute-start | bytes 196616 | tf_op jit(solution)/shard_map/ppermute | solution.py:312
  33.8 7.2 %collective-permute-start.21 = (bf16[32,1024]{1,0:T(8,128)(2,1)S(1)}, bf16[32,1024]{1,0:T(8,128)(2,1)S(1)}, u32[]{:S(2)}, u32[]{:S(2)}) collective-permute-start(bf16[32,1024]{1,0:T(8,128)(2,1)S(1)} %get-tuple-element.126), channel_id=1, source_target_pairs={{0,7},{1,6},{2,5},{3,4},{4,3},{5,2},{6,1},{7,0},{8,15},{9,14},{10,... | collective-permute-start | bytes 196616 | tf_op jit(solution)/shard_map/ppermute | solution.py:312
  34.7 9.4 %collective-permute-start.22 = (bf16[32,1024]{1,0:T(8,128)(2,1)S(1)}, bf16[32,1024]{1,0:T(8,128)(2,1)S(1)}, u32[]{:S(2)}, u32[]{:S(2)}) collective-permute-start(bf16[32,1024]{1,0:T(8,128)(2,1)S(1)} %get-tuple-element.127), channel_id=1, source_target_pairs={{0,8},{1,9},{2,10},{3,11},{4,12},{5,13},{6,14},{7,15},{8,0},{9,1},... | collective-permute-start | bytes 196616 | tf_op jit(solution)/shard_map/ppermute | solution.py:312
  36.6 11.9 %collective-permute-start.23 = (bf16[32,1024]{1,0:T(8,128)(2,1)S(1)}, bf16[32,1024]{1,0:T(8,128)(2,1)S(1)}, u32[]{:S(2)}, u32[]{:S(2)}) collective-permute-start(bf16[32,1024]{1,0:T(8,128)(2,1)S(1)} %get-tuple-element.128), channel_id=1, source_target_pairs={{0,9},{1,8},{2,11},{3,10},{4,13},{5,12},{6,15},{7,14},{8,1},{9,0},... | collective-permute-start | bytes 196616 | tf_op jit(solution)/shard_map/ppermute | solution.py:312
  37.4 14.2 %collective-permute-start.24 = (bf16[32,1024]{1,0:T(8,128)(2,1)S(1)}, bf16[32,1024]{1,0:T(8,128)(2,1)S(1)}, u32[]{:S(2)}, u32[]{:S(2)}) collective-permute-start(bf16[32,1024]{1,0:T(8,128)(2,1)S(1)} %get-tuple-element.129), channel_id=1, source_target_pairs={{0,10},{1,11},{2,8},{3,9},{4,14},{5,15},{6,12},{7,13},{8,2},{9,3},... | collective-permute-start | bytes 196616 | tf_op jit(solution)/shard_map/ppermute | solution.py:312
  39.3 14.3 %collective-permute-start.25 = (bf16[32,1024]{1,0:T(8,128)(2,1)S(1)}, bf16[32,1024]{1,0:T(8,128)(2,1)S(1)}, u32[]{:S(2)}, u32[]{:S(2)}) collective-permute-start(bf16[32,1024]{1,0:T(8,128)(2,1)S(1)} %get-tuple-element.130), channel_id=1, source_target_pairs={{0,11},{1,10},{2,9},{3,8},{4,15},{5,14},{6,13},{7,12},{8,3},{9,2},... | collective-permute-start | bytes 196616 | tf_op jit(solution)/shard_map/ppermute | solution.py:312
  40.9 12.7 %collective-permute-start.26 = (bf16[32,1024]{1,0:T(8,128)(2,1)S(1)}, bf16[32,1024]{1,0:T(8,128)(2,1)S(1)}, u32[]{:S(2)}, u32[]{:S(2)}) collective-permute-start(bf16[32,1024]{1,0:T(8,128)(2,1)S(1)} %get-tuple-element.131), channel_id=1, source_target_pairs={{0,12},{1,13},{2,14},{3,15},{4,8},{5,9},{6,10},{7,11},{8,4},{9,5},... | collective-permute-start | bytes 196616 | tf_op jit(solution)/shard_map/ppermute | solution.py:312
  44.2 11.3 %collective-permute-start.27 = (bf16[32,1024]{1,0:T(8,128)(2,1)S(1)}, bf16[32,1024]{1,0:T(8,128)(2,1)S(1)}, u32[]{:S(2)}, u32[]{:S(2)}) collective-permute-start(bf16[32,1024]{1,0:T(8,128)(2,1)S(1)} %get-tuple-element.132), channel_id=1, source_target_pairs={{0,13},{1,12},{2,15},{3,14},{4,9},{5,8},{6,11},{7,10},{8,5},{9,4},... | collective-permute-start | bytes 196616 | tf_op jit(solution)/shard_map/ppermute | solution.py:312
  48.5 8.7 %collective-permute-start.28 = (bf16[32,1024]{1,0:T(8,128)(2,1)S(1)}, bf16[32,1024]{1,0:T(8,128)(2,1)S(1)}, u32[]{:S(2)}, u32[]{:S(2)}) collective-permute-start(bf16[32,1024]{1,0:T(8,128)(2,1)S(1)} %get-tuple-element.133), channel_id=1, source_target_pairs={{0,14},{1,15},{2,12},{3,13},{4,10},{5,11},{6,8},{7,9},{8,6},{9,7},... | collective-permute-start | bytes 196616 | tf_op jit(solution)/shard_map/ppermute | solution.py:312
  51.6 8.1 %collective-permute-start.29 = (bf16[32,1024]{1,0:T(8,128)(2,1)S(1)}, bf16[32,1024]{1,0:T(8,128)(2,1)S(1)}, u32[]{:S(2)}, u32[]{:S(2)}) collective-permute-start(bf16[32,1024]{1,0:T(8,128)(2,1)S(1)} %get-tuple-element.134), channel_id=1, source_target_pairs={{0,15},{1,14},{2,13},{3,12},{4,11},{5,10},{6,9},{7,8},{8,7},{9,6},... | collective-permute-start | bytes 196616 | tf_op jit(solution)/shard_map/ppermute | solution.py:312
  53.6 21.7 %collective-permute-start.10 = (bf16[104,512]{1,0:T(8,128)(2,1)S(1)}, bf16[104,512]{1,0:T(8,128)(2,1)S(1)}, u32[]{:S(2)}, u32[]{:S(2)}) collective-permute-start(bf16[104,512]{1,0:T(8,128)(2,1)S(1)} %get-tuple-element.114), channel_id=1, source_target_pairs={{0,11},{1,10},{2,9},{3,8},{4,15},{5,14},{6,13},{7,12},{8,3},{9,2},... | collective-permute-start | bytes 319496 | tf_op jit(solution)/shard_map/ppermute | solution.py:312
  53.6 23.2 %collective-permute-start.11 = (bf16[104,512]{1,0:T(8,128)(2,1)S(1)}, bf16[104,512]{1,0:T(8,128)(2,1)S(1)}, u32[]{:S(2)}, u32[]{:S(2)}) collective-permute-start(bf16[104,512]{1,0:T(8,128)(2,1)S(1)} %get-tuple-element.115), channel_id=1, source_target_pairs={{0,12},{1,13},{2,14},{3,15},{4,8},{5,9},{6,10},{7,11},{8,4},{9,5},... | collective-permute-start | bytes 319496 | tf_op jit(solution)/shard_map/ppermute | solution.py:312
  55.5 21.4 %collective-permute-start.12 = (bf16[104,512]{1,0:T(8,128)(2,1)S(1)}, bf16[104,512]{1,0:T(8,128)(2,1)S(1)}, u32[]{:S(2)}, u32[]{:S(2)}) collective-permute-start(bf16[104,512]{1,0:T(8,128)(2,1)S(1)} %get-tuple-element.116), channel_id=1, source_target_pairs={{0,13},{1,12},{2,15},{3,14},{4,9},{5,8},{6,11},{7,10},{8,5},{9,4},... | collective-permute-start | bytes 319496 | tf_op jit(solution)/shard_map/ppermute | solution.py:312
  57.2 19.7 %collective-permute-start.13 = (bf16[104,512]{1,0:T(8,128)(2,1)S(1)}, bf16[104,512]{1,0:T(8,128)(2,1)S(1)}, u32[]{:S(2)}, u32[]{:S(2)}) collective-permute-start(bf16[104,512]{1,0:T(8,128)(2,1)S(1)} %get-tuple-element.117), channel_id=1, source_target_pairs={{0,14},{1,15},{2,12},{3,13},{4,10},{5,11},{6,8},{7,9},{8,6},{9,7},... | collective-permute-start | bytes 319496 | tf_op jit(solution)/shard_map/ppermute | solution.py:312
  59.7 17.2 %collective-permute-start.14 = (bf16[104,512]{1,0:T(8,128)(2,1)S(1)}, bf16[104,512]{1,0:T(8,128)(2,1)S(1)}, u32[]{:S(2)}, u32[]{:S(2)}) collective-permute-start(bf16[104,512]{1,0:T(8,128)(2,1)S(1)} %get-tuple-element.118), channel_id=1, source_target_pairs={{0,15},{1,14},{2,13},{3,12},{4,11},{5,10},{6,9},{7,8},{8,7},{9,6},... | collective-permute-start | bytes 319496 | tf_op jit(solution)/shard_map/ppermute | solution.py:312
  75.3 52.5 %collective-permute-start.45 = (bf16[512,1024]{1,0:T(8,128)(2,1)S(1)}, bf16[512,1024]{1,0:T(8,128)(2,1)S(1)}, u32[]{:S(2)}, u32[]{:S(2)}) collective-permute-start(bf16[512,1024]{1,0:T(8,128)(2,1)S(1)} %join_members.1.background_ref), channel_id=1, source_target_pairs={{0,16},{16,0},{1,17},{17,1},{2,18},{18,2},{3,19},{19,3},{4,20},{20... | collective-permute-start | bytes 3145736 | tf_op jit(solution)/shard_map/ppermute | solution.py:352
  95.6 10.1 %collective-permute-start.30 = (bf16[32,1024]{1,0:T(8,128)(2,1)S(1)}, bf16[32,1024]{1,0:T(8,128)(2,1)S(1)}, u32[]{:S(2)}, u32[]{:S(2)}) collective-permute-start(bf16[32,1024]{1,0:T(8,128)(2,1)S(1)} %get-tuple-element.136), channel_id=1, source_target_pairs={{0,1},{1,0},{2,3},{3,2},{4,5},{5,4},{6,7},{7,6},{8,9},{9,8},{10,11... | collective-permute-start | bytes 196616 | tf_op jit(solution)/shard_map/ppermute | solution.py:312
  95.7 10.0 %collective-permute-start.31 = (bf16[32,1024]{1,0:T(8,128)(2,1)S(1)}, bf16[32,1024]{1,0:T(8,128)(2,1)S(1)}, u32[]{:S(2)}, u32[]{:S(2)}) collective-permute-start(bf16[32,1024]{1,0:T(8,128)(2,1)S(1)} %get-tuple-element.137), channel_id=1, source_target_pairs={{0,2},{1,3},{2,0},{3,1},{4,6},{5,7},{6,4},{7,5},{8,10},{9,11},{10,... | collective-permute-start | bytes 196616 | tf_op jit(solution)/shard_map/ppermute | solution.py:312
  96.7 12.3 %collective-permute-start.32 = (bf16[32,1024]{1,0:T(8,128)(2,1)S(1)}, bf16[32,1024]{1,0:T(8,128)(2,1)S(1)}, u32[]{:S(2)}, u32[]{:S(2)}) collective-permute-start(bf16[32,1024]{1,0:T(8,128)(2,1)S(1)} %get-tuple-element.138), channel_id=1, source_target_pairs={{0,3},{1,2},{2,1},{3,0},{4,7},{5,6},{6,5},{7,4},{8,11},{9,10},{10,... | collective-permute-start | bytes 196616 | tf_op jit(solution)/shard_map/ppermute | solution.py:312
  97.5 12.3 %collective-permute-start.33 = (bf16[32,1024]{1,0:T(8,128)(2,1)S(1)}, bf16[32,1024]{1,0:T(8,128)(2,1)S(1)}, u32[]{:S(2)}, u32[]{:S(2)}) collective-permute-start(bf16[32,1024]{1,0:T(8,128)(2,1)S(1)} %get-tuple-element.139), channel_id=1, source_target_pairs={{0,4},{1,5},{2,6},{3,7},{4,0},{5,1},{6,2},{7,3},{8,12},{9,13},{10,... | collective-permute-start | bytes 196616 | tf_op jit(solution)/shard_map/ppermute | solution.py:312
  109.8 8.9 %collective-permute-start.37 = (bf16[32,1024]{1,0:T(8,128)(2,1)S(1)}, bf16[32,1024]{1,0:T(8,128)(2,1)S(1)}, u32[]{:S(2)}, u32[]{:S(2)}) collective-permute-start(bf16[32,1024]{1,0:T(8,128)(2,1)S(1)} %get-tuple-element.143), channel_id=1, source_target_pairs={{0,8},{1,9},{2,10},{3,11},{4,12},{5,13},{6,14},{7,15},{8,0},{9,1},... | collective-permute-start | bytes 196616 | tf_op jit(solution)/shard_map/ppermute | solution.py:312
  111.0 13.1 %collective-permute-start.38 = (bf16[32,1024]{1,0:T(8,128)(2,1)S(1)}, bf16[32,1024]{1,0:T(8,128)(2,1)S(1)}, u32[]{:S(2)}, u32[]{:S(2)}) collective-permute-start(bf16[32,1024]{1,0:T(8,128)(2,1)S(1)} %get-tuple-element.144), channel_id=1, source_target_pairs={{0,9},{1,8},{2,11},{3,10},{4,13},{5,12},{6,15},{7,14},{8,1},{9,0},... | collective-permute-start | bytes 196616 | tf_op jit(solution)/shard_map/ppermute | solution.py:312
  112.1 12.9 %collective-permute-start.39 = (bf16[32,1024]{1,0:T(8,128)(2,1)S(1)}, bf16[32,1024]{1,0:T(8,128)(2,1)S(1)}, u32[]{:S(2)}, u32[]{:S(2)}) collective-permute-start(bf16[32,1024]{1,0:T(8,128)(2,1)S(1)} %get-tuple-element.145), channel_id=1, source_target_pairs={{0,10},{1,11},{2,8},{3,9},{4,14},{5,15},{6,12},{7,13},{8,2},{9,3},... | collective-permute-start | bytes 196616 | tf_op jit(solution)/shard_map/ppermute | solution.py:312
  115.7 13.7 %collective-permute-start.40 = (bf16[32,1024]{1,0:T(8,128)(2,1)S(1)}, bf16[32,1024]{1,0:T(8,128)(2,1)S(1)}, u32[]{:S(2)}, u32[]{:S(2)}) collective-permute-start(bf16[32,1024]{1,0:T(8,128)(2,1)S(1)} %get-tuple-element.146), channel_id=1, source_target_pairs={{0,11},{1,10},{2,9},{3,8},{4,15},{5,14},{6,13},{7,12},{8,3},{9,2},... | collective-permute-start | bytes 196616 | tf_op jit(solution)/shard_map/ppermute | solution.py:312
  118.7 12.1 %collective-permute-start.41 = (bf16[32,1024]{1,0:T(8,128)(2,1)S(1)}, bf16[32,1024]{1,0:T(8,128)(2,1)S(1)}, u32[]{:S(2)}, u32[]{:S(2)}) collective-permute-start(bf16[32,1024]{1,0:T(8,128)(2,1)S(1)} %get-tuple-element.147), channel_id=1, source_target_pairs={{0,12},{1,13},{2,14},{3,15},{4,8},{5,9},{6,10},{7,11},{8,4},{9,5},... | collective-permute-start | bytes 196616 | tf_op jit(solution)/shard_map/ppermute | solution.py:312
  124.1 7.5 %collective-permute-start.42 = (bf16[32,1024]{1,0:T(8,128)(2,1)S(1)}, bf16[32,1024]{1,0:T(8,128)(2,1)S(1)}, u32[]{:S(2)}, u32[]{:S(2)}) collective-permute-start(bf16[32,1024]{1,0:T(8,128)(2,1)S(1)} %get-tuple-element.148), channel_id=1, source_target_pairs={{0,13},{1,12},{2,15},{3,14},{4,9},{5,8},{6,11},{7,10},{8,5},{9,4},... | collective-permute-start | bytes 196616 | tf_op jit(solution)/shard_map/ppermute | solution.py:312
  124.9 7.3 %collective-permute-start.43 = (bf16[32,1024]{1,0:T(8,128)(2,1)S(1)}, bf16[32,1024]{1,0:T(8,128)(2,1)S(1)}, u32[]{:S(2)}, u32[]{:S(2)}) collective-permute-start(bf16[32,1024]{1,0:T(8,128)(2,1)S(1)} %get-tuple-element.149), channel_id=1, source_target_pairs={{0,14},{1,15},{2,12},{3,13},{4,10},{5,11},{6,8},{7,9},{8,6},{9,7},... | collective-permute-start | bytes 196616 | tf_op jit(solution)/shard_map/ppermute | solution.py:312
  127.8 8.3 %collective-permute-start.44 = (bf16[32,1024]{1,0:T(8,128)(2,1)S(1)}, bf16[32,1024]{1,0:T(8,128)(2,1)S(1)}, u32[]{:S(2)}, u32[]{:S(2)}) collective-permute-start(bf16[32,1024]{1,0:T(8,128)(2,1)S(1)} %get-tuple-element.150), channel_id=1, source_target_pairs={{0,15},{1,14},{2,13},{3,12},{4,11},{5,10},{6,9},{7,8},{8,7},{9,6},... | collective-permute-start | bytes 196616 | tf_op jit(solution)/shard_map/ppermute | solution.py:312
  129.4 7.2 %collective-permute-start.46 = (bf16[32,1024]{1,0:T(8,128)(2,1)S(1)}, bf16[32,1024]{1,0:T(8,128)(2,1)S(1)}, u32[]{:S(2)}, u32[]{:S(2)}) collective-permute-start(bf16[32,1024]{1,0:T(8,128)(2,1)S(1)} %get-tuple-element.152), channel_id=1, source_target_pairs={{0,1},{1,0},{2,3},{3,2},{4,5},{5,4},{6,7},{7,6},{8,9},{9,8},{10,11... | collective-permute-start | bytes 196616 | tf_op jit(solution)/shard_map/ppermute | solution.py:312
  131.7 7.6 %collective-permute-start.48 = (bf16[32,1024]{1,0:T(8,128)(2,1)S(1)}, bf16[32,1024]{1,0:T(8,128)(2,1)S(1)}, u32[]{:S(2)}, u32[]{:S(2)}) collective-permute-start(bf16[32,1024]{1,0:T(8,128)(2,1)S(1)} %get-tuple-element.154), channel_id=1, source_target_pairs={{0,3},{1,2},{2,1},{3,0},{4,7},{5,6},{6,5},{7,4},{8,11},{9,10},{10,... | collective-permute-start | bytes 196616 | tf_op jit(solution)/shard_map/ppermute | solution.py:312
  132.3 8.9 %collective-permute-start.49 = (bf16[32,1024]{1,0:T(8,128)(2,1)S(1)}, bf16[32,1024]{1,0:T(8,128)(2,1)S(1)}, u32[]{:S(2)}, u32[]{:S(2)}) collective-permute-start(bf16[32,1024]{1,0:T(8,128)(2,1)S(1)} %get-tuple-element.155), channel_id=1, source_target_pairs={{0,4},{1,5},{2,6},{3,7},{4,0},{5,1},{6,2},{7,3},{8,12},{9,13},{10,... | collective-permute-start | bytes 196616 | tf_op jit(solution)/shard_map/ppermute | solution.py:312
  137.4 8.1 %collective-permute-start.52 = (bf16[32,1024]{1,0:T(8,128)(2,1)S(1)}, bf16[32,1024]{1,0:T(8,128)(2,1)S(1)}, u32[]{:S(2)}, u32[]{:S(2)}) collective-permute-start(bf16[32,1024]{1,0:T(8,128)(2,1)S(1)} %get-tuple-element.158), channel_id=1, source_target_pairs={{0,7},{1,6},{2,5},{3,4},{4,3},{5,2},{6,1},{7,0},{8,15},{9,14},{10,... | collective-permute-start | bytes 196616 | tf_op jit(solution)/shard_map/ppermute | solution.py:312
  139.3 8.1 %collective-permute-start.53 = (bf16[32,1024]{1,0:T(8,128)(2,1)S(1)}, bf16[32,1024]{1,0:T(8,128)(2,1)S(1)}, u32[]{:S(2)}, u32[]{:S(2)}) collective-permute-start(bf16[32,1024]{1,0:T(8,128)(2,1)S(1)} %get-tuple-element.159), channel_id=1, source_target_pairs={{0,8},{1,9},{2,10},{3,11},{4,12},{5,13},{6,14},{7,15},{8,0},{9,1},... | collective-permute-start | bytes 196616 | tf_op jit(solution)/shard_map/ppermute | solution.py:312
  141.2 12.8 %collective-permute-start.54 = (bf16[32,1024]{1,0:T(8,128)(2,1)S(1)}, bf16[32,1024]{1,0:T(8,128)(2,1)S(1)}, u32[]{:S(2)}, u32[]{:S(2)}) collective-permute-start(bf16[32,1024]{1,0:T(8,128)(2,1)S(1)} %get-tuple-element.160), channel_id=1, source_target_pairs={{0,9},{1,8},{2,11},{3,10},{4,13},{5,12},{6,15},{7,14},{8,1},{9,0},... | collective-permute-start | bytes 196616 | tf_op jit(solution)/shard_map/ppermute | solution.py:312
  142.0 13.4 %collective-permute-start.55 = (bf16[32,1024]{1,0:T(8,128)(2,1)S(1)}, bf16[32,1024]{1,0:T(8,128)(2,1)S(1)}, u32[]{:S(2)}, u32[]{:S(2)}) collective-permute-start(bf16[32,1024]{1,0:T(8,128)(2,1)S(1)} %get-tuple-element.161), channel_id=1, source_target_pairs={{0,10},{1,11},{2,8},{3,9},{4,14},{5,15},{6,12},{7,13},{8,2},{9,3},... | collective-permute-start | bytes 196616 | tf_op jit(solution)/shard_map/ppermute | solution.py:312
  143.0 15.0 %collective-permute-start.56 = (bf16[32,1024]{1,0:T(8,128)(2,1)S(1)}, bf16[32,1024]{1,0:T(8,128)(2,1)S(1)}, u32[]{:S(2)}, u32[]{:S(2)}) collective-permute-start(bf16[32,1024]{1,0:T(8,128)(2,1)S(1)} %get-tuple-element.162), channel_id=1, source_target_pairs={{0,11},{1,10},{2,9},{3,8},{4,15},{5,14},{6,13},{7,12},{8,3},{9,2},... | collective-permute-start | bytes 196616 | tf_op jit(solution)/shard_map/ppermute | solution.py:312
  145.5 12.6 %collective-permute-start.57 = (bf16[32,1024]{1,0:T(8,128)(2,1)S(1)}, bf16[32,1024]{1,0:T(8,128)(2,1)S(1)}, u32[]{:S(2)}, u32[]{:S(2)}) collective-permute-start(bf16[32,1024]{1,0:T(8,128)(2,1)S(1)} %get-tuple-element.163), channel_id=1, source_target_pairs={{0,12},{1,13},{2,14},{3,15},{4,8},{5,9},{6,10},{7,11},{8,4},{9,5},... | collective-permute-start | bytes 196616 | tf_op jit(solution)/shard_map/ppermute | solution.py:312
  147.4 10.7 %collective-permute-start.58 = (bf16[32,1024]{1,0:T(8,128)(2,1)S(1)}, bf16[32,1024]{1,0:T(8,128)(2,1)S(1)}, u32[]{:S(2)}, u32[]{:S(2)}) collective-permute-start(bf16[32,1024]{1,0:T(8,128)(2,1)S(1)} %get-tuple-element.164), channel_id=1, source_target_pairs={{0,13},{1,12},{2,15},{3,14},{4,9},{5,8},{6,11},{7,10},{8,5},{9,4},... | collective-permute-start | bytes 196616 | tf_op jit(solution)/shard_map/ppermute | solution.py:312
  (20 other events, 107.5 us)

commit v3 on v0

v3 whole, which is shorter than its diff:
```python
import functools

import jax
import jax.numpy as jnp
from jax import lax
from jax.experimental import pallas as pl
from jax.experimental.pallas import tpu as pltpu
from jax.sharding import PartitionSpec as P

NS_STEPS = 6
LANES = 128
TAIL = 8
FULL_STEPS = 2
VMEM_BYTES = 48 * 1024 * 1024
ALL_VMEM_BYTES = 64 * 1024 * 1024
F32 = jnp.float32
BF16 = jnp.bfloat16


def pack_kernel(groups, *refs):
    sources, slots_ref, fetched = refs[:6], refs[6], refs[7:13]
    info_ref, sems = refs[13:]
    run_copies(
        [
            pltpu.make_async_copy(source, target, sems.at[i])
            for i, (source, target) in enumerate(zip(sources, fetched))
        ]
    )
    targets_ref, local_ref, mult_ref, prec_ref, dep_ref, rows_ref = fetched
    patches, depth, members = slots_ref.shape
    share = depth - TAIL
    count = rows_ref.shape[0]
    mult = mult_ref[...].reshape(1, count).astype(F32)
    prec = prec_ref[...].reshape(1, count)
    weight = local_ref[...].astype(F32) / 1024.0 * (mult * prec)
    weight = weight.astype(BF16).astype(F32)
    dep = dep_ref[...].astype(F32).reshape(1, count)
    patch_id = lax.broadcasted_iota(jnp.int32, (patches, count), 0)
    first = patch_id == targets_ref[0:1, :]
    second = patch_id == targets_ref[1:2, :]
    named = jnp.logical_or(first, second)
    earlier = lax.broadcasted_iota(jnp.int32, (count, count), 0) < lax.broadcasted_iota(
        jnp.int32, (count, count), 1
    )
    rank = jnp.dot(
        named.astype(F32).astype(BF16), earlier.astype(F32).astype(BF16), preferred_element_type=F32
    )
    rank = jnp.where(named, rank, -1.0)
    by_patch = jnp.where(first, weight[0:1, :], jnp.where(second, weight[1:2, :], 0.0))
    slot_id = lax.broadcasted_iota(jnp.int32, (groups * share, count), 0).astype(F32)
    lane = lax.broadcasted_iota(jnp.int32, (groups * share, LANES), 1)
    info = jnp.zeros((groups * share, LANES), F32)
    for patch in range(patches):
        pick = slot_id == rank[patch : patch + 1, :]
        weight_col = jnp.sum(
            jnp.where(pick, by_patch[patch : patch + 1, :], 0.0), axis=1, keepdims=True
        )
        dep_col = jnp.sum(jnp.where(pick, dep, 0.0), axis=1, keepdims=True)
        info = jnp.where(lane == patch, weight_col, info)
        info = jnp.where(lane == patches + patch, dep_col, info)
    info_ref[...] = jnp.zeros((LANES, LANES), F32)
    info_ref[0 : groups * share, :] = info
    info = info_ref[...].T
    begin = lax.axis_index("boot") * share
    own_id = (lax.broadcasted_iota(jnp.int32, (share, count), 0) + begin).astype(F32)
    tail_id = lax.broadcasted_iota(jnp.int32, (TAIL, LANES), 0)
    blank = jnp.zeros((TAIL, members - LANES), F32)
    rows = rows_ref[...]
    for patch in range(patches):
        pick = jnp.where(own_id == rank[patch : patch + 1, :], 1.0, 0.0)
        block = jnp.dot(pick.astype(BF16), rows, preferred_element_type=F32)
        tail = jnp.where(
            tail_id == 0,
            info[patch : patch + 1, :],
            jnp.where(tail_id == 1, info[patches + patch : patches + patch + 1, :], 0.0),
        )
        tail = jnp.concatenate([tail, blank], axis=1)
        slots_ref[patch] = jnp.concatenate([block, tail], axis=0).astype(BF16)


def run_copies(copies):
    for copy in copies:
        copy.start()
    for copy in copies:
        copy.wait()


def pack(targets, local, mult, prec, dep, rows, patches, share, groups):
    count, members = rows.shape
    operands = (targets.T, local.T, mult, prec, dep, rows)
    return pl.pallas_call(
        functools.partial(pack_kernel, groups),
        out_shape=jax.ShapeDtypeStruct((patches, share + TAIL, members), BF16),
        in_specs=[pl.BlockSpec(memory_space=pl.ANY)] * len(operands),
        scratch_shapes=[pltpu.VMEM(operand.shape, operand.dtype) for operand in operands]
        + [pltpu.VMEM((LANES, LANES), F32), pltpu.SemaphoreType.DMA((len(operands),))],
        compiler_params=pltpu.CompilerParams(vmem_limit_bytes=ALL_VMEM_BYTES),
        cost_estimate=pl.CostEstimate(
            flops=2 * patches * share * count * members,
            bytes_accessed=2 * (patches * share + count) * members,
            transcendentals=0,
        ),
        name="pack_rows",
    )(*operands)


def halves(value):
    high = value.astype(BF16)
    return high, (value - high.astype(F32)).astype(BF16)


def product(left_high, left_low, right_high, right_low):
    dot = functools.partial(jnp.dot, preferred_element_type=F32)
    return dot(left_high, right_high) + (dot(left_high, right_low) + dot(left_low, right_high))


def weights_kernel(*refs):
    rows_refs, blended_ref, info_ref = refs[:-10], refs[-10], refs[-9]
    y_ref, z_ref, y_high, y_low, z_high, z_low, w_high, w_low = refs[-8:]
    groups = len(rows_refs)
    sources, depth, members = rows_refs[0].shape
    share = depth - TAIL
    for source in range(sources):
        tail = rows_refs[0][source].astype(F32)[share:depth, 0:LANES]
        info_ref[source : source + 1, :] = tail[0:1, :]
        info_ref[sources + source : sources + source + 1, :] = tail[1:2, :]
    info_ref[...] = info_ref[...].T
    gram = jnp.zeros((members, members), F32)
    drive = jnp.zeros((1, members), F32)
    for turn, rows_ref in enumerate(rows_refs):
        begin = lax.rem(lax.axis_index("boot") + turn, groups) * share
        info = info_ref[pl.ds(pl.multiple_of(begin, 8), share), :]
        rows, scaled = [], []
        for source in range(sources):
            block = rows_ref[source].astype(F32)[0:share, :]
            rows.append(block)
            block = (info[:, source : source + 1] * block).astype(BF16).astype(F32)
            scaled.append(block)
            dep_col = info[:, sources + source : sources + source + 1]
            drive += jnp.sum(dep_col * block, axis=0, keepdims=True)
        gram += lax.dot_general(
            jnp.concatenate(rows, axis=0).astype(BF16),
            jnp.concatenate(scaled, axis=0).astype(BF16),
            (((0,), (0,)), ((), ())),
            preferred_element_type=F32,
        )

    row_id = lax.broadcasted_iota(jnp.int32, (members, members), 0)
    col_id = lax.broadcasted_iota(jnp.int32, (members, members), 1)
    diagonal = row_id == col_id
    identity = jnp.where(diagonal, 1.0, 0.0)
    shifted = identity + gram / (members - 1.0)
    squares = jnp.sum(jnp.sum(shifted * shifted, axis=0, keepdims=True), axis=1, keepdims=True)
    frobenius = jnp.sqrt(squares)
    dot = functools.partial(jnp.dot, preferred_element_type=F32)

    def put(high_ref, low_ref, value):
        high_ref[...], low_ref[...] = halves(value)

    def step(_, carry):
        w_high[...] = dot(z_high[...], y_high[...]).astype(BF16)
        current = 1.5 * y_ref[...] - 0.5 * dot(y_high[...], w_high[...])
        root = 1.5 * z_ref[...] - 0.5 * dot(w_high[...], z_high[...])
        y_ref[...], z_ref[...] = current, root
        y_high[...], z_high[...] = current.astype(BF16), root.astype(BF16)
        return carry

    current = shifted / frobenius
    y_high[...] = current.astype(BF16)
    root = 1.5 * identity - 0.5 * current
    current = 1.5 * current - 0.5 * dot(y_high[...], y_high[...])
    y_ref[...], z_ref[...] = current, root
    y_high[...], z_high[...] = current.astype(BF16), root.astype(BF16)
    lax.fori_loop(1, NS_STEPS - FULL_STEPS, step, 0)
    for full in range(FULL_STEPS):
        put(y_high, y_low, y_ref[...])
        put(z_high, z_low, z_ref[...])
        put(w_high, w_low, product(z_high[...], z_low[...], y_high[...], y_low[...]))
        if full < FULL_STEPS - 1:
            change = product(y_high[...], y_low[...], w_high[...], w_low[...])
            y_ref[...] = 1.5 * y_ref[...] - 0.5 * change
        change = product(w_high[...], w_low[...], z_high[...], z_low[...])
        z_ref[...] = 1.5 * z_ref[...] - 0.5 * change
    root = z_ref[...] / jnp.sqrt(frobenius)

    drive_col = jnp.sum(jnp.where(diagonal, drive, 0.0), axis=1, keepdims=True)
    inner = jnp.sum(root * drive_col, axis=0, keepdims=True)
    inner_col = jnp.sum(jnp.where(diagonal, inner, 0.0), axis=1, keepdims=True)
    mean_weight = jnp.sum(root * inner_col, axis=0, keepdims=True) / (members - 1.0)
    blended_ref[...] = (root + mean_weight).astype(BF16)


def patch_weights(rows):
    sources, depth, members = rows[0].shape
    whole = pltpu.VMEM((members, members), F32)
    half = pltpu.VMEM((members, members), BF16)
    return pl.pallas_call(
        weights_kernel,
        out_shape=jax.ShapeDtypeStruct((members, members), BF16),
        scratch_shapes=[pltpu.VMEM((LANES, LANES), F32)] + [whole] * 2 + [half] * 6,
        compiler_params=pltpu.CompilerParams(vmem_limit_bytes=VMEM_BYTES),
        cost_estimate=pl.CostEstimate(
            flops=2 * members * members * (len(rows) * sources * depth + 25 * members),
            bytes_accessed=2 * len(rows) * sources * depth * members,
            transcendentals=0,
        ),
        name="patch_weights",
    )(*rows)


def update_kernel(blended_ref, background_ref, analysis_ref):
    members, points = background_ref.shape
    tile = min(points, 256)
    for begin in range(0, points, tile):
        columns = slice(begin, begin + tile)
        background = background_ref[:, columns].astype(F32)
        centre = jnp.sum(background, axis=0, keepdims=True) / members
        perturb = (background - centre).astype(BF16)
        update = jnp.dot(blended_ref[...], perturb, preferred_element_type=F32)
        analysis_ref[:, columns] = (centre + update).astype(BF16)


def update_points(blended, background):
    members, points = background.shape
    return pl.pallas_call(
        update_kernel,
        out_shape=jax.ShapeDtypeStruct((members, points), BF16),
        compiler_params=pltpu.CompilerParams(vmem_limit_bytes=VMEM_BYTES),
        cost_estimate=pl.CostEstimate(
            flops=2 * members * members * points,
            bytes_accessed=4 * members * points + 2 * members * members,
            transcendentals=0,
        ),
        name="update_points",
    )(blended, background)


def cut_kernel(states_ref, cut_ref):
    patches, _, share = cut_ref.shape
    region = states_ref.shape[1] // patches
    offset = lax.axis_index("boot") * share
    for patch in range(patches):
        begin = pl.multiple_of(patch * region + offset, LANES)
        cut_ref[patch] = states_ref[:, pl.ds(begin, share)]


def cut_share(states, patches, share):
    own_members = states.shape[0]
    return pl.pallas_call(
        cut_kernel,
        out_shape=jax.ShapeDtypeStruct((patches, own_members, share), BF16),
        compiler_params=pltpu.CompilerParams(vmem_limit_bytes=VMEM_BYTES),
        cost_estimate=pl.CostEstimate(
            flops=0, bytes_accessed=4 * patches * own_members * share, transcendentals=0
        ),
        name="cut_share",
    )(states)


def place_kernel(*refs):
    piece_refs, whole_ref = refs[:-1], refs[-1]
    groups = len(piece_refs)
    patches, _, share = piece_refs[0].shape
    for turn, piece_ref in enumerate(piece_refs):
        offset = lax.rem(lax.axis_index("boot") + turn, groups) * share
        for patch in range(patches):
            begin = pl.multiple_of(patch * groups * share + offset, LANES)
            whole_ref[:, pl.ds(begin, share)] = piece_ref[patch]


def place_pieces(pieces):
    patches, own_members, share = pieces[0].shape
    points = patches * share * len(pieces)
    return pl.pallas_call(
        place_kernel,
        out_shape=jax.ShapeDtypeStruct((own_members, points), BF16),
        compiler_params=pltpu.CompilerParams(vmem_limit_bytes=VMEM_BYTES),
        cost_estimate=pl.CostEstimate(
            flops=0, bytes_accessed=4 * own_members * points, transcendentals=0
        ),
        name="place_pieces",
    )(*pieces)


def exchange(blocks):
    return lax.all_to_all(blocks, "space", split_axis=0, concat_axis=0, tiled=True)


def swap_shares(own):
    groups = lax.axis_size("boot")
    return [
        lax.ppermute(own, "boot", [(g, (g - turn) % groups) for g in range(groups)])
        for turn in range(1, groups)
    ]


def local(
    background_states,
    measurement_anomaly_matrix,
    departure_vector,
    measurement_precision,
    measurement_region_targets,
    localization_factor_scaled,
    bootstrap_multiplicity,
):
    device_count = lax.axis_size("space")
    groups = lax.axis_size("boot")
    local_rows = measurement_anomaly_matrix.shape[0]
    targets_per = measurement_region_targets.shape[1]
    slot_cap = 2 * targets_per * local_rows // device_count
    slot_share = -(-slot_cap // (8 * groups)) * 8
    own_members, points = background_states.shape
    share = points // device_count // groups

    slots = pack(
        measurement_region_targets,
        localization_factor_scaled,
        bootstrap_multiplicity,
        measurement_precision,
        departure_vector,
        measurement_anomaly_matrix,
        device_count,
        slot_share,
        groups,
    )
    own_rows = exchange(slots)
    rows = [own_rows] + swap_shares(own_rows[:, :slot_share])
    own_rows, background_states = lax.optimization_barrier((own_rows, background_states))
    own_points = exchange(cut_share(background_states, device_count, share))
    own_points = own_points.reshape(-1, share)
    background = [own_points] + swap_shares(own_points)

    blended = patch_weights(rows)
    pieces = []
    for part in background:
        analysis = update_points(blended, part).reshape(device_count, own_members, share)
        pieces.append(exchange(analysis))
    return place_pieces(pieces)


def solution(mesh):
    in_specs = (
        P("space", None),
        P("space", None),
        P("space"),
        P("space"),
        P("space", None),
        P("space", None),
        P(("boot", "space")),
    )
    out_specs = P(("boot", "space"), None)
    return jax.shard_map(local, mesh=mesh, in_specs=in_specs, out_specs=out_specs, check_vma=False)
```

time: 191 us -> 137 us (0.72)
  blocking collectives: 110 us -> 60.4 us
  waiting for transfers between devices: 28.8 us -> 42.3 us
  local copies, waits for them, and re-layouts: 9.03 us -> 1.66 us
  other arithmetic: 4 us -> 0 us
  starting transfers between devices: 16.5 us -> 13.3 us
    all_gather x1 -> x0, blocking collectives: 55.9 us -> none  [local(): info_got = lax.all_gather(info, 'space', axis=0, tiled=False)]
    ppermute x0 -> x2, waiting for transfers between devices: none -> 42.3 us  [swap_shares(): lax.ppermute(own, 'boot', [(g, (g - turn) % groups) for g in range(groups)])]
    all_to_all x2, waiting for transfers between devices: 28.8 us -> 0.01 us  [exchange(): lax.all_to_all(blocks, 'space', split_axis=0, concat_axis=0, tiled=True)]
    pallas_call x1, Pallas kernels: 17.3 us -> 10.2 us  [patch_weights(): pl.pallas_call(weights_kernel, out_shape=jax.ShapeDtypeStruct((members, m...]
    all_to_all x2, starting transfers between devices: 16.5 us -> 10.2 us  [exchange(): lax.all_to_all(blocks, 'space', split_axis=0, concat_axis=0, tiled=True)]
    all_to_all x1 -> x2, blocking collectives: 54.3 us -> 60.4 us  [exchange(): lax.all_to_all(blocks, 'space', split_axis=0, concat_axis=0, tiled=True)]
    pallas_call x1 -> x5, Pallas kernels: 2.84 us -> 8.68 us  [the longest x1 3.48 us: pack(): pl.pallas_call(functools.partial(pack_kernel, groups), out_shape=jax.Shap...]
    all_to_all x2 -> x0, local copies, waits for them, and re-layouts: 4.62 us -> none  [the longest x1 3.16 us: local(): lax.all_to_all(background_states, 'space', split_axis=1, concat_axis=0, t...]
  transfers between devices with their start and end apart: 2 -> 4, of which waited for: 1 -> 2; matrix products, arithmetic and copies ran while one was open for 2% -> 0% of each run, Pallas kernels for 9% -> 8%
where the time goes in v3:
time: 137 us
  blocking collectives  60.4 us (44%)
  waiting for transfers between devices  42.3 us (31%)
  Pallas kernels  18.9 us (14%)
  starting transfers between devices  13.3 us (10%)
  local copies, waits for them, and re-layouts  1.66 us (1%)
    all_to_all x2, blocking collectives, exchange(): lax.all_to_all(blocks, 'space', split_axis=0, concat_axis=0, tiled=True)  60.4 us
    ppermute x2, waiting for transfers between devices, swap_shares(): lax.ppermute(own, 'boot', [(g, (g - turn) % groups) for g in range(groups)])  42.3 us
    pallas_call x1, Pallas kernels, patch_weights(): pl.pallas_call(weights_kernel, out_shape=jax.ShapeDtypeStruct((members, m...  10.2 us
    all_to_all x2, starting transfers between devices, exchange(): lax.all_to_all(blocks, 'space', split_axis=0, concat_axis=0, tiled=True)  10.2 us
    pallas_call x1, Pallas kernels, pack(): pl.pallas_call(functools.partial(pack_kernel, groups), out_shape=jax.Shap...  3.48 us
    ppermute x2, starting transfers between devices, swap_shares(): lax.ppermute(own, 'boot', [(g, (g - turn) % groups) for g in range(groups)])  3.11 us
  transfers between devices with their start and end apart: 4, of which 2 were waited for; matrix products, arithmetic and copies ran while one was open for 0% of the time, Pallas kernels for 8%

profile of v3, /device:TPU:0, one launch (start us, length us, event | category | flops | bytes accessed | tf_op | source)
XLA Modules:
  0.0 136.6 jit_solution(14277117379571792792)
XLA Ops:
  0.0 3.5 %pack_rows.1 = bf16[16,56,512]{2,1,0:T(8,128)(2,1)} custom-call(s32[2,384]{1,0:T(2,128)} %bitcast.8, s32[2,384]{1,0:T(2,128)} %bitcast.9, s32[384]{0:T(512)} %refs_2_.1, f32[384]{0:T(512)} %refs_3_.1, bf16[384]{0:T(512)(128)(2,1)} %refs_4_.1, bf16[384,512]{1,0:T(8,128)(2,1)} %refs_5_.1), custom_call_target="tpu_custom_call" | custom-call | flops 301989888 | bytes 1179648 | tf_op jit(solution)/shard_map/pack_rows/pallas_call | solution.py:91
  3.5 30.0 %all_to_all.20.refs_0_ = bf16[16,56,512]{2,1,0:T(8,128)(2,1)S(1)} all-to-all(bf16[16,56,512]{2,1,0:T(8,128)(2,1)} %pack_rows.1), channel_id=1, replica_groups=mesh['boot'=2,'space'=16] {'space'}, dimensions={0} | all-to-all | bytes 1835008 | tf_op jit(solution)/shard_map/all_to_all | solution.py:286
  33.4 0.0 copy-start
  33.4 1.6 %copy-done = bf16[32,32768]{1,0:T(8,128)(2,1)S(1)} copy-done((bf16[32,32768]{1,0:T(8,128)(2,1)S(1)}, bf16[32,32768]{1,0:T(8,128)(2,1)}, u32[]{:S(2)}) %copy-start) | copy-done | bytes 2097176
  35.0 1.0 cut_share.1
  36.1 4.5 %all-to-all-start.1 = ((bf16[16,32,1024]{2,1,0:T(8,128)(2,1)}), bf16[16,32,1024]{2,1,0:T(8,128)(2,1)S(1)}, u32[]{:S(2)}, u32[]{:S(2)}) async-start(bf16[16,32,1024]{2,1,0:T(8,128)(2,1)} %cut_share.1), calls=%async_computation.1 | async-start | bytes 2097152 | tf_op jit(solution)/shard_map/all_to_all | solution.py:286
  40.6 0.1 slice.4
  40.6 1.6 %collective-permute-start = (bf16[16,48,512]{2,1,0:T(8,128)(2,1)S(1)}, bf16[16,48,512]{2,1,0:T(8,128)(2,1)S(1)}, u32[]{:S(2)}, u32[]{:S(2)}) collective-permute-start(bf16[16,48,512]{2,1,0:T(8,128)(2,1)S(1)} %slice.4), channel_id=1, source_target_pairs={{0,16},{16,0},{1,17},{17,1},{2,18},{18,2},{3,19},{19,3},{4,20},{20... | collective-permute-start | bytes 2359304 | tf_op jit(solution)/shard_map/ppermute | solution.py:292
  42.2 18.4 %collective-permute-done.refs_1_ = bf16[16,48,512]{2,1,0:T(8,128)(2,1)S(1)} collective-permute-done((bf16[16,48,512]{2,1,0:T(8,128)(2,1)S(1)}, bf16[16,48,512]{2,1,0:T(8,128)(2,1)S(1)}, u32[]{:S(2)}, u32[]{:S(2)}) %collective-permute-start) | collective-permute-done | bytes 786464 | tf_op jit(solution)/shard_map/ppermute | solution.py:292
  60.6 10.2 %patch_weights.1.blended_ref = bf16[512,512]{1,0:T(8,128)(2,1)S(1)} custom-call(bf16[16,56,512]{2,1,0:T(8,128)(2,1)S(1)} %all_to_all.20.refs_0_, bf16[16,48,512]{2,1,0:T(8,128)(2,1)S(1)} %collective-permute-done.refs_1_), custom_call_target="tpu_custom_call" | custom-call | flops 7650410496 | bytes 1835008 | tf_op jit(solution)/shard_map/patch_weights/pallas_call | solution.py:197
  70.8 0.0 all-to-all-done.1
  70.8 1.8 %update_points.2 = bf16[512,1024]{1,0:T(8,128)(2,1)} custom-call(bf16[512,512]{1,0:T(8,128)(2,1)S(1)} %patch_weights.1.blended_ref, bf16[512,1024]{1,0:T(8,128)(2,1)S(1)} %bitcast.5), custom_call_target="tpu_custom_call" | custom-call | flops 536870912 | bytes 2621440 | tf_op jit(solution)/shard_map/update_points/pallas_call | solution.py:225
  72.7 5.7 %all-to-all-start.2 = ((bf16[16,32,1024]{2,1,0:T(8,128)(2,1)}), bf16[16,32,1024]{2,1,0:T(8,128)(2,1)S(1)}, u32[]{:S(2)}, u32[]{:S(2)}) async-start(bf16[16,32,1024]{2,1,0:T(8,128)(2,1)} %bitcast.3), calls=%async_computation.2 | async-start | bytes 2097152 | tf_op jit(solution)/shard_map/all_to_all | solution.py:286
  78.4 1.6 %collective-permute-start.1 = (bf16[512,1024]{1,0:T(8,128)(2,1)S(1)}, bf16[512,1024]{1,0:T(8,128)(2,1)S(1)}, u32[]{:S(2)}, u32[]{:S(2)}) collective-permute-start(bf16[512,1024]{1,0:T(8,128)(2,1)S(1)} %bitcast.6), channel_id=1, source_target_pairs={{0,16},{16,0},{1,17},{17,1},{2,18},{18,2},{3,19},{19,3},{4,20},{20... | collective-permute-start | bytes 3145736 | tf_op jit(solution)/shard_map/ppermute | solution.py:292
  79.9 23.9 %collective-permute-done.1.background_ref = bf16[512,1024]{1,0:T(8,128)(2,1)S(1)} collective-permute-done((bf16[512,1024]{1,0:T(8,128)(2,1)S(1)}, bf16[512,1024]{1,0:T(8,128)(2,1)S(1)}, u32[]{:S(2)}, u32[]{:S(2)}) %collective-permute-start.1) | collective-permute-done | bytes 1048608 | tf_op jit(solution)/shard_map/ppermute | solution.py:292
  103.9 0.9 update_points.3
  104.7 0.0 all-to-all-done.2.refs_0_
  104.7 30.4 %all_to_all.21.refs_1_ = bf16[16,32,1024]{2,1,0:T(8,128)(2,1)S(1)} all-to-all(bf16[16,32,1024]{2,1,0:T(8,128)(2,1)S(1)} %bitcast.7), channel_id=1, replica_groups=mesh['boot'=2,'space'=16] {'space'}, dimensions={0} | all-to-all | bytes 2097152 | tf_op jit(solution)/shard_map/all_to_all | solution.py:286
  135.1 1.5 %place_pieces.1 = bf16[32,32768]{1,0:T(8,128)(2,1)} custom-call(bf16[16,32,1024]{2,1,0:T(8,128)(2,1)S(1)} %all-to-all-done.2.refs_0_, bf16[16,32,1024]{2,1,0:T(8,128)(2,1)S(1)} %all_to_all.21.refs_1_), custom_call_target="tpu_custom_call" | custom-call | bytes 4194304 | tf_op jit(solution)/shard_map/place_pieces/pallas_call | solution.py:274
Async XLA Ops:
  33.4 1.6 %copy-start = (bf16[32,32768]{1,0:T(8,128)(2,1)S(1)}, bf16[32,32768]{1,0:T(8,128)(2,1)}, u32[]{:S(2)}) copy-start(bf16[32,32768]{1,0:T(8,128)(2,1)} %states_ref) | copy-start | bytes 6291460
  36.1 34.7 %all-to-all-start.1 = ((bf16[16,32,1024]{2,1,0:T(8,128)(2,1)}), bf16[16,32,1024]{2,1,0:T(8,128)(2,1)S(1)}, u32[]{:S(2)}, u32[]{:S(2)}) async-start(bf16[16,32,1024]{2,1,0:T(8,128)(2,1)} %cut_share.1), calls=%async_computation.1 | async-start | bytes 2097152 | tf_op jit(solution)/shard_map/all_to_all | solution.py:286
  40.6 19.9 %collective-permute-start = (bf16[16,48,512]{2,1,0:T(8,128)(2,1)S(1)}, bf16[16,48,512]{2,1,0:T(8,128)(2,1)S(1)}, u32[]{:S(2)}, u32[]{:S(2)}) collective-permute-start(bf16[16,48,512]{2,1,0:T(8,128)(2,1)S(1)} %slice.4), channel_id=1, source_target_pairs={{0,16},{16,0},{1,17},{17,1},{2,18},{18,2},{3,19},{19,3},{4,20},{20... | collective-permute-start | bytes 2359304 | tf_op jit(solution)/shard_map/ppermute | solution.py:292
  72.7 32.1 %all-to-all-start.2 = ((bf16[16,32,1024]{2,1,0:T(8,128)(2,1)}), bf16[16,32,1024]{2,1,0:T(8,128)(2,1)S(1)}, u32[]{:S(2)}, u32[]{:S(2)}) async-start(bf16[16,32,1024]{2,1,0:T(8,128)(2,1)} %bitcast.3), calls=%async_computation.2 | async-start | bytes 2097152 | tf_op jit(solution)/shard_map/all_to_all | solution.py:286
  78.4 25.5 %collective-permute-start.1 = (bf16[512,1024]{1,0:T(8,128)(2,1)S(1)}, bf16[512,1024]{1,0:T(8,128)(2,1)S(1)}, u32[]{:S(2)}, u32[]{:S(2)}) collective-permute-start(bf16[512,1024]{1,0:T(8,128)(2,1)S(1)} %bitcast.6), channel_id=1, source_target_pairs={{0,16},{16,0},{1,17},{17,1},{2,18},{18,2},{3,19},{19,3},{4,20},{20... | collective-permute-start | bytes 3145736 | tf_op jit(solution)/shard_map/ppermute | solution.py:292

commit v4 on v3

--- a/solution.py
+++ b/solution.py
@@ -9,8 +9,8 @@
 
 NS_STEPS = 6
 LANES = 128
-TAIL = 8
-FULL_STEPS = 2
+ROWS = 8
+FULL_STEPS = 1
 VMEM_BYTES = 48 * 1024 * 1024
 ALL_VMEM_BYTES = 64 * 1024 * 1024
 F32 = jnp.float32
@@ -27,9 +27,9 @@
         ]
     )
     targets_ref, local_ref, mult_ref, prec_ref, dep_ref, rows_ref = fetched
-    patches, depth, members = slots_ref.shape
-    share = depth - TAIL
-    count = rows_ref.shape[0]
+    patches = slots_ref.shape[0]
+    count, members = rows_ref.shape
+    share = (slots_ref.shape[2] - LANES) // members * ROWS
     mult = mult_ref[...].reshape(1, count).astype(F32)
     prec = prec_ref[...].reshape(1, count)
     weight = local_ref[...].astype(F32) / 1024.0 * (mult * prec)
@@ -63,19 +63,22 @@
     info = info_ref[...].T
     begin = lax.axis_index("boot") * share
     own_id = (lax.broadcasted_iota(jnp.int32, (share, count), 0) + begin).astype(F32)
-    tail_id = lax.broadcasted_iota(jnp.int32, (TAIL, LANES), 0)
-    blank = jnp.zeros((TAIL, members - LANES), F32)
-    rows = rows_ref[...]
+    tail_id = lax.broadcasted_iota(jnp.int32, (ROWS, LANES), 0)
+    picks = [
+        jnp.where(own_id == rank[patch : patch + 1, :], 1.0, 0.0) for patch in range(patches)
+    ]
+    picked = jnp.dot(
+        jnp.concatenate(picks, axis=0).astype(BF16), rows_ref[...], preferred_element_type=F32
+    )
     for patch in range(patches):
-        pick = jnp.where(own_id == rank[patch : patch + 1, :], 1.0, 0.0)
-        block = jnp.dot(pick.astype(BF16), rows, preferred_element_type=F32)
+        first = patch * share
+        blocks = [picked[first + i : first + i + ROWS, :] for i in range(0, share, ROWS)]
         tail = jnp.where(
             tail_id == 0,
             info[patch : patch + 1, :],
             jnp.where(tail_id == 1, info[patches + patch : patches + patch + 1, :], 0.0),
         )
-        tail = jnp.concatenate([tail, blank], axis=1)
-        slots_ref[patch] = jnp.concatenate([block, tail], axis=0).astype(BF16)
+        slots_ref[patch] = jnp.concatenate(blocks + [tail], axis=1).astype(BF16)
 
 
 def run_copies(copies):
@@ -90,7 +93,7 @@
     operands = (targets.T, local.T, mult, prec, dep, rows)
     return pl.pallas_call(
         functools.partial(pack_kernel, groups),
-        out_shape=jax.ShapeDtypeStruct((patches, share + TAIL, members), BF16),
+        out_shape=jax.ShapeDtypeStruct((patches, ROWS, share // ROWS * members + LANES), BF16),
         in_specs=[pl.BlockSpec(memory_space=pl.ANY)] * len(operands),
         scratch_shapes=[pltpu.VMEM(operand.shape, operand.dtype) for operand in operands]
         + [pltpu.VMEM((LANES, LANES), F32), pltpu.SemaphoreType.DMA((len(operands),))],
@@ -114,36 +117,79 @@
     return dot(left_high, right_high) + (dot(left_high, right_low) + dot(left_low, right_high))
 
 
-def weights_kernel(*refs):
-    rows_refs, blended_ref, info_ref = refs[:-10], refs[-10], refs[-9]
-    y_ref, z_ref, y_high, y_low, z_high, z_low, w_high, w_low = refs[-8:]
-    groups = len(rows_refs)
-    sources, depth, members = rows_refs[0].shape
-    share = depth - TAIL
+def add_rows(rows_ref, info, gram, drive):
+    sources = rows_ref.shape[0]
+    members = gram.shape[0]
+    share = info.shape[0]
+    rows, scaled = [], []
     for source in range(sources):
-        tail = rows_refs[0][source].astype(F32)[share:depth, 0:LANES]
+        block = rows_ref[source].astype(F32)
+        block = jnp.concatenate(
+            [block[:, i * members : (i + 1) * members] for i in range(share // ROWS)], axis=0
+        )
+        rows.append(block)
+        block = (info[:, source : source + 1] * block).astype(BF16).astype(F32)
+        scaled.append(block)
+        dep_col = info[:, sources + source : sources + source + 1]
+        drive = drive + jnp.sum(dep_col * block, axis=0, keepdims=True)
+    gram = gram + lax.dot_general(
+        jnp.concatenate(rows, axis=0).astype(BF16),
+        jnp.concatenate(scaled, axis=0).astype(BF16),
+        (((0,), (0,)), ((), ())),
+        preferred_element_type=F32,
+    )
+    return gram, drive
+
+
+def gram_kernel(share, rows_ref, gram_ref, drive_ref, info_ref):
+    sources, _, width = rows_ref.shape
+    members = gram_ref.shape[0]
+    for source in range(sources):
+        tail = rows_ref[source].astype(F32)[:, width - LANES :]
         info_ref[source : source + 1, :] = tail[0:1, :]
         info_ref[sources + source : sources + source + 1, :] = tail[1:2, :]
+    if 2 * sources < LANES:
+        info_ref[2 * sources :, :] = jnp.zeros((LANES - 2 * sources, LANES), F32)
     info_ref[...] = info_ref[...].T
-    gram = jnp.zeros((members, members), F32)
-    drive = jnp.zeros((1, members), F32)
+    begin = lax.axis_index("boot") * share
+    info = info_ref[pl.ds(pl.multiple_of(begin, ROWS), share), :]
+    gram, drive = add_rows(
+        rows_ref, info, jnp.zeros((members, members), F32), jnp.zeros((1, members), F32)
+    )
+    gram_ref[...] = gram
+    drive_ref[...] = drive
+
+
+def own_gram(rows, share, members):
+    sources, _, width = rows.shape
+    return pl.pallas_call(
+        functools.partial(gram_kernel, share),
+        out_shape=(
+            jax.ShapeDtypeStruct((members, members), F32),
+            jax.ShapeDtypeStruct((1, members), F32),
+            jax.ShapeDtypeStruct((LANES, LANES), F32),
+        ),
+        compiler_params=pltpu.CompilerParams(vmem_limit_bytes=VMEM_BYTES),
+        cost_estimate=pl.CostEstimate(
+            flops=4 * members * members * sources * share,
+            bytes_accessed=2 * sources * ROWS * width,
+            transcendentals=0,
+        ),
+        name="own_gram",
+    )(rows)
+
+
+def weights_kernel(share, *refs):
+    gram_ref, drive_ref, info_ref = refs[:3]
+    rows_refs, blended_ref = refs[3:-9], refs[-9]
+    y_ref, z_ref, y_high, y_low, z_high, z_low, w_high, w_low = refs[-8:]
+    groups = len(rows_refs) + 1
+    members = gram_ref.shape[0]
+    gram, drive = gram_ref[...], drive_ref[...]
     for turn, rows_ref in enumerate(rows_refs):
-        begin = lax.rem(lax.axis_index("boot") + turn, groups) * share
-        info = info_ref[pl.ds(pl.multiple_of(begin, 8), share), :]
-        rows, scaled = [], []
-        for source in range(sources):
-            block = rows_ref[source].astype(F32)[0:share, :]
-            rows.append(block)
-            block = (info[:, source : source + 1] * block).astype(BF16).astype(F32)
-            scaled.append(block)
-            dep_col = info[:, sources + source : sources + source + 1]
-            drive += jnp.sum(dep_col * block, axis=0, keepdims=True)
-        gram += lax.dot_general(
-            jnp.concatenate(rows, axis=0).astype(BF16),
-            jnp.concatenate(scaled, axis=0).astype(BF16),
-            (((0,), (0,)), ((), ())),
-            preferred_element_type=F32,
-        )
+        begin = lax.rem(lax.axis_index("boot") + turn + 1, groups) * share
+        info = info_ref[pl.ds(pl.multiple_of(begin, ROWS), share), :]
+        gram, drive = add_rows(rows_ref, info, gram, drive)
 
     row_id = lax.broadcasted_iota(jnp.int32, (members, members), 0)
     col_id = lax.broadcasted_iota(jnp.int32, (members, members), 1)
@@ -190,22 +236,22 @@
     blended_ref[...] = (root + mean_weight).astype(BF16)
 
 
-def patch_weights(rows):
-    sources, depth, members = rows[0].shape
+def patch_weights(gram, drive, info, rows, share):
+    members = gram.shape[0]
     whole = pltpu.VMEM((members, members), F32)
     half = pltpu.VMEM((members, members), BF16)
     return pl.pallas_call(
-        weights_kernel,
+        functools.partial(weights_kernel, share),
         out_shape=jax.ShapeDtypeStruct((members, members), BF16),
-        scratch_shapes=[pltpu.VMEM((LANES, LANES), F32)] + [whole] * 2 + [half] * 6,
+        scratch_shapes=[whole] * 2 + [half] * 6,
         compiler_params=pltpu.CompilerParams(vmem_limit_bytes=VMEM_BYTES),
         cost_estimate=pl.CostEstimate(
-            flops=2 * members * members * (len(rows) * sources * depth + 25 * members),
-            bytes_accessed=2 * len(rows) * sources * depth * members,
+            flops=80 * members * members * members,
+            bytes_accessed=8 * members * members,
             transcendentals=0,
         ),
         name="patch_weights",
-    )(*rows)
+    )(gram, drive, info, *rows)
 
 
 def update_kernel(blended_ref, background_ref, analysis_ref):
@@ -308,7 +354,7 @@
     local_rows = measurement_anomaly_matrix.shape[0]
     targets_per = measurement_region_targets.shape[1]
     slot_cap = 2 * targets_per * local_rows // device_count
-    slot_share = -(-slot_cap // (8 * groups)) * 8
+    slot_share = -(-slot_cap // (ROWS * groups)) * ROWS
     own_members, points = background_states.shape
     share = points // device_count // groups
 
@@ -324,13 +370,15 @@
         groups,
     )
     own_rows = exchange(slots)
-    rows = [own_rows] + swap_shares(own_rows[:, :slot_share])
-    own_rows, background_states = lax.optimization_barrier((own_rows, background_states))
-    own_points = exchange(cut_share(background_states, device_count, share))
-    own_points = own_points.reshape(-1, share)
+    other_rows = swap_shares(own_rows)
+    own_points = cut_share(background_states, device_count, share)
+    own_rows, own_points = lax.optimization_barrier((own_rows, own_points))
+    own_points = exchange(own_points).reshape(-1, share)
     background = [own_points] + swap_shares(own_points)
 
-    blended = patch_weights(rows)
+    members = measurement_anomaly_matrix.shape[1]
+    gram, drive, info = own_gram(own_rows, slot_share, members)
+    blended = patch_weights(gram, drive, info, other_rows, slot_share)
     pieces = []
     for part in background:
         analysis = update_points(blended, part).reshape(device_count, own_members, share)

time: 137 us -> 130 us (0.949)
  blocking collectives: 60.4 us -> 30.4 us
  waiting for transfers between devices: 42.3 us -> 58.7 us
  starting transfers between devices: 13.3 us -> 21.9 us
  Pallas kernels: 18.9 us -> 17 us
    all_to_all x2 -> x1, blocking collectives: 60.4 us -> 30.4 us  [exchange(): lax.all_to_all(blocks, 'space', split_axis=0, concat_axis=0, tiled=True)]
    all_to_all x2 -> x3, waiting for transfers between devices: 0.01 us -> 16.6 us  [exchange(): lax.all_to_all(blocks, 'space', split_axis=0, concat_axis=0, tiled=True)]
    all_to_all x2 -> x3, starting transfers between devices: 10.2 us -> 18.8 us  [exchange(): lax.all_to_all(blocks, 'space', split_axis=0, concat_axis=0, tiled=True)]
    pallas_call x1 -> x2, Pallas kernels: 10.2 us -> 8.93 us  [the longest x1 8.07 us: patch_weights(): pl.pallas_call(functools.partial(weights_kernel, share), out_shape=jax.Sh...]
  transfers between devices with their start and end apart: 4 -> 5, of which waited for: 2 -> 3; matrix products, arithmetic and copies ran while one was open for 0% -> 0% of each run, Pallas kernels for 8% -> 8%
where the time goes in v4:
time: 130 us
  waiting for transfers between devices  58.7 us (45%)
  blocking collectives  30.4 us (23%)
  starting transfers between devices  21.9 us (17%)
  Pallas kernels  17 us (13%)
  local copies, waits for them, and re-layouts  1.59 us (1%)
    ppermute x2, waiting for transfers between devices, swap_shares(): lax.ppermute(own, 'boot', [(g, (g - turn) % groups) for g in range(groups)])  42 us
    all_to_all x1, blocking collectives, exchange(): lax.all_to_all(blocks, 'space', split_axis=0, concat_axis=0, tiled=True)  30.4 us
    all_to_all x3, starting transfers between devices, exchange(): lax.all_to_all(blocks, 'space', split_axis=0, concat_axis=0, tiled=True)  18.8 us
    all_to_all x3, waiting for transfers between devices, exchange(): lax.all_to_all(blocks, 'space', split_axis=0, concat_axis=0, tiled=True)  16.6 us
    pallas_call x1, Pallas kernels, patch_weights(): pl.pallas_call(functools.partial(weights_kernel, share), out_shape=jax.Sh...  8.07 us
    ppermute x2, starting transfers between devices, swap_shares(): lax.ppermute(own, 'boot', [(g, (g - turn) % groups) for g in range(groups)])  3.14 us
    pallas_call x1, Pallas kernels, pack(): pl.pallas_call(functools.partial(pack_kernel, groups), out_shape=jax.Shap...  2.85 us
    pallas_call x2, Pallas kernels, update_points(): pl.pallas_call(update_kernel, out_shape=jax.ShapeDtypeStruct((members, po...  2.7 us
  transfers between devices with their start and end apart: 5, of which 3 were waited for; matrix products, arithmetic and copies ran while one was open for 0% of the time, Pallas kernels for 8%

profile of v4, /device:TPU:0, one launch (start us, length us, event | category | flops | bytes accessed | tf_op | source)
XLA Modules:
  0.0 129.6 jit_solution(4696282823482076299)
XLA Ops:
  0.0 2.8 %pack_rows.1 = bf16[16,8,3200]{2,1,0:T(8,128)(2,1)} custom-call(s32[2,384]{1,0:T(2,128)} %bitcast.8, s32[2,384]{1,0:T(2,128)} %bitcast.9, s32[384]{0:T(512)} %refs_2_.1, f32[384]{0:T(512)} %refs_3_.1, bf16[384]{0:T(512)(128)(2,1)} %refs_4_.1, bf16[384,512]{1,0:T(8,128)(2,1)} %refs_5_.1), custom_call_target="tpu_custom_call" | custom-call | flops 301989888 | bytes 1179648 | tf_op jit(solution)/shard_map/pack_rows/pallas_call | solution.py:94
  2.9 7.4 %all-to-all-start = ((bf16[16,8,3200]{2,1,0:T(8,128)(2,1)}), bf16[16,8,3200]{2,1,0:T(8,128)(2,1)S(1)}, u32[]{:S(2)}, u32[]{:S(2)}) async-start(bf16[16,8,3200]{2,1,0:T(8,128)(2,1)} %pack_rows.1), calls=%async_computation | async-start | bytes 1638400 | tf_op jit(solution)/shard_map/all_to_all | solution.py:332
  10.3 0.0 copy-start
  10.3 1.6 %copy-done = bf16[32,32768]{1,0:T(8,128)(2,1)S(1)} copy-done((bf16[32,32768]{1,0:T(8,128)(2,1)S(1)}, bf16[32,32768]{1,0:T(8,128)(2,1)}, u32[]{:S(2)}) %copy-start) | copy-done | bytes 2097176
  11.9 1.0 cut_share.1
  12.9 16.6 %all-to-all-done.rows_ref = bf16[16,8,3200]{2,1,0:T(8,128)(2,1)S(1)} async-done(((bf16[16,8,3200]{2,1,0:T(8,128)(2,1)}), bf16[16,8,3200]{2,1,0:T(8,128)(2,1)S(1)}, u32[]{:S(2)}, u32[]{:S(2)}) %all-to-all-start) | async-done | bytes 819232 | tf_op jit(solution)/shard_map/all_to_all | solution.py:332
  29.5 5.7 %all-to-all-start.1 = ((bf16[16,32,1024]{2,1,0:T(8,128)(2,1)}), bf16[16,32,1024]{2,1,0:T(8,128)(2,1)S(1)}, u32[]{:S(2)}, u32[]{:S(2)}) async-start(bf16[16,32,1024]{2,1,0:T(8,128)(2,1)} %cut_share.1), calls=%async_computation.1 | async-start | bytes 2097152 | tf_op jit(solution)/shard_map/all_to_all | solution.py:332
  35.1 1.6 %collective-permute-start = (bf16[16,8,3200]{2,1,0:T(8,128)(2,1)S(1)}, bf16[16,8,3200]{2,1,0:T(8,128)(2,1)S(1)}, u32[]{:S(2)}, u32[]{:S(2)}) collective-permute-start(bf16[16,8,3200]{2,1,0:T(8,128)(2,1)S(1)} %all-to-all-done.rows_ref), channel_id=1, source_target_pairs={{0,16},{16,0},{1,17},{17,1},{2,18},{18,2},{3,19},{19,3},{4,20},{20... | collective-permute-start | bytes 2457608 | tf_op jit(solution)/shard_map/ppermute | solution.py:338
  36.7 0.9 own_gram.1
  37.6 18.1 %collective-permute-done.refs_3_ = bf16[16,8,3200]{2,1,0:T(8,128)(2,1)S(1)} collective-permute-done((bf16[16,8,3200]{2,1,0:T(8,128)(2,1)S(1)}, bf16[16,8,3200]{2,1,0:T(8,128)(2,1)S(1)}, u32[]{:S(2)}, u32[]{:S(2)}) %collective-permute-start) | collective-permute-done | bytes 819232 | tf_op jit(solution)/shard_map/ppermute | solution.py:338
  55.7 8.1 %patch_weights.1.blended_ref = bf16[512,512]{1,0:T(8,128)(2,1)S(1)} custom-call(f32[512,512]{1,0:T(8,128)S(1)} %get-tuple-element.11.refs_0_, f32[1,512]{1,0:T(1,128)S(1)} %get-tuple-element.12.refs_1_, f32[128,128]{1,0:T(8,128)S(1)} %get-tuple-element.13.refs_2_, bf16[16,8,3200]{2,1,0:T(8,128)(2,1)S(1)} %collective-permute-done.refs_3_), custom_call_target="tpu_custom_call" | custom-call | flops 10737418240 | bytes 2097152 | tf_op jit(solution)/shard_map/patch_weights/pallas_call | solution.py:243
  63.8 0.0 all-to-all-done.1
  63.8 1.8 %update_points.2 = bf16[512,1024]{1,0:T(8,128)(2,1)} custom-call(bf16[512,512]{1,0:T(8,128)(2,1)S(1)} %patch_weights.1.blended_ref, bf16[512,1024]{1,0:T(8,128)(2,1)S(1)} %bitcast.5), custom_call_target="tpu_custom_call" | custom-call | flops 536870912 | bytes 2621440 | tf_op jit(solution)/shard_map/update_points/pallas_call | solution.py:271
  65.6 5.7 %all-to-all-start.2 = ((bf16[16,32,1024]{2,1,0:T(8,128)(2,1)}), bf16[16,32,1024]{2,1,0:T(8,128)(2,1)S(1)}, u32[]{:S(2)}, u32[]{:S(2)}) async-start(bf16[16,32,1024]{2,1,0:T(8,128)(2,1)} %bitcast.3), calls=%async_computation.2 | async-start | bytes 2097152 | tf_op jit(solution)/shard_map/all_to_all | solution.py:332
  71.4 1.6 %collective-permute-start.1 = (bf16[512,1024]{1,0:T(8,128)(2,1)S(1)}, bf16[512,1024]{1,0:T(8,128)(2,1)S(1)}, u32[]{:S(2)}, u32[]{:S(2)}) collective-permute-start(bf16[512,1024]{1,0:T(8,128)(2,1)S(1)} %bitcast.6), channel_id=1, source_target_pairs={{0,16},{16,0},{1,17},{17,1},{2,18},{18,2},{3,19},{19,3},{4,20},{20... | collective-permute-start | bytes 3145736 | tf_op jit(solution)/shard_map/ppermute | solution.py:338
  73.0 23.9 %collective-permute-done.1.background_ref = bf16[512,1024]{1,0:T(8,128)(2,1)S(1)} collective-permute-done((bf16[512,1024]{1,0:T(8,128)(2,1)S(1)}, bf16[512,1024]{1,0:T(8,128)(2,1)S(1)}, u32[]{:S(2)}, u32[]{:S(2)}) %collective-permute-start.1) | collective-permute-done | bytes 1048608 | tf_op jit(solution)/shard_map/ppermute | solution.py:338
  96.9 0.9 update_points.3
  97.7 0.0 all-to-all-done.2.refs_0_
  97.7 30.4 %all_to_all.20.refs_1_ = bf16[16,32,1024]{2,1,0:T(8,128)(2,1)S(1)} all-to-all(bf16[16,32,1024]{2,1,0:T(8,128)(2,1)S(1)} %bitcast.7), channel_id=1, replica_groups=mesh['boot'=2,'space'=16] {'space'}, dimensions={0} | all-to-all | bytes 2097152 | tf_op jit(solution)/shard_map/all_to_all | solution.py:332
  128.1 1.5 %place_pieces.1 = bf16[32,32768]{1,0:T(8,128)(2,1)} custom-call(bf16[16,32,1024]{2,1,0:T(8,128)(2,1)S(1)} %all-to-all-done.2.refs_0_, bf16[16,32,1024]{2,1,0:T(8,128)(2,1)S(1)} %all_to_all.20.refs_1_), custom_call_target="tpu_custom_call" | custom-call | bytes 4194304 | tf_op jit(solution)/shard_map/place_pieces/pallas_call | solution.py:320
Async XLA Ops:
  2.9 26.6 %all-to-all-start = ((bf16[16,8,3200]{2,1,0:T(8,128)(2,1)}), bf16[16,8,3200]{2,1,0:T(8,128)(2,1)S(1)}, u32[]{:S(2)}, u32[]{:S(2)}) async-start(bf16[16,8,3200]{2,1,0:T(8,128)(2,1)} %pack_rows.1), calls=%async_computation | async-start | bytes 1638400 | tf_op jit(solution)/shard_map/all_to_all | solution.py:332
  10.3 1.6 %copy-start = (bf16[32,32768]{1,0:T(8,128)(2,1)S(1)}, bf16[32,32768]{1,0:T(8,128)(2,1)}, u32[]{:S(2)}) copy-start(bf16[32,32768]{1,0:T(8,128)(2,1)} %states_ref.1) | copy-start | bytes 6291460
  29.5 34.3 %all-to-all-start.1 = ((bf16[16,32,1024]{2,1,0:T(8,128)(2,1)}), bf16[16,32,1024]{2,1,0:T(8,128)(2,1)S(1)}, u32[]{:S(2)}, u32[]{:S(2)}) async-start(bf16[16,32,1024]{2,1,0:T(8,128)(2,1)} %cut_share.1), calls=%async_computation.1 | async-start | bytes 2097152 | tf_op jit(solution)/shard_map/all_to_all | solution.py:332
  35.1 20.6 %collective-permute-start = (bf16[16,8,3200]{2,1,0:T(8,128)(2,1)S(1)}, bf16[16,8,3200]{2,1,0:T(8,128)(2,1)S(1)}, u32[]{:S(2)}, u32[]{:S(2)}) collective-permute-start(bf16[16,8,3200]{2,1,0:T(8,128)(2,1)S(1)} %all-to-all-done.rows_ref), channel_id=1, source_target_pairs={{0,16},{16,0},{1,17},{17,1},{2,18},{18,2},{3,19},{19,3},{4,20},{20... | collective-permute-start | bytes 2457608 | tf_op jit(solution)/shard_map/ppermute | solution.py:338
  65.6 32.1 %all-to-all-start.2 = ((bf16[16,32,1024]{2,1,0:T(8,128)(2,1)}), bf16[16,32,1024]{2,1,0:T(8,128)(2,1)S(1)}, u32[]{:S(2)}, u32[]{:S(2)}) async-start(bf16[16,32,1024]{2,1,0:T(8,128)(2,1)} %bitcast.3), calls=%async_computation.2 | async-start | bytes 2097152 | tf_op jit(solution)/shard_map/all_to_all | solution.py:332
  71.4 25.5 %collective-permute-start.1 = (bf16[512,1024]{1,0:T(8,128)(2,1)S(1)}, bf16[512,1024]{1,0:T(8,128)(2,1)S(1)}, u32[]{:S(2)}, u32[]{:S(2)}) collective-permute-start(bf16[512,1024]{1,0:T(8,128)(2,1)S(1)} %bitcast.6), channel_id=1, source_target_pairs={{0,16},{16,0},{1,17},{17,1},{2,18},{18,2},{3,19},{19,3},{4,20},{20... | collective-permute-start | bytes 3145736 | tf_op jit(solution)/shard_map/ppermute | solution.py:338

commit v5 on v4

--- a/solution.py
+++ b/solution.py
@@ -117,23 +117,39 @@
     return dot(left_high, right_high) + (dot(left_high, right_low) + dot(left_low, right_high))
 
 
-def add_rows(rows_ref, info, gram, drive):
-    sources = rows_ref.shape[0]
-    members = gram.shape[0]
-    share = info.shape[0]
-    rows, scaled = [], []
+def slot_rows(rows_ref, members):
+    blocks = []
+    for source in range(rows_ref.shape[0]):
+        block = rows_ref[source].astype(F32)
+        for begin in range(0, block.shape[1] - LANES, members):
+            blocks.append(block[:, begin : begin + members])
+    return jnp.concatenate(blocks, axis=0)
+
+
+def slot_info(rows_ref, info_ref):
+    sources, _, width = rows_ref.shape
+    if 2 * sources < LANES:
+        info_ref[2 * sources :, :] = jnp.zeros((LANES - 2 * sources, LANES), F32)
     for source in range(sources):
-        block = rows_ref[source].astype(F32)
-        block = jnp.concatenate(
-            [block[:, i * members : (i + 1) * members] for i in range(share // ROWS)], axis=0
-        )
-        rows.append(block)
+        tail = rows_ref[source].astype(F32)[:, width - LANES :]
+        info_ref[source : source + 1, :] = tail[0:1, :]
+        info_ref[sources + source : sources + source + 1, :] = tail[1:2, :]
+    info_ref[...] = info_ref[...].T
+
+
+def add_rows(rows, info_ref, turn, sources, gram, drive):
+    share = rows.shape[0] // sources
+    begin = lax.rem(lax.axis_index("boot") + turn, lax.axis_size("boot")) * share
+    info = info_ref[pl.ds(pl.multiple_of(begin, ROWS), share), :]
+    scaled = []
+    for source in range(sources):
+        block = rows[source * share : (source + 1) * share, :]
         block = (info[:, source : source + 1] * block).astype(BF16).astype(F32)
         scaled.append(block)
         dep_col = info[:, sources + source : sources + source + 1]
         drive = drive + jnp.sum(dep_col * block, axis=0, keepdims=True)
     gram = gram + lax.dot_general(
-        jnp.concatenate(rows, axis=0).astype(BF16),
+        rows.astype(BF16),
         jnp.concatenate(scaled, axis=0).astype(BF16),
         (((0,), (0,)), ((), ())),
         preferred_element_type=F32,
@@ -141,29 +157,23 @@
     return gram, drive
 
 
-def gram_kernel(share, rows_ref, gram_ref, drive_ref, info_ref):
-    sources, _, width = rows_ref.shape
+def gram_kernel(rows_ref, gram_ref, drive_ref, info_ref):
     members = gram_ref.shape[0]
-    for source in range(sources):
-        tail = rows_ref[source].astype(F32)[:, width - LANES :]
-        info_ref[source : source + 1, :] = tail[0:1, :]
-        info_ref[sources + source : sources + source + 1, :] = tail[1:2, :]
-    if 2 * sources < LANES:
-        info_ref[2 * sources :, :] = jnp.zeros((LANES - 2 * sources, LANES), F32)
-    info_ref[...] = info_ref[...].T
-    begin = lax.axis_index("boot") * share
-    info = info_ref[pl.ds(pl.multiple_of(begin, ROWS), share), :]
-    gram, drive = add_rows(
-        rows_ref, info, jnp.zeros((members, members), F32), jnp.zeros((1, members), F32)
-    )
-    gram_ref[...] = gram
-    drive_ref[...] = drive
-
-
-def own_gram(rows, share, members):
+    slot_info(rows_ref, info_ref)
+    gram_ref[...], drive_ref[...] = add_rows(
+        slot_rows(rows_ref, members),
+        info_ref,
+        0,
+        rows_ref.shape[0],
+        jnp.zeros((members, members), F32),
+        jnp.zeros((1, members), F32),
+    )
+
+
+def own_gram(rows, members):
     sources, _, width = rows.shape
     return pl.pallas_call(
-        functools.partial(gram_kernel, share),
+        gram_kernel,
         out_shape=(
             jax.ShapeDtypeStruct((members, members), F32),
             jax.ShapeDtypeStruct((1, members), F32),
@@ -171,7 +181,7 @@
         ),
         compiler_params=pltpu.CompilerParams(vmem_limit_bytes=VMEM_BYTES),
         cost_estimate=pl.CostEstimate(
-            flops=4 * members * members * sources * share,
+            flops=4 * members * sources * ROWS * width,
             bytes_accessed=2 * sources * ROWS * width,
             transcendentals=0,
         ),
@@ -179,74 +189,84 @@
     )(rows)
 
 
-def weights_kernel(share, *refs):
-    gram_ref, drive_ref, info_ref = refs[:3]
-    rows_refs, blended_ref = refs[3:-9], refs[-9]
+def weights_kernel(*refs):
+    gram_ref, drive_ref, own_info_ref = refs[:3]
+    rows_refs, blended_ref, info_ref = refs[3:-10], refs[-10], refs[-9]
     y_ref, z_ref, y_high, y_low, z_high, z_low, w_high, w_low = refs[-8:]
-    groups = len(rows_refs) + 1
-    members = gram_ref.shape[0]
-    gram, drive = gram_ref[...], drive_ref[...]
-    for turn, rows_ref in enumerate(rows_refs):
-        begin = lax.rem(lax.axis_index("boot") + turn + 1, groups) * share
-        info = info_ref[pl.ds(pl.multiple_of(begin, ROWS), share), :]
-        gram, drive = add_rows(rows_ref, info, gram, drive)
-
+    groups, members, _ = blended_ref.shape
+    sources = rows_refs[0].shape[0]
     row_id = lax.broadcasted_iota(jnp.int32, (members, members), 0)
     col_id = lax.broadcasted_iota(jnp.int32, (members, members), 1)
     diagonal = row_id == col_id
     identity = jnp.where(diagonal, 1.0, 0.0)
-    shifted = identity + gram / (members - 1.0)
-    squares = jnp.sum(jnp.sum(shifted * shifted, axis=0, keepdims=True), axis=1, keepdims=True)
-    frobenius = jnp.sqrt(squares)
     dot = functools.partial(jnp.dot, preferred_element_type=F32)
-
-    def put(high_ref, low_ref, value):
-        high_ref[...], low_ref[...] = halves(value)
+    rows = [slot_rows(rows_ref, members) for rows_ref in rows_refs]
+    frobenius, drives = [], []
+    for chain in range(groups):
+        if chain == 0:
+            gram, drive = gram_ref[...], drive_ref[...]
+        else:
+            slot_info(rows_refs[chain], info_ref.at[chain])
+            gram, drive = jnp.zeros((members, members), F32), jnp.zeros((1, members), F32)
+        for turn in range(groups):
+            if chain or turn:
+                gram, drive = add_rows(
+                    rows[turn],
+                    info_ref.at[chain] if chain else own_info_ref,
+                    turn,
+                    sources,
+                    gram,
+                    drive,
+                )
+        shifted = identity + gram / (members - 1.0)
+        squares = jnp.sum(jnp.sum(shifted * shifted, axis=0, keepdims=True), axis=1, keepdims=True)
+        frobenius.append(jnp.sqrt(squares))
+        drives.append(drive)
+        current = shifted / frobenius[chain]
+        y_high[chain] = current.astype(BF16)
+        z_ref[chain] = 1.5 * identity - 0.5 * current
+        y_ref[chain] = 1.5 * current - 0.5 * dot(y_high[chain], y_high[chain])
+        y_high[chain], z_high[chain] = y_ref[chain].astype(BF16), z_ref[chain].astype(BF16)
 
     def step(_, carry):
-        w_high[...] = dot(z_high[...], y_high[...]).astype(BF16)
-        current = 1.5 * y_ref[...] - 0.5 * dot(y_high[...], w_high[...])
-        root = 1.5 * z_ref[...] - 0.5 * dot(w_high[...], z_high[...])
-        y_ref[...], z_ref[...] = current, root
-        y_high[...], z_high[...] = current.astype(BF16), root.astype(BF16)
+        for chain in range(groups):
+            w_high[chain] = dot(z_high[chain], y_high[chain]).astype(BF16)
+        for chain in range(groups):
+            current = 1.5 * y_ref[chain] - 0.5 * dot(y_high[chain], w_high[chain])
+            root = 1.5 * z_ref[chain] - 0.5 * dot(w_high[chain], z_high[chain])
+            y_ref[chain], z_ref[chain] = current, root
+            y_high[chain], z_high[chain] = current.astype(BF16), root.astype(BF16)
         return carry
 
-    current = shifted / frobenius
-    y_high[...] = current.astype(BF16)
-    root = 1.5 * identity - 0.5 * current
-    current = 1.5 * current - 0.5 * dot(y_high[...], y_high[...])
-    y_ref[...], z_ref[...] = current, root
-    y_high[...], z_high[...] = current.astype(BF16), root.astype(BF16)
-    lax.fori_loop(1, NS_STEPS - FULL_STEPS, step, 0)
-    for full in range(FULL_STEPS):
-        put(y_high, y_low, y_ref[...])
-        put(z_high, z_low, z_ref[...])
-        put(w_high, w_low, product(z_high[...], z_low[...], y_high[...], y_low[...]))
-        if full < FULL_STEPS - 1:
-            change = product(y_high[...], y_low[...], w_high[...], w_low[...])
-            y_ref[...] = 1.5 * y_ref[...] - 0.5 * change
-        change = product(w_high[...], w_low[...], z_high[...], z_low[...])
-        z_ref[...] = 1.5 * z_ref[...] - 0.5 * change
-    root = z_ref[...] / jnp.sqrt(frobenius)
-
-    drive_col = jnp.sum(jnp.where(diagonal, drive, 0.0), axis=1, keepdims=True)
-    inner = jnp.sum(root * drive_col, axis=0, keepdims=True)
-    inner_col = jnp.sum(jnp.where(diagonal, inner, 0.0), axis=1, keepdims=True)
-    mean_weight = jnp.sum(root * inner_col, axis=0, keepdims=True) / (members - 1.0)
-    blended_ref[...] = (root + mean_weight).astype(BF16)
-
-
-def patch_weights(gram, drive, info, rows, share):
-    members = gram.shape[0]
-    whole = pltpu.VMEM((members, members), F32)
-    half = pltpu.VMEM((members, members), BF16)
-    return pl.pallas_call(
-        functools.partial(weights_kernel, share),
-        out_shape=jax.ShapeDtypeStruct((members, members), BF16),
-        scratch_shapes=[whole] * 2 + [half] * 6,
+    lax.fori_loop(1, NS_STEPS - 1, step, 0)
+    for chain in range(groups):
+        y_low[chain] = (y_ref[chain] - y_high[chain].astype(F32)).astype(BF16)
+        z_low[chain] = (z_ref[chain] - z_high[chain].astype(F32)).astype(BF16)
+    for chain in range(groups):
+        w_high[chain], w_low[chain] = halves(
+            product(z_high[chain], z_low[chain], y_high[chain], y_low[chain])
+        )
+    for chain in range(groups):
+        change = product(w_high[chain], w_low[chain], z_high[chain], z_low[chain])
+        root = (1.5 * z_ref[chain] - 0.5 * change) / jnp.sqrt(frobenius[chain])
+        drive_col = jnp.sum(jnp.where(diagonal, drives[chain], 0.0), axis=1, keepdims=True)
+        inner = jnp.sum(root * drive_col, axis=0, keepdims=True)
+        inner_col = jnp.sum(jnp.where(diagonal, inner, 0.0), axis=1, keepdims=True)
+        mean_weight = jnp.sum(root * inner_col, axis=0, keepdims=True) / (members - 1.0)
+        blended_ref[chain] = (root + mean_weight).astype(BF16)
+
+
+def patch_weights(gram, drive, info, rows):
+    groups, members = len(rows), gram.shape[0]
+    whole = pltpu.VMEM((groups, members, members), F32)
+    half = pltpu.VMEM((groups, members, members), BF16)
+    return pl.pallas_call(
+        weights_kernel,
+        out_shape=jax.ShapeDtypeStruct((groups, members, members), BF16),
+        scratch_shapes=[pltpu.VMEM((groups, LANES, LANES), F32)] + [whole] * 2 + [half] * 6,
         compiler_params=pltpu.CompilerParams(vmem_limit_bytes=VMEM_BYTES),
         cost_estimate=pl.CostEstimate(
-            flops=80 * members * members * members,
+            flops=80 * groups * members * members * members,
             bytes_accessed=8 * members * members,
             transcendentals=0,
         ),
@@ -255,6 +275,7 @@
 
 
 def update_kernel(blended_ref, background_ref, analysis_ref):
+    groups = blended_ref.shape[0]
     members, points = background_ref.shape
     tile = min(points, 256)
     for begin in range(0, points, tile):
@@ -262,19 +283,22 @@
         background = background_ref[:, columns].astype(F32)
         centre = jnp.sum(background, axis=0, keepdims=True) / members
         perturb = (background - centre).astype(BF16)
-        update = jnp.dot(blended_ref[...], perturb, preferred_element_type=F32)
-        analysis_ref[:, columns] = (centre + update).astype(BF16)
+        for turn in range(groups):
+            update = jnp.dot(blended_ref[turn], perturb, preferred_element_type=F32)
+            group = lax.rem(lax.axis_index("boot") + turn, groups)
+            analysis_ref[group, :, columns] = (centre + update).astype(BF16)
 
 
 def update_points(blended, background):
+    groups = blended.shape[0]
     members, points = background.shape
     return pl.pallas_call(
         update_kernel,
-        out_shape=jax.ShapeDtypeStruct((members, points), BF16),
+        out_shape=jax.ShapeDtypeStruct((groups, members, points), BF16),
         compiler_params=pltpu.CompilerParams(vmem_limit_bytes=VMEM_BYTES),
         cost_estimate=pl.CostEstimate(
-            flops=2 * members * members * points,
-            bytes_accessed=4 * members * points + 2 * members * members,
+            flops=2 * groups * members * members * points,
+            bytes_accessed=2 * (groups + 1) * members * points,
             transcendentals=0,
         ),
         name="update_points",
@@ -303,20 +327,17 @@
     )(states)
 
 
-def place_kernel(*refs):
-    piece_refs, whole_ref = refs[:-1], refs[-1]
-    groups = len(piece_refs)
-    patches, _, share = piece_refs[0].shape
-    for turn, piece_ref in enumerate(piece_refs):
-        offset = lax.rem(lax.axis_index("boot") + turn, groups) * share
-        for patch in range(patches):
-            begin = pl.multiple_of(patch * groups * share + offset, LANES)
-            whole_ref[:, pl.ds(begin, share)] = piece_ref[patch]
+def place_kernel(pieces_ref, whole_ref):
+    groups, patches, _, share = pieces_ref.shape
+    for patch in range(patches):
+        for group in range(groups):
+            begin = (patch * groups + group) * share
+            whole_ref[:, begin : begin + share] = pieces_ref[group, patch]
 
 
 def place_pieces(pieces):
-    patches, own_members, share = pieces[0].shape
-    points = patches * share * len(pieces)
+    groups, patches, own_members, share = pieces.shape
+    points = groups * patches * share
     return pl.pallas_call(
         place_kernel,
         out_shape=jax.ShapeDtypeStruct((own_members, points), BF16),
@@ -325,11 +346,11 @@
             flops=0, bytes_accessed=4 * own_members * points, transcendentals=0
         ),
         name="place_pieces",
-    )(*pieces)
-
-
-def exchange(blocks):
-    return lax.all_to_all(blocks, "space", split_axis=0, concat_axis=0, tiled=True)
+    )(pieces)
+
+
+def exchange(blocks, axes="space"):
+    return lax.all_to_all(blocks, axes, split_axis=0, concat_axis=0, tiled=True)
 
 
 def swap_shares(own):
@@ -374,16 +395,12 @@
     own_points = cut_share(background_states, device_count, share)
     own_rows, own_points = lax.optimization_barrier((own_rows, own_points))
     own_points = exchange(own_points).reshape(-1, share)
-    background = [own_points] + swap_shares(own_points)
-
-    members = measurement_anomaly_matrix.shape[1]
-    gram, drive, info = own_gram(own_rows, slot_share, members)
-    blended = patch_weights(gram, drive, info, other_rows, slot_share)
-    pieces = []
-    for part in background:
-        analysis = update_points(blended, part).reshape(device_count, own_members, share)
-        pieces.append(exchange(analysis))
-    return place_pieces(pieces)
+
+    gram, drive, info = own_gram(own_rows, measurement_anomaly_matrix.shape[1])
+    blended = patch_weights(gram, drive, info, [own_rows] + other_rows)
+    analysis = update_points(blended, own_points)
+    analysis = exchange(analysis.reshape(-1, own_members, share), ("boot", "space"))
+    return place_pieces(analysis.reshape(groups, device_count, own_members, share))
 
 
 def solution(mesh):

time: 130 us -> 125 us (0.962)
  blocking collectives: 30.4 us -> 81.2 us
  waiting for transfers between devices: 58.7 us -> 11.9 us
  starting transfers between devices: 21.9 us -> 5.54 us
  Pallas kernels: 17 us -> 22.4 us
  local copies, waits for them, and re-layouts: 1.59 us -> 3.63 us
    all_to_all x1 -> x2, blocking collectives: 30.4 us -> 81.2 us  [exchange(): return lax.all_to_all(blocks, axes, split_axis=0, concat_axis=0, tiled=True)]
    ppermute x2 -> x1, waiting for transfers between devices: 42 us -> 11.9 us  [swap_shares(): lax.ppermute(own, 'boot', [(g, (g - turn) % groups) for g in range(groups)])]
    all_to_all x3 -> x1, waiting for transfers between devices: 16.6 us -> 0.01 us  [exchange(): return lax.all_to_all(blocks, axes, split_axis=0, concat_axis=0, tiled=True)]
    all_to_all x3 -> x1, starting transfers between devices: 18.8 us -> 4.04 us  [exchange(): return lax.all_to_all(blocks, axes, split_axis=0, concat_axis=0, tiled=True)]
    pallas_call x4 -> x3, Pallas kernels: 11.6 us -> 17 us  [the longest x1 14.8 us: patch_weights(): pl.pallas_call(weights_kernel, out_shape=jax.ShapeDtypeStruct((groups, me...]
    unnamed x2 -> x6, local copies, waits for them, and re-layouts: 1.59 us -> 3.63 us
    ppermute x2 -> x1, starting transfers between devices: 3.14 us -> 1.5 us  [swap_shares(): lax.ppermute(own, 'boot', [(g, (g - turn) % groups) for g in range(groups)])]
  transfers between devices with their start and end apart: 5 -> 2, of which waited for: 3 -> 1; matrix products, arithmetic and copies ran while one was open for 0% -> 0% of each run, Pallas kernels for 8% -> 13%
where the time goes in v5:
time: 125 us
  blocking collectives  81.2 us (65%)
  Pallas kernels  22.4 us (18%)
  waiting for transfers between devices  11.9 us (10%)
  starting transfers between devices  5.54 us (4%)
  local copies, waits for them, and re-layouts  3.63 us (3%)
    all_to_all x2, blocking collectives, exchange(): return lax.all_to_all(blocks, axes, split_axis=0, concat_axis=0, tiled=True)  81.2 us
    pallas_call x1, Pallas kernels, patch_weights(): pl.pallas_call(weights_kernel, out_shape=jax.ShapeDtypeStruct((groups, me...  14.8 us
    ppermute x1, waiting for transfers between devices, swap_shares(): lax.ppermute(own, 'boot', [(g, (g - turn) % groups) for g in range(groups)])  11.9 us
    all_to_all x1, starting transfers between devices, exchange(): return lax.all_to_all(blocks, axes, split_axis=0, concat_axis=0, tiled=True)  4.04 us
    unnamed x6, local copies, waits for them, and re-layouts  3.63 us
    pallas_call x1, Pallas kernels, pack(): pl.pallas_call(functools.partial(pack_kernel, groups), out_shape=jax.Shap...  2.84 us
  transfers between devices with their start and end apart: 2, of which 1 were waited for; matrix products, arithmetic and copies ran while one was open for 0% of the time, Pallas kernels for 13%

profile of v5, /device:TPU:0, one launch (start us, length us, event | category | flops | bytes accessed | tf_op | source)
XLA Modules:
  0.0 124.6 jit_solution(11793329388651081142)
XLA Ops:
  0.0 2.8 %pack_rows.1 = bf16[16,8,3200]{2,1,0:T(8,128)(2,1)} custom-call(s32[2,384]{1,0:T(2,128)} %bitcast.8, s32[2,384]{1,0:T(2,128)} %bitcast.9, s32[384]{0:T(512)} %refs_2_.1, f32[384]{0:T(512)} %refs_3_.1, bf16[384]{0:T(512)(128)(2,1)} %refs_4_.1, bf16[384,512]{1,0:T(8,128)(2,1)} %refs_5_.1), custom_call_target="tpu_custom_call" | custom-call | flops 301989888 | bytes 1179648 | tf_op jit(solution)/shard_map/pack_rows/pallas_call | solution.py:94
  2.8 28.2 %all_to_all.15.rows_ref.refs_3_ = bf16[16,8,3200]{2,1,0:T(8,128)(2,1)S(1)} all-to-all(bf16[16,8,3200]{2,1,0:T(8,128)(2,1)} %pack_rows.1), channel_id=1, replica_groups=mesh['boot'=2,'space'=16] {'space'}, dimensions={0} | all-to-all | bytes 1638400 | tf_op jit(solution)/shard_map/all_to_all | solution.py:353
  31.1 1.5 %collective-permute-start = (bf16[16,8,3200]{2,1,0:T(8,128)(2,1)S(1)}, bf16[16,8,3200]{2,1,0:T(8,128)(2,1)S(1)}, u32[]{:S(2)}, u32[]{:S(2)}) collective-permute-start(bf16[16,8,3200]{2,1,0:T(8,128)(2,1)S(1)} %all_to_all.15.rows_ref.refs_3_), channel_id=1, source_target_pairs={{0,16},{16,0},{1,17},{17,1},{2,18},{18,2},{3,19},{19,3},{4,20},{20... | collective-permute-start | bytes 2457608 | tf_op jit(solution)/shard_map/ppermute | solution.py:359
  32.6 0.0 copy-start
  32.6 1.6 %copy-done = bf16[32,32768]{1,0:T(8,128)(2,1)S(1)} copy-done((bf16[32,32768]{1,0:T(8,128)(2,1)S(1)}, bf16[32,32768]{1,0:T(8,128)(2,1)}, u32[]{:S(2)}) %copy-start) | copy-done | bytes 2097176
  34.2 1.0 cut_share.1
  35.2 4.0 %all-to-all-start.1 = ((bf16[16,32,1024]{2,1,0:T(8,128)(2,1)}), bf16[16,32,1024]{2,1,0:T(8,128)(2,1)S(1)}, u32[]{:S(2)}, u32[]{:S(2)}) async-start(bf16[16,32,1024]{2,1,0:T(8,128)(2,1)} %cut_share.1), calls=%async_computation.1 | async-start | bytes 2097152 | tf_op jit(solution)/shard_map/all_to_all | solution.py:353
  39.3 0.9 own_gram.1
  40.1 11.9 %collective-permute-done.refs_4_ = bf16[16,8,3200]{2,1,0:T(8,128)(2,1)S(1)} collective-permute-done((bf16[16,8,3200]{2,1,0:T(8,128)(2,1)S(1)}, bf16[16,8,3200]{2,1,0:T(8,128)(2,1)S(1)}, u32[]{:S(2)}, u32[]{:S(2)}) %collective-permute-start) | collective-permute-done | bytes 819232 | tf_op jit(solution)/shard_map/ppermute | solution.py:359
  52.0 0.0 copy-start.1
  52.0 0.9 copy-done.1
  52.9 0.0 copy-start.2
  52.9 1.1 copy-done.2
  54.0 14.8 %patch_weights.1.blended_ref = bf16[2,512,512]{2,1,0:T(8,128)(2,1)S(1)} custom-call(f32[512,512]{1,0:T(8,128)S(1)} %get-tuple-element.11.refs_0_, f32[1,512]{1,0:T(1,128)S(1)} %get-tuple-element.12.refs_1_, f32[128,128]{1,0:T(8,128)S(1)} %get-tuple-element.13.refs_2_, bf16[16,8,3200]{2,1,0:T(8,128)(2,1)S(1)} %all_to_all.15.rows_ref.refs_3_, ...), custom_call_target="tpu_custom_call" | custom-call | flops 21474836480 | bytes 2097152 | tf_op jit(solution)/shard_map/patch_weights/pallas_call | solution.py:263
  68.9 0.0 all-to-all-done.1
  68.9 1.4 %update_points.1 = bf16[2,512,1024]{2,1,0:T(8,128)(2,1)S(1)} custom-call(bf16[2,512,512]{2,1,0:T(8,128)(2,1)S(1)} %patch_weights.1.blended_ref, bf16[512,1024]{1,0:T(8,128)(2,1)S(1)} %bitcast.7), custom_call_target="tpu_custom_call" | custom-call | flops 1073741824 | bytes 3145728 | tf_op jit(solution)/shard_map/update_points/pallas_call | solution.py:295
  70.2 52.9 %all_to_all.16 = bf16[32,32,1024]{2,1,0:T(8,128)(2,1)S(1)} all-to-all(bf16[32,32,1024]{2,1,0:T(8,128)(2,1)S(1)} %bitcast.5), channel_id=1, replica_groups=mesh['boot'=2,'space'=16] {'boot','space'}, dimensions={0} | all-to-all | bytes 4194304 | tf_op jit(solution)/shard_map/all_to_all | solution.py:353
  123.2 1.5 %place_pieces.1 = bf16[32,32768]{1,0:T(8,128)(2,1)} custom-call(bf16[2,16,32,1024]{3,2,1,0:T(8,128)(2,1)S(1)} %bitcast.6), custom_call_target="tpu_custom_call" | custom-call | bytes 4194304 | tf_op jit(solution)/shard_map/place_pieces/pallas_call | solution.py:341
Async XLA Ops:
  31.1 20.9 %collective-permute-start = (bf16[16,8,3200]{2,1,0:T(8,128)(2,1)S(1)}, bf16[16,8,3200]{2,1,0:T(8,128)(2,1)S(1)}, u32[]{:S(2)}, u32[]{:S(2)}) collective-permute-start(bf16[16,8,3200]{2,1,0:T(8,128)(2,1)S(1)} %all_to_all.15.rows_ref.refs_3_), channel_id=1, source_target_pairs={{0,16},{16,0},{1,17},{17,1},{2,18},{18,2},{3,19},{19,3},{4,20},{20... | collective-permute-start | bytes 2457608 | tf_op jit(solution)/shard_map/ppermute | solution.py:359
  32.6 1.6 %copy-start = (bf16[32,32768]{1,0:T(8,128)(2,1)S(1)}, bf16[32,32768]{1,0:T(8,128)(2,1)}, u32[]{:S(2)}) copy-start(bf16[32,32768]{1,0:T(8,128)(2,1)} %states_ref.1) | copy-start | bytes 6291460
  35.2 33.7 %all-to-all-start.1 = ((bf16[16,32,1024]{2,1,0:T(8,128)(2,1)}), bf16[16,32,1024]{2,1,0:T(8,128)(2,1)S(1)}, u32[]{:S(2)}, u32[]{:S(2)}) async-start(bf16[16,32,1024]{2,1,0:T(8,128)(2,1)} %cut_share.1), calls=%async_computation.1 | async-start | bytes 2097152 | tf_op jit(solution)/shard_map/all_to_all | solution.py:353
  52.0 0.9 copy-start.1
  52.9 1.1 copy-start.2

commit v6 on v5

--- a/solution.py
+++ b/solution.py
@@ -10,9 +10,7 @@
 NS_STEPS = 6
 LANES = 128
 ROWS = 8
-FULL_STEPS = 1
-VMEM_BYTES = 48 * 1024 * 1024
-ALL_VMEM_BYTES = 64 * 1024 * 1024
+MEBI = 1024 * 1024
 F32 = jnp.float32
 BF16 = jnp.bfloat16
 
@@ -97,7 +95,7 @@
         in_specs=[pl.BlockSpec(memory_space=pl.ANY)] * len(operands),
         scratch_shapes=[pltpu.VMEM(operand.shape, operand.dtype) for operand in operands]
         + [pltpu.VMEM((LANES, LANES), F32), pltpu.SemaphoreType.DMA((len(operands),))],
-        compiler_params=pltpu.CompilerParams(vmem_limit_bytes=ALL_VMEM_BYTES),
+        compiler_params=pltpu.CompilerParams(vmem_limit_bytes=64 * MEBI),
         cost_estimate=pl.CostEstimate(
             flops=2 * patches * share * count * members,
             bytes_accessed=2 * (patches * share + count) * members,
@@ -105,16 +103,6 @@
         ),
         name="pack_rows",
     )(*operands)
-
-
-def halves(value):
-    high = value.astype(BF16)
-    return high, (value - high.astype(F32)).astype(BF16)
-
-
-def product(left_high, left_low, right_high, right_low):
-    dot = functools.partial(jnp.dot, preferred_element_type=F32)
-    return dot(left_high, right_high) + (dot(left_high, right_low) + dot(left_low, right_high))
 
 
 def slot_rows(rows_ref, members):
@@ -137,37 +125,32 @@
     info_ref[...] = info_ref[...].T
 
 
-def add_rows(rows, info_ref, turn, sources, gram, drive):
+def scaled_rows(rows, info_ref, turn, sources):
     share = rows.shape[0] // sources
     begin = lax.rem(lax.axis_index("boot") + turn, lax.axis_size("boot")) * share
     info = info_ref[pl.ds(pl.multiple_of(begin, ROWS), share), :]
-    scaled = []
+    blocks, drive = [], jnp.zeros((1, rows.shape[1]), F32)
     for source in range(sources):
         block = rows[source * share : (source + 1) * share, :]
         block = (info[:, source : source + 1] * block).astype(BF16).astype(F32)
-        scaled.append(block)
+        blocks.append(block)
         dep_col = info[:, sources + source : sources + source + 1]
         drive = drive + jnp.sum(dep_col * block, axis=0, keepdims=True)
-    gram = gram + lax.dot_general(
-        rows.astype(BF16),
-        jnp.concatenate(scaled, axis=0).astype(BF16),
-        (((0,), (0,)), ((), ())),
-        preferred_element_type=F32,
-    )
-    return gram, drive
+    return jnp.concatenate(blocks, axis=0).astype(BF16), drive
+
+
+def outer_sum(rows, scaled):
+    return lax.dot_general(
+        rows.astype(BF16), scaled, (((0,), (0,)), ((), ())), preferred_element_type=F32
+    )
 
 
 def gram_kernel(rows_ref, gram_ref, drive_ref, info_ref):
     members = gram_ref.shape[0]
     slot_info(rows_ref, info_ref)
-    gram_ref[...], drive_ref[...] = add_rows(
-        slot_rows(rows_ref, members),
-        info_ref,
-        0,
-        rows_ref.shape[0],
-        jnp.zeros((members, members), F32),
-        jnp.zeros((1, members), F32),
-    )
+    rows = slot_rows(rows_ref, members)
+    scaled, drive_ref[...] = scaled_rows(rows, info_ref, 0, rows_ref.shape[0])
+    gram_ref[...] = outer_sum(rows, scaled)
 
 
 def own_gram(rows, members):
@@ -179,7 +162,7 @@
             jax.ShapeDtypeStruct((1, members), F32),
             jax.ShapeDtypeStruct((LANES, LANES), F32),
         ),
-        compiler_params=pltpu.CompilerParams(vmem_limit_bytes=VMEM_BYTES),
+        compiler_params=pltpu.CompilerParams(vmem_limit_bytes=16 * MEBI),
         cost_estimate=pl.CostEstimate(
             flops=4 * members * sources * ROWS * width,
             bytes_accessed=2 * sources * ROWS * width,
@@ -189,71 +172,90 @@
     )(rows)
 
 
+def diagonal_column(value, eye):
+    size = value.shape[1]
+    parts = []
+    for begin in range(0, size, LANES):
+        block = value[:, begin : begin + LANES]
+        block = block if value.shape[0] == 1 else block[begin : begin + LANES, :]
+        parts.append(jnp.sum(jnp.where(eye, block, 0.0), axis=1, keepdims=True))
+    return jnp.concatenate(parts, axis=0)
+
+
 def weights_kernel(*refs):
     gram_ref, drive_ref, own_info_ref = refs[:3]
-    rows_refs, blended_ref, info_ref = refs[3:-10], refs[-10], refs[-9]
-    y_ref, z_ref, y_high, y_low, z_high, z_low, w_high, w_low = refs[-8:]
+    rows_refs, blended_ref, info_ref = refs[3:-8], refs[-8], refs[-7]
+    y_ref, z_ref, y_high, z_high, low, w_high = refs[-6:]
     groups, members, _ = blended_ref.shape
     sources = rows_refs[0].shape[0]
     row_id = lax.broadcasted_iota(jnp.int32, (members, members), 0)
     col_id = lax.broadcasted_iota(jnp.int32, (members, members), 1)
-    diagonal = row_id == col_id
-    identity = jnp.where(diagonal, 1.0, 0.0)
+    identity = jnp.where(row_id == col_id, 1.0, 0.0)
+    eye = lax.broadcasted_iota(jnp.int32, (LANES, LANES), 0) == lax.broadcasted_iota(
+        jnp.int32, (LANES, LANES), 1
+    )
     dot = functools.partial(jnp.dot, preferred_element_type=F32)
-    rows = [slot_rows(rows_ref, members) for rows_ref in rows_refs]
-    frobenius, drives = [], []
+
+    def split(chain, value):
+        w_high[chain] = value.astype(BF16)
+        for begin in range(0, members, LANES):
+            block = slice(begin, begin + LANES)
+            w_high[chain, block, block] = jnp.where(eye, 0.0, value[block, block]).astype(BF16)
+        return 1.5 - 0.5 * diagonal_column(value, eye)
+
+    grams = [gram_ref[...]] + [jnp.zeros((members, members), F32)] * (groups - 1)
+    drives = [drive_ref[...]] + [jnp.zeros((1, members), F32)] * (groups - 1)
+    for chain in range(1, groups):
+        slot_info(rows_refs[chain], info_ref.at[chain])
+    for turn, rows_ref in enumerate(rows_refs):
+        rows = slot_rows(rows_ref, members)
+        chains = [chain for chain in range(groups) if chain or turn]
+        scaled = []
+        for chain in chains:
+            info = info_ref.at[chain] if chain else own_info_ref
+            block, drive = scaled_rows(rows, info, turn, sources)
+            scaled.append(block)
+            drives[chain] = drives[chain] + drive
+        sums = outer_sum(rows, jnp.concatenate(scaled, axis=1))
+        for place, chain in enumerate(chains):
+            columns = slice(place * members, (place + 1) * members)
+            grams[chain] = grams[chain] + sums[:, columns]
+
+    frobenius = []
     for chain in range(groups):
-        if chain == 0:
-            gram, drive = gram_ref[...], drive_ref[...]
-        else:
-            slot_info(rows_refs[chain], info_ref.at[chain])
-            gram, drive = jnp.zeros((members, members), F32), jnp.zeros((1, members), F32)
-        for turn in range(groups):
-            if chain or turn:
-                gram, drive = add_rows(
-                    rows[turn],
-                    info_ref.at[chain] if chain else own_info_ref,
-                    turn,
-                    sources,
-                    gram,
-                    drive,
-                )
-        shifted = identity + gram / (members - 1.0)
+        shifted = identity + grams[chain] / (members - 1.0)
         squares = jnp.sum(jnp.sum(shifted * shifted, axis=0, keepdims=True), axis=1, keepdims=True)
         frobenius.append(jnp.sqrt(squares))
-        drives.append(drive)
         current = shifted / frobenius[chain]
+        factor = split(chain, current)
         y_high[chain] = current.astype(BF16)
         z_ref[chain] = 1.5 * identity - 0.5 * current
-        y_ref[chain] = 1.5 * current - 0.5 * dot(y_high[chain], y_high[chain])
+        y_ref[chain] = factor * current - 0.5 * dot(w_high[chain], y_high[chain])
         y_high[chain], z_high[chain] = y_ref[chain].astype(BF16), z_ref[chain].astype(BF16)
 
     def step(_, carry):
+        factors = [split(c, dot(z_high[c], y_high[c])) for c in range(groups)]
         for chain in range(groups):
-            w_high[chain] = dot(z_high[chain], y_high[chain]).astype(BF16)
-        for chain in range(groups):
-            current = 1.5 * y_ref[chain] - 0.5 * dot(y_high[chain], w_high[chain])
-            root = 1.5 * z_ref[chain] - 0.5 * dot(w_high[chain], z_high[chain])
+            current = factors[chain] * y_ref[chain] - 0.5 * dot(w_high[chain], y_high[chain])
+            root = factors[chain] * z_ref[chain] - 0.5 * dot(w_high[chain], z_high[chain])
             y_ref[chain], z_ref[chain] = current, root
             y_high[chain], z_high[chain] = current.astype(BF16), root.astype(BF16)
         return carry
 
     lax.fori_loop(1, NS_STEPS - 1, step, 0)
     for chain in range(groups):
-        y_low[chain] = (y_ref[chain] - y_high[chain].astype(F32)).astype(BF16)
-        z_low[chain] = (z_ref[chain] - z_high[chain].astype(F32)).astype(BF16)
+        low[2 * chain] = (y_ref[chain] - y_high[chain].astype(F32)).astype(BF16)
+        low[2 * chain + 1] = (z_ref[chain] - z_high[chain].astype(F32)).astype(BF16)
+    factors = []
     for chain in range(groups):
-        w_high[chain], w_low[chain] = halves(
-            product(z_high[chain], z_low[chain], y_high[chain], y_low[chain])
-        )
+        small = dot(z_high[chain], low[2 * chain]) + dot(low[2 * chain + 1], y_high[chain])
+        factors.append(split(chain, dot(z_high[chain], y_high[chain]) + small))
     for chain in range(groups):
-        change = product(w_high[chain], w_low[chain], z_high[chain], z_low[chain])
-        root = (1.5 * z_ref[chain] - 0.5 * change) / jnp.sqrt(frobenius[chain])
-        drive_col = jnp.sum(jnp.where(diagonal, drives[chain], 0.0), axis=1, keepdims=True)
-        inner = jnp.sum(root * drive_col, axis=0, keepdims=True)
-        inner_col = jnp.sum(jnp.where(diagonal, inner, 0.0), axis=1, keepdims=True)
-        mean_weight = jnp.sum(root * inner_col, axis=0, keepdims=True) / (members - 1.0)
-        blended_ref[chain] = (root + mean_weight).astype(BF16)
+        root = factors[chain] * z_ref[chain] - 0.5 * dot(w_high[chain], z_high[chain])
+        root = root / jnp.sqrt(frobenius[chain])
+        inner = jnp.sum(root * diagonal_column(drives[chain], eye), axis=0, keepdims=True)
+        mean_weight = jnp.sum(root * diagonal_column(inner, eye), axis=0, keepdims=True)
+        blended_ref[chain] = (root + mean_weight / (members - 1.0)).astype(BF16)
 
 
 def patch_weights(gram, drive, info, rows):
@@ -263,8 +265,16 @@
     return pl.pallas_call(
         weights_kernel,
         out_shape=jax.ShapeDtypeStruct((groups, members, members), BF16),
-        scratch_shapes=[pltpu.VMEM((groups, LANES, LANES), F32)] + [whole] * 2 + [half] * 6,
-        compiler_params=pltpu.CompilerParams(vmem_limit_bytes=VMEM_BYTES),
+        scratch_shapes=[
+            pltpu.VMEM((groups, LANES, LANES), F32),
+            whole,
+            whole,
+            half,
+            half,
+            pltpu.VMEM((2 * groups, members, members), BF16),
+            half,
+        ],
+        compiler_params=pltpu.CompilerParams(vmem_limit_bytes=(8 + 10 * groups) * MEBI),
         cost_estimate=pl.CostEstimate(
             flops=80 * groups * members * members * members,
             bytes_accessed=8 * members * members,
@@ -295,7 +305,7 @@
     return pl.pallas_call(
         update_kernel,
         out_shape=jax.ShapeDtypeStruct((groups, members, points), BF16),
-        compiler_params=pltpu.CompilerParams(vmem_limit_bytes=VMEM_BYTES),
+        compiler_params=pltpu.CompilerParams(vmem_limit_bytes=16 * MEBI),
         cost_estimate=pl.CostEstimate(
             flops=2 * groups * members * members * points,
             bytes_accessed=2 * (groups + 1) * members * points,
@@ -319,7 +329,7 @@
     return pl.pallas_call(
         cut_kernel,
         out_shape=jax.ShapeDtypeStruct((patches, own_members, share), BF16),
-        compiler_params=pltpu.CompilerParams(vmem_limit_bytes=VMEM_BYTES),
+        compiler_params=pltpu.CompilerParams(vmem_limit_bytes=16 * MEBI),
         cost_estimate=pl.CostEstimate(
             flops=0, bytes_accessed=4 * patches * own_members * share, transcendentals=0
         ),
@@ -341,7 +351,7 @@
     return pl.pallas_call(
         place_kernel,
         out_shape=jax.ShapeDtypeStruct((own_members, points), BF16),
-        compiler_params=pltpu.CompilerParams(vmem_limit_bytes=VMEM_BYTES),
+        compiler_params=pltpu.CompilerParams(vmem_limit_bytes=16 * MEBI),
         cost_estimate=pl.CostEstimate(
             flops=0, bytes_accessed=4 * own_members * points, transcendentals=0
         ),
@@ -390,10 +400,9 @@
         slot_share,
         groups,
     )
-    own_rows = exchange(slots)
+    own_points = cut_share(background_states, device_count, share)
+    own_rows, own_points = lax.optimization_barrier((exchange(slots), own_points))
     other_rows = swap_shares(own_rows)
-    own_points = cut_share(background_states, device_count, share)
-    own_rows, own_points = lax.optimization_barrier((own_rows, own_points))
     own_points = exchange(own_points).reshape(-1, share)
 
     gram, drive, info = own_gram(own_rows, measurement_anomaly_matrix.shape[1])

time: 125 us -> 124 us (level)
  blocking collectives: 81.2 us -> 55 us
  waiting for transfers between devices: 11.9 us -> 29 us
  starting transfers between devices: 5.54 us -> 14.5 us
    all_to_all x2 -> x1, blocking collectives: 81.2 us -> 55 us  [exchange(): return lax.all_to_all(blocks, axes, split_axis=0, concat_axis=0, tiled=True)]
    all_to_all x1 -> x2, waiting for transfers between devices: 0.01 us -> 16.6 us  [exchange(): return lax.all_to_all(blocks, axes, split_axis=0, concat_axis=0, tiled=True)]
    all_to_all x1 -> x2, starting transfers between devices: 4.04 us -> 13 us  [exchange(): return lax.all_to_all(blocks, axes, split_axis=0, concat_axis=0, tiled=True)]
  transfers between devices with their start and end apart: 2 -> 3, of which waited for: 1 -> 2; matrix products, arithmetic and copies ran while one was open for 0% -> 0% of each run, Pallas kernels for 13% -> 13%
where the time goes in v6:
time: 124 us
  blocking collectives  55 us (44%)
  waiting for transfers between devices  29 us (23%)
  Pallas kernels  21.4 us (17%)
  starting transfers between devices  14.5 us (12%)
  local copies, waits for them, and re-layouts  3.62 us (3%)
    all_to_all x1, blocking collectives, exchange(): return lax.all_to_all(blocks, axes, split_axis=0, concat_axis=0, tiled=True)  55 us
    all_to_all x2, waiting for transfers between devices, exchange(): return lax.all_to_all(blocks, axes, split_axis=0, concat_axis=0, tiled=True)  16.6 us
    pallas_call x1, Pallas kernels, patch_weights(): pl.pallas_call(weights_kernel, out_shape=jax.ShapeDtypeStruct((groups, me...  13.8 us
    all_to_all x2, starting transfers between devices, exchange(): return lax.all_to_all(blocks, axes, split_axis=0, concat_axis=0, tiled=True)  13 us
    ppermute x1, waiting for transfers between devices, swap_shares(): lax.ppermute(own, 'boot', [(g, (g - turn) % groups) for g in range(groups)])  12.4 us
    unnamed x6, local copies, waits for them, and re-layouts  3.62 us
    pallas_call x1, Pallas kernels, pack(): pl.pallas_call(functools.partial(pack_kernel, groups), out_shape=jax.Shap...  2.83 us
  transfers between devices with their start and end apart: 3, of which 2 were waited for; matrix products, arithmetic and copies ran while one was open for 0% of the time, Pallas kernels for 13%

profile of v6, /device:TPU:0, one launch (start us, length us, event | category | flops | bytes accessed | tf_op | source)
XLA Modules:
  0.0 123.7 jit_solution(6031756353839149106)
XLA Ops:
  0.0 2.8 %pack_rows.1 = bf16[16,8,3200]{2,1,0:T(8,128)(2,1)} custom-call(s32[2,384]{1,0:T(2,128)} %bitcast.8, s32[2,384]{1,0:T(2,128)} %bitcast.9, s32[384]{0:T(512)} %refs_2_.1, f32[384]{0:T(512)} %refs_3_.1, bf16[384]{0:T(512)(128)(2,1)} %refs_4_.1, bf16[384,512]{1,0:T(8,128)(2,1)} %refs_5_.1), custom_call_target="tpu_custom_call" | custom-call | flops 301989888 | bytes 1179648 | tf_op jit(solution)/shard_map/pack_rows/pallas_call | solution.py:92
  2.8 7.4 %all-to-all-start = ((bf16[16,8,3200]{2,1,0:T(8,128)(2,1)}), bf16[16,8,3200]{2,1,0:T(8,128)(2,1)S(1)}, u32[]{:S(2)}, u32[]{:S(2)}) async-start(bf16[16,8,3200]{2,1,0:T(8,128)(2,1)} %pack_rows.1), calls=%async_computation | async-start | bytes 1638400 | tf_op jit(solution)/shard_map/all_to_all | solution.py:363
  10.2 0.0 copy-start
  10.3 1.6 %copy-done = bf16[32,32768]{1,0:T(8,128)(2,1)S(1)} copy-done((bf16[32,32768]{1,0:T(8,128)(2,1)S(1)}, bf16[32,32768]{1,0:T(8,128)(2,1)}, u32[]{:S(2)}) %copy-start) | copy-done | bytes 2097176
  11.8 1.0 cut_share.1
  12.9 16.6 %all-to-all-done.rows_ref.refs_3_ = bf16[16,8,3200]{2,1,0:T(8,128)(2,1)S(1)} async-done(((bf16[16,8,3200]{2,1,0:T(8,128)(2,1)}), bf16[16,8,3200]{2,1,0:T(8,128)(2,1)S(1)}, u32[]{:S(2)}, u32[]{:S(2)}) %all-to-all-start) | async-done | bytes 819232 | tf_op jit(solution)/shard_map/all_to_all | solution.py:363
  29.5 1.5 %collective-permute-start = (bf16[16,8,3200]{2,1,0:T(8,128)(2,1)S(1)}, bf16[16,8,3200]{2,1,0:T(8,128)(2,1)S(1)}, u32[]{:S(2)}, u32[]{:S(2)}) collective-permute-start(bf16[16,8,3200]{2,1,0:T(8,128)(2,1)S(1)} %all-to-all-done.rows_ref.refs_3_), channel_id=1, source_target_pairs={{0,16},{16,0},{1,17},{17,1},{2,18},{18,2},{3,19},{19,3},{4,20},{20... | collective-permute-start | bytes 2457608 | tf_op jit(solution)/shard_map/ppermute | solution.py:369
  31.0 5.7 %all-to-all-start.1 = ((bf16[16,32,1024]{2,1,0:T(8,128)(2,1)}), bf16[16,32,1024]{2,1,0:T(8,128)(2,1)S(1)}, u32[]{:S(2)}, u32[]{:S(2)}) async-start(bf16[16,32,1024]{2,1,0:T(8,128)(2,1)} %cut_share.1), calls=%async_computation.1 | async-start | bytes 2097152 | tf_op jit(solution)/shard_map/all_to_all | solution.py:363
  36.6 0.9 own_gram.1
  37.5 12.4 %collective-permute-done.refs_4_ = bf16[16,8,3200]{2,1,0:T(8,128)(2,1)S(1)} collective-permute-done((bf16[16,8,3200]{2,1,0:T(8,128)(2,1)S(1)}, bf16[16,8,3200]{2,1,0:T(8,128)(2,1)S(1)}, u32[]{:S(2)}, u32[]{:S(2)}) %collective-permute-start) | collective-permute-done | bytes 819232 | tf_op jit(solution)/shard_map/ppermute | solution.py:369
  49.9 0.0 copy-start.1
  49.9 0.9 copy-done.1
  50.8 0.0 copy-start.2
  50.8 1.1 copy-done.2
  52.0 13.8 %patch_weights.1.blended_ref = bf16[2,512,512]{2,1,0:T(8,128)(2,1)S(1)} custom-call(f32[512,512]{1,0:T(8,128)S(1)} %get-tuple-element.11.refs_0_, f32[1,512]{1,0:T(1,128)S(1)} %get-tuple-element.12.refs_1_, f32[128,128]{1,0:T(8,128)S(1)} %get-tuple-element.13.refs_2_, bf16[16,8,3200]{2,1,0:T(8,128)(2,1)S(1)} %all-to-all-done.rows_ref.refs_3_, ...), custom_call_target="tpu_custom_call" | custom-call | flops 21474836480 | bytes 2097152 | tf_op jit(solution)/shard_map/patch_weights/pallas_call | solution.py:265
  65.8 0.0 all-to-all-done.1
  65.8 1.4 %update_points.1 = bf16[2,512,1024]{2,1,0:T(8,128)(2,1)S(1)} custom-call(bf16[2,512,512]{2,1,0:T(8,128)(2,1)S(1)} %patch_weights.1.blended_ref, bf16[512,1024]{1,0:T(8,128)(2,1)S(1)} %bitcast.7), custom_call_target="tpu_custom_call" | custom-call | flops 1073741824 | bytes 3145728 | tf_op jit(solution)/shard_map/update_points/pallas_call | solution.py:305
  67.2 55.0 %all_to_all.15 = bf16[32,32,1024]{2,1,0:T(8,128)(2,1)S(1)} all-to-all(bf16[32,32,1024]{2,1,0:T(8,128)(2,1)S(1)} %bitcast.5), channel_id=1, replica_groups=mesh['boot'=2,'space'=16] {'boot','space'}, dimensions={0} | all-to-all | bytes 4194304 | tf_op jit(solution)/shard_map/all_to_all | solution.py:363
  122.2 1.5 %place_pieces.1 = bf16[32,32768]{1,0:T(8,128)(2,1)} custom-call(bf16[2,16,32,1024]{3,2,1,0:T(8,128)(2,1)S(1)} %bitcast.6), custom_call_target="tpu_custom_call" | custom-call | bytes 4194304 | tf_op jit(solution)/shard_map/place_pieces/pallas_call | solution.py:351
Async XLA Ops:
  2.8 26.6 %all-to-all-start = ((bf16[16,8,3200]{2,1,0:T(8,128)(2,1)}), bf16[16,8,3200]{2,1,0:T(8,128)(2,1)S(1)}, u32[]{:S(2)}, u32[]{:S(2)}) async-start(bf16[16,8,3200]{2,1,0:T(8,128)(2,1)} %pack_rows.1), calls=%async_computation | async-start | bytes 1638400 | tf_op jit(solution)/shard_map/all_to_all | solution.py:363
  10.2 1.6 %copy-start = (bf16[32,32768]{1,0:T(8,128)(2,1)S(1)}, bf16[32,32768]{1,0:T(8,128)(2,1)}, u32[]{:S(2)}) copy-start(bf16[32,32768]{1,0:T(8,128)(2,1)} %states_ref.1) | copy-start | bytes 6291460
  29.5 20.4 %collective-permute-start = (bf16[16,8,3200]{2,1,0:T(8,128)(2,1)S(1)}, bf16[16,8,3200]{2,1,0:T(8,128)(2,1)S(1)}, u32[]{:S(2)}, u32[]{:S(2)}) collective-permute-start(bf16[16,8,3200]{2,1,0:T(8,128)(2,1)S(1)} %all-to-all-done.rows_ref.refs_3_), channel_id=1, source_target_pairs={{0,16},{16,0},{1,17},{17,1},{2,18},{18,2},{3,19},{19,3},{4,20},{20... | collective-permute-start | bytes 2457608 | tf_op jit(solution)/shard_map/ppermute | solution.py:369
  31.0 34.8 %all-to-all-start.1 = ((bf16[16,32,1024]{2,1,0:T(8,128)(2,1)}), bf16[16,32,1024]{2,1,0:T(8,128)(2,1)S(1)}, u32[]{:S(2)}, u32[]{:S(2)}) async-start(bf16[16,32,1024]{2,1,0:T(8,128)(2,1)} %cut_share.1), calls=%async_computation.1 | async-start | bytes 2097152 | tf_op jit(solution)/shard_map/all_to_all | solution.py:363
  49.9 0.9 copy-start.1
  50.8 1.1 copy-start.2

commit v7 on v6

--- a/solution.py
+++ b/solution.py
@@ -9,7 +9,7 @@
 
 NS_STEPS = 6
 LANES = 128
-ROWS = 8
+ROWS = 16
 MEBI = 1024 * 1024
 F32 = jnp.float32
 BF16 = jnp.bfloat16
@@ -18,12 +18,14 @@
 def pack_kernel(groups, *refs):
     sources, slots_ref, fetched = refs[:6], refs[6], refs[7:13]
     info_ref, sems = refs[13:]
-    run_copies(
-        [
-            pltpu.make_async_copy(source, target, sems.at[i])
-            for i, (source, target) in enumerate(zip(sources, fetched))
-        ]
-    )
+    copies = [
+        pltpu.make_async_copy(source, target, sems.at[i])
+        for i, (source, target) in enumerate(zip(sources, fetched))
+    ]
+    for copy in copies:
+        copy.start()
+    for copy in copies[:-1]:
+        copy.wait()
     targets_ref, local_ref, mult_ref, prec_ref, dep_ref, rows_ref = fetched
     patches = slots_ref.shape[0]
     count, members = rows_ref.shape
@@ -65,6 +67,7 @@
     picks = [
         jnp.where(own_id == rank[patch : patch + 1, :], 1.0, 0.0) for patch in range(patches)
     ]
+    copies[-1].wait()
     picked = jnp.dot(
         jnp.concatenate(picks, axis=0).astype(BF16), rows_ref[...], preferred_element_type=F32
     )
@@ -79,13 +82,6 @@
         slots_ref[patch] = jnp.concatenate(blocks + [tail], axis=1).astype(BF16)
 
 
-def run_copies(copies):
-    for copy in copies:
-        copy.start()
-    for copy in copies:
-        copy.wait()
-
-
 def pack(targets, local, mult, prec, dep, rows, patches, share, groups):
     count, members = rows.shape
     operands = (targets.T, local.T, mult, prec, dep, rows)
@@ -106,12 +102,15 @@
 
 
 def slot_rows(rows_ref, members):
-    blocks = []
-    for source in range(rows_ref.shape[0]):
-        block = rows_ref[source].astype(F32)
-        for begin in range(0, block.shape[1] - LANES, members):
-            blocks.append(block[:, begin : begin + members])
-    return jnp.concatenate(blocks, axis=0)
+    sources, _, width = rows_ref.shape
+    return jnp.concatenate(
+        [
+            rows_ref[source, :, begin : begin + members]
+            for source in range(sources)
+            for begin in range(0, width - LANES, members)
+        ],
+        axis=0,
+    )
 
 
 def slot_info(rows_ref, info_ref):
@@ -119,37 +118,51 @@
     if 2 * sources < LANES:
         info_ref[2 * sources :, :] = jnp.zeros((LANES - 2 * sources, LANES), F32)
     for source in range(sources):
-        tail = rows_ref[source].astype(F32)[:, width - LANES :]
+        tail = rows_ref[source, :, width - LANES :].astype(F32)
         info_ref[source : source + 1, :] = tail[0:1, :]
         info_ref[sources + source : sources + source + 1, :] = tail[1:2, :]
     info_ref[...] = info_ref[...].T
 
 
 def scaled_rows(rows, info_ref, turn, sources):
-    share = rows.shape[0] // sources
+    share, members = rows.shape[0] // sources, rows.shape[1]
     begin = lax.rem(lax.axis_index("boot") + turn, lax.axis_size("boot")) * share
     info = info_ref[pl.ds(pl.multiple_of(begin, ROWS), share), :]
-    blocks, drive = [], jnp.zeros((1, rows.shape[1]), F32)
+    weights, drives = [], []
     for source in range(sources):
-        block = rows[source * share : (source + 1) * share, :]
-        block = (info[:, source : source + 1] * block).astype(BF16).astype(F32)
-        blocks.append(block)
-        dep_col = info[:, sources + source : sources + source + 1]
-        drive = drive + jnp.sum(dep_col * block, axis=0, keepdims=True)
-    return jnp.concatenate(blocks, axis=0).astype(BF16), drive
-
-
-def outer_sum(rows, scaled):
-    return lax.dot_general(
-        rows.astype(BF16), scaled, (((0,), (0,)), ((), ())), preferred_element_type=F32
-    )
+        weight = jnp.broadcast_to(info[:, source : source + 1], (share, LANES))
+        dep = jnp.broadcast_to(info[:, sources + source : sources + source + 1], (share, LANES))
+        weights.append(weight.astype(BF16))
+        drives.append(weight * dep)
+    weights = jnp.concatenate(weights, axis=0)
+    weights = jnp.concatenate([weights] * (members // LANES), axis=1)
+    return rows * weights, jnp.concatenate(drives, axis=0)
+
+
+def outer_sum(rows, right):
+    return lax.dot_general(rows, right, (((0,), (0,)), ((), ())), preferred_element_type=F32)
+
+
+def drive_sum(drives, rows):
+    lane = lax.broadcasted_iota(jnp.int32, drives[0].shape, 1)
+    parts = jnp.zeros(drives[0].shape, F32)
+    for place, weight in enumerate(drives):
+        high = weight.astype(BF16).astype(F32)
+        parts = jnp.where(lane == 2 * place, high, parts)
+        parts = jnp.where(lane == 2 * place + 1, weight - high, parts)
+    sums = outer_sum(parts.astype(BF16), rows)
+    return [
+        sums[2 * place : 2 * place + 1, :] + sums[2 * place + 1 : 2 * place + 2, :]
+        for place in range(len(drives))
+    ]
 
 
 def gram_kernel(rows_ref, gram_ref, drive_ref, info_ref):
     members = gram_ref.shape[0]
     slot_info(rows_ref, info_ref)
     rows = slot_rows(rows_ref, members)
-    scaled, drive_ref[...] = scaled_rows(rows, info_ref, 0, rows_ref.shape[0])
+    scaled, drive = scaled_rows(rows, info_ref, 0, rows_ref.shape[0])
+    (drive_ref[...],) = drive_sum([drive], rows)
     gram_ref[...] = outer_sum(rows, scaled)
 
 
@@ -183,11 +196,18 @@
 
 
 def weights_kernel(*refs):
-    gram_ref, drive_ref, own_info_ref = refs[:3]
-    rows_refs, blended_ref, info_ref = refs[3:-8], refs[-8], refs[-7]
-    y_ref, z_ref, y_high, z_high, low, w_high = refs[-6:]
+    gram_ref, drive_ref, own_info_ref, own_rows_ref = refs[:4]
+    far_refs, blended_ref, info_ref = refs[4:-10], refs[-10], refs[-9]
+    y_ref, z_ref, y_high, z_high, low, w_high, near_ref, sems = refs[-8:]
     groups, members, _ = blended_ref.shape
-    sources = rows_refs[0].shape[0]
+    sources = own_rows_ref.shape[0]
+    copies = [
+        pltpu.make_async_copy(far_ref, near_ref.at[place], sems.at[place])
+        for place, far_ref in enumerate(far_refs)
+    ]
+    for copy in copies:
+        copy.start()
+    rows_refs = [own_rows_ref] + [near_ref.at[place] for place in range(groups - 1)]
     row_id = lax.broadcasted_iota(jnp.int32, (members, members), 0)
     col_id = lax.broadcasted_iota(jnp.int32, (members, members), 1)
     identity = jnp.where(row_id == col_id, 1.0, 0.0)
@@ -206,20 +226,22 @@
     grams = [gram_ref[...]] + [jnp.zeros((members, members), F32)] * (groups - 1)
     drives = [drive_ref[...]] + [jnp.zeros((1, members), F32)] * (groups - 1)
     for chain in range(1, groups):
+        copies[chain - 1].wait()
         slot_info(rows_refs[chain], info_ref.at[chain])
     for turn, rows_ref in enumerate(rows_refs):
         rows = slot_rows(rows_ref, members)
         chains = [chain for chain in range(groups) if chain or turn]
-        scaled = []
+        scaled, parts = [], []
         for chain in chains:
             info = info_ref.at[chain] if chain else own_info_ref
-            block, drive = scaled_rows(rows, info, turn, sources)
+            block, part = scaled_rows(rows, info, turn, sources)
             scaled.append(block)
-            drives[chain] = drives[chain] + drive
+            parts.append(part)
         sums = outer_sum(rows, jnp.concatenate(scaled, axis=1))
-        for place, chain in enumerate(chains):
+        for place, (chain, drive) in enumerate(zip(chains, drive_sum(parts, rows))):
             columns = slice(place * members, (place + 1) * members)
             grams[chain] = grams[chain] + sums[:, columns]
+            drives[chain] = drives[chain] + drive
 
     frobenius = []
     for chain in range(groups):
@@ -242,7 +264,7 @@
             y_high[chain], z_high[chain] = current.astype(BF16), root.astype(BF16)
         return carry
 
-    lax.fori_loop(1, NS_STEPS - 1, step, 0)
+    lax.fori_loop(1, NS_STEPS - 1, step, 0, unroll=True)
     for chain in range(groups):
         low[2 * chain] = (y_ref[chain] - y_high[chain].astype(F32)).astype(BF16)
         low[2 * chain + 1] = (z_ref[chain] - z_high[chain].astype(F32)).astype(BF16)
@@ -258,12 +280,14 @@
         blended_ref[chain] = (root + mean_weight / (members - 1.0)).astype(BF16)
 
 
-def patch_weights(gram, drive, info, rows):
-    groups, members = len(rows), gram.shape[0]
+def patch_weights(gram, drive, info, own_rows, other_rows):
+    groups, members = len(other_rows) + 1, gram.shape[0]
+    resident, far = pl.BlockSpec(memory_space=pltpu.VMEM), pl.BlockSpec(memory_space=pl.ANY)
     whole = pltpu.VMEM((groups, members, members), F32)
     half = pltpu.VMEM((groups, members, members), BF16)
     return pl.pallas_call(
         weights_kernel,
+        in_specs=[resident] * 4 + [far] * (groups - 1),
         out_shape=jax.ShapeDtypeStruct((groups, members, members), BF16),
         scratch_shapes=[
             pltpu.VMEM((groups, LANES, LANES), F32),
@@ -273,6 +297,8 @@
             half,
             pltpu.VMEM((2 * groups, members, members), BF16),
             half,
+            pltpu.VMEM((max(groups - 1, 1),) + own_rows.shape, BF16),
+            pltpu.SemaphoreType.DMA((max(groups - 1, 1),)),
         ],
         compiler_params=pltpu.CompilerParams(vmem_limit_bytes=(8 + 10 * groups) * MEBI),
         cost_estimate=pl.CostEstimate(
@@ -281,7 +307,7 @@
             transcendentals=0,
         ),
         name="patch_weights",
-    )(gram, drive, info, *rows)
+    )(gram, drive, info, own_rows, *other_rows)
 
 
 def update_kernel(blended_ref, background_ref, analysis_ref):
@@ -406,7 +432,7 @@
     own_points = exchange(own_points).reshape(-1, share)
 
     gram, drive, info = own_gram(own_rows, measurement_anomaly_matrix.shape[1])
-    blended = patch_weights(gram, drive, info, [own_rows] + other_rows)
+    blended = patch_weights(gram, drive, info, own_rows, other_rows)
     analysis = update_points(blended, own_points)
     analysis = exchange(analysis.reshape(-1, own_members, share), ("boot", "space"))
     return place_pieces(analysis.reshape(groups, device_count, own_members, share))

time: 124 us -> 126 us (1.016)
  no operation moved by 1% of the time
where the time goes in v7:
time: 126 us
  blocking collectives  55.2 us (44%)
  waiting for transfers between devices  29.8 us (24%)
  Pallas kernels  22.3 us (18%)
  starting transfers between devices  14.7 us (12%)
  local copies, waits for them, and re-layouts  3.65 us (3%)
    all_to_all x1, blocking collectives, exchange(): return lax.all_to_all(blocks, axes, split_axis=0, concat_axis=0, tiled=True)  55.2 us
    all_to_all x2, waiting for transfers between devices, exchange(): return lax.all_to_all(blocks, axes, split_axis=0, concat_axis=0, tiled=True)  17.1 us
    pallas_call x1, Pallas kernels, patch_weights(): pl.pallas_call(weights_kernel, in_specs=[resident] * 4 + [far] * (groups...  14.2 us
    all_to_all x2, starting transfers between devices, exchange(): return lax.all_to_all(blocks, axes, split_axis=0, concat_axis=0, tiled=True)  13.2 us
    ppermute x1, waiting for transfers between devices, swap_shares(): lax.ppermute(own, 'boot', [(g, (g - turn) % groups) for g in range(groups)])  12.7 us
    unnamed x6, local copies, waits for them, and re-layouts  3.65 us
    pallas_call x1, Pallas kernels, pack(): pl.pallas_call(functools.partial(pack_kernel, groups), out_shape=jax.Shap...  3 us
  transfers between devices with their start and end apart: 3, of which 2 were waited for; matrix products, arithmetic and copies ran while one was open for 0% of the time, Pallas kernels for 13%

profile of v7, /device:TPU:0, one launch (start us, length us, event | category | flops | bytes accessed | tf_op | source)
XLA Modules:
  0.0 125.7 jit_solution(749168799330169144)
XLA Ops:
  0.0 3.0 %pack_rows.1 = bf16[16,16,1664]{2,1,0:T(8,128)(2,1)} custom-call(s32[2,384]{1,0:T(2,128)} %bitcast.8, s32[2,384]{1,0:T(2,128)} %bitcast.9, s32[384]{0:T(512)} %refs_2_.1, f32[384]{0:T(512)} %refs_3_.1, bf16[384]{0:T(512)(128)(2,1)} %refs_4_.1, bf16[384,512]{1,0:T(8,128)(2,1)} %refs_5_.1), custom_call_target="tpu_custom_call" | custom-call | flops 301989888 | bytes 1179648 | tf_op jit(solution)/shard_map/pack_rows/pallas_call | solution.py:88
  3.0 7.4 %all-to-all-start = ((bf16[16,16,1664]{2,1,0:T(8,128)(2,1)}), bf16[16,16,1664]{2,1,0:T(8,128)(2,1)S(1)}, u32[]{:S(2)}, u32[]{:S(2)}) async-start(bf16[16,16,1664]{2,1,0:T(8,128)(2,1)} %pack_rows.1), calls=%async_computation | async-start | bytes 1703936 | tf_op jit(solution)/shard_map/all_to_all | solution.py:389
  10.4 0.0 copy-start
  10.4 1.6 %copy-done = bf16[32,32768]{1,0:T(8,128)(2,1)S(1)} copy-done((bf16[32,32768]{1,0:T(8,128)(2,1)S(1)}, bf16[32,32768]{1,0:T(8,128)(2,1)}, u32[]{:S(2)}) %copy-start) | copy-done | bytes 2097176
  12.0 1.0 cut_share.1
  13.0 17.1 %all-to-all-done.rows_ref.refs_3_ = bf16[16,16,1664]{2,1,0:T(8,128)(2,1)S(1)} async-done(((bf16[16,16,1664]{2,1,0:T(8,128)(2,1)}), bf16[16,16,1664]{2,1,0:T(8,128)(2,1)S(1)}, u32[]{:S(2)}, u32[]{:S(2)}) %all-to-all-start) | async-done | bytes 852000 | tf_op jit(solution)/shard_map/all_to_all | solution.py:389
  30.2 1.5 %collective-permute-start = (bf16[16,16,1664]{2,1,0:T(8,128)(2,1)S(1)}, bf16[16,16,1664]{2,1,0:T(8,128)(2,1)S(1)}, u32[]{:S(2)}, u32[]{:S(2)}) collective-permute-start(bf16[16,16,1664]{2,1,0:T(8,128)(2,1)S(1)} %all-to-all-done.rows_ref.refs_3_), channel_id=1, source_target_pairs={{0,16},{16,0},{1,17},{17,1},{2,18},{18,2},{3,19},{19,3},{4,20},{20... | collective-permute-start | bytes 2555912 | tf_op jit(solution)/shard_map/ppermute | solution.py:395
  31.7 5.8 %all-to-all-start.1 = ((bf16[16,32,1024]{2,1,0:T(8,128)(2,1)}), bf16[16,32,1024]{2,1,0:T(8,128)(2,1)S(1)}, u32[]{:S(2)}, u32[]{:S(2)}) async-start(bf16[16,32,1024]{2,1,0:T(8,128)(2,1)} %cut_share.1), calls=%async_computation.1 | async-start | bytes 2097152 | tf_op jit(solution)/shard_map/all_to_all | solution.py:389
  37.5 1.2 own_gram.1
  38.7 12.7 %collective-permute-done.refs_4_ = bf16[16,16,1664]{2,1,0:T(8,128)(2,1)S(1)} collective-permute-done((bf16[16,16,1664]{2,1,0:T(8,128)(2,1)S(1)}, bf16[16,16,1664]{2,1,0:T(8,128)(2,1)S(1)}, u32[]{:S(2)}, u32[]{:S(2)}) %collective-permute-start) | collective-permute-done | bytes 852000 | tf_op jit(solution)/shard_map/ppermute | solution.py:395
  51.4 0.0 copy-start.1
  51.4 0.9 copy-done.1
  52.3 0.0 copy-start.2
  52.3 1.2 copy-done.2
  53.4 14.2 %patch_weights.1.blended_ref = bf16[2,512,512]{2,1,0:T(8,128)(2,1)S(1)} custom-call(f32[512,512]{1,0:T(8,128)S(1)} %get-tuple-element.11.refs_0_, f32[1,512]{1,0:T(1,128)S(1)} %get-tuple-element.12.refs_1_, f32[128,128]{1,0:T(8,128)S(1)} %get-tuple-element.13.refs_2_, bf16[16,16,1664]{2,1,0:T(8,128)(2,1)S(1)} %all-to-all-done.rows_ref.refs_3_, ...), custom_call_target="tpu_custom_call" | custom-call | flops 21474836480 | bytes 2097152 | tf_op jit(solution)/shard_map/patch_weights/pallas_call | solution.py:288
  67.7 0.0 all-to-all-done.1
  67.7 1.4 %update_points.1 = bf16[2,512,1024]{2,1,0:T(8,128)(2,1)S(1)} custom-call(bf16[2,512,512]{2,1,0:T(8,128)(2,1)S(1)} %patch_weights.1.blended_ref, bf16[512,1024]{1,0:T(8,128)(2,1)S(1)} %bitcast.7), custom_call_target="tpu_custom_call" | custom-call | flops 1073741824 | bytes 3145728 | tf_op jit(solution)/shard_map/update_points/pallas_call | solution.py:331
  69.0 55.2 %all_to_all.15 = bf16[32,32,1024]{2,1,0:T(8,128)(2,1)S(1)} all-to-all(bf16[32,32,1024]{2,1,0:T(8,128)(2,1)S(1)} %bitcast.5), channel_id=1, replica_groups=mesh['boot'=2,'space'=16] {'boot','space'}, dimensions={0} | all-to-all | bytes 4194304 | tf_op jit(solution)/shard_map/all_to_all | solution.py:389
  124.2 1.5 %place_pieces.1 = bf16[32,32768]{1,0:T(8,128)(2,1)} custom-call(bf16[2,16,32,1024]{3,2,1,0:T(8,128)(2,1)S(1)} %bitcast.6), custom_call_target="tpu_custom_call" | custom-call | bytes 4194304 | tf_op jit(solution)/shard_map/place_pieces/pallas_call | solution.py:377
Async XLA Ops:
  3.0 27.2 %all-to-all-start = ((bf16[16,16,1664]{2,1,0:T(8,128)(2,1)}), bf16[16,16,1664]{2,1,0:T(8,128)(2,1)S(1)}, u32[]{:S(2)}, u32[]{:S(2)}) async-start(bf16[16,16,1664]{2,1,0:T(8,128)(2,1)} %pack_rows.1), calls=%async_computation | async-start | bytes 1703936 | tf_op jit(solution)/shard_map/all_to_all | solution.py:389
  10.4 1.6 %copy-start = (bf16[32,32768]{1,0:T(8,128)(2,1)S(1)}, bf16[32,32768]{1,0:T(8,128)(2,1)}, u32[]{:S(2)}) copy-start(bf16[32,32768]{1,0:T(8,128)(2,1)} %states_ref.1) | copy-start | bytes 6291460
  30.2 21.2 %collective-permute-start = (bf16[16,16,1664]{2,1,0:T(8,128)(2,1)S(1)}, bf16[16,16,1664]{2,1,0:T(8,128)(2,1)S(1)}, u32[]{:S(2)}, u32[]{:S(2)}) collective-permute-start(bf16[16,16,1664]{2,1,0:T(8,128)(2,1)S(1)} %all-to-all-done.rows_ref.refs_3_), channel_id=1, source_target_pairs={{0,16},{16,0},{1,17},{17,1},{2,18},{18,2},{3,19},{19,3},{4,20},{20... | collective-permute-start | bytes 2555912 | tf_op jit(solution)/shard_map/ppermute | solution.py:395
  31.7 36.0 %all-to-all-start.1 = ((bf16[16,32,1024]{2,1,0:T(8,128)(2,1)}), bf16[16,32,1024]{2,1,0:T(8,128)(2,1)S(1)}, u32[]{:S(2)}, u32[]{:S(2)}) async-start(bf16[16,32,1024]{2,1,0:T(8,128)(2,1)} %cut_share.1), calls=%async_computation.1 | async-start | bytes 2097152 | tf_op jit(solution)/shard_map/all_to_all | solution.py:389
  51.4 0.9 copy-start.1
  52.3 1.2 copy-start.2

commit v8 on v6

--- a/solution.py
+++ b/solution.py
@@ -125,32 +125,40 @@
     info_ref[...] = info_ref[...].T
 
 
-def scaled_rows(rows, info_ref, turn, sources):
+def share_info(info_ref, turn, share):
+    begin = lax.rem(lax.axis_index("boot") + turn, lax.axis_size("boot")) * share
+    return info_ref[pl.ds(pl.multiple_of(begin, ROWS), share), :]
+
+
+def scaled_rows(rows, info, sources):
     share = rows.shape[0] // sources
-    begin = lax.rem(lax.axis_index("boot") + turn, lax.axis_size("boot")) * share
-    info = info_ref[pl.ds(pl.multiple_of(begin, ROWS), share), :]
-    blocks, drive = [], jnp.zeros((1, rows.shape[1]), F32)
-    for source in range(sources):
-        block = rows[source * share : (source + 1) * share, :]
-        block = (info[:, source : source + 1] * block).astype(BF16).astype(F32)
-        blocks.append(block)
-        dep_col = info[:, sources + source : sources + source + 1]
-        drive = drive + jnp.sum(dep_col * block, axis=0, keepdims=True)
-    return jnp.concatenate(blocks, axis=0).astype(BF16), drive
-
-
-def outer_sum(rows, scaled):
-    return lax.dot_general(
-        rows.astype(BF16), scaled, (((0,), (0,)), ((), ())), preferred_element_type=F32
-    )
+    blocks = [
+        info[:, source : source + 1] * rows[source * share : (source + 1) * share, :]
+        for source in range(sources)
+    ]
+    return jnp.concatenate(blocks, axis=0).astype(BF16)
+
+
+def gram_sums(rows, info, scaled, sources):
+    share, members = rows.shape[0] // sources, rows.shape[1]
+    deps = [
+        jnp.broadcast_to(info[:, sources + source : sources + source + 1], (share, LANES))
+        for source in range(sources)
+    ]
+    left = jnp.concatenate([rows, jnp.concatenate(deps, axis=0)], axis=1).astype(BF16)
+    sums = lax.dot_general(left, scaled, (((0,), (0,)), ((), ())), preferred_element_type=F32)
+    return sums[0:members, :], sums[members : members + 1, :]
 
 
 def gram_kernel(rows_ref, gram_ref, drive_ref, info_ref):
     members = gram_ref.shape[0]
     slot_info(rows_ref, info_ref)
     rows = slot_rows(rows_ref, members)
-    scaled, drive_ref[...] = scaled_rows(rows, info_ref, 0, rows_ref.shape[0])
-    gram_ref[...] = outer_sum(rows, scaled)
+    sources = rows_ref.shape[0]
+    info = share_info(info_ref, 0, rows.shape[0] // sources)
+    gram_ref[...], drive_ref[...] = gram_sums(
+        rows, info, scaled_rows(rows, info, sources), sources
+    )
 
 
 def own_gram(rows, members):
@@ -183,11 +191,21 @@
 
 
 def weights_kernel(*refs):
-    gram_ref, drive_ref, own_info_ref = refs[:3]
-    rows_refs, blended_ref, info_ref = refs[3:-8], refs[-8], refs[-7]
-    y_ref, z_ref, y_high, z_high, low, w_high = refs[-6:]
+    count = (len(refs) - 7) // 2
+    far_refs, blended_ref, refs = refs[:count], refs[count], refs[count + 1 :]
+    gram_ref, drive_ref, own_info_ref, rows_refs = refs[0], refs[1], refs[2], refs[3:count]
+    info_ref, yz_ref, yz_high, low, w_high, sems = refs[count:]
     groups, members, _ = blended_ref.shape
     sources = rows_refs[0].shape[0]
+    copies = [
+        pltpu.make_async_copy(far_ref, near_ref, sems.at[place])
+        for place, (far_ref, near_ref) in enumerate(zip(far_refs, refs[:count]))
+    ]
+    for copy in reversed(copies):
+        copy.start()
+    for copy in reversed(copies):
+        copy.wait()
+    y_part, z_part = slice(0, members), slice(members, 2 * members)
     row_id = lax.broadcasted_iota(jnp.int32, (members, members), 0)
     col_id = lax.broadcasted_iota(jnp.int32, (members, members), 1)
     identity = jnp.where(row_id == col_id, 1.0, 0.0)
@@ -197,11 +215,12 @@
     dot = functools.partial(jnp.dot, preferred_element_type=F32)
 
     def split(chain, value):
+        value = -0.5 * value
         w_high[chain] = value.astype(BF16)
         for begin in range(0, members, LANES):
             block = slice(begin, begin + LANES)
             w_high[chain, block, block] = jnp.where(eye, 0.0, value[block, block]).astype(BF16)
-        return 1.5 - 0.5 * diagonal_column(value, eye)
+        return 1.5 + diagonal_column(value, eye)
 
     grams = [gram_ref[...]] + [jnp.zeros((members, members), F32)] * (groups - 1)
     drives = [drive_ref[...]] + [jnp.zeros((1, members), F32)] * (groups - 1)
@@ -209,17 +228,18 @@
         slot_info(rows_refs[chain], info_ref.at[chain])
     for turn, rows_ref in enumerate(rows_refs):
         rows = slot_rows(rows_ref, members)
+        share = rows.shape[0] // sources
         chains = [chain for chain in range(groups) if chain or turn]
-        scaled = []
-        for chain in chains:
-            info = info_ref.at[chain] if chain else own_info_ref
-            block, drive = scaled_rows(rows, info, turn, sources)
-            scaled.append(block)
-            drives[chain] = drives[chain] + drive
-        sums = outer_sum(rows, jnp.concatenate(scaled, axis=1))
+        infos = [
+            share_info(info_ref.at[chain] if chain else own_info_ref, turn, share)
+            for chain in chains
+        ]
+        scaled = jnp.concatenate([scaled_rows(rows, info, sources) for info in infos], axis=1)
+        gram, drive = gram_sums(rows, infos[0], scaled, sources)
         for place, chain in enumerate(chains):
             columns = slice(place * members, (place + 1) * members)
-            grams[chain] = grams[chain] + sums[:, columns]
+            grams[chain] = grams[chain] + gram[:, columns]
+            drives[chain] = drives[chain] + drive[:, columns]
 
     frobenius = []
     for chain in range(groups):
@@ -228,30 +248,34 @@
         frobenius.append(jnp.sqrt(squares))
         current = shifted / frobenius[chain]
         factor = split(chain, current)
-        y_high[chain] = current.astype(BF16)
-        z_ref[chain] = 1.5 * identity - 0.5 * current
-        y_ref[chain] = factor * current - 0.5 * dot(w_high[chain], y_high[chain])
-        y_high[chain], z_high[chain] = y_ref[chain].astype(BF16), z_ref[chain].astype(BF16)
+        yz_high[chain, :, y_part] = current.astype(BF16)
+        yz_ref[chain, :, z_part] = 1.5 * identity - 0.5 * current
+        change = dot(w_high[chain], yz_high[chain, :, y_part])
+        yz_ref[chain, :, y_part] = factor * current + change
+        yz_high[chain] = yz_ref[chain].astype(BF16)
+
+    def high_product(chain):
+        return dot(yz_high[chain, :, z_part], yz_high[chain, :, y_part])
 
     def step(_, carry):
-        factors = [split(c, dot(z_high[c], y_high[c])) for c in range(groups)]
+        factors = [split(chain, high_product(chain)) for chain in range(groups)]
         for chain in range(groups):
-            current = factors[chain] * y_ref[chain] - 0.5 * dot(w_high[chain], y_high[chain])
-            root = factors[chain] * z_ref[chain] - 0.5 * dot(w_high[chain], z_high[chain])
-            y_ref[chain], z_ref[chain] = current, root
-            y_high[chain], z_high[chain] = current.astype(BF16), root.astype(BF16)
+            value = factors[chain] * yz_ref[chain] + dot(w_high[chain], yz_high[chain])
+            yz_ref[chain] = value
+            yz_high[chain] = value.astype(BF16)
         return carry
 
-    lax.fori_loop(1, NS_STEPS - 1, step, 0)
+    lax.fori_loop(1, NS_STEPS - 1, step, 0, unroll=True)
     for chain in range(groups):
-        low[2 * chain] = (y_ref[chain] - y_high[chain].astype(F32)).astype(BF16)
-        low[2 * chain + 1] = (z_ref[chain] - z_high[chain].astype(F32)).astype(BF16)
+        low[chain] = (yz_ref[chain] - yz_high[chain].astype(F32)).astype(BF16)
     factors = []
     for chain in range(groups):
-        small = dot(z_high[chain], low[2 * chain]) + dot(low[2 * chain + 1], y_high[chain])
-        factors.append(split(chain, dot(z_high[chain], y_high[chain]) + small))
+        small = dot(yz_high[chain, :, z_part], low[chain, :, y_part])
+        small += dot(low[chain, :, z_part], yz_high[chain, :, y_part])
+        factors.append(split(chain, high_product(chain) + small))
     for chain in range(groups):
-        root = factors[chain] * z_ref[chain] - 0.5 * dot(w_high[chain], z_high[chain])
+        root = factors[chain] * yz_ref[chain, :, z_part]
+        root += dot(w_high[chain], yz_high[chain, :, z_part])
         root = root / jnp.sqrt(frobenius[chain])
         inner = jnp.sum(root * diagonal_column(drives[chain], eye), axis=0, keepdims=True)
         mean_weight = jnp.sum(root * diagonal_column(inner, eye), axis=0, keepdims=True)
@@ -260,28 +284,29 @@
 
 def patch_weights(gram, drive, info, rows):
     groups, members = len(rows), gram.shape[0]
-    whole = pltpu.VMEM((groups, members, members), F32)
-    half = pltpu.VMEM((groups, members, members), BF16)
+    operands = (gram, drive, info, *rows)
+    half = pltpu.VMEM((groups, members, 2 * members), BF16)
     return pl.pallas_call(
         weights_kernel,
+        in_specs=[pl.BlockSpec(memory_space=pl.ANY)] * len(operands),
         out_shape=jax.ShapeDtypeStruct((groups, members, members), BF16),
-        scratch_shapes=[
+        scratch_shapes=[pltpu.VMEM(operand.shape, operand.dtype) for operand in operands]
+        + [
             pltpu.VMEM((groups, LANES, LANES), F32),
-            whole,
-            whole,
+            pltpu.VMEM((groups, members, 2 * members), F32),
             half,
             half,
-            pltpu.VMEM((2 * groups, members, members), BF16),
-            half,
+            pltpu.VMEM((groups, members, members), BF16),
+            pltpu.SemaphoreType.DMA((len(operands),)),
         ],
-        compiler_params=pltpu.CompilerParams(vmem_limit_bytes=(8 + 10 * groups) * MEBI),
+        compiler_params=pltpu.CompilerParams(vmem_limit_bytes=64 * MEBI),
         cost_estimate=pl.CostEstimate(
             flops=80 * groups * members * members * members,
             bytes_accessed=8 * members * members,
             transcendentals=0,
         ),
         name="patch_weights",
-    )(gram, drive, info, *rows)
+    )(*operands)
 
 
 def update_kernel(blended_ref, background_ref, analysis_ref):
@@ -348,8 +373,13 @@
 def place_pieces(pieces):
     groups, patches, own_members, share = pieces.shape
     points = groups * patches * share
+    steps = 4
+    held = patches // steps
     return pl.pallas_call(
         place_kernel,
+        grid=(steps,),
+        in_specs=[pl.BlockSpec((groups, held, own_members, share), lambda i: (0, i, 0, 0))],
+        out_specs=pl.BlockSpec((own_members, points // steps), lambda i: (0, i)),
         out_shape=jax.ShapeDtypeStruct((own_members, points), BF16),
         compiler_params=pltpu.CompilerParams(vmem_limit_bytes=16 * MEBI),
         cost_estimate=pl.CostEstimate(

time: 124 us -> 129 us (1.040)
  Pallas kernels: 21.4 us -> 26.6 us
  waiting for transfers between devices: 29 us -> 26.5 us
  local copies, waits for them, and re-layouts: 3.62 us -> 5.89 us
    pallas_call x2, Pallas kernels: 15.3 us -> 19 us  [the longest x1 17.1 us: patch_weights(): pl.pallas_call(weights_kernel, in_specs=[pl.BlockSpec(memory_space=pl.ANY...]
    ppermute x1, waiting for transfers between devices: 12.4 us -> 9.97 us  [swap_shares(): lax.ppermute(own, 'boot', [(g, (g - turn) % groups) for g in range(groups)])]
    unnamed x6 -> x14, local copies, waits for them, and re-layouts: 3.62 us -> 5.89 us
  transfers between devices with their start and end apart: 3 -> 3, of which waited for: 2 -> 2; matrix products, arithmetic and copies ran while one was open for 0% -> 0% of each run, Pallas kernels for 13% -> 15%
where the time goes in v8:
time: 129 us
  blocking collectives  55 us (43%)
  Pallas kernels  26.6 us (21%)
  waiting for transfers between devices  26.5 us (21%)
  starting transfers between devices  14.6 us (11%)
  local copies, waits for them, and re-layouts  5.89 us (5%)
    all_to_all x1, blocking collectives, exchange(): return lax.all_to_all(blocks, axes, split_axis=0, concat_axis=0, tiled=True)  55 us
    pallas_call x1, Pallas kernels, patch_weights(): pl.pallas_call(weights_kernel, in_specs=[pl.BlockSpec(memory_space=pl.ANY...  17.1 us
    all_to_all x2, waiting for transfers between devices, exchange(): return lax.all_to_all(blocks, axes, split_axis=0, concat_axis=0, tiled=True)  16.6 us
    all_to_all x2, starting transfers between devices, exchange(): return lax.all_to_all(blocks, axes, split_axis=0, concat_axis=0, tiled=True)  13.1 us
    ppermute x1, waiting for transfers between devices, swap_shares(): lax.ppermute(own, 'boot', [(g, (g - turn) % groups) for g in range(groups)])  9.97 us
    unnamed x14, local copies, waits for them, and re-layouts  5.89 us
    pallas_call x1, Pallas kernels, pack(): pl.pallas_call(functools.partial(pack_kernel, groups), out_shape=jax.Shap...  2.83 us
  transfers between devices with their start and end apart: 3, of which 2 were waited for; matrix products, arithmetic and copies ran while one was open for 0% of the time, Pallas kernels for 15%

profile of v8, /device:TPU:0, one launch (start us, length us, event | category | flops | bytes accessed | tf_op | source)
XLA Modules:
  0.0 128.7 jit_solution(8232230373020585443)
XLA Ops:
  0.0 2.8 %pack_rows.1 = bf16[16,8,3200]{2,1,0:T(8,128)(2,1)} custom-call(s32[2,384]{1,0:T(2,128)} %bitcast.7, s32[2,384]{1,0:T(2,128)} %bitcast.8, s32[384]{0:T(512)} %refs_2_.1, f32[384]{0:T(512)} %refs_3_.1, bf16[384]{0:T(512)(128)(2,1)} %refs_4_.1, bf16[384,512]{1,0:T(8,128)(2,1)} %refs_5_.1), custom_call_target="tpu_custom_call" | custom-call | flops 301989888 | bytes 1179648 | tf_op jit(solution)/shard_map/pack_rows/pallas_call | solution.py:92
  2.8 7.4 %all-to-all-start = ((bf16[16,8,3200]{2,1,0:T(8,128)(2,1)}), bf16[16,8,3200]{2,1,0:T(8,128)(2,1)S(1)}, u32[]{:S(2)}, u32[]{:S(2)}) async-start(bf16[16,8,3200]{2,1,0:T(8,128)(2,1)} %pack_rows.1), calls=%async_computation | async-start | bytes 1638400 | tf_op jit(solution)/shard_map/all_to_all | solution.py:393
  10.3 0.0 copy-start
  10.3 1.6 %copy-done = bf16[32,32768]{1,0:T(8,128)(2,1)S(1)} copy-done((bf16[32,32768]{1,0:T(8,128)(2,1)S(1)}, bf16[32,32768]{1,0:T(8,128)(2,1)}, u32[]{:S(2)}) %copy-start) | copy-done | bytes 2097176
  11.8 1.1 cut_share.1
  12.9 16.6 %all-to-all-done.rows_ref.refs_3_ = bf16[16,8,3200]{2,1,0:T(8,128)(2,1)S(1)} async-done(((bf16[16,8,3200]{2,1,0:T(8,128)(2,1)}), bf16[16,8,3200]{2,1,0:T(8,128)(2,1)S(1)}, u32[]{:S(2)}, u32[]{:S(2)}) %all-to-all-start) | async-done | bytes 819232 | tf_op jit(solution)/shard_map/all_to_all | solution.py:393
  29.5 0.0 copy-start.2
  29.5 1.5 %collective-permute-start = (bf16[16,8,3200]{2,1,0:T(8,128)(2,1)S(1)}, bf16[16,8,3200]{2,1,0:T(8,128)(2,1)S(1)}, u32[]{:S(2)}, u32[]{:S(2)}) collective-permute-start(bf16[16,8,3200]{2,1,0:T(8,128)(2,1)S(1)} %all-to-all-done.rows_ref.refs_3_), channel_id=1, source_target_pairs={{0,16},{16,0},{1,17},{17,1},{2,18},{18,2},{3,19},{19,3},{4,20},{20... | collective-permute-start | bytes 2457608 | tf_op jit(solution)/shard_map/ppermute | solution.py:399
  31.0 5.7 %all-to-all-start.1 = ((bf16[16,32,1024]{2,1,0:T(8,128)(2,1)}), bf16[16,32,1024]{2,1,0:T(8,128)(2,1)}, u32[]{:S(2)}, u32[]{:S(2)}) async-start(bf16[16,32,1024]{2,1,0:T(8,128)(2,1)} %cut_share.1), calls=%async_computation.1 | async-start | bytes 2097152 | tf_op jit(solution)/shard_map/all_to_all | solution.py:393
  36.7 1.1 own_gram.1
  37.8 0.0 copy-done.2
  37.8 0.0 copy-start.3
  37.8 1.0 copy-done.3
  38.8 0.0 copy-start.4
  38.8 0.6 copy-done.4
  39.4 0.0 copy-start.5
  39.4 0.6 copy-done.5
  40.0 10.0 %collective-permute-done.refs_4_ = bf16[16,8,3200]{2,1,0:T(8,128)(2,1)S(1)} collective-permute-done((bf16[16,8,3200]{2,1,0:T(8,128)(2,1)S(1)}, bf16[16,8,3200]{2,1,0:T(8,128)(2,1)S(1)}, u32[]{:S(2)}, u32[]{:S(2)}) %collective-permute-start) | collective-permute-done | bytes 819232 | tf_op jit(solution)/shard_map/ppermute | solution.py:399
  49.9 0.0 copy-start.6
  49.9 0.9 copy-done.6
  50.8 17.1 %patch_weights.1.blended_ref = bf16[2,512,512]{2,1,0:T(8,128)(2,1)} custom-call(f32[512,512]{1,0:T(8,128)} %copy-done.3, f32[1,512]{1,0:T(1,128)} %copy-done.5, f32[128,128]{1,0:T(8,128)} %copy-done.4, bf16[16,8,3200]{2,1,0:T(8,128)(2,1)} %copy-done.2, bf16[16,8,3200]{2,1,0:T(8,128)(2,1)} %copy-done.6), custom_call_target="tpu_custom_call" | custom-call | flops 21474836480 | bytes 2097152 | tf_op jit(solution)/shard_map/patch_weights/pallas_call | solution.py:289
  67.9 0.0 all-to-all-done.1
  68.0 0.0 copy-start.1
  68.0 1.2 copy-done.1
  69.2 2.6 %update_points.1 = bf16[2,512,1024]{2,1,0:T(8,128)(2,1)S(1)} custom-call(bf16[2,512,512]{2,1,0:T(8,128)(2,1)S(1)} %copy-done.1, bf16[512,1024]{1,0:T(8,128)(2,1)} %bitcast.2.background_ref), custom_call_target="tpu_custom_call" | custom-call | flops 1073741824 | bytes 3145728 | tf_op jit(solution)/shard_map/update_points/pallas_call | solution.py:330
  71.8 55.0 %all_to_all.15 = bf16[32,32,1024]{2,1,0:T(8,128)(2,1)S(1)} all-to-all(bf16[32,32,1024]{2,1,0:T(8,128)(2,1)S(1)} %bitcast.5), channel_id=1, replica_groups=mesh['boot'=2,'space'=16] {'boot','space'}, dimensions={0} | all-to-all | bytes 4194304 | tf_op jit(solution)/shard_map/all_to_all | solution.py:393
  126.8 1.9 %place_pieces.1 = bf16[32,32768]{1,0:T(8,128)(2,1)} custom-call(bf16[2,16,32,1024]{3,2,1,0:T(8,128)(2,1)S(1)} %bitcast.6), custom_call_target="tpu_custom_call" | custom-call | bytes 4194304 | tf_op jit(solution)/shard_map/place_pieces/pallas_call | solution.py:378
Async XLA Ops:
  2.8 26.6 %all-to-all-start = ((bf16[16,8,3200]{2,1,0:T(8,128)(2,1)}), bf16[16,8,3200]{2,1,0:T(8,128)(2,1)S(1)}, u32[]{:S(2)}, u32[]{:S(2)}) async-start(bf16[16,8,3200]{2,1,0:T(8,128)(2,1)} %pack_rows.1), calls=%async_computation | async-start | bytes 1638400 | tf_op jit(solution)/shard_map/all_to_all | solution.py:393
  10.3 1.6 %copy-start = (bf16[32,32768]{1,0:T(8,128)(2,1)S(1)}, bf16[32,32768]{1,0:T(8,128)(2,1)}, u32[]{:S(2)}) copy-start(bf16[32,32768]{1,0:T(8,128)(2,1)} %states_ref.1) | copy-start | bytes 6291460
  29.5 8.3 %copy-start.2 = (bf16[16,8,3200]{2,1,0:T(8,128)(2,1)}, bf16[16,8,3200]{2,1,0:T(8,128)(2,1)S(1)}, u32[]{:S(2)}) copy-start(bf16[16,8,3200]{2,1,0:T(8,128)(2,1)S(1)} %all-to-all-done.rows_ref.refs_3_) | copy-start | bytes 2457604
  29.5 20.4 %collective-permute-start = (bf16[16,8,3200]{2,1,0:T(8,128)(2,1)S(1)}, bf16[16,8,3200]{2,1,0:T(8,128)(2,1)S(1)}, u32[]{:S(2)}, u32[]{:S(2)}) collective-permute-start(bf16[16,8,3200]{2,1,0:T(8,128)(2,1)S(1)} %all-to-all-done.rows_ref.refs_3_), channel_id=1, source_target_pairs={{0,16},{16,0},{1,17},{17,1},{2,18},{18,2},{3,19},{19,3},{4,20},{20... | collective-permute-start | bytes 2457608 | tf_op jit(solution)/shard_map/ppermute | solution.py:399
  31.0 37.0 %all-to-all-start.1 = ((bf16[16,32,1024]{2,1,0:T(8,128)(2,1)}), bf16[16,32,1024]{2,1,0:T(8,128)(2,1)}, u32[]{:S(2)}, u32[]{:S(2)}) async-start(bf16[16,32,1024]{2,1,0:T(8,128)(2,1)} %cut_share.1), calls=%async_computation.1 | async-start | bytes 2097152 | tf_op jit(solution)/shard_map/all_to_all | solution.py:393
  37.8 1.0 copy-start.3
  38.8 0.6 copy-start.4
  39.4 0.6 copy-start.5
  49.9 0.9 copy-start.6
  68.0 1.2 copy-start.1

commit v9 on v6

--- a/solution.py
+++ b/solution.py
@@ -139,33 +139,32 @@
     return jnp.concatenate(blocks, axis=0).astype(BF16), drive
 
 
-def outer_sum(rows, scaled):
-    return lax.dot_general(
-        rows.astype(BF16), scaled, (((0,), (0,)), ((), ())), preferred_element_type=F32
-    )
-
-
-def gram_kernel(rows_ref, gram_ref, drive_ref, info_ref):
+def gram_kernel(rows_ref, gram_ref, drive_ref, info_ref, ordered_ref, turned_ref):
     members = gram_ref.shape[0]
     slot_info(rows_ref, info_ref)
     rows = slot_rows(rows_ref, members)
+    ordered_ref[...] = rows.astype(BF16)
+    turned_ref[...] = rows.T.astype(BF16)
     scaled, drive_ref[...] = scaled_rows(rows, info_ref, 0, rows_ref.shape[0])
-    gram_ref[...] = outer_sum(rows, scaled)
+    gram_ref[...] = jnp.dot(turned_ref[...], scaled, preferred_element_type=F32)
 
 
 def own_gram(rows, members):
-    sources, _, width = rows.shape
+    sources, height, width = rows.shape
+    slots = sources * height * ((width - LANES) // members)
     return pl.pallas_call(
         gram_kernel,
         out_shape=(
             jax.ShapeDtypeStruct((members, members), F32),
             jax.ShapeDtypeStruct((1, members), F32),
             jax.ShapeDtypeStruct((LANES, LANES), F32),
+            jax.ShapeDtypeStruct((slots, members), BF16),
+            jax.ShapeDtypeStruct((members, slots), BF16),
         ),
         compiler_params=pltpu.CompilerParams(vmem_limit_bytes=16 * MEBI),
         cost_estimate=pl.CostEstimate(
-            flops=4 * members * sources * ROWS * width,
-            bytes_accessed=2 * sources * ROWS * width,
+            flops=4 * members * members * slots,
+            bytes_accessed=6 * slots * members,
             transcendentals=0,
         ),
         name="own_gram",
@@ -183,11 +182,11 @@
 
 
 def weights_kernel(*refs):
-    gram_ref, drive_ref, own_info_ref = refs[:3]
-    rows_refs, blended_ref, info_ref = refs[3:-8], refs[-8], refs[-7]
+    gram_ref, drive_ref, own_info_ref, ordered_ref, turned_ref = refs[:5]
+    rows_refs, blended_ref, info_ref = refs[5:-8], refs[-8], refs[-7]
     y_ref, z_ref, y_high, z_high, low, w_high = refs[-6:]
     groups, members, _ = blended_ref.shape
-    sources = rows_refs[0].shape[0]
+    sources = rows_refs[0].shape[0] if rows_refs else 1
     row_id = lax.broadcasted_iota(jnp.int32, (members, members), 0)
     col_id = lax.broadcasted_iota(jnp.int32, (members, members), 1)
     identity = jnp.where(row_id == col_id, 1.0, 0.0)
@@ -205,20 +204,28 @@
 
     grams = [gram_ref[...]] + [jnp.zeros((members, members), F32)] * (groups - 1)
     drives = [drive_ref[...]] + [jnp.zeros((1, members), F32)] * (groups - 1)
+    infos = [own_info_ref] + [info_ref.at[chain] for chain in range(1, groups)]
     for chain in range(1, groups):
-        slot_info(rows_refs[chain], info_ref.at[chain])
-    for turn, rows_ref in enumerate(rows_refs):
+        slot_info(rows_refs[chain - 1], infos[chain])
+    for chain in range(1, groups):
+        scaled, drive = scaled_rows(ordered_ref[...].astype(F32), infos[chain], 0, sources)
+        grams[chain] = grams[chain] + dot(turned_ref[...], scaled)
+        drives[chain] = drives[chain] + drive
+    for turn, rows_ref in enumerate(rows_refs, 1):
         rows = slot_rows(rows_ref, members)
-        chains = [chain for chain in range(groups) if chain or turn]
         scaled = []
-        for chain in chains:
-            info = info_ref.at[chain] if chain else own_info_ref
-            block, drive = scaled_rows(rows, info, turn, sources)
+        for chain in range(groups):
+            block, drive = scaled_rows(rows, infos[chain], turn, sources)
             scaled.append(block)
             drives[chain] = drives[chain] + drive
-        sums = outer_sum(rows, jnp.concatenate(scaled, axis=1))
-        for place, chain in enumerate(chains):
-            columns = slice(place * members, (place + 1) * members)
+        sums = lax.dot_general(
+            rows.astype(BF16),
+            jnp.concatenate(scaled, axis=1),
+            (((0,), (0,)), ((), ())),
+            preferred_element_type=F32,
+        )
+        for chain in range(groups):
+            columns = slice(chain * members, (chain + 1) * members)
             grams[chain] = grams[chain] + sums[:, columns]
 
     frobenius = []
@@ -242,7 +249,7 @@
             y_high[chain], z_high[chain] = current.astype(BF16), root.astype(BF16)
         return carry
 
-    lax.fori_loop(1, NS_STEPS - 1, step, 0)
+    lax.fori_loop(1, NS_STEPS - 1, step, 0, unroll=True)
     for chain in range(groups):
         low[2 * chain] = (y_ref[chain] - y_high[chain].astype(F32)).astype(BF16)
         low[2 * chain + 1] = (z_ref[chain] - z_high[chain].astype(F32)).astype(BF16)
@@ -258,8 +265,8 @@
         blended_ref[chain] = (root + mean_weight / (members - 1.0)).astype(BF16)
 
 
-def patch_weights(gram, drive, info, rows):
-    groups, members = len(rows), gram.shape[0]
+def patch_weights(own, other_rows):
+    groups, members = len(other_rows) + 1, own[0].shape[0]
     whole = pltpu.VMEM((groups, members, members), F32)
     half = pltpu.VMEM((groups, members, members), BF16)
     return pl.pallas_call(
@@ -281,7 +288,7 @@
             transcendentals=0,
         ),
         name="patch_weights",
-    )(gram, drive, info, *rows)
+    )(*own, *other_rows)
 
 
 def update_kernel(blended_ref, background_ref, analysis_ref):
@@ -405,8 +412,8 @@
     other_rows = swap_shares(own_rows)
     own_points = exchange(own_points).reshape(-1, share)
 
-    gram, drive, info = own_gram(own_rows, measurement_anomaly_matrix.shape[1])
-    blended = patch_weights(gram, drive, info, [own_rows] + other_rows)
+    own = own_gram(own_rows, measurement_anomaly_matrix.shape[1])
+    blended = patch_weights(own, other_rows)
     analysis = update_points(blended, own_points)
     analysis = exchange(analysis.reshape(-1, own_members, share), ("boot", "space"))
     return place_pieces(analysis.reshape(groups, device_count, own_members, share))

time: 124 us -> 122 us (0.984)
  local copies, waits for them, and re-layouts: 3.62 us -> 1.59 us
    unnamed x6 -> x2, local copies, waits for them, and re-layouts: 3.62 us -> 1.59 us
where the time goes in v9:
time: 122 us
  blocking collectives  55 us (45%)
  waiting for transfers between devices  29 us (24%)
  Pallas kernels  21.3 us (17%)
  starting transfers between devices  14.5 us (12%)
  local copies, waits for them, and re-layouts  1.59 us (1%)
    all_to_all x1, blocking collectives, exchange(): return lax.all_to_all(blocks, axes, split_axis=0, concat_axis=0, tiled=True)  55 us
    all_to_all x2, waiting for transfers between devices, exchange(): return lax.all_to_all(blocks, axes, split_axis=0, concat_axis=0, tiled=True)  16.6 us
    pallas_call x1, Pallas kernels, patch_weights(): pl.pallas_call(weights_kernel, out_shape=jax.ShapeDtypeStruct((groups, me...  13.7 us
    all_to_all x2, starting transfers between devices, exchange(): return lax.all_to_all(blocks, axes, split_axis=0, concat_axis=0, tiled=True)  13.1 us
    ppermute x1, waiting for transfers between devices, swap_shares(): lax.ppermute(own, 'boot', [(g, (g - turn) % groups) for g in range(groups)])  12.4 us
    pallas_call x1, Pallas kernels, pack(): pl.pallas_call(functools.partial(pack_kernel, groups), out_shape=jax.Shap...  2.84 us
  transfers between devices with their start and end apart: 3, of which 2 were waited for; matrix products, arithmetic and copies ran while one was open for 0% of the time, Pallas kernels for 13%

profile of v9, /device:TPU:0, one launch (start us, length us, event | category | flops | bytes accessed | tf_op | source)
XLA Modules:
  0.0 121.5 jit_solution(4973159530872057677)
XLA Ops:
  0.0 2.8 %pack_rows.1 = bf16[16,8,3200]{2,1,0:T(8,128)(2,1)} custom-call(s32[2,384]{1,0:T(2,128)} %bitcast.8, s32[2,384]{1,0:T(2,128)} %bitcast.9, s32[384]{0:T(512)} %refs_2_.1, f32[384]{0:T(512)} %refs_3_.1, bf16[384]{0:T(512)(128)(2,1)} %refs_4_.1, bf16[384,512]{1,0:T(8,128)(2,1)} %refs_5_.1), custom_call_target="tpu_custom_call" | custom-call | flops 301989888 | bytes 1179648 | tf_op jit(solution)/shard_map/pack_rows/pallas_call | solution.py:92
  2.9 7.4 %all-to-all-start = ((bf16[16,8,3200]{2,1,0:T(8,128)(2,1)}), bf16[16,8,3200]{2,1,0:T(8,128)(2,1)S(1)}, u32[]{:S(2)}, u32[]{:S(2)}) async-start(bf16[16,8,3200]{2,1,0:T(8,128)(2,1)} %pack_rows.1), calls=%async_computation | async-start | bytes 1638400 | tf_op jit(solution)/shard_map/all_to_all | solution.py:370
  10.3 0.0 copy-start
  10.3 1.6 %copy-done = bf16[32,32768]{1,0:T(8,128)(2,1)S(1)} copy-done((bf16[32,32768]{1,0:T(8,128)(2,1)S(1)}, bf16[32,32768]{1,0:T(8,128)(2,1)}, u32[]{:S(2)}) %copy-start) | copy-done | bytes 2097176
  11.9 1.0 cut_share.1
  12.9 16.6 %all-to-all-done.rows_ref = bf16[16,8,3200]{2,1,0:T(8,128)(2,1)S(1)} async-done(((bf16[16,8,3200]{2,1,0:T(8,128)(2,1)}), bf16[16,8,3200]{2,1,0:T(8,128)(2,1)S(1)}, u32[]{:S(2)}, u32[]{:S(2)}) %all-to-all-start) | async-done | bytes 819232 | tf_op jit(solution)/shard_map/all_to_all | solution.py:370
  29.5 1.5 %collective-permute-start = (bf16[16,8,3200]{2,1,0:T(8,128)(2,1)S(1)}, bf16[16,8,3200]{2,1,0:T(8,128)(2,1)S(1)}, u32[]{:S(2)}, u32[]{:S(2)}) collective-permute-start(bf16[16,8,3200]{2,1,0:T(8,128)(2,1)S(1)} %all-to-all-done.rows_ref), channel_id=1, source_target_pairs={{0,16},{16,0},{1,17},{17,1},{2,18},{18,2},{3,19},{19,3},{4,20},{20... | collective-permute-start | bytes 2457608 | tf_op jit(solution)/shard_map/ppermute | solution.py:376
  31.0 5.7 %all-to-all-start.1 = ((bf16[16,32,1024]{2,1,0:T(8,128)(2,1)}), bf16[16,32,1024]{2,1,0:T(8,128)(2,1)S(1)}, u32[]{:S(2)}, u32[]{:S(2)}) async-start(bf16[16,32,1024]{2,1,0:T(8,128)(2,1)} %cut_share.1), calls=%async_computation.1 | async-start | bytes 2097152 | tf_op jit(solution)/shard_map/all_to_all | solution.py:370
  36.6 0.9 own_gram.1
  37.6 12.4 %collective-permute-done.refs_5_ = bf16[16,8,3200]{2,1,0:T(8,128)(2,1)S(1)} collective-permute-done((bf16[16,8,3200]{2,1,0:T(8,128)(2,1)S(1)}, bf16[16,8,3200]{2,1,0:T(8,128)(2,1)S(1)}, u32[]{:S(2)}, u32[]{:S(2)}) %collective-permute-start) | collective-permute-done | bytes 819232 | tf_op jit(solution)/shard_map/ppermute | solution.py:376
  49.9 13.7 %patch_weights.1.blended_ref = bf16[2,512,512]{2,1,0:T(8,128)(2,1)S(1)} custom-call(f32[512,512]{1,0:T(8,128)S(1)} %get-tuple-element.13.refs_0_, f32[1,512]{1,0:T(1,128)S(1)} %get-tuple-element.14.refs_1_, f32[128,128]{1,0:T(8,128)S(1)} %get-tuple-element.15.refs_2_, bf16[768,512]{1,0:T(8,128)(2,1)S(1)} %get-tuple-element.16.refs_3_, ...), custom_call_target="tpu_custom_call" | custom-call | flops 21474836480 | bytes 2097152 | tf_op jit(solution)/shard_map/patch_weights/pallas_call | solution.py:272
  63.7 0.0 all-to-all-done.1
  63.7 1.4 %update_points.1 = bf16[2,512,1024]{2,1,0:T(8,128)(2,1)S(1)} custom-call(bf16[2,512,512]{2,1,0:T(8,128)(2,1)S(1)} %patch_weights.1.blended_ref, bf16[512,1024]{1,0:T(8,128)(2,1)S(1)} %bitcast.7), custom_call_target="tpu_custom_call" | custom-call | flops 1073741824 | bytes 3145728 | tf_op jit(solution)/shard_map/update_points/pallas_call | solution.py:312
  65.1 55.0 %all_to_all.15 = bf16[32,32,1024]{2,1,0:T(8,128)(2,1)S(1)} all-to-all(bf16[32,32,1024]{2,1,0:T(8,128)(2,1)S(1)} %bitcast.5), channel_id=1, replica_groups=mesh['boot'=2,'space'=16] {'boot','space'}, dimensions={0} | all-to-all | bytes 4194304 | tf_op jit(solution)/shard_map/all_to_all | solution.py:370
  120.1 1.5 %place_pieces.1 = bf16[32,32768]{1,0:T(8,128)(2,1)} custom-call(bf16[2,16,32,1024]{3,2,1,0:T(8,128)(2,1)S(1)} %bitcast.6), custom_call_target="tpu_custom_call" | custom-call | bytes 4194304 | tf_op jit(solution)/shard_map/place_pieces/pallas_call | solution.py:358
Async XLA Ops:
  2.9 26.6 %all-to-all-start = ((bf16[16,8,3200]{2,1,0:T(8,128)(2,1)}), bf16[16,8,3200]{2,1,0:T(8,128)(2,1)S(1)}, u32[]{:S(2)}, u32[]{:S(2)}) async-start(bf16[16,8,3200]{2,1,0:T(8,128)(2,1)} %pack_rows.1), calls=%async_computation | async-start | bytes 1638400 | tf_op jit(solution)/shard_map/all_to_all | solution.py:370
  10.3 1.6 %copy-start = (bf16[32,32768]{1,0:T(8,128)(2,1)S(1)}, bf16[32,32768]{1,0:T(8,128)(2,1)}, u32[]{:S(2)}) copy-start(bf16[32,32768]{1,0:T(8,128)(2,1)} %states_ref.1) | copy-start | bytes 6291460
  29.5 20.4 %collective-permute-start = (bf16[16,8,3200]{2,1,0:T(8,128)(2,1)S(1)}, bf16[16,8,3200]{2,1,0:T(8,128)(2,1)S(1)}, u32[]{:S(2)}, u32[]{:S(2)}) collective-permute-start(bf16[16,8,3200]{2,1,0:T(8,128)(2,1)S(1)} %all-to-all-done.rows_ref), channel_id=1, source_target_pairs={{0,16},{16,0},{1,17},{17,1},{2,18},{18,2},{3,19},{19,3},{4,20},{20... | collective-permute-start | bytes 2457608 | tf_op jit(solution)/shard_map/ppermute | solution.py:376
  31.0 32.7 %all-to-all-start.1 = ((bf16[16,32,1024]{2,1,0:T(8,128)(2,1)}), bf16[16,32,1024]{2,1,0:T(8,128)(2,1)S(1)}, u32[]{:S(2)}, u32[]{:S(2)}) async-start(bf16[16,32,1024]{2,1,0:T(8,128)(2,1)} %cut_share.1), calls=%async_computation.1 | async-start | bytes 2097152 | tf_op jit(solution)/shard_map/all_to_all | solution.py:370

commit v10 on v9

--- a/solution.py
+++ b/solution.py
@@ -181,11 +181,31 @@
     return jnp.concatenate(parts, axis=0)
 
 
+def symmetric_product(left_ref, right_ref):
+    half = left_ref.shape[0] // 2
+    dot = functools.partial(jnp.dot, preferred_element_type=F32)
+    return (
+        dot(left_ref[...], right_ref[:, half:]),
+        dot(left_ref[0:half, :], right_ref[:, 0:half]),
+    )
+
+
+def put_symmetric(ref, right, corner):
+    half = corner.shape[0]
+    right = right.astype(BF16)
+    ref[:, half:] = right
+    ref[0:half, 0:half] = corner.astype(BF16)
+    ref[half:, 0:half] = right[0:half, :].T
+
+
 def weights_kernel(*refs):
     gram_ref, drive_ref, own_info_ref, ordered_ref, turned_ref = refs[:5]
-    rows_refs, blended_ref, info_ref = refs[5:-8], refs[-8], refs[-7]
-    y_ref, z_ref, y_high, z_high, low, w_high = refs[-6:]
-    groups, members, _ = blended_ref.shape
+    groups = (len(refs) - 5) // 11
+    rows_refs, blended_ref = refs[5 : 4 + groups], refs[4 + groups]
+    info_refs = refs[5 + groups : 5 + 2 * groups]
+    chains = [refs[5 + 2 * groups + 9 * c : 14 + 2 * groups + 9 * c] for c in range(groups)]
+    members = gram_ref.shape[0]
+    half = members // 2
     sources = rows_refs[0].shape[0] if rows_refs else 1
     row_id = lax.broadcasted_iota(jnp.int32, (members, members), 0)
     col_id = lax.broadcasted_iota(jnp.int32, (members, members), 1)
@@ -195,16 +215,21 @@
     )
     dot = functools.partial(jnp.dot, preferred_element_type=F32)
 
-    def split(chain, value):
-        w_high[chain] = value.astype(BF16)
-        for begin in range(0, members, LANES):
+    def split(w_high, right, corner):
+        right, corner = -0.5 * right, -0.5 * corner
+        put_symmetric(w_high, right, corner)
+        for begin in range(0, half, LANES):
             block = slice(begin, begin + LANES)
-            w_high[chain, block, block] = jnp.where(eye, 0.0, value[block, block]).astype(BF16)
-        return 1.5 - 0.5 * diagonal_column(value, eye)
+            for first, part in ((0, corner), (half, right[half:, :])):
+                place = slice(first + begin, first + begin + LANES)
+                w_high[place, place] = jnp.where(eye, 0.0, part[block, block]).astype(BF16)
+        return 1.5 + jnp.concatenate(
+            [diagonal_column(corner, eye), diagonal_column(right[half:, :], eye)], axis=0
+        )
 
     grams = [gram_ref[...]] + [jnp.zeros((members, members), F32)] * (groups - 1)
     drives = [drive_ref[...]] + [jnp.zeros((1, members), F32)] * (groups - 1)
-    infos = [own_info_ref] + [info_ref.at[chain] for chain in range(1, groups)]
+    infos = [own_info_ref] + list(info_refs[1:])
     for chain in range(1, groups):
         slot_info(rows_refs[chain - 1], infos[chain])
     for chain in range(1, groups):
@@ -229,37 +254,64 @@
             grams[chain] = grams[chain] + sums[:, columns]
 
     frobenius = []
-    for chain in range(groups):
+    for chain, (y_right, y_corner, z_right, z_corner, y_high, z_high, _, _, w_high) in enumerate(
+        chains
+    ):
         shifted = identity + grams[chain] / (members - 1.0)
         squares = jnp.sum(jnp.sum(shifted * shifted, axis=0, keepdims=True), axis=1, keepdims=True)
         frobenius.append(jnp.sqrt(squares))
         current = shifted / frobenius[chain]
-        factor = split(chain, current)
-        y_high[chain] = current.astype(BF16)
-        z_ref[chain] = 1.5 * identity - 0.5 * current
-        y_ref[chain] = factor * current - 0.5 * dot(w_high[chain], y_high[chain])
-        y_high[chain], z_high[chain] = y_ref[chain].astype(BF16), z_ref[chain].astype(BF16)
+        right, corner = current[:, half:], current[0:half, 0:half]
+        factor = split(w_high, right, corner)
+        put_symmetric(y_high, right, corner)
+        z_right[...] = 1.5 * identity[:, half:] - 0.5 * right
+        z_corner[...] = 1.5 * identity[0:half, 0:half] - 0.5 * corner
+        change_right, change_corner = symmetric_product(w_high, y_high)
+        y_right[...] = factor * right + change_right
+        y_corner[...] = factor[0:half, :] * corner + change_corner
+        put_symmetric(y_high, y_right[...], y_corner[...])
+        put_symmetric(z_high, z_right[...], z_corner[...])
 
     def step(_, carry):
-        factors = [split(c, dot(z_high[c], y_high[c])) for c in range(groups)]
-        for chain in range(groups):
-            current = factors[chain] * y_ref[chain] - 0.5 * dot(w_high[chain], y_high[chain])
-            root = factors[chain] * z_ref[chain] - 0.5 * dot(w_high[chain], z_high[chain])
-            y_ref[chain], z_ref[chain] = current, root
-            y_high[chain], z_high[chain] = current.astype(BF16), root.astype(BF16)
+        factors = [
+            split(chain[8], *symmetric_product(chain[5], chain[4])) for chain in chains
+        ]
+        for factor, chain in zip(factors, chains):
+            w_high = chain[8]
+            for right, corner, high in (
+                (chain[0], chain[1], chain[4]),
+                (chain[2], chain[3], chain[5]),
+            ):
+                change_right, change_corner = symmetric_product(w_high, high)
+                new_right = factor * right[...] + change_right
+                new_corner = factor[0:half, :] * corner[...] + change_corner
+                right[...], corner[...] = new_right, new_corner
+                put_symmetric(high, new_right, new_corner)
         return carry
 
-    lax.fori_loop(1, NS_STEPS - 1, step, 0, unroll=True)
-    for chain in range(groups):
-        low[2 * chain] = (y_ref[chain] - y_high[chain].astype(F32)).astype(BF16)
-        low[2 * chain + 1] = (z_ref[chain] - z_high[chain].astype(F32)).astype(BF16)
+    lax.fori_loop(1, NS_STEPS - 1, step, 0)
     factors = []
-    for chain in range(groups):
-        small = dot(z_high[chain], low[2 * chain]) + dot(low[2 * chain + 1], y_high[chain])
-        factors.append(split(chain, dot(z_high[chain], y_high[chain]) + small))
-    for chain in range(groups):
-        root = factors[chain] * z_ref[chain] - 0.5 * dot(w_high[chain], z_high[chain])
-        root = root / jnp.sqrt(frobenius[chain])
+    for y_right, y_corner, z_right, z_corner, y_high, z_high, y_low, z_low, w_high in chains:
+        for right, corner, high, low in (
+            (y_right, y_corner, y_high, y_low),
+            (z_right, z_corner, z_high, z_low),
+        ):
+            put_symmetric(
+                low,
+                right[...] - high[:, half:].astype(F32),
+                corner[...] - high[0:half, 0:half].astype(F32),
+            )
+        large = symmetric_product(z_high, y_high)
+        small = zip(symmetric_product(z_high, y_low), symmetric_product(z_low, y_high))
+        factors.append(
+            split(w_high, *[first + (one + two) for first, (one, two) in zip(large, small)])
+        )
+    for chain, (_, _, z_right, z_corner, _, z_high, _, _, w_high) in enumerate(chains):
+        right, corner = symmetric_product(w_high, z_high)
+        right = factors[chain] * z_right[...] + right
+        corner = factors[chain][0:half, :] * z_corner[...] + corner
+        left = jnp.concatenate([corner, right[0:half, :].T], axis=0)
+        root = jnp.concatenate([left, right], axis=1) / jnp.sqrt(frobenius[chain])
         inner = jnp.sum(root * diagonal_column(drives[chain], eye), axis=0, keepdims=True)
         mean_weight = jnp.sum(root * diagonal_column(inner, eye), axis=0, keepdims=True)
         blended_ref[chain] = (root + mean_weight / (members - 1.0)).astype(BF16)
@@ -267,20 +319,13 @@
 
 def patch_weights(own, other_rows):
     groups, members = len(other_rows) + 1, own[0].shape[0]
-    whole = pltpu.VMEM((groups, members, members), F32)
-    half = pltpu.VMEM((groups, members, members), BF16)
+    half = members // 2
+    right, corner = pltpu.VMEM((members, half), F32), pltpu.VMEM((half, half), F32)
+    chain = [right, corner] * 2 + [pltpu.VMEM((members, members), BF16)] * 5
     return pl.pallas_call(
         weights_kernel,
         out_shape=jax.ShapeDtypeStruct((groups, members, members), BF16),
-        scratch_shapes=[
-            pltpu.VMEM((groups, LANES, LANES), F32),
-            whole,
-            whole,
-            half,
-            half,
-            pltpu.VMEM((2 * groups, members, members), BF16),
-            half,
-        ],
+        scratch_shapes=[pltpu.VMEM((LANES, LANES), F32)] * groups + chain * groups,
         compiler_params=pltpu.CompilerParams(vmem_limit_bytes=(8 + 10 * groups) * MEBI),
         cost_estimate=pl.CostEstimate(
             flops=80 * groups * members * members * members,

time: 122 us -> 120 us (0.984)
  Pallas kernels: 21.3 us -> 19.7 us
    pallas_call x1, Pallas kernels: 13.7 us -> 12.1 us  [patch_weights(): pl.pallas_call(weights_kernel, out_shape=jax.ShapeDtypeStruct((groups, me...]
  transfers between devices with their start and end apart: 3 -> 3, of which waited for: 2 -> 2; matrix products, arithmetic and copies ran while one was open for 0% -> 0% of each run, Pallas kernels for 13% -> 12%
where the time goes in v10:
time: 120 us
  blocking collectives  55 us (46%)
  waiting for transfers between devices  29 us (24%)
  Pallas kernels  19.7 us (16%)
  starting transfers between devices  14.5 us (12%)
  local copies, waits for them, and re-layouts  1.59 us (1%)
    all_to_all x1, blocking collectives, exchange(): return lax.all_to_all(blocks, axes, split_axis=0, concat_axis=0, tiled=True)  55 us
    all_to_all x2, waiting for transfers between devices, exchange(): return lax.all_to_all(blocks, axes, split_axis=0, concat_axis=0, tiled=True)  16.6 us
    all_to_all x2, starting transfers between devices, exchange(): return lax.all_to_all(blocks, axes, split_axis=0, concat_axis=0, tiled=True)  13 us
    ppermute x1, waiting for transfers between devices, swap_shares(): lax.ppermute(own, 'boot', [(g, (g - turn) % groups) for g in range(groups)])  12.4 us
    pallas_call x1, Pallas kernels, patch_weights(): pl.pallas_call(weights_kernel, out_shape=jax.ShapeDtypeStruct((groups, me...  12.1 us
    pallas_call x1, Pallas kernels, pack(): pl.pallas_call(functools.partial(pack_kernel, groups), out_shape=jax.Shap...  2.85 us
  transfers between devices with their start and end apart: 3, of which 2 were waited for; matrix products, arithmetic and copies ran while one was open for 0% of the time, Pallas kernels for 12%

profile of v10, /device:TPU:0, one launch (start us, length us, event | category | flops | bytes accessed | tf_op | source)
XLA Modules:
  0.0 119.9 jit_solution(9313921454502163633)
XLA Ops:
  0.0 2.8 %pack_rows.1 = bf16[16,8,3200]{2,1,0:T(8,128)(2,1)} custom-call(s32[2,384]{1,0:T(2,128)} %bitcast.8, s32[2,384]{1,0:T(2,128)} %bitcast.9, s32[384]{0:T(512)} %refs_2_.1, f32[384]{0:T(512)} %refs_3_.1, bf16[384]{0:T(512)(128)(2,1)} %refs_4_.1, bf16[384,512]{1,0:T(8,128)(2,1)} %refs_5_.1), custom_call_target="tpu_custom_call" | custom-call | flops 301989888 | bytes 1179648 | tf_op jit(solution)/shard_map/pack_rows/pallas_call | solution.py:92
  2.9 7.4 %all-to-all-start = ((bf16[16,8,3200]{2,1,0:T(8,128)(2,1)}), bf16[16,8,3200]{2,1,0:T(8,128)(2,1)S(1)}, u32[]{:S(2)}, u32[]{:S(2)}) async-start(bf16[16,8,3200]{2,1,0:T(8,128)(2,1)} %pack_rows.1), calls=%async_computation | async-start | bytes 1638400 | tf_op jit(solution)/shard_map/all_to_all | solution.py:415
  10.3 0.0 copy-start
  10.3 1.6 %copy-done = bf16[32,32768]{1,0:T(8,128)(2,1)S(1)} copy-done((bf16[32,32768]{1,0:T(8,128)(2,1)S(1)}, bf16[32,32768]{1,0:T(8,128)(2,1)}, u32[]{:S(2)}) %copy-start) | copy-done | bytes 2097176
  11.8 1.0 cut_share.1
  12.9 16.6 %all-to-all-done.rows_ref = bf16[16,8,3200]{2,1,0:T(8,128)(2,1)S(1)} async-done(((bf16[16,8,3200]{2,1,0:T(8,128)(2,1)}), bf16[16,8,3200]{2,1,0:T(8,128)(2,1)S(1)}, u32[]{:S(2)}, u32[]{:S(2)}) %all-to-all-start) | async-done | bytes 819232 | tf_op jit(solution)/shard_map/all_to_all | solution.py:415
  29.5 1.5 %collective-permute-start = (bf16[16,8,3200]{2,1,0:T(8,128)(2,1)S(1)}, bf16[16,8,3200]{2,1,0:T(8,128)(2,1)S(1)}, u32[]{:S(2)}, u32[]{:S(2)}) collective-permute-start(bf16[16,8,3200]{2,1,0:T(8,128)(2,1)S(1)} %all-to-all-done.rows_ref), channel_id=1, source_target_pairs={{0,16},{16,0},{1,17},{17,1},{2,18},{18,2},{3,19},{19,3},{4,20},{20... | collective-permute-start | bytes 2457608 | tf_op jit(solution)/shard_map/ppermute | solution.py:421
  31.0 5.7 %all-to-all-start.1 = ((bf16[16,32,1024]{2,1,0:T(8,128)(2,1)}), bf16[16,32,1024]{2,1,0:T(8,128)(2,1)S(1)}, u32[]{:S(2)}, u32[]{:S(2)}) async-start(bf16[16,32,1024]{2,1,0:T(8,128)(2,1)} %cut_share.1), calls=%async_computation.1 | async-start | bytes 2097152 | tf_op jit(solution)/shard_map/all_to_all | solution.py:415
  36.6 0.9 own_gram.1
  37.6 12.4 %collective-permute-done.refs_5_ = bf16[16,8,3200]{2,1,0:T(8,128)(2,1)S(1)} collective-permute-done((bf16[16,8,3200]{2,1,0:T(8,128)(2,1)S(1)}, bf16[16,8,3200]{2,1,0:T(8,128)(2,1)S(1)}, u32[]{:S(2)}, u32[]{:S(2)}) %collective-permute-start) | collective-permute-done | bytes 819232 | tf_op jit(solution)/shard_map/ppermute | solution.py:421
  49.9 12.1 %patch_weights.1.blended_ref = bf16[2,512,512]{2,1,0:T(8,128)(2,1)S(1)} custom-call(f32[512,512]{1,0:T(8,128)S(1)} %get-tuple-element.13.refs_0_, f32[1,512]{1,0:T(1,128)S(1)} %get-tuple-element.14.refs_1_, f32[128,128]{1,0:T(8,128)S(1)} %get-tuple-element.15.refs_2_, bf16[768,512]{1,0:T(8,128)(2,1)S(1)} %get-tuple-element.16.refs_3_, ...), custom_call_target="tpu_custom_call" | custom-call | flops 21474836480 | bytes 2097152 | tf_op jit(solution)/shard_map/patch_weights/pallas_call | solution.py:325
  62.0 0.0 all-to-all-done.1
  62.0 1.4 %update_points.1 = bf16[2,512,1024]{2,1,0:T(8,128)(2,1)S(1)} custom-call(bf16[2,512,512]{2,1,0:T(8,128)(2,1)S(1)} %patch_weights.1.blended_ref, bf16[512,1024]{1,0:T(8,128)(2,1)S(1)} %bitcast.7), custom_call_target="tpu_custom_call" | custom-call | flops 1073741824 | bytes 3145728 | tf_op jit(solution)/shard_map/update_points/pallas_call | solution.py:357
  63.4 55.0 %all_to_all.15 = bf16[32,32,1024]{2,1,0:T(8,128)(2,1)S(1)} all-to-all(bf16[32,32,1024]{2,1,0:T(8,128)(2,1)S(1)} %bitcast.5), channel_id=1, replica_groups=mesh['boot'=2,'space'=16] {'boot','space'}, dimensions={0} | all-to-all | bytes 4194304 | tf_op jit(solution)/shard_map/all_to_all | solution.py:415
  118.4 1.5 %place_pieces.1 = bf16[32,32768]{1,0:T(8,128)(2,1)} custom-call(bf16[2,16,32,1024]{3,2,1,0:T(8,128)(2,1)S(1)} %bitcast.6), custom_call_target="tpu_custom_call" | custom-call | bytes 4194304 | tf_op jit(solution)/shard_map/place_pieces/pallas_call | solution.py:403
Async XLA Ops:
  2.9 26.6 %all-to-all-start = ((bf16[16,8,3200]{2,1,0:T(8,128)(2,1)}), bf16[16,8,3200]{2,1,0:T(8,128)(2,1)S(1)}, u32[]{:S(2)}, u32[]{:S(2)}) async-start(bf16[16,8,3200]{2,1,0:T(8,128)(2,1)} %pack_rows.1), calls=%async_computation | async-start | bytes 1638400 | tf_op jit(solution)/shard_map/all_to_all | solution.py:415
  10.3 1.6 %copy-start = (bf16[32,32768]{1,0:T(8,128)(2,1)S(1)}, bf16[32,32768]{1,0:T(8,128)(2,1)}, u32[]{:S(2)}) copy-start(bf16[32,32768]{1,0:T(8,128)(2,1)} %states_ref.1) | copy-start | bytes 6291460
  29.5 20.4 %collective-permute-start = (bf16[16,8,3200]{2,1,0:T(8,128)(2,1)S(1)}, bf16[16,8,3200]{2,1,0:T(8,128)(2,1)S(1)}, u32[]{:S(2)}, u32[]{:S(2)}) collective-permute-start(bf16[16,8,3200]{2,1,0:T(8,128)(2,1)S(1)} %all-to-all-done.rows_ref), channel_id=1, source_target_pairs={{0,16},{16,0},{1,17},{17,1},{2,18},{18,2},{3,19},{19,3},{4,20},{20... | collective-permute-start | bytes 2457608 | tf_op jit(solution)/shard_map/ppermute | solution.py:421
  31.0 31.0 %all-to-all-start.1 = ((bf16[16,32,1024]{2,1,0:T(8,128)(2,1)}), bf16[16,32,1024]{2,1,0:T(8,128)(2,1)S(1)}, u32[]{:S(2)}, u32[]{:S(2)}) async-start(bf16[16,32,1024]{2,1,0:T(8,128)(2,1)} %cut_share.1), calls=%async_computation.1 | async-start | bytes 2097152 | tf_op jit(solution)/shard_map/all_to_all | solution.py:415

commit v11 on v10

--- a/solution.py
+++ b/solution.py
@@ -216,15 +216,21 @@
     dot = functools.partial(jnp.dot, preferred_element_type=F32)
 
     def split(w_high, right, corner):
-        right, corner = -0.5 * right, -0.5 * corner
         put_symmetric(w_high, right, corner)
-        for begin in range(0, half, LANES):
-            block = slice(begin, begin + LANES)
-            for first, part in ((0, corner), (half, right[half:, :])):
+        diagonal = []
+        for first, part in ((0, corner), (half, right[half:, :])):
+            for begin in range(0, half, LANES):
+                block = part[begin : begin + LANES, begin : begin + LANES]
                 place = slice(first + begin, first + begin + LANES)
-                w_high[place, place] = jnp.where(eye, 0.0, part[block, block]).astype(BF16)
-        return 1.5 + jnp.concatenate(
-            [diagonal_column(corner, eye), diagonal_column(right[half:, :], eye)], axis=0
+                w_high[place, place] = jnp.where(eye, 0.0, block).astype(BF16)
+                diagonal.append(jnp.sum(jnp.where(eye, block, 0.0), axis=0, keepdims=True))
+        return 1.5 + jnp.concatenate(diagonal, axis=1)
+
+    def advance(factor, w_high, right, corner, high):
+        change_right, change_corner = symmetric_product(high, w_high)
+        return (
+            factor[:, half:] * right + change_right,
+            factor[:, 0:half] * corner + change_corner,
         )
 
     grams = [gram_ref[...]] + [jnp.zeros((members, members), F32)] * (groups - 1)
@@ -262,13 +268,11 @@
         frobenius.append(jnp.sqrt(squares))
         current = shifted / frobenius[chain]
         right, corner = current[:, half:], current[0:half, 0:half]
-        factor = split(w_high, right, corner)
+        factor = split(w_high, -0.5 * right, -0.5 * corner)
         put_symmetric(y_high, right, corner)
-        z_right[...] = 1.5 * identity[:, half:] - 0.5 * right
-        z_corner[...] = 1.5 * identity[0:half, 0:half] - 0.5 * corner
-        change_right, change_corner = symmetric_product(w_high, y_high)
-        y_right[...] = factor * right + change_right
-        y_corner[...] = factor[0:half, :] * corner + change_corner
+        y_right[...], y_corner[...] = advance(factor, w_high, right, corner, y_high)
+        z_right[...] = 0.25 * right - 0.75 * identity[:, half:]
+        z_corner[...] = 0.25 * corner - 0.75 * identity[0:half, 0:half]
         put_symmetric(y_high, y_right[...], y_corner[...])
         put_symmetric(z_high, z_right[...], z_corner[...])
 
@@ -277,14 +281,11 @@
             split(chain[8], *symmetric_product(chain[5], chain[4])) for chain in chains
         ]
         for factor, chain in zip(factors, chains):
-            w_high = chain[8]
             for right, corner, high in (
                 (chain[0], chain[1], chain[4]),
                 (chain[2], chain[3], chain[5]),
             ):
-                change_right, change_corner = symmetric_product(w_high, high)
-                new_right = factor * right[...] + change_right
-                new_corner = factor[0:half, :] * corner[...] + change_corner
+                new_right, new_corner = advance(factor, chain[8], right[...], corner[...], high)
                 right[...], corner[...] = new_right, new_corner
                 put_symmetric(high, new_right, new_corner)
         return carry
@@ -307,11 +308,9 @@
             split(w_high, *[first + (one + two) for first, (one, two) in zip(large, small)])
         )
     for chain, (_, _, z_right, z_corner, _, z_high, _, _, w_high) in enumerate(chains):
-        right, corner = symmetric_product(w_high, z_high)
-        right = factors[chain] * z_right[...] + right
-        corner = factors[chain][0:half, :] * z_corner[...] + corner
+        right, corner = advance(factors[chain], w_high, z_right[...], z_corner[...], z_high)
         left = jnp.concatenate([corner, right[0:half, :].T], axis=0)
-        root = jnp.concatenate([left, right], axis=1) / jnp.sqrt(frobenius[chain])
+        root = jnp.concatenate([left, right], axis=1) * (-2.0 / jnp.sqrt(frobenius[chain]))
         inner = jnp.sum(root * diagonal_column(drives[chain], eye), axis=0, keepdims=True)
         mean_weight = jnp.sum(root * diagonal_column(inner, eye), axis=0, keepdims=True)
         blended_ref[chain] = (root + mean_weight / (members - 1.0)).astype(BF16)
@@ -389,12 +388,23 @@
     )(states)
 
 
-def place_kernel(pieces_ref, whole_ref):
+def place_kernel(pieces_ref, whole_ref, sems):
     groups, patches, _, share = pieces_ref.shape
-    for patch in range(patches):
-        for group in range(groups):
+    copies = []
+    for group in range(groups):
+        for patch in range(patches):
             begin = (patch * groups + group) * share
-            whole_ref[:, begin : begin + share] = pieces_ref[group, patch]
+            copies.append(
+                pltpu.make_async_copy(
+                    pieces_ref.at[group, patch],
+                    whole_ref.at[:, begin : begin + share],
+                    sems.at[group, patch],
+                )
+            )
+    for copy in copies:
+        copy.start()
+    for copy in copies:
+        copy.wait()
 
 
 def place_pieces(pieces):
@@ -402,7 +412,10 @@
     points = groups * patches * share
     return pl.pallas_call(
         place_kernel,
+        in_specs=[pl.BlockSpec(memory_space=pltpu.VMEM)],
+        out_specs=pl.BlockSpec(memory_space=pl.ANY),
         out_shape=jax.ShapeDtypeStruct((own_members, points), BF16),
+        scratch_shapes=[pltpu.SemaphoreType.DMA((groups, patches))],
         compiler_params=pltpu.CompilerParams(vmem_limit_bytes=16 * MEBI),
         cost_estimate=pl.CostEstimate(
             flops=0, bytes_accessed=4 * own_members * points, transcendentals=0

time: 120 us -> 120 us (level)
  transfers between devices with their start and end apart: 3 -> 3, of which waited for: 2 -> 2; matrix products, arithmetic and copies ran while one was open for 0% -> 0% of each run, Pallas kernels for 12% -> 11%
where the time goes in v11:
time: 120 us; the launch traced here: 119 us
  blocking collectives  55 us (46%)
  waiting for transfers between devices  29 us (24%)
  Pallas kernels  19.2 us (16%)
  starting transfers between devices  14.5 us (12%)
  local copies, waits for them, and re-layouts  1.59 us (1%)
    all_to_all x1, blocking collectives, exchange(): return lax.all_to_all(blocks, axes, split_axis=0, concat_axis=0, tiled=True)  55 us
    all_to_all x2, waiting for transfers between devices, exchange(): return lax.all_to_all(blocks, axes, split_axis=0, concat_axis=0, tiled=True)  16.6 us
    all_to_all x2, starting transfers between devices, exchange(): return lax.all_to_all(blocks, axes, split_axis=0, concat_axis=0, tiled=True)  13 us
    ppermute x1, waiting for transfers between devices, swap_shares(): lax.ppermute(own, 'boot', [(g, (g - turn) % groups) for g in range(groups)])  12.4 us
    pallas_call x1, Pallas kernels, patch_weights(): pl.pallas_call(weights_kernel, out_shape=jax.ShapeDtypeStruct((groups, me...  11.5 us
    pallas_call x1, Pallas kernels, pack(): pl.pallas_call(functools.partial(pack_kernel, groups), out_shape=jax.Shap...  2.85 us
  transfers between devices with their start and end apart: 3, of which 2 were waited for; matrix products, arithmetic and copies ran while one was open for 0% of the time, Pallas kernels for 11%

profile of v11, /device:TPU:0, one launch (start us, length us, event | category | flops | bytes accessed | tf_op | source)
XLA Modules:
  0.0 119.4 jit_solution(16810236915289730937)
XLA Ops:
  0.0 2.8 %pack_rows.1 = bf16[16,8,3200]{2,1,0:T(8,128)(2,1)} custom-call(s32[2,384]{1,0:T(2,128)} %bitcast.8, s32[2,384]{1,0:T(2,128)} %bitcast.9, s32[384]{0:T(512)} %refs_2_.1, f32[384]{0:T(512)} %refs_3_.1, bf16[384]{0:T(512)(128)(2,1)} %refs_4_.1, bf16[384,512]{1,0:T(8,128)(2,1)} %refs_5_.1), custom_call_target="tpu_custom_call" | custom-call | flops 301989888 | bytes 1179648 | tf_op jit(solution)/shard_map/pack_rows/pallas_call | solution.py:92
  2.9 7.4 %all-to-all-start = ((bf16[16,8,3200]{2,1,0:T(8,128)(2,1)}), bf16[16,8,3200]{2,1,0:T(8,128)(2,1)S(1)}, u32[]{:S(2)}, u32[]{:S(2)}) async-start(bf16[16,8,3200]{2,1,0:T(8,128)(2,1)} %pack_rows.1), calls=%async_computation | async-start | bytes 1638400 | tf_op jit(solution)/shard_map/all_to_all | solution.py:428
  10.3 0.0 copy-start
  10.3 1.6 %copy-done = bf16[32,32768]{1,0:T(8,128)(2,1)S(1)} copy-done((bf16[32,32768]{1,0:T(8,128)(2,1)S(1)}, bf16[32,32768]{1,0:T(8,128)(2,1)}, u32[]{:S(2)}) %copy-start) | copy-done | bytes 2097176
  11.8 1.0 cut_share.1
  12.9 16.6 %all-to-all-done.rows_ref = bf16[16,8,3200]{2,1,0:T(8,128)(2,1)S(1)} async-done(((bf16[16,8,3200]{2,1,0:T(8,128)(2,1)}), bf16[16,8,3200]{2,1,0:T(8,128)(2,1)S(1)}, u32[]{:S(2)}, u32[]{:S(2)}) %all-to-all-start) | async-done | bytes 819232 | tf_op jit(solution)/shard_map/all_to_all | solution.py:428
  29.5 1.5 %collective-permute-start = (bf16[16,8,3200]{2,1,0:T(8,128)(2,1)S(1)}, bf16[16,8,3200]{2,1,0:T(8,128)(2,1)S(1)}, u32[]{:S(2)}, u32[]{:S(2)}) collective-permute-start(bf16[16,8,3200]{2,1,0:T(8,128)(2,1)S(1)} %all-to-all-done.rows_ref), channel_id=1, source_target_pairs={{0,16},{16,0},{1,17},{17,1},{2,18},{18,2},{3,19},{19,3},{4,20},{20... | collective-permute-start | bytes 2457608 | tf_op jit(solution)/shard_map/ppermute | solution.py:434
  31.0 5.7 %all-to-all-start.1 = ((bf16[16,32,1024]{2,1,0:T(8,128)(2,1)}), bf16[16,32,1024]{2,1,0:T(8,128)(2,1)S(1)}, u32[]{:S(2)}, u32[]{:S(2)}) async-start(bf16[16,32,1024]{2,1,0:T(8,128)(2,1)} %cut_share.1), calls=%async_computation.1 | async-start | bytes 2097152 | tf_op jit(solution)/shard_map/all_to_all | solution.py:428
  36.6 0.9 own_gram.1
  37.6 12.4 %collective-permute-done.refs_5_ = bf16[16,8,3200]{2,1,0:T(8,128)(2,1)S(1)} collective-permute-done((bf16[16,8,3200]{2,1,0:T(8,128)(2,1)S(1)}, bf16[16,8,3200]{2,1,0:T(8,128)(2,1)S(1)}, u32[]{:S(2)}, u32[]{:S(2)}) %collective-permute-start) | collective-permute-done | bytes 819232 | tf_op jit(solution)/shard_map/ppermute | solution.py:434
  49.9 11.5 %patch_weights.1.blended_ref = bf16[2,512,512]{2,1,0:T(8,128)(2,1)S(1)} custom-call(f32[512,512]{1,0:T(8,128)S(1)} %get-tuple-element.13.refs_0_, f32[1,512]{1,0:T(1,128)S(1)} %get-tuple-element.14.refs_1_, f32[128,128]{1,0:T(8,128)S(1)} %get-tuple-element.15.refs_2_, bf16[768,512]{1,0:T(8,128)(2,1)S(1)} %get-tuple-element.16.refs_3_, ...), custom_call_target="tpu_custom_call" | custom-call | flops 21474836480 | bytes 2097152 | tf_op jit(solution)/shard_map/patch_weights/pallas_call | solution.py:324
  61.4 0.0 all-to-all-done.1
  61.4 1.4 %update_points.1 = bf16[2,512,1024]{2,1,0:T(8,128)(2,1)S(1)} custom-call(bf16[2,512,512]{2,1,0:T(8,128)(2,1)S(1)} %patch_weights.1.blended_ref, bf16[512,1024]{1,0:T(8,128)(2,1)S(1)} %bitcast.7), custom_call_target="tpu_custom_call" | custom-call | flops 1073741824 | bytes 3145728 | tf_op jit(solution)/shard_map/update_points/pallas_call | solution.py:356
  62.8 55.0 %all_to_all.15 = bf16[32,32,1024]{2,1,0:T(8,128)(2,1)S(1)} all-to-all(bf16[32,32,1024]{2,1,0:T(8,128)(2,1)S(1)} %bitcast.5), channel_id=1, replica_groups=mesh['boot'=2,'space'=16] {'boot','space'}, dimensions={0} | all-to-all | bytes 4194304 | tf_op jit(solution)/shard_map/all_to_all | solution.py:428
  117.8 1.6 %place_pieces.1 = bf16[32,32768]{1,0:T(8,128)(2,1)} custom-call(bf16[2,16,32,1024]{3,2,1,0:T(8,128)(2,1)S(1)} %bitcast.6), custom_call_target="tpu_custom_call" | custom-call | bytes 4194304 | tf_op jit(solution)/shard_map/place_pieces/pallas_call | solution.py:413
Async XLA Ops:
  2.9 26.6 %all-to-all-start = ((bf16[16,8,3200]{2,1,0:T(8,128)(2,1)}), bf16[16,8,3200]{2,1,0:T(8,128)(2,1)S(1)}, u32[]{:S(2)}, u32[]{:S(2)}) async-start(bf16[16,8,3200]{2,1,0:T(8,128)(2,1)} %pack_rows.1), calls=%async_computation | async-start | bytes 1638400 | tf_op jit(solution)/shard_map/all_to_all | solution.py:428
  10.3 1.6 %copy-start = (bf16[32,32768]{1,0:T(8,128)(2,1)S(1)}, bf16[32,32768]{1,0:T(8,128)(2,1)}, u32[]{:S(2)}) copy-start(bf16[32,32768]{1,0:T(8,128)(2,1)} %states_ref.1) | copy-start | bytes 6291460
  29.5 20.4 %collective-permute-start = (bf16[16,8,3200]{2,1,0:T(8,128)(2,1)S(1)}, bf16[16,8,3200]{2,1,0:T(8,128)(2,1)S(1)}, u32[]{:S(2)}, u32[]{:S(2)}) collective-permute-start(bf16[16,8,3200]{2,1,0:T(8,128)(2,1)S(1)} %all-to-all-done.rows_ref), channel_id=1, source_target_pairs={{0,16},{16,0},{1,17},{17,1},{2,18},{18,2},{3,19},{19,3},{4,20},{20... | collective-permute-start | bytes 2457608 | tf_op jit(solution)/shard_map/ppermute | solution.py:434
  31.0 30.4 %all-to-all-start.1 = ((bf16[16,32,1024]{2,1,0:T(8,128)(2,1)}), bf16[16,32,1024]{2,1,0:T(8,128)(2,1)S(1)}, u32[]{:S(2)}, u32[]{:S(2)}) async-start(bf16[16,32,1024]{2,1,0:T(8,128)(2,1)} %cut_share.1), calls=%async_computation.1 | async-start | bytes 2097152 | tf_op jit(solution)/shard_map/all_to_all | solution.py:428

commit v12 on v11

--- a/solution.py
+++ b/solution.py
@@ -17,22 +17,19 @@
 
 def pack_kernel(groups, *refs):
     sources, slots_ref, fetched = refs[:6], refs[6], refs[7:13]
-    info_ref, sems = refs[13:]
-    run_copies(
-        [
-            pltpu.make_async_copy(source, target, sems.at[i])
-            for i, (source, target) in enumerate(zip(sources, fetched))
-        ]
-    )
+    block_ref, tail_ref, info_ref, sems = refs[13:]
+    copies = [
+        pltpu.make_async_copy(source, target, sems.at[i])
+        for i, (source, target) in enumerate(zip(sources, fetched))
+    ]
+    for copy in copies:
+        copy.start()
+    for copy in copies[:-1]:
+        copy.wait()
     targets_ref, local_ref, mult_ref, prec_ref, dep_ref, rows_ref = fetched
-    patches = slots_ref.shape[0]
+    patches, _, width = block_ref.shape
     count, members = rows_ref.shape
-    share = (slots_ref.shape[2] - LANES) // members * ROWS
-    mult = mult_ref[...].reshape(1, count).astype(F32)
-    prec = prec_ref[...].reshape(1, count)
-    weight = local_ref[...].astype(F32) / 1024.0 * (mult * prec)
-    weight = weight.astype(BF16).astype(F32)
-    dep = dep_ref[...].astype(F32).reshape(1, count)
+    share = width // members * ROWS
     patch_id = lax.broadcasted_iota(jnp.int32, (patches, count), 0)
     first = patch_id == targets_ref[0:1, :]
     second = patch_id == targets_ref[1:2, :]
@@ -44,6 +41,27 @@
         named.astype(F32).astype(BF16), earlier.astype(F32).astype(BF16), preferred_element_type=F32
     )
     rank = jnp.where(named, rank, -1.0)
+
+    begin = lax.axis_index("boot") * share
+    own_id = (lax.broadcasted_iota(jnp.int32, (share, count), 0) + begin).astype(F32)
+    picks = [
+        jnp.where(own_id == rank[patch : patch + 1, :], 1.0, 0.0) for patch in range(patches)
+    ]
+    picks = jnp.concatenate(picks, axis=0).astype(BF16)
+    copies[-1].wait()
+    picked = jnp.dot(picks, rows_ref[...], preferred_element_type=F32)
+    for patch in range(patches):
+        place = patch * share
+        blocks = [picked[place + i : place + i + ROWS, :] for i in range(0, share, ROWS)]
+        block_ref[patch] = jnp.concatenate(blocks, axis=1).astype(BF16)
+    blocks_out = pltpu.make_async_copy(block_ref, slots_ref.at[:, :, 0:width], sems.at[6])
+    blocks_out.start()
+
+    mult = mult_ref[...].reshape(1, count).astype(F32)
+    prec = prec_ref[...].reshape(1, count)
+    weight = local_ref[...].astype(F32) / 1024.0 * (mult * prec)
+    weight = weight.astype(BF16).astype(F32)
+    dep = dep_ref[...].astype(F32).reshape(1, count)
     by_patch = jnp.where(first, weight[0:1, :], jnp.where(second, weight[1:2, :], 0.0))
     slot_id = lax.broadcasted_iota(jnp.int32, (groups * share, count), 0).astype(F32)
     lane = lax.broadcasted_iota(jnp.int32, (groups * share, LANES), 1)
@@ -59,42 +77,36 @@
     info_ref[...] = jnp.zeros((LANES, LANES), F32)
     info_ref[0 : groups * share, :] = info
     info = info_ref[...].T
-    begin = lax.axis_index("boot") * share
-    own_id = (lax.broadcasted_iota(jnp.int32, (share, count), 0) + begin).astype(F32)
     tail_id = lax.broadcasted_iota(jnp.int32, (ROWS, LANES), 0)
-    picks = [
-        jnp.where(own_id == rank[patch : patch + 1, :], 1.0, 0.0) for patch in range(patches)
-    ]
-    picked = jnp.dot(
-        jnp.concatenate(picks, axis=0).astype(BF16), rows_ref[...], preferred_element_type=F32
-    )
     for patch in range(patches):
-        first = patch * share
-        blocks = [picked[first + i : first + i + ROWS, :] for i in range(0, share, ROWS)]
         tail = jnp.where(
             tail_id == 0,
             info[patch : patch + 1, :],
             jnp.where(tail_id == 1, info[patches + patch : patches + patch + 1, :], 0.0),
         )
-        slots_ref[patch] = jnp.concatenate(blocks + [tail], axis=1).astype(BF16)
-
-
-def run_copies(copies):
-    for copy in copies:
-        copy.start()
-    for copy in copies:
-        copy.wait()
+        tail_ref[patch] = tail.astype(BF16)
+    tails_out = pltpu.make_async_copy(tail_ref, slots_ref.at[:, :, width:], sems.at[7])
+    tails_out.start()
+    blocks_out.wait()
+    tails_out.wait()
 
 
 def pack(targets, local, mult, prec, dep, rows, patches, share, groups):
     count, members = rows.shape
     operands = (targets.T, local.T, mult, prec, dep, rows)
+    width = share // ROWS * members
     return pl.pallas_call(
         functools.partial(pack_kernel, groups),
-        out_shape=jax.ShapeDtypeStruct((patches, ROWS, share // ROWS * members + LANES), BF16),
+        out_shape=jax.ShapeDtypeStruct((patches, ROWS, width + LANES), BF16),
         in_specs=[pl.BlockSpec(memory_space=pl.ANY)] * len(operands),
+        out_specs=pl.BlockSpec(memory_space=pl.ANY),
         scratch_shapes=[pltpu.VMEM(operand.shape, operand.dtype) for operand in operands]
-        + [pltpu.VMEM((LANES, LANES), F32), pltpu.SemaphoreType.DMA((len(operands),))],
+        + [
+            pltpu.VMEM((patches, ROWS, width), BF16),
+            pltpu.VMEM((patches, ROWS, LANES), BF16),
+            pltpu.VMEM((LANES, LANES), F32),
+            pltpu.SemaphoreType.DMA((len(operands) + 2,)),
+        ],
         compiler_params=pltpu.CompilerParams(vmem_limit_bytes=64 * MEBI),
         cost_estimate=pl.CostEstimate(
             flops=2 * patches * share * count * members,
@@ -139,14 +151,16 @@
     return jnp.concatenate(blocks, axis=0).astype(BF16), drive
 
 
-def gram_kernel(rows_ref, gram_ref, drive_ref, info_ref, ordered_ref, turned_ref):
-    members = gram_ref.shape[0]
+def gram_kernel(rows_ref, right_ref, corner_ref, drive_ref, info_ref, ordered_ref, turned_ref):
+    members, half = right_ref.shape
     slot_info(rows_ref, info_ref)
     rows = slot_rows(rows_ref, members)
     ordered_ref[...] = rows.astype(BF16)
     turned_ref[...] = rows.T.astype(BF16)
     scaled, drive_ref[...] = scaled_rows(rows, info_ref, 0, rows_ref.shape[0])
-    gram_ref[...] = jnp.dot(turned_ref[...], scaled, preferred_element_type=F32)
+    dot = functools.partial(jnp.dot, preferred_element_type=F32)
+    right_ref[...] = dot(turned_ref[...], scaled[:, half:])
+    corner_ref[...] = dot(turned_ref[0:half, :], scaled[:, 0:half])
 
 
 def own_gram(rows, members):
@@ -155,7 +169,8 @@
     return pl.pallas_call(
         gram_kernel,
         out_shape=(
-            jax.ShapeDtypeStruct((members, members), F32),
+            jax.ShapeDtypeStruct((members, members // 2), F32),
+            jax.ShapeDtypeStruct((members // 2, members // 2), F32),
             jax.ShapeDtypeStruct((1, members), F32),
             jax.ShapeDtypeStruct((LANES, LANES), F32),
             jax.ShapeDtypeStruct((slots, members), BF16),
@@ -199,13 +214,12 @@
 
 
 def weights_kernel(*refs):
-    gram_ref, drive_ref, own_info_ref, ordered_ref, turned_ref = refs[:5]
-    groups = (len(refs) - 5) // 11
-    rows_refs, blended_ref = refs[5 : 4 + groups], refs[4 + groups]
-    info_refs = refs[5 + groups : 5 + 2 * groups]
-    chains = [refs[5 + 2 * groups + 9 * c : 14 + 2 * groups + 9 * c] for c in range(groups)]
-    members = gram_ref.shape[0]
-    half = members // 2
+    right_ref, corner_ref, drive_ref, own_info_ref, ordered_ref, turned_ref = refs[:6]
+    groups = (len(refs) - 6) // 11
+    rows_refs, blended_ref = refs[6 : 5 + groups], refs[5 + groups]
+    info_refs = refs[6 + groups : 6 + 2 * groups]
+    chains = [refs[6 + 2 * groups + 9 * c : 15 + 2 * groups + 9 * c] for c in range(groups)]
+    members, half = right_ref.shape
     sources = rows_refs[0].shape[0] if rows_refs else 1
     row_id = lax.broadcasted_iota(jnp.int32, (members, members), 0)
     col_id = lax.broadcasted_iota(jnp.int32, (members, members), 1)
@@ -233,41 +247,34 @@
             factor[:, 0:half] * corner + change_corner,
         )
 
-    grams = [gram_ref[...]] + [jnp.zeros((members, members), F32)] * (groups - 1)
-    drives = [drive_ref[...]] + [jnp.zeros((1, members), F32)] * (groups - 1)
     infos = [own_info_ref] + list(info_refs[1:])
+    rights, corners, drives = [right_ref[...]], [corner_ref[...]], [drive_ref[...]]
     for chain in range(1, groups):
         slot_info(rows_refs[chain - 1], infos[chain])
-    for chain in range(1, groups):
         scaled, drive = scaled_rows(ordered_ref[...].astype(F32), infos[chain], 0, sources)
-        grams[chain] = grams[chain] + dot(turned_ref[...], scaled)
-        drives[chain] = drives[chain] + drive
+        rights.append(dot(turned_ref[...], scaled[:, half:]))
+        corners.append(dot(turned_ref[0:half, :], scaled[:, 0:half]))
+        drives.append(drive)
     for turn, rows_ref in enumerate(rows_refs, 1):
         rows = slot_rows(rows_ref, members)
-        scaled = []
+        turned = rows.T.astype(BF16)
         for chain in range(groups):
-            block, drive = scaled_rows(rows, infos[chain], turn, sources)
-            scaled.append(block)
+            scaled, drive = scaled_rows(rows, infos[chain], turn, sources)
+            rights[chain] = rights[chain] + dot(turned, scaled[:, half:])
+            corners[chain] = corners[chain] + dot(turned[0:half, :], scaled[:, 0:half])
             drives[chain] = drives[chain] + drive
-        sums = lax.dot_general(
-            rows.astype(BF16),
-            jnp.concatenate(scaled, axis=1),
-            (((0,), (0,)), ((), ())),
-            preferred_element_type=F32,
-        )
-        for chain in range(groups):
-            columns = slice(chain * members, (chain + 1) * members)
-            grams[chain] = grams[chain] + sums[:, columns]
 
     frobenius = []
     for chain, (y_right, y_corner, z_right, z_corner, y_high, z_high, _, _, w_high) in enumerate(
         chains
     ):
-        shifted = identity + grams[chain] / (members - 1.0)
-        squares = jnp.sum(jnp.sum(shifted * shifted, axis=0, keepdims=True), axis=1, keepdims=True)
+        right = identity[:, half:] + rights[chain] / (members - 1.0)
+        corner = identity[0:half, 0:half] + corners[chain] / (members - 1.0)
+        squares = right * right
+        squares = 2.0 * squares[0:half, :] + squares[half:, :] + corner * corner
+        squares = jnp.sum(jnp.sum(squares, axis=0, keepdims=True), axis=1, keepdims=True)
         frobenius.append(jnp.sqrt(squares))
-        current = shifted / frobenius[chain]
-        right, corner = current[:, half:], current[0:half, 0:half]
+        right, corner = right / frobenius[chain], corner / frobenius[chain]
         factor = split(w_high, -0.5 * right, -0.5 * corner)
         put_symmetric(y_high, right, corner)
         y_right[...], y_corner[...] = advance(factor, w_high, right, corner, y_high)
@@ -388,23 +395,12 @@
     )(states)
 
 
-def place_kernel(pieces_ref, whole_ref, sems):
+def place_kernel(pieces_ref, whole_ref):
     groups, patches, _, share = pieces_ref.shape
-    copies = []
-    for group in range(groups):
-        for patch in range(patches):
+    for patch in range(patches):
+        for group in range(groups):
             begin = (patch * groups + group) * share
-            copies.append(
-                pltpu.make_async_copy(
-                    pieces_ref.at[group, patch],
-                    whole_ref.at[:, begin : begin + share],
-                    sems.at[group, patch],
-                )
-            )
-    for copy in copies:
-        copy.start()
-    for copy in copies:
-        copy.wait()
+            whole_ref[:, begin : begin + share] = pieces_ref[group, patch]
 
 
 def place_pieces(pieces):
@@ -412,10 +408,7 @@
     points = groups * patches * share
     return pl.pallas_call(
         place_kernel,
-        in_specs=[pl.BlockSpec(memory_space=pltpu.VMEM)],
-        out_specs=pl.BlockSpec(memory_space=pl.ANY),
         out_shape=jax.ShapeDtypeStruct((own_members, points), BF16),
-        scratch_shapes=[pltpu.SemaphoreType.DMA((groups, patches))],
         compiler_params=pltpu.CompilerParams(vmem_limit_bytes=16 * MEBI),
         cost_estimate=pl.CostEstimate(
             flops=0, bytes_accessed=4 * own_members * points, transcendentals=0

time: 120 us -> 120 us (level)
  no operation moved by 1% of the time
where the time goes in v12:
time: 120 us; the launch traced here: 119 us
  blocking collectives  55 us (46%)
  waiting for transfers between devices  29 us (24%)
  Pallas kernels  19.1 us (16%)
  starting transfers between devices  14.5 us (12%)
  local copies, waits for them, and re-layouts  1.59 us (1%)
    all_to_all x1, blocking collectives, exchange(): return lax.all_to_all(blocks, axes, split_axis=0, concat_axis=0, tiled=True)  55 us
    all_to_all x2, waiting for transfers between devices, exchange(): return lax.all_to_all(blocks, axes, split_axis=0, concat_axis=0, tiled=True)  16.6 us
    all_to_all x2, starting transfers between devices, exchange(): return lax.all_to_all(blocks, axes, split_axis=0, concat_axis=0, tiled=True)  13 us
    ppermute x1, waiting for transfers between devices, swap_shares(): lax.ppermute(own, 'boot', [(g, (g - turn) % groups) for g in range(groups)])  12.4 us
    pallas_call x1, Pallas kernels, patch_weights(): pl.pallas_call(weights_kernel, out_shape=jax.ShapeDtypeStruct((groups, me...  11.5 us
    pallas_call x1, Pallas kernels, pack(): pl.pallas_call(functools.partial(pack_kernel, groups), out_shape=jax.Shap...  2.77 us
  transfers between devices with their start and end apart: 3, of which 2 were waited for; matrix products, arithmetic and copies ran while one was open for 0% of the time, Pallas kernels for 11%

profile of v12, /device:TPU:0, one launch (start us, length us, event | category | flops | bytes accessed | tf_op | source)
XLA Modules:
  0.0 119.2 jit_solution(8087003520859682427)
XLA Ops:
  0.0 2.8 %pack_rows.1 = bf16[16,8,3200]{2,1,0:T(8,128)(2,1)} custom-call(s32[2,384]{1,0:T(2,128)} %bitcast.8, s32[2,384]{1,0:T(2,128)} %bitcast.9, s32[384]{0:T(512)} %refs_2_.1, f32[384]{0:T(512)} %refs_3_.1, bf16[384]{0:T(512)(128)(2,1)} %refs_4_.1, bf16[384,512]{1,0:T(8,128)(2,1)} %refs_5_.1), custom_call_target="tpu_custom_call" | custom-call | flops 301989888 | bytes 1179648 | tf_op jit(solution)/shard_map/pack_rows/pallas_call | solution.py:98
  2.8 7.4 %all-to-all-start = ((bf16[16,8,3200]{2,1,0:T(8,128)(2,1)}), bf16[16,8,3200]{2,1,0:T(8,128)(2,1)S(1)}, u32[]{:S(2)}, u32[]{:S(2)}) async-start(bf16[16,8,3200]{2,1,0:T(8,128)(2,1)} %pack_rows.1), calls=%async_computation | async-start | bytes 1638400 | tf_op jit(solution)/shard_map/all_to_all | solution.py:421
  10.2 0.0 copy-start
  10.2 1.6 %copy-done = bf16[32,32768]{1,0:T(8,128)(2,1)S(1)} copy-done((bf16[32,32768]{1,0:T(8,128)(2,1)S(1)}, bf16[32,32768]{1,0:T(8,128)(2,1)}, u32[]{:S(2)}) %copy-start) | copy-done | bytes 2097176
  11.8 1.0 cut_share.1
  12.8 16.6 %all-to-all-done.rows_ref = bf16[16,8,3200]{2,1,0:T(8,128)(2,1)S(1)} async-done(((bf16[16,8,3200]{2,1,0:T(8,128)(2,1)}), bf16[16,8,3200]{2,1,0:T(8,128)(2,1)S(1)}, u32[]{:S(2)}, u32[]{:S(2)}) %all-to-all-start) | async-done | bytes 819232 | tf_op jit(solution)/shard_map/all_to_all | solution.py:421
  29.4 1.5 %collective-permute-start = (bf16[16,8,3200]{2,1,0:T(8,128)(2,1)S(1)}, bf16[16,8,3200]{2,1,0:T(8,128)(2,1)S(1)}, u32[]{:S(2)}, u32[]{:S(2)}) collective-permute-start(bf16[16,8,3200]{2,1,0:T(8,128)(2,1)S(1)} %all-to-all-done.rows_ref), channel_id=1, source_target_pairs={{0,16},{16,0},{1,17},{17,1},{2,18},{18,2},{3,19},{19,3},{4,20},{20... | collective-permute-start | bytes 2457608 | tf_op jit(solution)/shard_map/ppermute | solution.py:427
  30.9 5.7 %all-to-all-start.1 = ((bf16[16,32,1024]{2,1,0:T(8,128)(2,1)}), bf16[16,32,1024]{2,1,0:T(8,128)(2,1)S(1)}, u32[]{:S(2)}, u32[]{:S(2)}) async-start(bf16[16,32,1024]{2,1,0:T(8,128)(2,1)} %cut_share.1), calls=%async_computation.1 | async-start | bytes 2097152 | tf_op jit(solution)/shard_map/all_to_all | solution.py:421
  36.6 0.9 own_gram.1
  37.5 12.4 %collective-permute-done.refs_6_ = bf16[16,8,3200]{2,1,0:T(8,128)(2,1)S(1)} collective-permute-done((bf16[16,8,3200]{2,1,0:T(8,128)(2,1)S(1)}, bf16[16,8,3200]{2,1,0:T(8,128)(2,1)S(1)}, u32[]{:S(2)}, u32[]{:S(2)}) %collective-permute-start) | collective-permute-done | bytes 819232 | tf_op jit(solution)/shard_map/ppermute | solution.py:427
  49.9 11.5 %patch_weights.1.blended_ref = bf16[2,512,512]{2,1,0:T(8,128)(2,1)S(1)} custom-call(f32[512,256]{1,0:T(8,128)S(1)} %get-tuple-element.14.refs_0_, f32[256,256]{1,0:T(8,128)S(1)} %get-tuple-element.15.refs_1_, f32[1,512]{1,0:T(1,128)S(1)} %get-tuple-element.16.refs_2_, f32[128,128]{1,0:T(8,128)S(1)} %get-tuple-element.17.refs_3_, ...), custom_call_target="tpu_custom_call" | custom-call | flops 21474836480 | bytes 2097152 | tf_op jit(solution)/shard_map/patch_weights/pallas_call | solution.py:331
  61.4 0.0 all-to-all-done.1
  61.4 1.4 %update_points.1 = bf16[2,512,1024]{2,1,0:T(8,128)(2,1)S(1)} custom-call(bf16[2,512,512]{2,1,0:T(8,128)(2,1)S(1)} %patch_weights.1.blended_ref, bf16[512,1024]{1,0:T(8,128)(2,1)S(1)} %bitcast.7), custom_call_target="tpu_custom_call" | custom-call | flops 1073741824 | bytes 3145728 | tf_op jit(solution)/shard_map/update_points/pallas_call | solution.py:363
  62.8 55.0 %all_to_all.15 = bf16[32,32,1024]{2,1,0:T(8,128)(2,1)S(1)} all-to-all(bf16[32,32,1024]{2,1,0:T(8,128)(2,1)S(1)} %bitcast.5), channel_id=1, replica_groups=mesh['boot'=2,'space'=16] {'boot','space'}, dimensions={0} | all-to-all | bytes 4194304 | tf_op jit(solution)/shard_map/all_to_all | solution.py:421
  117.8 1.5 %place_pieces.1 = bf16[32,32768]{1,0:T(8,128)(2,1)} custom-call(bf16[2,16,32,1024]{3,2,1,0:T(8,128)(2,1)S(1)} %bitcast.6), custom_call_target="tpu_custom_call" | custom-call | bytes 4194304 | tf_op jit(solution)/shard_map/place_pieces/pallas_call | solution.py:409
Async XLA Ops:
  2.8 26.6 %all-to-all-start = ((bf16[16,8,3200]{2,1,0:T(8,128)(2,1)}), bf16[16,8,3200]{2,1,0:T(8,128)(2,1)S(1)}, u32[]{:S(2)}, u32[]{:S(2)}) async-start(bf16[16,8,3200]{2,1,0:T(8,128)(2,1)} %pack_rows.1), calls=%async_computation | async-start | bytes 1638400 | tf_op jit(solution)/shard_map/all_to_all | solution.py:421
  10.2 1.6 %copy-start = (bf16[32,32768]{1,0:T(8,128)(2,1)S(1)}, bf16[32,32768]{1,0:T(8,128)(2,1)}, u32[]{:S(2)}) copy-start(bf16[32,32768]{1,0:T(8,128)(2,1)} %states_ref.1) | copy-start | bytes 6291460
  29.4 20.4 %collective-permute-start = (bf16[16,8,3200]{2,1,0:T(8,128)(2,1)S(1)}, bf16[16,8,3200]{2,1,0:T(8,128)(2,1)S(1)}, u32[]{:S(2)}, u32[]{:S(2)}) collective-permute-start(bf16[16,8,3200]{2,1,0:T(8,128)(2,1)S(1)} %all-to-all-done.rows_ref), channel_id=1, source_target_pairs={{0,16},{16,0},{1,17},{17,1},{2,18},{18,2},{3,19},{19,3},{4,20},{20... | collective-permute-start | bytes 2457608 | tf_op jit(solution)/shard_map/ppermute | solution.py:427
  30.9 30.5 %all-to-all-start.1 = ((bf16[16,32,1024]{2,1,0:T(8,128)(2,1)}), bf16[16,32,1024]{2,1,0:T(8,128)(2,1)S(1)}, u32[]{:S(2)}, u32[]{:S(2)}) async-start(bf16[16,32,1024]{2,1,0:T(8,128)(2,1)} %cut_share.1), calls=%async_computation.1 | async-start | bytes 2097152 | tf_op jit(solution)/shard_map/all_to_all | solution.py:421

commit v13 on v12

--- a/solution.py
+++ b/solution.py
@@ -215,10 +215,10 @@
 
 def weights_kernel(*refs):
     right_ref, corner_ref, drive_ref, own_info_ref, ordered_ref, turned_ref = refs[:6]
-    groups = (len(refs) - 6) // 11
+    groups = (len(refs) - 6) // 10
     rows_refs, blended_ref = refs[6 : 5 + groups], refs[5 + groups]
     info_refs = refs[6 + groups : 6 + 2 * groups]
-    chains = [refs[6 + 2 * groups + 9 * c : 15 + 2 * groups + 9 * c] for c in range(groups)]
+    chains = [refs[6 + 2 * groups + 8 * c : 14 + 2 * groups + 8 * c] for c in range(groups)]
     members, half = right_ref.shape
     sources = rows_refs[0].shape[0] if rows_refs else 1
     row_id = lax.broadcasted_iota(jnp.int32, (members, members), 0)
@@ -229,16 +229,28 @@
     )
     dot = functools.partial(jnp.dot, preferred_element_type=F32)
 
+    def diagonal_row(lower, corner):
+        return jnp.concatenate(
+            [
+                jnp.sum(
+                    jnp.where(eye, part[begin : begin + LANES, begin : begin + LANES], 0.0),
+                    axis=0,
+                    keepdims=True,
+                )
+                for part in (corner, lower)
+                for begin in range(0, half, LANES)
+            ],
+            axis=1,
+        )
+
     def split(w_high, right, corner):
         put_symmetric(w_high, right, corner)
-        diagonal = []
         for first, part in ((0, corner), (half, right[half:, :])):
             for begin in range(0, half, LANES):
                 block = part[begin : begin + LANES, begin : begin + LANES]
                 place = slice(first + begin, first + begin + LANES)
                 w_high[place, place] = jnp.where(eye, 0.0, block).astype(BF16)
-                diagonal.append(jnp.sum(jnp.where(eye, block, 0.0), axis=0, keepdims=True))
-        return 1.5 + jnp.concatenate(diagonal, axis=1)
+        return 1.5 + diagonal_row(right[half:, :], corner)
 
     def advance(factor, w_high, right, corner, high):
         change_right, change_corner = symmetric_product(high, w_high)
@@ -265,7 +277,7 @@
             drives[chain] = drives[chain] + drive
 
     frobenius = []
-    for chain, (y_right, y_corner, z_right, z_corner, y_high, z_high, _, _, w_high) in enumerate(
+    for chain, (y_right, y_corner, z_right, z_corner, y_high, z_high, _, w_high) in enumerate(
         chains
     ):
         right = identity[:, half:] + rights[chain] / (members - 1.0)
@@ -285,36 +297,36 @@
 
     def step(_, carry):
         factors = [
-            split(chain[8], *symmetric_product(chain[5], chain[4])) for chain in chains
+            split(chain[7], *symmetric_product(chain[5], chain[4])) for chain in chains
         ]
         for factor, chain in zip(factors, chains):
             for right, corner, high in (
                 (chain[0], chain[1], chain[4]),
                 (chain[2], chain[3], chain[5]),
             ):
-                new_right, new_corner = advance(factor, chain[8], right[...], corner[...], high)
+                new_right, new_corner = advance(factor, chain[7], right[...], corner[...], high)
                 right[...], corner[...] = new_right, new_corner
                 put_symmetric(high, new_right, new_corner)
         return carry
 
     lax.fori_loop(1, NS_STEPS - 1, step, 0)
     factors = []
-    for y_right, y_corner, z_right, z_corner, y_high, z_high, y_low, z_low, w_high in chains:
-        for right, corner, high, low in (
-            (y_right, y_corner, y_high, y_low),
-            (z_right, z_corner, z_high, z_low),
-        ):
-            put_symmetric(
-                low,
-                right[...] - high[:, half:].astype(F32),
-                corner[...] - high[0:half, 0:half].astype(F32),
-            )
-        large = symmetric_product(z_high, y_high)
-        small = zip(symmetric_product(z_high, y_low), symmetric_product(z_low, y_high))
-        factors.append(
-            split(w_high, *[first + (one + two) for first, (one, two) in zip(large, small)])
-        )
-    for chain, (_, _, z_right, z_corner, _, z_high, _, _, w_high) in enumerate(chains):
+    for y_right, y_corner, z_right, z_corner, y_high, z_high, z_off, w_high in chains:
+        z_off[...] = z_high[...]
+        for right, corner, off in ((y_right, y_corner, y_high), (z_right, z_corner, z_off)):
+            for first, part in ((0, corner), (half, right)):
+                for begin in range(0, half, LANES):
+                    place = slice(first + begin, first + begin + LANES)
+                    block = part[place, begin : begin + LANES]
+                    off[place, place] = jnp.where(eye, 0.0, block).astype(BF16)
+        y_row = diagonal_row(y_right[half:, :], y_corner[...])
+        z_row = diagonal_row(z_right[half:, :], z_corner[...])
+        z_column = diagonal_column(z_row, eye)
+        right, corner = symmetric_product(z_off, y_high)
+        right += z_column * y_right[...] + z_right[...] * y_row[:, half:]
+        corner += z_column[0:half, :] * y_corner[...] + z_corner[...] * y_row[:, 0:half]
+        factors.append(split(w_high, right, corner) - z_row * y_row)
+    for chain, (_, _, z_right, z_corner, _, z_high, _, w_high) in enumerate(chains):
         right, corner = advance(factors[chain], w_high, z_right[...], z_corner[...], z_high)
         left = jnp.concatenate([corner, right[0:half, :].T], axis=0)
         root = jnp.concatenate([left, right], axis=1) * (-2.0 / jnp.sqrt(frobenius[chain]))
@@ -327,7 +339,7 @@
     groups, members = len(other_rows) + 1, own[0].shape[0]
     half = members // 2
     right, corner = pltpu.VMEM((members, half), F32), pltpu.VMEM((half, half), F32)
-    chain = [right, corner] * 2 + [pltpu.VMEM((members, members), BF16)] * 5
+    chain = [right, corner] * 2 + [pltpu.VMEM((members, members), BF16)] * 4
     return pl.pallas_call(
         weights_kernel,
         out_shape=jax.ShapeDtypeStruct((groups, members, members), BF16),

time: 120 us -> 119 us (level)
  no operation moved by 1% of the time
where the time goes in v13:
time: 119 us
  blocking collectives  55 us (46%)
  waiting for transfers between devices  29 us (24%)
  Pallas kernels  18.5 us (16%)
  starting transfers between devices  14.5 us (12%)
  local copies, waits for them, and re-layouts  1.59 us (1%)
    all_to_all x1, blocking collectives, exchange(): return lax.all_to_all(blocks, axes, split_axis=0, concat_axis=0, tiled=True)  55 us
    all_to_all x2, waiting for transfers between devices, exchange(): return lax.all_to_all(blocks, axes, split_axis=0, concat_axis=0, tiled=True)  16.6 us
    all_to_all x2, starting transfers between devices, exchange(): return lax.all_to_all(blocks, axes, split_axis=0, concat_axis=0, tiled=True)  13 us
    ppermute x1, waiting for transfers between devices, swap_shares(): lax.ppermute(own, 'boot', [(g, (g - turn) % groups) for g in range(groups)])  12.4 us
    pallas_call x1, Pallas kernels, patch_weights(): pl.pallas_call(weights_kernel, out_shape=jax.ShapeDtypeStruct((groups, me...  11 us
    pallas_call x1, Pallas kernels, pack(): pl.pallas_call(functools.partial(pack_kernel, groups), out_shape=jax.Shap...  2.77 us
  transfers between devices with their start and end apart: 3, of which 2 were waited for; matrix products, arithmetic and copies ran while one was open for 0% of the time, Pallas kernels for 11%

profile of v13, /device:TPU:0, one launch (start us, length us, event | category | flops | bytes accessed | tf_op | source)
XLA Modules:
  0.0 118.7 jit_solution(8335734306464296569)
XLA Ops:
  0.0 2.8 %pack_rows.1 = bf16[16,8,3200]{2,1,0:T(8,128)(2,1)} custom-call(s32[2,384]{1,0:T(2,128)} %bitcast.8, s32[2,384]{1,0:T(2,128)} %bitcast.9, s32[384]{0:T(512)} %refs_2_.1, f32[384]{0:T(512)} %refs_3_.1, bf16[384]{0:T(512)(128)(2,1)} %refs_4_.1, bf16[384,512]{1,0:T(8,128)(2,1)} %refs_5_.1), custom_call_target="tpu_custom_call" | custom-call | flops 301989888 | bytes 1179648 | tf_op jit(solution)/shard_map/pack_rows/pallas_call | solution.py:98
  2.8 7.4 %all-to-all-start = ((bf16[16,8,3200]{2,1,0:T(8,128)(2,1)}), bf16[16,8,3200]{2,1,0:T(8,128)(2,1)S(1)}, u32[]{:S(2)}, u32[]{:S(2)}) async-start(bf16[16,8,3200]{2,1,0:T(8,128)(2,1)} %pack_rows.1), calls=%async_computation | async-start | bytes 1638400 | tf_op jit(solution)/shard_map/all_to_all | solution.py:433
  10.2 0.0 copy-start
  10.2 1.6 %copy-done = bf16[32,32768]{1,0:T(8,128)(2,1)S(1)} copy-done((bf16[32,32768]{1,0:T(8,128)(2,1)S(1)}, bf16[32,32768]{1,0:T(8,128)(2,1)}, u32[]{:S(2)}) %copy-start) | copy-done | bytes 2097176
  11.8 1.0 cut_share.1
  12.8 16.6 %all-to-all-done.rows_ref = bf16[16,8,3200]{2,1,0:T(8,128)(2,1)S(1)} async-done(((bf16[16,8,3200]{2,1,0:T(8,128)(2,1)}), bf16[16,8,3200]{2,1,0:T(8,128)(2,1)S(1)}, u32[]{:S(2)}, u32[]{:S(2)}) %all-to-all-start) | async-done | bytes 819232 | tf_op jit(solution)/shard_map/all_to_all | solution.py:433
  29.4 1.5 %collective-permute-start = (bf16[16,8,3200]{2,1,0:T(8,128)(2,1)S(1)}, bf16[16,8,3200]{2,1,0:T(8,128)(2,1)S(1)}, u32[]{:S(2)}, u32[]{:S(2)}) collective-permute-start(bf16[16,8,3200]{2,1,0:T(8,128)(2,1)S(1)} %all-to-all-done.rows_ref), channel_id=1, source_target_pairs={{0,16},{16,0},{1,17},{17,1},{2,18},{18,2},{3,19},{19,3},{4,20},{20... | collective-permute-start | bytes 2457608 | tf_op jit(solution)/shard_map/ppermute | solution.py:439
  30.9 5.7 %all-to-all-start.1 = ((bf16[16,32,1024]{2,1,0:T(8,128)(2,1)}), bf16[16,32,1024]{2,1,0:T(8,128)(2,1)S(1)}, u32[]{:S(2)}, u32[]{:S(2)}) async-start(bf16[16,32,1024]{2,1,0:T(8,128)(2,1)} %cut_share.1), calls=%async_computation.1 | async-start | bytes 2097152 | tf_op jit(solution)/shard_map/all_to_all | solution.py:433
  36.6 0.9 own_gram.1
  37.5 12.4 %collective-permute-done.refs_6_ = bf16[16,8,3200]{2,1,0:T(8,128)(2,1)S(1)} collective-permute-done((bf16[16,8,3200]{2,1,0:T(8,128)(2,1)S(1)}, bf16[16,8,3200]{2,1,0:T(8,128)(2,1)S(1)}, u32[]{:S(2)}, u32[]{:S(2)}) %collective-permute-start) | collective-permute-done | bytes 819232 | tf_op jit(solution)/shard_map/ppermute | solution.py:439
  49.9 11.0 %patch_weights.1.blended_ref = bf16[2,512,512]{2,1,0:T(8,128)(2,1)S(1)} custom-call(f32[512,256]{1,0:T(8,128)S(1)} %get-tuple-element.14.refs_0_, f32[256,256]{1,0:T(8,128)S(1)} %get-tuple-element.15.refs_1_, f32[1,512]{1,0:T(1,128)S(1)} %get-tuple-element.16.refs_2_, f32[128,128]{1,0:T(8,128)S(1)} %get-tuple-element.17.refs_3_, ...), custom_call_target="tpu_custom_call" | custom-call | flops 21474836480 | bytes 2097152 | tf_op jit(solution)/shard_map/patch_weights/pallas_call | solution.py:343
  60.8 0.0 all-to-all-done.1
  60.8 1.4 %update_points.1 = bf16[2,512,1024]{2,1,0:T(8,128)(2,1)S(1)} custom-call(bf16[2,512,512]{2,1,0:T(8,128)(2,1)S(1)} %patch_weights.1.blended_ref, bf16[512,1024]{1,0:T(8,128)(2,1)S(1)} %bitcast.7), custom_call_target="tpu_custom_call" | custom-call | flops 1073741824 | bytes 3145728 | tf_op jit(solution)/shard_map/update_points/pallas_call | solution.py:375
  62.2 55.0 %all_to_all.15 = bf16[32,32,1024]{2,1,0:T(8,128)(2,1)S(1)} all-to-all(bf16[32,32,1024]{2,1,0:T(8,128)(2,1)S(1)} %bitcast.5), channel_id=1, replica_groups=mesh['boot'=2,'space'=16] {'boot','space'}, dimensions={0} | all-to-all | bytes 4194304 | tf_op jit(solution)/shard_map/all_to_all | solution.py:433
  117.2 1.5 %place_pieces.1 = bf16[32,32768]{1,0:T(8,128)(2,1)} custom-call(bf16[2,16,32,1024]{3,2,1,0:T(8,128)(2,1)S(1)} %bitcast.6), custom_call_target="tpu_custom_call" | custom-call | bytes 4194304 | tf_op jit(solution)/shard_map/place_pieces/pallas_call | solution.py:421
Async XLA Ops:
  2.8 26.6 %all-to-all-start = ((bf16[16,8,3200]{2,1,0:T(8,128)(2,1)}), bf16[16,8,3200]{2,1,0:T(8,128)(2,1)S(1)}, u32[]{:S(2)}, u32[]{:S(2)}) async-start(bf16[16,8,3200]{2,1,0:T(8,128)(2,1)} %pack_rows.1), calls=%async_computation | async-start | bytes 1638400 | tf_op jit(solution)/shard_map/all_to_all | solution.py:433
  10.2 1.6 %copy-start = (bf16[32,32768]{1,0:T(8,128)(2,1)S(1)}, bf16[32,32768]{1,0:T(8,128)(2,1)}, u32[]{:S(2)}) copy-start(bf16[32,32768]{1,0:T(8,128)(2,1)} %states_ref.1) | copy-start | bytes 6291460
  29.4 20.4 %collective-permute-start = (bf16[16,8,3200]{2,1,0:T(8,128)(2,1)S(1)}, bf16[16,8,3200]{2,1,0:T(8,128)(2,1)S(1)}, u32[]{:S(2)}, u32[]{:S(2)}) collective-permute-start(bf16[16,8,3200]{2,1,0:T(8,128)(2,1)S(1)} %all-to-all-done.rows_ref), channel_id=1, source_target_pairs={{0,16},{16,0},{1,17},{17,1},{2,18},{18,2},{3,19},{19,3},{4,20},{20... | collective-permute-start | bytes 2457608 | tf_op jit(solution)/shard_map/ppermute | solution.py:439
  30.9 29.9 %all-to-all-start.1 = ((bf16[16,32,1024]{2,1,0:T(8,128)(2,1)}), bf16[16,32,1024]{2,1,0:T(8,128)(2,1)S(1)}, u32[]{:S(2)}, u32[]{:S(2)}) async-start(bf16[16,32,1024]{2,1,0:T(8,128)(2,1)} %cut_share.1), calls=%async_computation.1 | async-start | bytes 2097152 | tf_op jit(solution)/shard_map/all_to_all | solution.py:433

commit v14 on v13

--- a/solution.py
+++ b/solution.py
@@ -5,9 +5,12 @@
 from jax import lax
 from jax.experimental import pallas as pl
 from jax.experimental.pallas import tpu as pltpu
+from jax.sharding import Mesh
 from jax.sharding import PartitionSpec as P
 
 NS_STEPS = 6
+SPACE = ("za", "zb", "near")
+PARTNERS = ("near", "zb", "za")
 LANES = 128
 ROWS = 8
 MEBI = 1024 * 1024
@@ -15,7 +18,12 @@
 BF16 = jnp.bfloat16
 
 
-def pack_kernel(groups, *refs):
+def partner_order(sizes):
+    za, zb, near = sizes
+    return [(a * zb + b) * near + c for c in range(near) for b in range(zb) for a in range(za)]
+
+
+def pack_kernel(groups, order, *refs):
     sources, slots_ref, fetched = refs[:6], refs[6], refs[7:13]
     block_ref, tail_ref, info_ref, sems = refs[13:]
     copies = [
@@ -45,7 +53,7 @@
     begin = lax.axis_index("boot") * share
     own_id = (lax.broadcasted_iota(jnp.int32, (share, count), 0) + begin).astype(F32)
     picks = [
-        jnp.where(own_id == rank[patch : patch + 1, :], 1.0, 0.0) for patch in range(patches)
+        jnp.where(own_id == rank[patch : patch + 1, :], 1.0, 0.0) for patch in order
     ]
     picks = jnp.concatenate(picks, axis=0).astype(BF16)
     copies[-1].wait()
@@ -78,25 +86,26 @@
     info_ref[0 : groups * share, :] = info
     info = info_ref[...].T
     tail_id = lax.broadcasted_iota(jnp.int32, (ROWS, LANES), 0)
-    for patch in range(patches):
+    for place, patch in enumerate(order):
         tail = jnp.where(
             tail_id == 0,
             info[patch : patch + 1, :],
             jnp.where(tail_id == 1, info[patches + patch : patches + patch + 1, :], 0.0),
         )
-        tail_ref[patch] = tail.astype(BF16)
+        tail_ref[place] = tail.astype(BF16)
     tails_out = pltpu.make_async_copy(tail_ref, slots_ref.at[:, :, width:], sems.at[7])
     tails_out.start()
     blocks_out.wait()
     tails_out.wait()
 
 
-def pack(targets, local, mult, prec, dep, rows, patches, share, groups):
+def pack(targets, local, mult, prec, dep, rows, order, share, groups):
     count, members = rows.shape
+    patches = len(order)
     operands = (targets.T, local.T, mult, prec, dep, rows)
     width = share // ROWS * members
     return pl.pallas_call(
-        functools.partial(pack_kernel, groups),
+        functools.partial(pack_kernel, groups, order),
         out_shape=jax.ShapeDtypeStruct((patches, ROWS, width + LANES), BF16),
         in_specs=[pl.BlockSpec(memory_space=pl.ANY)] * len(operands),
         out_specs=pl.BlockSpec(memory_space=pl.ANY),
@@ -354,26 +363,35 @@
     )(*own, *other_rows)
 
 
-def update_kernel(blended_ref, background_ref, analysis_ref):
+def update_kernel(order, blended_ref, background_ref, analysis_ref):
     groups = blended_ref.shape[0]
     members, points = background_ref.shape
+    rows = members // len(order)
+    places = [order.index(holder) for holder in range(len(order))]
     tile = min(points, 256)
     for begin in range(0, points, tile):
         columns = slice(begin, begin + tile)
         background = background_ref[:, columns].astype(F32)
+        background = jnp.concatenate(
+            [background[place * rows : (place + 1) * rows, :] for place in places], axis=0
+        )
         centre = jnp.sum(background, axis=0, keepdims=True) / members
         perturb = (background - centre).astype(BF16)
         for turn in range(groups):
             update = jnp.dot(blended_ref[turn], perturb, preferred_element_type=F32)
             group = lax.rem(lax.axis_index("boot") + turn, groups)
-            analysis_ref[group, :, columns] = (centre + update).astype(BF16)
-
-
-def update_points(blended, background):
+            update = centre + update
+            update = jnp.concatenate(
+                [update[holder * rows : (holder + 1) * rows, :] for holder in order], axis=0
+            )
+            analysis_ref[group, :, columns] = update.astype(BF16)
+
+
+def update_points(blended, background, order):
     groups = blended.shape[0]
     members, points = background.shape
     return pl.pallas_call(
-        update_kernel,
+        functools.partial(update_kernel, order),
         out_shape=jax.ShapeDtypeStruct((groups, members, points), BF16),
         compiler_params=pltpu.CompilerParams(vmem_limit_bytes=16 * MEBI),
         cost_estimate=pl.CostEstimate(
@@ -385,19 +403,19 @@
     )(blended, background)
 
 
-def cut_kernel(states_ref, cut_ref):
+def cut_kernel(order, states_ref, cut_ref):
     patches, _, share = cut_ref.shape
     region = states_ref.shape[1] // patches
     offset = lax.axis_index("boot") * share
-    for patch in range(patches):
+    for place, patch in enumerate(order):
         begin = pl.multiple_of(patch * region + offset, LANES)
-        cut_ref[patch] = states_ref[:, pl.ds(begin, share)]
-
-
-def cut_share(states, patches, share):
-    own_members = states.shape[0]
+        cut_ref[place] = states_ref[:, pl.ds(begin, share)]
+
+
+def cut_share(states, order, share):
+    own_members, patches = states.shape[0], len(order)
     return pl.pallas_call(
-        cut_kernel,
+        functools.partial(cut_kernel, order),
         out_shape=jax.ShapeDtypeStruct((patches, own_members, share), BF16),
         compiler_params=pltpu.CompilerParams(vmem_limit_bytes=16 * MEBI),
         cost_estimate=pl.CostEstimate(
@@ -407,19 +425,19 @@
     )(states)
 
 
-def place_kernel(pieces_ref, whole_ref):
-    groups, patches, _, share = pieces_ref.shape
-    for patch in range(patches):
+def place_kernel(order, pieces_ref, whole_ref):
+    groups, _, _, share = pieces_ref.shape
+    for place, patch in enumerate(order):
         for group in range(groups):
             begin = (patch * groups + group) * share
-            whole_ref[:, begin : begin + share] = pieces_ref[group, patch]
-
-
-def place_pieces(pieces):
+            whole_ref[:, begin : begin + share] = pieces_ref[group, place]
+
+
+def place_pieces(pieces, order):
     groups, patches, own_members, share = pieces.shape
     points = groups * patches * share
     return pl.pallas_call(
-        place_kernel,
+        functools.partial(place_kernel, order),
         out_shape=jax.ShapeDtypeStruct((own_members, points), BF16),
         compiler_params=pltpu.CompilerParams(vmem_limit_bytes=16 * MEBI),
         cost_estimate=pl.CostEstimate(
@@ -429,7 +447,7 @@
     )(pieces)
 
 
-def exchange(blocks, axes="space"):
+def exchange(blocks, axes=PARTNERS):
     return lax.all_to_all(blocks, axes, split_axis=0, concat_axis=0, tiled=True)
 
 
@@ -450,7 +468,8 @@
     localization_factor_scaled,
     bootstrap_multiplicity,
 ):
-    device_count = lax.axis_size("space")
+    order = partner_order([lax.axis_size(axis) for axis in SPACE])
+    device_count = len(order)
     groups = lax.axis_size("boot")
     local_rows = measurement_anomaly_matrix.shape[0]
     targets_per = measurement_region_targets.shape[1]
@@ -466,31 +485,36 @@
         measurement_precision,
         departure_vector,
         measurement_anomaly_matrix,
-        device_count,
+        order,
         slot_share,
         groups,
     )
-    own_points = cut_share(background_states, device_count, share)
+    own_points = cut_share(background_states, order, share)
     own_rows, own_points = lax.optimization_barrier((exchange(slots), own_points))
     other_rows = swap_shares(own_rows)
     own_points = exchange(own_points).reshape(-1, share)
 
     own = own_gram(own_rows, measurement_anomaly_matrix.shape[1])
     blended = patch_weights(own, other_rows)
-    analysis = update_points(blended, own_points)
-    analysis = exchange(analysis.reshape(-1, own_members, share), ("boot", "space"))
-    return place_pieces(analysis.reshape(groups, device_count, own_members, share))
+    analysis = update_points(blended, own_points, order)
+    analysis = exchange(analysis.reshape(-1, own_members, share), ("boot",) + PARTNERS)
+    return place_pieces(analysis.reshape(groups, device_count, own_members, share), order)
 
 
 def solution(mesh):
+    groups, devices = mesh.shape["boot"], mesh.shape["space"]
+    cut = 2 if devices % 4 == 0 else 1
+    mesh = Mesh(
+        mesh.devices.reshape(groups, cut, cut, devices // cut**2), ("boot",) + SPACE
+    )
     in_specs = (
-        P("space", None),
-        P("space", None),
-        P("space"),
-        P("space"),
-        P("space", None),
-        P("space", None),
-        P(("boot", "space")),
-    )
-    out_specs = P(("boot", "space"), None)
+        P(SPACE, None),
+        P(SPACE, None),
+        P(SPACE),
+        P(SPACE),
+        P(SPACE, None),
+        P(SPACE, None),
+        P(("boot",) + SPACE),
+    )
+    out_specs = P(("boot",) + SPACE, None)
     return jax.shard_map(local, mesh=mesh, in_specs=in_specs, out_specs=out_specs, check_vma=False)

time: 119 us -> 119 us (level)
  waiting for transfers between devices: 29 us -> 33.5 us
  blocking collectives: 55 us -> 52.3 us
  starting transfers between devices: 14.5 us -> 12.5 us
    all_to_all x2, waiting for transfers between devices: 16.6 us -> 19.8 us  [exchange(): return lax.all_to_all(blocks, axes, split_axis=0, concat_axis=0, tiled=True)]
    all_to_all x1, blocking collectives: 55 us -> 52.3 us  [exchange(): return lax.all_to_all(blocks, axes, split_axis=0, concat_axis=0, tiled=True)]
    all_to_all x2, starting transfers between devices: 13 us -> 11.1 us  [exchange(): return lax.all_to_all(blocks, axes, split_axis=0, concat_axis=0, tiled=True)]
    ppermute x1, waiting for transfers between devices: 12.4 us -> 13.7 us  [swap_shares(): lax.ppermute(own, 'boot', [(g, (g - turn) % groups) for g in range(groups)])]
  transfers between devices with their start and end apart: 3 -> 3, of which waited for: 2 -> 3; matrix products, arithmetic and copies ran while one was open for 0% -> 0% of each run, Pallas kernels for 11% -> 11%
where the time goes in v14:
time: 119 us; the launch traced here: 118 us
  blocking collectives  52.3 us (44%)
  waiting for transfers between devices  33.5 us (28%)
  Pallas kernels  18.5 us (16%)
  starting transfers between devices  12.5 us (11%)
  local copies, waits for them, and re-layouts  1.59 us (1%)
    all_to_all x1, blocking collectives, exchange(): return lax.all_to_all(blocks, axes, split_axis=0, concat_axis=0, tiled=True)  52.3 us
    all_to_all x2, waiting for transfers between devices, exchange(): return lax.all_to_all(blocks, axes, split_axis=0, concat_axis=0, tiled=True)  19.8 us
    ppermute x1, waiting for transfers between devices, swap_shares(): lax.ppermute(own, 'boot', [(g, (g - turn) % groups) for g in range(groups)])  13.7 us
    all_to_all x2, starting transfers between devices, exchange(): return lax.all_to_all(blocks, axes, split_axis=0, concat_axis=0, tiled=True)  11.1 us
    pallas_call x1, Pallas kernels, patch_weights(): pl.pallas_call(weights_kernel, out_shape=jax.ShapeDtypeStruct((groups, me...  11 us
    pallas_call x1, Pallas kernels, pack(): pl.pallas_call(functools.partial(pack_kernel, groups, order), out_shape=j...  2.77 us
  transfers between devices with their start and end apart: 3, of which 3 were waited for; matrix products, arithmetic and copies ran while one was open for 0% of the time, Pallas kernels for 11%

profile of v14, /device:TPU:0, one launch (start us, length us, event | category | flops | bytes accessed | tf_op | source)
XLA Modules:
  0.0 118.4 jit_solution(369219652647054038)
XLA Ops:
  0.0 2.8 %pack_rows.1 = bf16[16,8,3200]{2,1,0:T(8,128)(2,1)} custom-call(s32[2,384]{1,0:T(2,128)} %bitcast.8, s32[2,384]{1,0:T(2,128)} %bitcast.9, s32[384]{0:T(512)} %refs_2_.1, f32[384]{0:T(512)} %refs_3_.1, bf16[384]{0:T(512)(128)(2,1)} %refs_4_.1, bf16[384,512]{1,0:T(8,128)(2,1)} %refs_5_.1), custom_call_target="tpu_custom_call" | custom-call | flops 301989888 | bytes 1179648 | tf_op jit(solution)/shard_map/pack_rows/pallas_call | solution.py:107
  2.8 7.4 %all-to-all-start = ((bf16[16,8,3200]{2,1,0:T(8,128)(2,1)}), bf16[16,8,3200]{2,1,0:T(8,128)(2,1)S(1)}, u32[]{:S(2)}, u32[]{:S(2)}) async-start(bf16[16,8,3200]{2,1,0:T(8,128)(2,1)} %pack_rows.1), calls=%async_computation | async-start | bytes 1638400 | tf_op jit(solution)/shard_map/all_to_all | solution.py:451
  10.2 0.0 copy-start
  10.2 1.6 %copy-done = bf16[32,32768]{1,0:T(8,128)(2,1)S(1)} copy-done((bf16[32,32768]{1,0:T(8,128)(2,1)S(1)}, bf16[32,32768]{1,0:T(8,128)(2,1)}, u32[]{:S(2)}) %copy-start) | copy-done | bytes 2097176
  11.8 1.0 cut_share.1
  12.8 18.9 %all-to-all-done.rows_ref = bf16[16,8,3200]{2,1,0:T(8,128)(2,1)S(1)} async-done(((bf16[16,8,3200]{2,1,0:T(8,128)(2,1)}), bf16[16,8,3200]{2,1,0:T(8,128)(2,1)S(1)}, u32[]{:S(2)}, u32[]{:S(2)}) %all-to-all-start) | async-done | bytes 819232 | tf_op jit(solution)/shard_map/all_to_all | solution.py:451
  31.8 1.5 %collective-permute-start = (bf16[16,8,3200]{2,1,0:T(8,128)(2,1)S(1)}, bf16[16,8,3200]{2,1,0:T(8,128)(2,1)S(1)}, u32[]{:S(2)}, u32[]{:S(2)}) collective-permute-start(bf16[16,8,3200]{2,1,0:T(8,128)(2,1)S(1)} %all-to-all-done.rows_ref), channel_id=1, source_target_pairs={{0,16},{16,0},{1,17},{17,1},{2,18},{18,2},{3,19},{19,3},{4,20},{20... | collective-permute-start | bytes 2457608 | tf_op jit(solution)/shard_map/ppermute | solution.py:457
  33.3 3.7 %all-to-all-start.1 = ((bf16[16,32,1024]{2,1,0:T(8,128)(2,1)}), bf16[16,32,1024]{2,1,0:T(8,128)(2,1)S(1)}, u32[]{:S(2)}, u32[]{:S(2)}) async-start(bf16[16,32,1024]{2,1,0:T(8,128)(2,1)} %cut_share.1), calls=%async_computation.1 | async-start | bytes 2097152 | tf_op jit(solution)/shard_map/all_to_all | solution.py:451
  36.9 0.9 own_gram.1
  37.8 13.7 %collective-permute-done.refs_6_ = bf16[16,8,3200]{2,1,0:T(8,128)(2,1)S(1)} collective-permute-done((bf16[16,8,3200]{2,1,0:T(8,128)(2,1)S(1)}, bf16[16,8,3200]{2,1,0:T(8,128)(2,1)S(1)}, u32[]{:S(2)}, u32[]{:S(2)}) %collective-permute-start) | collective-permute-done | bytes 819232 | tf_op jit(solution)/shard_map/ppermute | solution.py:457
  51.6 11.0 %patch_weights.1.blended_ref = bf16[2,512,512]{2,1,0:T(8,128)(2,1)S(1)} custom-call(f32[512,256]{1,0:T(8,128)S(1)} %get-tuple-element.14.refs_0_, f32[256,256]{1,0:T(8,128)S(1)} %get-tuple-element.15.refs_1_, f32[1,512]{1,0:T(1,128)S(1)} %get-tuple-element.16.refs_2_, f32[128,128]{1,0:T(8,128)S(1)} %get-tuple-element.17.refs_3_, ...), custom_call_target="tpu_custom_call" | custom-call | flops 21474836480 | bytes 2097152 | tf_op jit(solution)/shard_map/patch_weights/pallas_call | solution.py:352
  62.5 0.8 all-to-all-done.1
  63.3 1.4 %update_points.1 = bf16[2,512,1024]{2,1,0:T(8,128)(2,1)S(1)} custom-call(bf16[2,512,512]{2,1,0:T(8,128)(2,1)S(1)} %patch_weights.1.blended_ref, bf16[512,1024]{1,0:T(8,128)(2,1)S(1)} %bitcast.7), custom_call_target="tpu_custom_call" | custom-call | flops 1073741824 | bytes 3145728 | tf_op jit(solution)/shard_map/update_points/pallas_call | solution.py:393
  64.7 52.3 %all_to_all.15 = bf16[32,32,1024]{2,1,0:T(8,128)(2,1)S(1)} all-to-all(bf16[32,32,1024]{2,1,0:T(8,128)(2,1)S(1)} %bitcast.5), channel_id=1, replica_groups=mesh['boot'=2,'za'=2,'zb'=2,'near'=4] {'boot','near','zb','za'}, dimensions={0} | all-to-all | bytes 4194304 | tf_op jit(solution)/shard_map/all_to_all | solution.py:451
  117.0 1.5 %place_pieces.1 = bf16[32,32768]{1,0:T(8,128)(2,1)} custom-call(bf16[2,16,32,1024]{3,2,1,0:T(8,128)(2,1)S(1)} %bitcast.6), custom_call_target="tpu_custom_call" | custom-call | bytes 4194304 | tf_op jit(solution)/shard_map/place_pieces/pallas_call | solution.py:439
Async XLA Ops:
  2.8 29.0 %all-to-all-start = ((bf16[16,8,3200]{2,1,0:T(8,128)(2,1)}), bf16[16,8,3200]{2,1,0:T(8,128)(2,1)S(1)}, u32[]{:S(2)}, u32[]{:S(2)}) async-start(bf16[16,8,3200]{2,1,0:T(8,128)(2,1)} %pack_rows.1), calls=%async_computation | async-start | bytes 1638400 | tf_op jit(solution)/shard_map/all_to_all | solution.py:451
  10.2 1.6 %copy-start = (bf16[32,32768]{1,0:T(8,128)(2,1)S(1)}, bf16[32,32768]{1,0:T(8,128)(2,1)}, u32[]{:S(2)}) copy-start(bf16[32,32768]{1,0:T(8,128)(2,1)} %states_ref.1) | copy-start | bytes 6291460
  31.8 19.8 %collective-permute-start = (bf16[16,8,3200]{2,1,0:T(8,128)(2,1)S(1)}, bf16[16,8,3200]{2,1,0:T(8,128)(2,1)S(1)}, u32[]{:S(2)}, u32[]{:S(2)}) collective-permute-start(bf16[16,8,3200]{2,1,0:T(8,128)(2,1)S(1)} %all-to-all-done.rows_ref), channel_id=1, source_target_pairs={{0,16},{16,0},{1,17},{17,1},{2,18},{18,2},{3,19},{19,3},{4,20},{20... | collective-permute-start | bytes 2457608 | tf_op jit(solution)/shard_map/ppermute | solution.py:457
  33.3 30.1 %all-to-all-start.1 = ((bf16[16,32,1024]{2,1,0:T(8,128)(2,1)}), bf16[16,32,1024]{2,1,0:T(8,128)(2,1)S(1)}, u32[]{:S(2)}, u32[]{:S(2)}) async-start(bf16[16,32,1024]{2,1,0:T(8,128)(2,1)} %cut_share.1), calls=%async_computation.1 | async-start | bytes 2097152 | tf_op jit(solution)/shard_map/all_to_all | solution.py:451

commit v15 on v14

--- a/solution.py
+++ b/solution.py
@@ -355,7 +355,7 @@
         scratch_shapes=[pltpu.VMEM((LANES, LANES), F32)] * groups + chain * groups,
         compiler_params=pltpu.CompilerParams(vmem_limit_bytes=(8 + 10 * groups) * MEBI),
         cost_estimate=pl.CostEstimate(
-            flops=80 * groups * members * members * members,
+            flops=8 * groups * members * members * members,
             bytes_accessed=8 * members * members,
             transcendentals=0,
         ),
@@ -363,18 +363,22 @@
     )(*own, *other_rows)
 
 
-def update_kernel(order, blended_ref, background_ref, analysis_ref):
+def update_kernel(order, blended_ref, *refs):
+    piece_refs, analysis_ref, members_ref = refs[:-2], refs[-2], refs[-1]
     groups = blended_ref.shape[0]
-    members, points = background_ref.shape
-    rows = members // len(order)
-    places = [order.index(holder) for holder in range(len(order))]
+    near, rows, points = piece_refs[0].shape
+    slabs = len(piece_refs)
+    members = slabs * near * rows
+    slab, place = lax.axis_index(SPACE[:2]), lax.axis_index(SPACE[2])
+    for far, piece_ref in enumerate(piece_refs):
+        for step in range(near):
+            holder = lax.rem(slab + slabs - far, slabs) * near + lax.rem(place + near - step, near)
+            begin = pl.multiple_of(holder * rows, rows)
+            members_ref[pl.ds(begin, rows), :] = piece_ref[step].astype(members_ref.dtype)
     tile = min(points, 256)
     for begin in range(0, points, tile):
         columns = slice(begin, begin + tile)
-        background = background_ref[:, columns].astype(F32)
-        background = jnp.concatenate(
-            [background[place * rows : (place + 1) * rows, :] for place in places], axis=0
-        )
+        background = members_ref[:, columns].astype(F32)
         centre = jnp.sum(background, axis=0, keepdims=True) / members
         perturb = (background - centre).astype(BF16)
         for turn in range(groups):
@@ -387,12 +391,14 @@
             analysis_ref[group, :, columns] = update.astype(BF16)
 
 
-def update_points(blended, background, order):
-    groups = blended.shape[0]
-    members, points = background.shape
+def update_points(blended, pieces, order):
+    groups, members, _ = blended.shape
+    rows, points = pieces[0].shape[1:]
+    held = BF16 if rows % 16 == 0 else F32
     return pl.pallas_call(
         functools.partial(update_kernel, order),
         out_shape=jax.ShapeDtypeStruct((groups, members, points), BF16),
+        scratch_shapes=[pltpu.VMEM((members, points), held)],
         compiler_params=pltpu.CompilerParams(vmem_limit_bytes=16 * MEBI),
         cost_estimate=pl.CostEstimate(
             flops=2 * groups * members * members * points,
@@ -400,37 +406,84 @@
             transcendentals=0,
         ),
         name="update_points",
-    )(blended, background)
-
-
-def cut_kernel(order, states_ref, cut_ref):
-    patches, _, share = cut_ref.shape
-    region = states_ref.shape[1] // patches
+    )(blended, *pieces)
+
+
+def slab_sizes():
+    return lax.axis_size(SPACE[:2]), lax.axis_size(SPACE[2])
+
+
+def cut_kernel(slabs, states_ref, *cut_refs):
+    share = cut_refs[0].shape[2]
+    near = len(cut_refs)
+    region = states_ref.shape[1] // (slabs * near)
     offset = lax.axis_index("boot") * share
-    for place, patch in enumerate(order):
-        begin = pl.multiple_of(patch * region + offset, LANES)
-        cut_ref[place] = states_ref[:, pl.ds(begin, share)]
-
-
-def cut_share(states, order, share):
-    own_members, patches = states.shape[0], len(order)
-    return pl.pallas_call(
-        functools.partial(cut_kernel, order),
-        out_shape=jax.ShapeDtypeStruct((patches, own_members, share), BF16),
+    slab, place = lax.axis_index(SPACE[:2]), lax.axis_index(SPACE[2])
+    for step, cut_ref in enumerate(cut_refs):
+        for far in range(slabs):
+            patch = lax.rem(slab + far, slabs) * near + lax.rem(place + step, near)
+            begin = pl.multiple_of(patch * region + offset, LANES)
+            cut_ref[far] = states_ref[:, pl.ds(begin, share)]
+
+
+def cut_share(states, share):
+    slabs, near = slab_sizes()
+    own_members = states.shape[0]
+    return pl.pallas_call(
+        functools.partial(cut_kernel, slabs),
+        out_shape=[jax.ShapeDtypeStruct((slabs, own_members, share), BF16)] * near,
         compiler_params=pltpu.CompilerParams(vmem_limit_bytes=16 * MEBI),
         cost_estimate=pl.CostEstimate(
-            flops=0, bytes_accessed=4 * patches * own_members * share, transcendentals=0
+            flops=0, bytes_accessed=4 * slabs * near * own_members * share, transcendentals=0
         ),
         name="cut_share",
     )(states)
 
 
-def place_kernel(order, pieces_ref, whole_ref):
+def regroup_kernel(near, *refs):
+    for far, group_ref in enumerate(refs[near:]):
+        for step, cut_ref in enumerate(refs[:near]):
+            group_ref[step] = cut_ref[far]
+
+
+def regroup(cuts):
+    slabs, own_members, share = cuts[0].shape
+    return pl.pallas_call(
+        functools.partial(regroup_kernel, len(cuts)),
+        out_shape=[jax.ShapeDtypeStruct((len(cuts), own_members, share), BF16)] * slabs,
+        compiler_params=pltpu.CompilerParams(vmem_limit_bytes=16 * MEBI),
+        cost_estimate=pl.CostEstimate(
+            flops=0, bytes_accessed=4 * len(cuts) * slabs * own_members * share, transcendentals=0
+        ),
+        name="regroup",
+    )(*cuts)
+
+
+def shift_all(pieces, axes):
+    count = len(pieces)
+    return [pieces[0]] + [
+        lax.ppermute(pieces[step], axes, [(d, (d + step) % count) for d in range(count)])
+        for step in range(1, count)
+    ]
+
+
+def place_kernel(order, pieces_ref, whole_ref, held_ref, sems):
     groups, _, _, share = pieces_ref.shape
-    for place, patch in enumerate(order):
-        for group in range(groups):
-            begin = (patch * groups + group) * share
-            whole_ref[:, begin : begin + share] = pieces_ref[group, place]
+    steps = sems.shape[0]
+    width = held_ref.shape[1] // steps
+    copies = []
+    for step in range(steps):
+        for patch in range(step * len(order) // steps, (step + 1) * len(order) // steps):
+            for group in range(groups):
+                begin = (patch * groups + group) * share
+                held_ref[:, begin : begin + share] = pieces_ref[group, order.index(patch)]
+        columns = slice(step * width, (step + 1) * width)
+        copies.append(
+            pltpu.make_async_copy(held_ref.at[:, columns], whole_ref.at[:, columns], sems.at[step])
+        )
+        copies[step].start()
+    for copy in copies:
+        copy.wait()
 
 
 def place_pieces(pieces, order):
@@ -438,7 +491,9 @@
     points = groups * patches * share
     return pl.pallas_call(
         functools.partial(place_kernel, order),
+        out_specs=pl.BlockSpec(memory_space=pl.ANY),
         out_shape=jax.ShapeDtypeStruct((own_members, points), BF16),
+        scratch_shapes=[pltpu.VMEM((own_members, points), BF16), pltpu.SemaphoreType.DMA((4,))],
         compiler_params=pltpu.CompilerParams(vmem_limit_bytes=16 * MEBI),
         cost_estimate=pl.CostEstimate(
             flops=0, bytes_accessed=4 * own_members * points, transcendentals=0
@@ -489,14 +544,15 @@
         slot_share,
         groups,
     )
-    own_points = cut_share(background_states, order, share)
-    own_rows, own_points = lax.optimization_barrier((exchange(slots), own_points))
+    slots, background_states = lax.optimization_barrier((slots, background_states))
+    by_slab = regroup(shift_all(cut_share(background_states, share), SPACE[2]))
+    own_rows, by_slab = lax.optimization_barrier((exchange(slots), by_slab))
     other_rows = swap_shares(own_rows)
-    own_points = exchange(own_points).reshape(-1, share)
+    points_by_slab = shift_all(by_slab, SPACE[:2])
 
     own = own_gram(own_rows, measurement_anomaly_matrix.shape[1])
     blended = patch_weights(own, other_rows)
-    analysis = update_points(blended, own_points, order)
+    analysis = update_points(blended, points_by_slab, order)
     analysis = exchange(analysis.reshape(-1, own_members, share), ("boot",) + PARTNERS)
     return place_pieces(analysis.reshape(groups, device_count, own_members, share), order)
 

time: 119 us -> 122 us (1.025)
  starting transfers between devices: 12.5 us -> 17.4 us
  waiting for transfers between devices: 33.5 us -> 29.5 us
  blocking collectives: 52.3 us -> 55.5 us
    all_to_all x2 -> x1, waiting for transfers between devices: 19.8 us -> 0.49 us  [exchange(): return lax.all_to_all(blocks, axes, split_axis=0, concat_axis=0, tiled=True)]
    ppermute x0 -> x6, waiting for transfers between devices: none -> 15.9 us  [shift_all(): lax.ppermute(pieces[step], axes, [(d, (d + step) % count) for d in range(...]
    ppermute x0 -> x6, starting transfers between devices: none -> 8.52 us  [shift_all(): lax.ppermute(pieces[step], axes, [(d, (d + step) % count) for d in range(...]
    all_to_all x2 -> x1, starting transfers between devices: 11.1 us -> 7.4 us  [exchange(): return lax.all_to_all(blocks, axes, split_axis=0, concat_axis=0, tiled=True)]
    all_to_all x1, blocking collectives: 52.3 us -> 55.5 us  [exchange(): return lax.all_to_all(blocks, axes, split_axis=0, concat_axis=0, tiled=True)]
    pallas_call x2 -> x3, Pallas kernels: 2.49 us -> 1.52 us  [the longest x1 1.38 us: place_pieces(): pl.pallas_call(functools.partial(place_kernel, order), out_specs=pl.Block...]
  transfers between devices with their start and end apart: 3 -> 8, of which waited for: 3 -> 5; matrix products, arithmetic and copies ran while one was open for 0% -> 0% of each run, Pallas kernels for 11% -> 10%
where the time goes in v15:
time: 122 us
  blocking collectives  55.5 us (45%)
  waiting for transfers between devices  29.5 us (24%)
  Pallas kernels  17.6 us (14%)
  starting transfers between devices  17.4 us (14%)
  local copies, waits for them, and re-layouts  1.59 us (1%)
    all_to_all x1, blocking collectives, exchange(): return lax.all_to_all(blocks, axes, split_axis=0, concat_axis=0, tiled=True)  55.5 us
    ppermute x6, waiting for transfers between devices, shift_all(): lax.ppermute(pieces[step], axes, [(d, (d + step) % count) for d in range(...  15.9 us
    ppermute x1, waiting for transfers between devices, swap_shares(): lax.ppermute(own, 'boot', [(g, (g - turn) % groups) for g in range(groups)])  13.1 us
    pallas_call x1, Pallas kernels, patch_weights(): pl.pallas_call(weights_kernel, out_shape=jax.ShapeDtypeStruct((groups, me...  11 us
    ppermute x6, starting transfers between devices, shift_all(): lax.ppermute(pieces[step], axes, [(d, (d + step) % count) for d in range(...  8.52 us
    all_to_all x1, starting transfers between devices, exchange(): return lax.all_to_all(blocks, axes, split_axis=0, concat_axis=0, tiled=True)  7.4 us
    pallas_call x1, Pallas kernels, pack(): pl.pallas_call(functools.partial(pack_kernel, groups, order), out_shape=j...  2.75 us
  transfers between devices with their start and end apart: 8, of which 5 were waited for; matrix products, arithmetic and copies ran while one was open for 0% of the time, Pallas kernels for 10%

profile of v15, /device:TPU:0, one launch (start us, length us, event | category | flops | bytes accessed | tf_op | source)
XLA Modules:
  0.0 121.7 jit_solution(4270386237833964456)
XLA Ops:
  0.0 2.7 %pack_rows.1 = bf16[16,8,3200]{2,1,0:T(8,128)(2,1)} custom-call(s32[2,384]{1,0:T(2,128)} %bitcast.6, s32[2,384]{1,0:T(2,128)} %bitcast.7, s32[384]{0:T(512)} %refs_2_.1, f32[384]{0:T(512)} %refs_3_.1, bf16[384]{0:T(512)(128)(2,1)} %refs_4_.1, bf16[384,512]{1,0:T(8,128)(2,1)} %refs_5_.1), custom_call_target="tpu_custom_call" | custom-call | flops 301989888 | bytes 1179648 | tf_op jit(solution)/shard_map/pack_rows/pallas_call | solution.py:107
  2.8 7.4 %all-to-all-start = ((bf16[16,8,3200]{2,1,0:T(8,128)(2,1)}), bf16[16,8,3200]{2,1,0:T(8,128)(2,1)S(1)}, u32[]{:S(2)}, u32[]{:S(2)}) async-start(bf16[16,8,3200]{2,1,0:T(8,128)(2,1)} %pack_rows.1), calls=%async_computation | async-start | bytes 1638400 | tf_op jit(solution)/shard_map/all_to_all | solution.py:506
  10.2 0.0 copy-start
  10.2 1.6 %copy-done = bf16[32,32768]{1,0:T(8,128)(2,1)S(1)} copy-done((bf16[32,32768]{1,0:T(8,128)(2,1)S(1)}, bf16[32,32768]{1,0:T(8,128)(2,1)}, u32[]{:S(2)}) %copy-start) | copy-done | bytes 2097176
  11.8 0.1 cut_share.1
  11.8 0.5 collective-permute-start
  12.3 1.7 %collective-permute-start.1 = (bf16[4,32,1024]{2,1,0:T(8,128)(2,1)S(1)}, bf16[4,32,1024]{2,1,0:T(8,128)(2,1)S(1)}, u32[]{:S(2)}, u32[]{:S(2)}) collective-permute-start(bf16[4,32,1024]{2,1,0:T(8,128)(2,1)S(1)} %get-tuple-element.30), channel_id=1, source_target_pairs={{0,2},{1,3},{2,0},{3,1},{4,6},{5,7},{6,4},{7,5},{8,10},{9,11},{10,... | collective-permute-start | bytes 786440 | tf_op jit(solution)/shard_map/ppermute | solution.py:465
  14.0 1.3 %collective-permute-start.2 = (bf16[4,32,1024]{2,1,0:T(8,128)(2,1)S(1)}, bf16[4,32,1024]{2,1,0:T(8,128)(2,1)S(1)}, u32[]{:S(2)}, u32[]{:S(2)}) collective-permute-start(bf16[4,32,1024]{2,1,0:T(8,128)(2,1)S(1)} %get-tuple-element.31), channel_id=1, source_target_pairs={{0,3},{1,0},{2,1},{3,2},{4,7},{5,4},{6,5},{7,6},{8,11},{9,8},{10,9... | collective-permute-start | bytes 786440 | tf_op jit(solution)/shard_map/ppermute | solution.py:465
  15.3 11.1 %collective-permute-done.refs_1_ = bf16[4,32,1024]{2,1,0:T(8,128)(2,1)S(1)} collective-permute-done((bf16[4,32,1024]{2,1,0:T(8,128)(2,1)S(1)}, bf16[4,32,1024]{2,1,0:T(8,128)(2,1)S(1)}, u32[]{:S(2)}, u32[]{:S(2)}) %collective-permute-start) | collective-permute-done | bytes 262176 | tf_op jit(solution)/shard_map/ppermute | solution.py:465
  26.4 0.9 collective-permute-done.1.refs_2_
  27.3 3.9 %collective-permute-done.2.refs_3_ = bf16[4,32,1024]{2,1,0:T(8,128)(2,1)S(1)} collective-permute-done((bf16[4,32,1024]{2,1,0:T(8,128)(2,1)S(1)}, bf16[4,32,1024]{2,1,0:T(8,128)(2,1)S(1)}, u32[]{:S(2)}, u32[]{:S(2)}) %collective-permute-start.2) | collective-permute-done | bytes 262176 | tf_op jit(solution)/shard_map/ppermute | solution.py:465
  31.2 0.1 regroup.1
  31.3 0.5 all-to-all-done.rows_ref
  31.7 1.5 %collective-permute-start.3 = (bf16[16,8,3200]{2,1,0:T(8,128)(2,1)S(1)}, bf16[16,8,3200]{2,1,0:T(8,128)(2,1)S(1)}, u32[]{:S(2)}, u32[]{:S(2)}) collective-permute-start(bf16[16,8,3200]{2,1,0:T(8,128)(2,1)S(1)} %all-to-all-done.rows_ref), channel_id=1, source_target_pairs={{0,16},{16,0},{1,17},{17,1},{2,18},{18,2},{3,19},{19,3},{4,20},{20... | collective-permute-start | bytes 2457608 | tf_op jit(solution)/shard_map/ppermute | solution.py:512
  33.2 1.1 collective-permute-start.4
  34.3 2.6 %collective-permute-start.5 = (bf16[4,32,1024]{2,1,0:T(8,128)(2,1)S(1)}, bf16[4,32,1024]{2,1,0:T(8,128)(2,1)S(1)}, u32[]{:S(2)}, u32[]{:S(2)}) collective-permute-start(bf16[4,32,1024]{2,1,0:T(8,128)(2,1)S(1)} %get-tuple-element.45), channel_id=1, source_target_pairs={{0,8},{4,12},{8,0},{12,4},{1,9},{5,13},{9,1},{13,5},{2,10},{6,14},... | collective-permute-start | bytes 786440 | tf_op jit(solution)/shard_map/ppermute | solution.py:465
  36.8 1.5 %collective-permute-start.6 = (bf16[4,32,1024]{2,1,0:T(8,128)(2,1)S(1)}, bf16[4,32,1024]{2,1,0:T(8,128)(2,1)S(1)}, u32[]{:S(2)}, u32[]{:S(2)}) collective-permute-start(bf16[4,32,1024]{2,1,0:T(8,128)(2,1)S(1)} %get-tuple-element.46), channel_id=1, source_target_pairs={{0,12},{4,0},{8,4},{12,8},{1,13},{5,1},{9,5},{13,9},{2,14},{6,2},{... | collective-permute-start | bytes 786440 | tf_op jit(solution)/shard_map/ppermute | solution.py:465
  38.3 0.9 own_gram.1
  39.2 13.1 %collective-permute-done.3.refs_6_ = bf16[16,8,3200]{2,1,0:T(8,128)(2,1)S(1)} collective-permute-done((bf16[16,8,3200]{2,1,0:T(8,128)(2,1)S(1)}, bf16[16,8,3200]{2,1,0:T(8,128)(2,1)S(1)}, u32[]{:S(2)}, u32[]{:S(2)}) %collective-permute-start.3) | collective-permute-done | bytes 819232 | tf_op jit(solution)/shard_map/ppermute | solution.py:512
  52.4 11.0 %patch_weights.1.blended_ref = bf16[2,512,512]{2,1,0:T(8,128)(2,1)S(1)} custom-call(f32[512,256]{1,0:T(8,128)S(1)} %get-tuple-element.37.refs_0_, f32[256,256]{1,0:T(8,128)S(1)} %get-tuple-element.38.refs_1_, f32[1,512]{1,0:T(1,128)S(1)} %get-tuple-element.39.refs_2_, f32[128,128]{1,0:T(8,128)S(1)} %get-tuple-element.40.refs_3_, ...), custom_call_target="tpu_custom_call" | custom-call | flops 2147483648 | bytes 2097152 | tf_op jit(solution)/shard_map/patch_weights/pallas_call | solution.py:352
  63.3 0.0 collective-permute-done.4.refs_1_
  63.3 0.0 collective-permute-done.5.refs_2_
  63.4 0.0 collective-permute-done.6.refs_3_
  63.4 1.5 %update_points.1 = bf16[2,512,1024]{2,1,0:T(8,128)(2,1)S(1)} custom-call(bf16[2,512,512]{2,1,0:T(8,128)(2,1)S(1)} %patch_weights.1.blended_ref, bf16[4,32,1024]{2,1,0:T(8,128)(2,1)S(1)} %get-tuple-element.43.refs_0_, bf16[4,32,1024]{2,1,0:T(8,128)(2,1)S(1)} %collective-permute-done.4.refs_1_, bf16[4,32,1024]{2,1,0:T(8,128)(2,1)S(1)} %collective-permute-done.5.refs_2_, ...), custom_call_target="tpu_custom_call" | custom-call | flops 1073741824 | bytes 3145728 | tf_op jit(solution)/shard_map/update_points/pallas_call | solution.py:398
  64.9 55.5 %all_to_all.10 = bf16[32,32,1024]{2,1,0:T(8,128)(2,1)S(1)} all-to-all(bf16[32,32,1024]{2,1,0:T(8,128)(2,1)S(1)} %bitcast.4), channel_id=1, replica_groups=mesh['boot'=2,'za'=2,'zb'=2,'near'=4] {'boot','near','zb','za'}, dimensions={0} | all-to-all | bytes 4194304 | tf_op jit(solution)/shard_map/all_to_all | solution.py:506
  120.3 1.4 %place_pieces.1 = bf16[32,32768]{1,0:T(8,128)(2,1)} custom-call(bf16[2,16,32,1024]{3,2,1,0:T(8,128)(2,1)S(1)} %bitcast.5), custom_call_target="tpu_custom_call" | custom-call | bytes 4194304 | tf_op jit(solution)/shard_map/place_pieces/pallas_call | solution.py:492
Async XLA Ops:
  2.8 29.0 %all-to-all-start = ((bf16[16,8,3200]{2,1,0:T(8,128)(2,1)}), bf16[16,8,3200]{2,1,0:T(8,128)(2,1)S(1)}, u32[]{:S(2)}, u32[]{:S(2)}) async-start(bf16[16,8,3200]{2,1,0:T(8,128)(2,1)} %pack_rows.1), calls=%async_computation | async-start | bytes 1638400 | tf_op jit(solution)/shard_map/all_to_all | solution.py:506
  10.2 1.6 %copy-start = (bf16[32,32768]{1,0:T(8,128)(2,1)S(1)}, bf16[32,32768]{1,0:T(8,128)(2,1)}, u32[]{:S(2)}) copy-start(bf16[32,32768]{1,0:T(8,128)(2,1)} %states_ref) | copy-start | bytes 6291460
  11.8 14.5 %collective-permute-start = (bf16[4,32,1024]{2,1,0:T(8,128)(2,1)S(1)}, bf16[4,32,1024]{2,1,0:T(8,128)(2,1)S(1)}, u32[]{:S(2)}, u32[]{:S(2)}) collective-permute-start(bf16[4,32,1024]{2,1,0:T(8,128)(2,1)S(1)} %get-tuple-element.29), channel_id=1, source_target_pairs={{0,1},{1,2},{2,3},{3,0},{4,5},{5,6},{6,7},{7,4},{8,9},{9,10},{10,1... | collective-permute-start | bytes 786440 | tf_op jit(solution)/shard_map/ppermute | solution.py:465
  12.3 15.0 %collective-permute-start.1 = (bf16[4,32,1024]{2,1,0:T(8,128)(2,1)S(1)}, bf16[4,32,1024]{2,1,0:T(8,128)(2,1)S(1)}, u32[]{:S(2)}, u32[]{:S(2)}) collective-permute-start(bf16[4,32,1024]{2,1,0:T(8,128)(2,1)S(1)} %get-tuple-element.30), channel_id=1, source_target_pairs={{0,2},{1,3},{2,0},{3,1},{4,6},{5,7},{6,4},{7,5},{8,10},{9,11},{10,... | collective-permute-start | bytes 786440 | tf_op jit(solution)/shard_map/ppermute | solution.py:465
  14.0 17.2 %collective-permute-start.2 = (bf16[4,32,1024]{2,1,0:T(8,128)(2,1)S(1)}, bf16[4,32,1024]{2,1,0:T(8,128)(2,1)S(1)}, u32[]{:S(2)}, u32[]{:S(2)}) collective-permute-start(bf16[4,32,1024]{2,1,0:T(8,128)(2,1)S(1)} %get-tuple-element.31), channel_id=1, source_target_pairs={{0,3},{1,0},{2,1},{3,2},{4,7},{5,4},{6,5},{7,6},{8,11},{9,8},{10,9... | collective-permute-start | bytes 786440 | tf_op jit(solution)/shard_map/ppermute | solution.py:465
  31.7 20.6 %collective-permute-start.3 = (bf16[16,8,3200]{2,1,0:T(8,128)(2,1)S(1)}, bf16[16,8,3200]{2,1,0:T(8,128)(2,1)S(1)}, u32[]{:S(2)}, u32[]{:S(2)}) collective-permute-start(bf16[16,8,3200]{2,1,0:T(8,128)(2,1)S(1)} %all-to-all-done.rows_ref), channel_id=1, source_target_pairs={{0,16},{16,0},{1,17},{17,1},{2,18},{18,2},{3,19},{19,3},{4,20},{20... | collective-permute-start | bytes 2457608 | tf_op jit(solution)/shard_map/ppermute | solution.py:512
  33.2 30.1 %collective-permute-start.4 = (bf16[4,32,1024]{2,1,0:T(8,128)(2,1)S(1)}, bf16[4,32,1024]{2,1,0:T(8,128)(2,1)S(1)}, u32[]{:S(2)}, u32[]{:S(2)}) collective-permute-start(bf16[4,32,1024]{2,1,0:T(8,128)(2,1)S(1)} %get-tuple-element.44), channel_id=1, source_target_pairs={{0,4},{4,8},{8,12},{12,0},{1,5},{5,9},{9,13},{13,1},{2,6},{6,10},{... | collective-permute-start | bytes 786440 | tf_op jit(solution)/shard_map/ppermute | solution.py:465
  34.3 29.1 %collective-permute-start.5 = (bf16[4,32,1024]{2,1,0:T(8,128)(2,1)S(1)}, bf16[4,32,1024]{2,1,0:T(8,128)(2,1)S(1)}, u32[]{:S(2)}, u32[]{:S(2)}) collective-permute-start(bf16[4,32,1024]{2,1,0:T(8,128)(2,1)S(1)} %get-tuple-element.45), channel_id=1, source_target_pairs={{0,8},{4,12},{8,0},{12,4},{1,9},{5,13},{9,1},{13,5},{2,10},{6,14},... | collective-permute-start | bytes 786440 | tf_op jit(solution)/shard_map/ppermute | solution.py:465
  36.8 26.5 %collective-permute-start.6 = (bf16[4,32,1024]{2,1,0:T(8,128)(2,1)S(1)}, bf16[4,32,1024]{2,1,0:T(8,128)(2,1)S(1)}, u32[]{:S(2)}, u32[]{:S(2)}) collective-permute-start(bf16[4,32,1024]{2,1,0:T(8,128)(2,1)S(1)} %get-tuple-element.46), channel_id=1, source_target_pairs={{0,12},{4,0},{8,4},{12,8},{1,13},{5,1},{9,5},{13,9},{2,14},{6,2},{... | collective-permute-start | bytes 786440 | tf_op jit(solution)/shard_map/ppermute | solution.py:465

commit v16 on v14

--- a/solution.py
+++ b/solution.py
@@ -384,7 +384,8 @@
             update = jnp.concatenate(
                 [update[holder * rows : (holder + 1) * rows, :] for holder in order], axis=0
             )
-            analysis_ref[group, :, columns] = update.astype(BF16)
+            update = update.astype(BF16).reshape(len(order), rows, tile)
+            analysis_ref[:, group, :, columns] = update
 
 
 def update_points(blended, background, order):
@@ -392,7 +393,9 @@
     members, points = background.shape
     return pl.pallas_call(
         functools.partial(update_kernel, order),
-        out_shape=jax.ShapeDtypeStruct((groups, members, points), BF16),
+        out_shape=jax.ShapeDtypeStruct(
+            (len(order), groups, members // len(order), points), BF16
+        ),
         compiler_params=pltpu.CompilerParams(vmem_limit_bytes=16 * MEBI),
         cost_estimate=pl.CostEstimate(
             flops=2 * groups * members * members * points,
@@ -425,20 +428,33 @@
     )(states)
 
 
-def place_kernel(order, pieces_ref, whole_ref):
-    groups, _, _, share = pieces_ref.shape
-    for place, patch in enumerate(order):
-        for group in range(groups):
-            begin = (patch * groups + group) * share
-            whole_ref[:, begin : begin + share] = pieces_ref[group, place]
+def place_kernel(order, pieces_ref, whole_ref, held_ref, sems):
+    groups, share = pieces_ref.shape[1], pieces_ref.shape[3]
+    steps = sems.shape[0]
+    width = held_ref.shape[1] // steps
+    copies = []
+    for step in range(steps):
+        for patch in range(step * len(order) // steps, (step + 1) * len(order) // steps):
+            for group in range(groups):
+                begin = (patch * groups + group) * share
+                held_ref[:, begin : begin + share] = pieces_ref[order.index(patch), group]
+        columns = slice(step * width, (step + 1) * width)
+        copies.append(
+            pltpu.make_async_copy(held_ref.at[:, columns], whole_ref.at[:, columns], sems.at[step])
+        )
+        copies[step].start()
+    for copy in copies:
+        copy.wait()
 
 
 def place_pieces(pieces, order):
-    groups, patches, own_members, share = pieces.shape
+    patches, groups, own_members, share = pieces.shape
     points = groups * patches * share
     return pl.pallas_call(
         functools.partial(place_kernel, order),
+        out_specs=pl.BlockSpec(memory_space=pl.ANY),
         out_shape=jax.ShapeDtypeStruct((own_members, points), BF16),
+        scratch_shapes=[pltpu.VMEM((own_members, points), BF16), pltpu.SemaphoreType.DMA((4,))],
         compiler_params=pltpu.CompilerParams(vmem_limit_bytes=16 * MEBI),
         cost_estimate=pl.CostEstimate(
             flops=0, bytes_accessed=4 * own_members * points, transcendentals=0
@@ -497,8 +513,8 @@
     own = own_gram(own_rows, measurement_anomaly_matrix.shape[1])
     blended = patch_weights(own, other_rows)
     analysis = update_points(blended, own_points, order)
-    analysis = exchange(analysis.reshape(-1, own_members, share), ("boot",) + PARTNERS)
-    return place_pieces(analysis.reshape(groups, device_count, own_members, share), order)
+    analysis = exchange(analysis.reshape(-1, own_members, share), PARTNERS + ("boot",))
+    return place_pieces(analysis.reshape(device_count, groups, own_members, share), order)
 
 
 def solution(mesh):

time: 119 us -> 119 us (level)
  no operation moved by 1% of the time
where the time goes in v16:
time: 119 us; the launch traced here: 118 us
  blocking collectives  51.8 us (44%)
  waiting for transfers between devices  33.5 us (28%)
  Pallas kernels  18.6 us (16%)
  starting transfers between devices  12.5 us (11%)
  local copies, waits for them, and re-layouts  1.59 us (1%)
    all_to_all x1, blocking collectives, exchange(): return lax.all_to_all(blocks, axes, split_axis=0, concat_axis=0, tiled=True)  51.8 us
    all_to_all x2, waiting for transfers between devices, exchange(): return lax.all_to_all(blocks, axes, split_axis=0, concat_axis=0, tiled=True)  19.8 us
    ppermute x1, waiting for transfers between devices, swap_shares(): lax.ppermute(own, 'boot', [(g, (g - turn) % groups) for g in range(groups)])  13.7 us
    all_to_all x2, starting transfers between devices, exchange(): return lax.all_to_all(blocks, axes, split_axis=0, concat_axis=0, tiled=True)  11.1 us
    pallas_call x1, Pallas kernels, patch_weights(): pl.pallas_call(weights_kernel, out_shape=jax.ShapeDtypeStruct((groups, me...  11 us
    pallas_call x1, Pallas kernels, pack(): pl.pallas_call(functools.partial(pack_kernel, groups, order), out_shape=j...  2.77 us
  transfers between devices with their start and end apart: 3, of which 3 were waited for; matrix products, arithmetic and copies ran while one was open for 0% of the time, Pallas kernels for 11%

profile of v16, /device:TPU:0, one launch (start us, length us, event | category | flops | bytes accessed | tf_op | source)
XLA Modules:
  0.0 118.0 jit_solution(3502012249339485789)
XLA Ops:
  0.0 2.8 %pack_rows.1 = bf16[16,8,3200]{2,1,0:T(8,128)(2,1)} custom-call(s32[2,384]{1,0:T(2,128)} %bitcast.8, s32[2,384]{1,0:T(2,128)} %bitcast.9, s32[384]{0:T(512)} %refs_2_.1, f32[384]{0:T(512)} %refs_3_.1, bf16[384]{0:T(512)(128)(2,1)} %refs_4_.1, bf16[384,512]{1,0:T(8,128)(2,1)} %refs_5_.1), custom_call_target="tpu_custom_call" | custom-call | flops 301989888 | bytes 1179648 | tf_op jit(solution)/shard_map/pack_rows/pallas_call | solution.py:107
  2.8 7.4 %all-to-all-start = ((bf16[16,8,3200]{2,1,0:T(8,128)(2,1)}), bf16[16,8,3200]{2,1,0:T(8,128)(2,1)S(1)}, u32[]{:S(2)}, u32[]{:S(2)}) async-start(bf16[16,8,3200]{2,1,0:T(8,128)(2,1)} %pack_rows.1), calls=%async_computation | async-start | bytes 1638400 | tf_op jit(solution)/shard_map/all_to_all | solution.py:467
  10.2 0.0 copy-start
  10.2 1.6 %copy-done = bf16[32,32768]{1,0:T(8,128)(2,1)S(1)} copy-done((bf16[32,32768]{1,0:T(8,128)(2,1)S(1)}, bf16[32,32768]{1,0:T(8,128)(2,1)}, u32[]{:S(2)}) %copy-start) | copy-done | bytes 2097176
  11.8 1.0 cut_share.1
  12.8 18.9 %all-to-all-done.rows_ref = bf16[16,8,3200]{2,1,0:T(8,128)(2,1)S(1)} async-done(((bf16[16,8,3200]{2,1,0:T(8,128)(2,1)}), bf16[16,8,3200]{2,1,0:T(8,128)(2,1)S(1)}, u32[]{:S(2)}, u32[]{:S(2)}) %all-to-all-start) | async-done | bytes 819232 | tf_op jit(solution)/shard_map/all_to_all | solution.py:467
  31.8 1.5 %collective-permute-start = (bf16[16,8,3200]{2,1,0:T(8,128)(2,1)S(1)}, bf16[16,8,3200]{2,1,0:T(8,128)(2,1)S(1)}, u32[]{:S(2)}, u32[]{:S(2)}) collective-permute-start(bf16[16,8,3200]{2,1,0:T(8,128)(2,1)S(1)} %all-to-all-done.rows_ref), channel_id=1, source_target_pairs={{0,16},{16,0},{1,17},{17,1},{2,18},{18,2},{3,19},{19,3},{4,20},{20... | collective-permute-start | bytes 2457608 | tf_op jit(solution)/shard_map/ppermute | solution.py:473
  33.3 3.7 %all-to-all-start.1 = ((bf16[16,32,1024]{2,1,0:T(8,128)(2,1)}), bf16[16,32,1024]{2,1,0:T(8,128)(2,1)S(1)}, u32[]{:S(2)}, u32[]{:S(2)}) async-start(bf16[16,32,1024]{2,1,0:T(8,128)(2,1)} %cut_share.1), calls=%async_computation.1 | async-start | bytes 2097152 | tf_op jit(solution)/shard_map/all_to_all | solution.py:467
  36.9 0.9 own_gram.1
  37.8 13.7 %collective-permute-done.refs_6_ = bf16[16,8,3200]{2,1,0:T(8,128)(2,1)S(1)} collective-permute-done((bf16[16,8,3200]{2,1,0:T(8,128)(2,1)S(1)}, bf16[16,8,3200]{2,1,0:T(8,128)(2,1)S(1)}, u32[]{:S(2)}, u32[]{:S(2)}) %collective-permute-start) | collective-permute-done | bytes 819232 | tf_op jit(solution)/shard_map/ppermute | solution.py:473
  51.6 11.0 %patch_weights.1.blended_ref = bf16[2,512,512]{2,1,0:T(8,128)(2,1)S(1)} custom-call(f32[512,256]{1,0:T(8,128)S(1)} %get-tuple-element.14.refs_0_, f32[256,256]{1,0:T(8,128)S(1)} %get-tuple-element.15.refs_1_, f32[1,512]{1,0:T(1,128)S(1)} %get-tuple-element.16.refs_2_, f32[128,128]{1,0:T(8,128)S(1)} %get-tuple-element.17.refs_3_, ...), custom_call_target="tpu_custom_call" | custom-call | flops 21474836480 | bytes 2097152 | tf_op jit(solution)/shard_map/patch_weights/pallas_call | solution.py:352
  62.5 0.8 all-to-all-done.1
  63.3 1.5 %update_points.1 = bf16[16,2,32,1024]{3,2,1,0:T(8,128)(2,1)S(1)} custom-call(bf16[2,512,512]{2,1,0:T(8,128)(2,1)S(1)} %patch_weights.1.blended_ref, bf16[512,1024]{1,0:T(8,128)(2,1)S(1)} %bitcast.7), custom_call_target="tpu_custom_call" | custom-call | flops 1073741824 | bytes 3145728 | tf_op jit(solution)/shard_map/update_points/pallas_call | solution.py:394
  64.9 51.8 %all_to_all.15 = bf16[32,32,1024]{2,1,0:T(8,128)(2,1)S(1)} all-to-all(bf16[32,32,1024]{2,1,0:T(8,128)(2,1)S(1)} %bitcast.5), channel_id=1, replica_groups=mesh['boot'=2,'za'=2,'zb'=2,'near'=4] {'near','zb','za','boot'}, dimensions={0} | all-to-all | bytes 4194304 | tf_op jit(solution)/shard_map/all_to_all | solution.py:467
  116.7 1.4 %place_pieces.1 = bf16[32,32768]{1,0:T(8,128)(2,1)} custom-call(bf16[16,2,32,1024]{3,2,1,0:T(8,128)(2,1)S(1)} %bitcast.6), custom_call_target="tpu_custom_call" | custom-call | bytes 4194304 | tf_op jit(solution)/shard_map/place_pieces/pallas_call | solution.py:453
Async XLA Ops:
  2.8 29.0 %all-to-all-start = ((bf16[16,8,3200]{2,1,0:T(8,128)(2,1)}), bf16[16,8,3200]{2,1,0:T(8,128)(2,1)S(1)}, u32[]{:S(2)}, u32[]{:S(2)}) async-start(bf16[16,8,3200]{2,1,0:T(8,128)(2,1)} %pack_rows.1), calls=%async_computation | async-start | bytes 1638400 | tf_op jit(solution)/shard_map/all_to_all | solution.py:467
  10.2 1.6 %copy-start = (bf16[32,32768]{1,0:T(8,128)(2,1)S(1)}, bf16[32,32768]{1,0:T(8,128)(2,1)}, u32[]{:S(2)}) copy-start(bf16[32,32768]{1,0:T(8,128)(2,1)} %states_ref.1) | copy-start | bytes 6291460
  31.8 19.8 %collective-permute-start = (bf16[16,8,3200]{2,1,0:T(8,128)(2,1)S(1)}, bf16[16,8,3200]{2,1,0:T(8,128)(2,1)S(1)}, u32[]{:S(2)}, u32[]{:S(2)}) collective-permute-start(bf16[16,8,3200]{2,1,0:T(8,128)(2,1)S(1)} %all-to-all-done.rows_ref), channel_id=1, source_target_pairs={{0,16},{16,0},{1,17},{17,1},{2,18},{18,2},{3,19},{19,3},{4,20},{20... | collective-permute-start | bytes 2457608 | tf_op jit(solution)/shard_map/ppermute | solution.py:473
  33.3 30.1 %all-to-all-start.1 = ((bf16[16,32,1024]{2,1,0:T(8,128)(2,1)}), bf16[16,32,1024]{2,1,0:T(8,128)(2,1)S(1)}, u32[]{:S(2)}, u32[]{:S(2)}) async-start(bf16[16,32,1024]{2,1,0:T(8,128)(2,1)} %cut_share.1), calls=%async_computation.1 | async-start | bytes 2097152 | tf_op jit(solution)/shard_map/all_to_all | solution.py:467

commit v17 on v16

--- a/solution.py
+++ b/solution.py
@@ -10,7 +10,7 @@
 
 NS_STEPS = 6
 SPACE = ("za", "zb", "near")
-PARTNERS = ("near", "zb", "za")
+PARTNERS = ("near", "za", "zb")
 LANES = 128
 ROWS = 8
 MEBI = 1024 * 1024
@@ -20,7 +20,7 @@
 
 def partner_order(sizes):
     za, zb, near = sizes
-    return [(a * zb + b) * near + c for c in range(near) for b in range(zb) for a in range(za)]
+    return [(a * zb + b) * near + c for c in range(near) for a in range(za) for b in range(zb)]
 
 
 def pack_kernel(groups, order, *refs):

time: 119 us -> 120 us (level)
  no operation moved by 1% of the time
where the time goes in v17:
time: 120 us; the launch traced here: 119 us
  blocking collectives  52.2 us (44%)
  waiting for transfers between devices  34.4 us (29%)
  Pallas kernels  18.6 us (16%)
  starting transfers between devices  12.5 us (10%)
  local copies, waits for them, and re-layouts  1.59 us (1%)
    all_to_all x1, blocking collectives, exchange(): return lax.all_to_all(blocks, axes, split_axis=0, concat_axis=0, tiled=True)  52.2 us
    all_to_all x2, waiting for transfers between devices, exchange(): return lax.all_to_all(blocks, axes, split_axis=0, concat_axis=0, tiled=True)  20.7 us
    ppermute x1, waiting for transfers between devices, swap_shares(): lax.ppermute(own, 'boot', [(g, (g - turn) % groups) for g in range(groups)])  13.8 us
    all_to_all x2, starting transfers between devices, exchange(): return lax.all_to_all(blocks, axes, split_axis=0, concat_axis=0, tiled=True)  11.1 us
    pallas_call x1, Pallas kernels, patch_weights(): pl.pallas_call(weights_kernel, out_shape=jax.ShapeDtypeStruct((groups, me...  11 us
    pallas_call x1, Pallas kernels, pack(): pl.pallas_call(functools.partial(pack_kernel, groups, order), out_shape=j...  2.77 us
  transfers between devices with their start and end apart: 3, of which 3 were waited for; matrix products, arithmetic and copies ran while one was open for 0% of the time, Pallas kernels for 11%

profile of v17, /device:TPU:0, one launch (start us, length us, event | category | flops | bytes accessed | tf_op | source)
XLA Modules:
  0.0 119.4 jit_solution(7480823447918141746)
XLA Ops:
  0.0 2.8 %pack_rows.1 = bf16[16,8,3200]{2,1,0:T(8,128)(2,1)} custom-call(s32[2,384]{1,0:T(2,128)} %bitcast.8, s32[2,384]{1,0:T(2,128)} %bitcast.9, s32[384]{0:T(512)} %refs_2_.1, f32[384]{0:T(512)} %refs_3_.1, bf16[384]{0:T(512)(128)(2,1)} %refs_4_.1, bf16[384,512]{1,0:T(8,128)(2,1)} %refs_5_.1), custom_call_target="tpu_custom_call" | custom-call | flops 301989888 | bytes 1179648 | tf_op jit(solution)/shard_map/pack_rows/pallas_call | solution.py:107
  2.8 7.4 %all-to-all-start = ((bf16[16,8,3200]{2,1,0:T(8,128)(2,1)}), bf16[16,8,3200]{2,1,0:T(8,128)(2,1)S(1)}, u32[]{:S(2)}, u32[]{:S(2)}) async-start(bf16[16,8,3200]{2,1,0:T(8,128)(2,1)} %pack_rows.1), calls=%async_computation | async-start | bytes 1638400 | tf_op jit(solution)/shard_map/all_to_all | solution.py:467
  10.2 0.0 copy-start
  10.2 1.6 %copy-done = bf16[32,32768]{1,0:T(8,128)(2,1)S(1)} copy-done((bf16[32,32768]{1,0:T(8,128)(2,1)S(1)}, bf16[32,32768]{1,0:T(8,128)(2,1)}, u32[]{:S(2)}) %copy-start) | copy-done | bytes 2097176
  11.8 1.0 cut_share.1
  12.8 19.4 %all-to-all-done.rows_ref = bf16[16,8,3200]{2,1,0:T(8,128)(2,1)S(1)} async-done(((bf16[16,8,3200]{2,1,0:T(8,128)(2,1)}), bf16[16,8,3200]{2,1,0:T(8,128)(2,1)S(1)}, u32[]{:S(2)}, u32[]{:S(2)}) %all-to-all-start) | async-done | bytes 819232 | tf_op jit(solution)/shard_map/all_to_all | solution.py:467
  32.2 1.5 %collective-permute-start = (bf16[16,8,3200]{2,1,0:T(8,128)(2,1)S(1)}, bf16[16,8,3200]{2,1,0:T(8,128)(2,1)S(1)}, u32[]{:S(2)}, u32[]{:S(2)}) collective-permute-start(bf16[16,8,3200]{2,1,0:T(8,128)(2,1)S(1)} %all-to-all-done.rows_ref), channel_id=1, source_target_pairs={{0,16},{16,0},{1,17},{17,1},{2,18},{18,2},{3,19},{19,3},{4,20},{20... | collective-permute-start | bytes 2457608 | tf_op jit(solution)/shard_map/ppermute | solution.py:473
  33.7 3.7 %all-to-all-start.1 = ((bf16[16,32,1024]{2,1,0:T(8,128)(2,1)}), bf16[16,32,1024]{2,1,0:T(8,128)(2,1)S(1)}, u32[]{:S(2)}, u32[]{:S(2)}) async-start(bf16[16,32,1024]{2,1,0:T(8,128)(2,1)} %cut_share.1), calls=%async_computation.1 | async-start | bytes 2097152 | tf_op jit(solution)/shard_map/all_to_all | solution.py:467
  37.4 0.9 own_gram.1
  38.3 13.8 %collective-permute-done.refs_6_ = bf16[16,8,3200]{2,1,0:T(8,128)(2,1)S(1)} collective-permute-done((bf16[16,8,3200]{2,1,0:T(8,128)(2,1)S(1)}, bf16[16,8,3200]{2,1,0:T(8,128)(2,1)S(1)}, u32[]{:S(2)}, u32[]{:S(2)}) %collective-permute-start) | collective-permute-done | bytes 819232 | tf_op jit(solution)/shard_map/ppermute | solution.py:473
  52.1 11.0 %patch_weights.1.blended_ref = bf16[2,512,512]{2,1,0:T(8,128)(2,1)S(1)} custom-call(f32[512,256]{1,0:T(8,128)S(1)} %get-tuple-element.14.refs_0_, f32[256,256]{1,0:T(8,128)S(1)} %get-tuple-element.15.refs_1_, f32[1,512]{1,0:T(1,128)S(1)} %get-tuple-element.16.refs_2_, f32[128,128]{1,0:T(8,128)S(1)} %get-tuple-element.17.refs_3_, ...), custom_call_target="tpu_custom_call" | custom-call | flops 21474836480 | bytes 2097152 | tf_op jit(solution)/shard_map/patch_weights/pallas_call | solution.py:352
  63.0 1.3 %all-to-all-done.1 = bf16[16,32,1024]{2,1,0:T(8,128)(2,1)S(1)} async-done(((bf16[16,32,1024]{2,1,0:T(8,128)(2,1)}), bf16[16,32,1024]{2,1,0:T(8,128)(2,1)S(1)}, u32[]{:S(2)}, u32[]{:S(2)}) %all-to-all-start.1) | async-done | bytes 1048608 | tf_op jit(solution)/shard_map/all_to_all | solution.py:467
  64.3 1.5 %update_points.1 = bf16[16,2,32,1024]{3,2,1,0:T(8,128)(2,1)S(1)} custom-call(bf16[2,512,512]{2,1,0:T(8,128)(2,1)S(1)} %patch_weights.1.blended_ref, bf16[512,1024]{1,0:T(8,128)(2,1)S(1)} %bitcast.7), custom_call_target="tpu_custom_call" | custom-call | flops 1073741824 | bytes 3145728 | tf_op jit(solution)/shard_map/update_points/pallas_call | solution.py:394
  65.8 52.2 %all_to_all.15 = bf16[32,32,1024]{2,1,0:T(8,128)(2,1)S(1)} all-to-all(bf16[32,32,1024]{2,1,0:T(8,128)(2,1)S(1)} %bitcast.5), channel_id=1, replica_groups=mesh['boot'=2,'za'=2,'zb'=2,'near'=4] {'near','za','zb','boot'}, dimensions={0} | all-to-all | bytes 4194304 | tf_op jit(solution)/shard_map/all_to_all | solution.py:467
  118.0 1.4 %place_pieces.1 = bf16[32,32768]{1,0:T(8,128)(2,1)} custom-call(bf16[16,2,32,1024]{3,2,1,0:T(8,128)(2,1)S(1)} %bitcast.6), custom_call_target="tpu_custom_call" | custom-call | bytes 4194304 | tf_op jit(solution)/shard_map/place_pieces/pallas_call | solution.py:453
Async XLA Ops:
  2.8 29.5 %all-to-all-start = ((bf16[16,8,3200]{2,1,0:T(8,128)(2,1)}), bf16[16,8,3200]{2,1,0:T(8,128)(2,1)S(1)}, u32[]{:S(2)}, u32[]{:S(2)}) async-start(bf16[16,8,3200]{2,1,0:T(8,128)(2,1)} %pack_rows.1), calls=%async_computation | async-start | bytes 1638400 | tf_op jit(solution)/shard_map/all_to_all | solution.py:467
  10.2 1.6 %copy-start = (bf16[32,32768]{1,0:T(8,128)(2,1)S(1)}, bf16[32,32768]{1,0:T(8,128)(2,1)}, u32[]{:S(2)}) copy-start(bf16[32,32768]{1,0:T(8,128)(2,1)} %states_ref.1) | copy-start | bytes 6291460
  32.2 19.8 %collective-permute-start = (bf16[16,8,3200]{2,1,0:T(8,128)(2,1)S(1)}, bf16[16,8,3200]{2,1,0:T(8,128)(2,1)S(1)}, u32[]{:S(2)}, u32[]{:S(2)}) collective-permute-start(bf16[16,8,3200]{2,1,0:T(8,128)(2,1)S(1)} %all-to-all-done.rows_ref), channel_id=1, source_target_pairs={{0,16},{16,0},{1,17},{17,1},{2,18},{18,2},{3,19},{19,3},{4,20},{20... | collective-permute-start | bytes 2457608 | tf_op jit(solution)/shard_map/ppermute | solution.py:473
  33.7 30.6 %all-to-all-start.1 = ((bf16[16,32,1024]{2,1,0:T(8,128)(2,1)}), bf16[16,32,1024]{2,1,0:T(8,128)(2,1)S(1)}, u32[]{:S(2)}, u32[]{:S(2)}) async-start(bf16[16,32,1024]{2,1,0:T(8,128)(2,1)} %cut_share.1), calls=%async_computation.1 | async-start | bytes 2097152 | tf_op jit(solution)/shard_map/all_to_all | solution.py:467

commit v18 on v16

--- a/solution.py
+++ b/solution.py
@@ -50,12 +50,13 @@
     )
     rank = jnp.where(named, rank, -1.0)
 
-    begin = lax.axis_index("boot") * share
-    own_id = (lax.broadcasted_iota(jnp.int32, (share, count), 0) + begin).astype(F32)
-    picks = [
-        jnp.where(own_id == rank[patch : patch + 1, :], 1.0, 0.0) for patch in order
+    slots = groups * share
+    slot_id = lax.broadcasted_iota(jnp.int32, (slots, count), 0) + lax.axis_index("boot") * share
+    slot_id = jnp.where(slot_id < slots, slot_id, slot_id - slots).astype(F32)
+    named_by = [
+        jnp.where(slot_id == rank[patch : patch + 1, :], 1.0, 0.0) for patch in order
     ]
-    picks = jnp.concatenate(picks, axis=0).astype(BF16)
+    picks = jnp.concatenate([pick[0:share, :] for pick in named_by], axis=0).astype(BF16)
     copies[-1].wait()
     picked = jnp.dot(picks, rows_ref[...], preferred_element_type=F32)
     for patch in range(patches):
@@ -71,27 +72,23 @@
     weight = weight.astype(BF16).astype(F32)
     dep = dep_ref[...].astype(F32).reshape(1, count)
     by_patch = jnp.where(first, weight[0:1, :], jnp.where(second, weight[1:2, :], 0.0))
-    slot_id = lax.broadcasted_iota(jnp.int32, (groups * share, count), 0).astype(F32)
-    lane = lax.broadcasted_iota(jnp.int32, (groups * share, LANES), 1)
-    info = jnp.zeros((groups * share, LANES), F32)
-    for patch in range(patches):
-        pick = slot_id == rank[patch : patch + 1, :]
-        weight_col = jnp.sum(
-            jnp.where(pick, by_patch[patch : patch + 1, :], 0.0), axis=1, keepdims=True
-        )
-        dep_col = jnp.sum(jnp.where(pick, dep, 0.0), axis=1, keepdims=True)
-        info = jnp.where(lane == patch, weight_col, info)
-        info = jnp.where(lane == patches + patch, dep_col, info)
-    info_ref[...] = jnp.zeros((LANES, LANES), F32)
-    info_ref[0 : groups * share, :] = info
-    info = info_ref[...].T
-    tail_id = lax.broadcasted_iota(jnp.int32, (ROWS, LANES), 0)
+    info_ref[...] = jnp.zeros(info_ref.shape, F32)
+    info_ref[0:patches, :] = by_patch
+    info_ref[patches : patches + 1, :] = dep
+    info = jnp.dot(
+        jnp.concatenate(named_by, axis=0).astype(BF16),
+        info_ref[...].T.astype(BF16),
+        preferred_element_type=F32,
+    )
+    lane = lax.broadcasted_iota(jnp.int32, (ROWS, LANES), 1)
+    height = slots // ROWS
     for place, patch in enumerate(order):
-        tail = jnp.where(
-            tail_id == 0,
-            info[patch : patch + 1, :],
-            jnp.where(tail_id == 1, info[patches + patch : patches + patch + 1, :], 0.0),
-        )
+        tail = jnp.zeros((ROWS, LANES), F32)
+        for i in range(height):
+            begin = place * slots + i * ROWS
+            block = info[begin : begin + ROWS, :]
+            tail = jnp.where(lane == i, block[:, patch : patch + 1], tail)
+            tail = jnp.where(lane == height + i, block[:, patches : patches + 1], tail)
         tail_ref[place] = tail.astype(BF16)
     tails_out = pltpu.make_async_copy(tail_ref, slots_ref.at[:, :, width:], sems.at[7])
     tails_out.start()
@@ -113,7 +110,7 @@
         + [
             pltpu.VMEM((patches, ROWS, width), BF16),
             pltpu.VMEM((patches, ROWS, LANES), BF16),
-            pltpu.VMEM((LANES, LANES), F32),
+            pltpu.VMEM((LANES, count), F32),
             pltpu.SemaphoreType.DMA((len(operands) + 2,)),
         ],
         compiler_params=pltpu.CompilerParams(vmem_limit_bytes=64 * MEBI),
@@ -135,53 +132,53 @@
     return jnp.concatenate(blocks, axis=0)
 
 
-def slot_info(rows_ref, info_ref):
-    sources, _, width = rows_ref.shape
-    if 2 * sources < LANES:
-        info_ref[2 * sources :, :] = jnp.zeros((LANES - 2 * sources, LANES), F32)
-    for source in range(sources):
-        tail = rows_ref[source].astype(F32)[:, width - LANES :]
-        info_ref[source : source + 1, :] = tail[0:1, :]
-        info_ref[sources + source : sources + source + 1, :] = tail[1:2, :]
-    info_ref[...] = info_ref[...].T
-
-
-def scaled_rows(rows, info_ref, turn, sources):
-    share = rows.shape[0] // sources
-    begin = lax.rem(lax.axis_index("boot") + turn, lax.axis_size("boot")) * share
-    info = info_ref[pl.ds(pl.multiple_of(begin, ROWS), share), :]
-    blocks, drive = [], jnp.zeros((1, rows.shape[1]), F32)
-    for source in range(sources):
-        block = rows[source * share : (source + 1) * share, :]
-        block = (info[:, source : source + 1] * block).astype(BF16).astype(F32)
-        blocks.append(block)
-        dep_col = info[:, sources + source : sources + source + 1]
-        drive = drive + jnp.sum(dep_col * block, axis=0, keepdims=True)
-    return jnp.concatenate(blocks, axis=0).astype(BF16), drive
-
-
-def gram_kernel(rows_ref, right_ref, corner_ref, drive_ref, info_ref, ordered_ref, turned_ref):
+def slot_tails(rows_ref):
+    return [
+        rows_ref[source, :, rows_ref.shape[2] - LANES :].astype(F32)
+        for source in range(rows_ref.shape[0])
+    ]
+
+
+def scaled_rows(rows, tails, position, groups):
+    height = rows.shape[0] // len(tails) // ROWS
+    blocks, drive = [], jnp.zeros((ROWS, rows.shape[1]), F32)
+    for source, tail in enumerate(tails):
+        for i in range(height):
+            begin = (source * height + i) * ROWS
+            column = position * height + i
+            block = tail[:, column : column + 1] * rows[begin : begin + ROWS, :]
+            block = block.astype(BF16).astype(F32)
+            blocks.append(block)
+            column += groups * height
+            drive = drive + tail[:, column : column + 1] * block
+    return jnp.concatenate(blocks, axis=0).astype(BF16), jnp.sum(drive, axis=0, keepdims=True)
+
+
+def gram_kernel(groups, *refs):
+    rows_ref, right_ref, corner_ref, drive_ref, tails_ref, ordered_ref, turned_ref = refs
     members, half = right_ref.shape
-    slot_info(rows_ref, info_ref)
     rows = slot_rows(rows_ref, members)
     ordered_ref[...] = rows.astype(BF16)
     turned_ref[...] = rows.T.astype(BF16)
-    scaled, drive_ref[...] = scaled_rows(rows, info_ref, 0, rows_ref.shape[0])
+    tails = slot_tails(rows_ref)
+    for source, tail in enumerate(tails):
+        tails_ref[source] = tail
+    scaled, drive_ref[...] = scaled_rows(rows, tails, 0, groups)
     dot = functools.partial(jnp.dot, preferred_element_type=F32)
     right_ref[...] = dot(turned_ref[...], scaled[:, half:])
     corner_ref[...] = dot(turned_ref[0:half, :], scaled[:, 0:half])
 
 
-def own_gram(rows, members):
+def own_gram(rows, members, groups):
     sources, height, width = rows.shape
     slots = sources * height * ((width - LANES) // members)
     return pl.pallas_call(
-        gram_kernel,
+        functools.partial(gram_kernel, groups),
         out_shape=(
             jax.ShapeDtypeStruct((members, members // 2), F32),
             jax.ShapeDtypeStruct((members // 2, members // 2), F32),
             jax.ShapeDtypeStruct((1, members), F32),
-            jax.ShapeDtypeStruct((LANES, LANES), F32),
+            jax.ShapeDtypeStruct((sources, height, LANES), F32),
             jax.ShapeDtypeStruct((slots, members), BF16),
             jax.ShapeDtypeStruct((members, slots), BF16),
         ),
@@ -223,13 +220,11 @@
 
 
 def weights_kernel(*refs):
-    right_ref, corner_ref, drive_ref, own_info_ref, ordered_ref, turned_ref = refs[:6]
-    groups = (len(refs) - 6) // 10
+    right_ref, corner_ref, drive_ref, tails_ref, ordered_ref, turned_ref = refs[:6]
+    groups = (len(refs) - 6) // 9
     rows_refs, blended_ref = refs[6 : 5 + groups], refs[5 + groups]
-    info_refs = refs[6 + groups : 6 + 2 * groups]
-    chains = [refs[6 + 2 * groups + 8 * c : 14 + 2 * groups + 8 * c] for c in range(groups)]
+    chains = [refs[6 + groups + 8 * c : 14 + groups + 8 * c] for c in range(groups)]
     members, half = right_ref.shape
-    sources = rows_refs[0].shape[0] if rows_refs else 1
     row_id = lax.broadcasted_iota(jnp.int32, (members, members), 0)
     col_id = lax.broadcasted_iota(jnp.int32, (members, members), 1)
     identity = jnp.where(row_id == col_id, 1.0, 0.0)
@@ -268,11 +263,12 @@
             factor[:, 0:half] * corner + change_corner,
         )
 
-    infos = [own_info_ref] + list(info_refs[1:])
+    tails = [[tails_ref[source] for source in range(tails_ref.shape[0])]]
+    tails += [slot_tails(rows_ref) for rows_ref in rows_refs]
     rights, corners, drives = [right_ref[...]], [corner_ref[...]], [drive_ref[...]]
+    rows = ordered_ref[...].astype(F32)
     for chain in range(1, groups):
-        slot_info(rows_refs[chain - 1], infos[chain])
-        scaled, drive = scaled_rows(ordered_ref[...].astype(F32), infos[chain], 0, sources)
+        scaled, drive = scaled_rows(rows, tails[chain], groups - chain, groups)
         rights.append(dot(turned_ref[...], scaled[:, half:]))
         corners.append(dot(turned_ref[0:half, :], scaled[:, 0:half]))
         drives.append(drive)
@@ -280,7 +276,7 @@
         rows = slot_rows(rows_ref, members)
         turned = rows.T.astype(BF16)
         for chain in range(groups):
-            scaled, drive = scaled_rows(rows, infos[chain], turn, sources)
+            scaled, drive = scaled_rows(rows, tails[chain], (turn - chain) % groups, groups)
             rights[chain] = rights[chain] + dot(turned, scaled[:, half:])
             corners[chain] = corners[chain] + dot(turned[0:half, :], scaled[:, 0:half])
             drives[chain] = drives[chain] + drive
@@ -352,7 +348,7 @@
     return pl.pallas_call(
         weights_kernel,
         out_shape=jax.ShapeDtypeStruct((groups, members, members), BF16),
-        scratch_shapes=[pltpu.VMEM((LANES, LANES), F32)] * groups + chain * groups,
+        scratch_shapes=chain * groups,
         compiler_params=pltpu.CompilerParams(vmem_limit_bytes=(8 + 10 * groups) * MEBI),
         cost_estimate=pl.CostEstimate(
             flops=80 * groups * members * members * members,
@@ -510,7 +506,7 @@
     other_rows = swap_shares(own_rows)
     own_points = exchange(own_points).reshape(-1, share)
 
-    own = own_gram(own_rows, measurement_anomaly_matrix.shape[1])
+    own = own_gram(own_rows, measurement_anomaly_matrix.shape[1], groups)
     blended = patch_weights(own, other_rows)
     analysis = update_points(blended, own_points, order)
     analysis = exchange(analysis.reshape(-1, own_members, share), PARTNERS + ("boot",))

time: 119 us -> 119 us (level)
  no operation moved by 1% of the time
where the time goes in v18:
time: 119 us; the launch traced here: 118 us
  blocking collectives  51.8 us (44%)
  waiting for transfers between devices  33.5 us (28%)
  Pallas kernels  18.5 us (16%)
  starting transfers between devices  12.5 us (11%)
  local copies, waits for them, and re-layouts  1.59 us (1%)
    all_to_all x1, blocking collectives, exchange(): return lax.all_to_all(blocks, axes, split_axis=0, concat_axis=0, tiled=True)  51.8 us
    all_to_all x2, waiting for transfers between devices, exchange(): return lax.all_to_all(blocks, axes, split_axis=0, concat_axis=0, tiled=True)  19.8 us
    ppermute x1, waiting for transfers between devices, swap_shares(): lax.ppermute(own, 'boot', [(g, (g - turn) % groups) for g in range(groups)])  13.7 us
    all_to_all x2, starting transfers between devices, exchange(): return lax.all_to_all(blocks, axes, split_axis=0, concat_axis=0, tiled=True)  11.1 us
    pallas_call x1, Pallas kernels, patch_weights(): pl.pallas_call(weights_kernel, out_shape=jax.ShapeDtypeStruct((groups, me...  10.9 us
    pallas_call x1, Pallas kernels, pack(): pl.pallas_call(functools.partial(pack_kernel, groups, order), out_shape=j...  2.8 us
  transfers between devices with their start and end apart: 3, of which 3 were waited for; matrix products, arithmetic and copies ran while one was open for 0% of the time, Pallas kernels for 11%

profile of v18, /device:TPU:0, one launch (start us, length us, event | category | flops | bytes accessed | tf_op | source)
XLA Modules:
  0.0 118.1 jit_solution(3516437816789113291)
XLA Ops:
  0.0 2.8 %pack_rows.1 = bf16[16,8,3200]{2,1,0:T(8,128)(2,1)} custom-call(s32[2,384]{1,0:T(2,128)} %bitcast.8, s32[2,384]{1,0:T(2,128)} %bitcast.9, s32[384]{0:T(512)} %refs_2_.1, f32[384]{0:T(512)} %refs_3_.1, bf16[384]{0:T(512)(128)(2,1)} %refs_4_.1, bf16[384,512]{1,0:T(8,128)(2,1)} %refs_5_.1), custom_call_target="tpu_custom_call" | custom-call | flops 301989888 | bytes 1179648 | tf_op jit(solution)/shard_map/pack_rows/pallas_call | solution.py:104
  2.8 7.4 %all-to-all-start = ((bf16[16,8,3200]{2,1,0:T(8,128)(2,1)}), bf16[16,8,3200]{2,1,0:T(8,128)(2,1)S(1)}, u32[]{:S(2)}, u32[]{:S(2)}) async-start(bf16[16,8,3200]{2,1,0:T(8,128)(2,1)} %pack_rows.1), calls=%async_computation | async-start | bytes 1638400 | tf_op jit(solution)/shard_map/all_to_all | solution.py:463
  10.2 0.0 copy-start
  10.2 1.6 %copy-done = bf16[32,32768]{1,0:T(8,128)(2,1)S(1)} copy-done((bf16[32,32768]{1,0:T(8,128)(2,1)S(1)}, bf16[32,32768]{1,0:T(8,128)(2,1)}, u32[]{:S(2)}) %copy-start) | copy-done | bytes 2097176
  11.8 1.0 cut_share.1
  12.8 18.9 %all-to-all-done.refs_0_ = bf16[16,8,3200]{2,1,0:T(8,128)(2,1)S(1)} async-done(((bf16[16,8,3200]{2,1,0:T(8,128)(2,1)}), bf16[16,8,3200]{2,1,0:T(8,128)(2,1)S(1)}, u32[]{:S(2)}, u32[]{:S(2)}) %all-to-all-start) | async-done | bytes 819232 | tf_op jit(solution)/shard_map/all_to_all | solution.py:463
  31.8 1.5 %collective-permute-start = (bf16[16,8,3200]{2,1,0:T(8,128)(2,1)S(1)}, bf16[16,8,3200]{2,1,0:T(8,128)(2,1)S(1)}, u32[]{:S(2)}, u32[]{:S(2)}) collective-permute-start(bf16[16,8,3200]{2,1,0:T(8,128)(2,1)S(1)} %all-to-all-done.refs_0_), channel_id=1, source_target_pairs={{0,16},{16,0},{1,17},{17,1},{2,18},{18,2},{3,19},{19,3},{4,20},{20... | collective-permute-start | bytes 2457608 | tf_op jit(solution)/shard_map/ppermute | solution.py:469
  33.3 3.7 %all-to-all-start.1 = ((bf16[16,32,1024]{2,1,0:T(8,128)(2,1)}), bf16[16,32,1024]{2,1,0:T(8,128)(2,1)S(1)}, u32[]{:S(2)}, u32[]{:S(2)}) async-start(bf16[16,32,1024]{2,1,0:T(8,128)(2,1)} %cut_share.1), calls=%async_computation.1 | async-start | bytes 2097152 | tf_op jit(solution)/shard_map/all_to_all | solution.py:463
  37.0 0.9 own_gram.1
  37.8 13.7 %collective-permute-done.refs_6_ = bf16[16,8,3200]{2,1,0:T(8,128)(2,1)S(1)} collective-permute-done((bf16[16,8,3200]{2,1,0:T(8,128)(2,1)S(1)}, bf16[16,8,3200]{2,1,0:T(8,128)(2,1)S(1)}, u32[]{:S(2)}, u32[]{:S(2)}) %collective-permute-start) | collective-permute-done | bytes 819232 | tf_op jit(solution)/shard_map/ppermute | solution.py:469
  51.6 10.9 %patch_weights.1.blended_ref = bf16[2,512,512]{2,1,0:T(8,128)(2,1)S(1)} custom-call(f32[512,256]{1,0:T(8,128)S(1)} %get-tuple-element.14.refs_0_, f32[256,256]{1,0:T(8,128)S(1)} %get-tuple-element.15.refs_1_, f32[1,512]{1,0:T(1,128)S(1)} %get-tuple-element.16.refs_2_, f32[16,8,128]{2,1,0:T(8,128)S(1)} %get-tuple-element.17.refs_3_, ...), custom_call_target="tpu_custom_call" | custom-call | flops 21474836480 | bytes 2097152 | tf_op jit(solution)/shard_map/patch_weights/pallas_call | solution.py:348
  62.5 0.9 all-to-all-done.1
  63.4 1.5 %update_points.1 = bf16[16,2,32,1024]{3,2,1,0:T(8,128)(2,1)S(1)} custom-call(bf16[2,512,512]{2,1,0:T(8,128)(2,1)S(1)} %patch_weights.1.blended_ref, bf16[512,1024]{1,0:T(8,128)(2,1)S(1)} %bitcast.7), custom_call_target="tpu_custom_call" | custom-call | flops 1073741824 | bytes 3145728 | tf_op jit(solution)/shard_map/update_points/pallas_call | solution.py:390
  64.9 51.8 %all_to_all.15 = bf16[32,32,1024]{2,1,0:T(8,128)(2,1)S(1)} all-to-all(bf16[32,32,1024]{2,1,0:T(8,128)(2,1)S(1)} %bitcast.5), channel_id=1, replica_groups=mesh['boot'=2,'za'=2,'zb'=2,'near'=4] {'near','zb','za','boot'}, dimensions={0} | all-to-all | bytes 4194304 | tf_op jit(solution)/shard_map/all_to_all | solution.py:463
  116.7 1.4 %place_pieces.1 = bf16[32,32768]{1,0:T(8,128)(2,1)} custom-call(bf16[16,2,32,1024]{3,2,1,0:T(8,128)(2,1)S(1)} %bitcast.6), custom_call_target="tpu_custom_call" | custom-call | bytes 4194304 | tf_op jit(solution)/shard_map/place_pieces/pallas_call | solution.py:449
Async XLA Ops:
  2.8 29.0 %all-to-all-start = ((bf16[16,8,3200]{2,1,0:T(8,128)(2,1)}), bf16[16,8,3200]{2,1,0:T(8,128)(2,1)S(1)}, u32[]{:S(2)}, u32[]{:S(2)}) async-start(bf16[16,8,3200]{2,1,0:T(8,128)(2,1)} %pack_rows.1), calls=%async_computation | async-start | bytes 1638400 | tf_op jit(solution)/shard_map/all_to_all | solution.py:463
  10.2 1.6 %copy-start = (bf16[32,32768]{1,0:T(8,128)(2,1)S(1)}, bf16[32,32768]{1,0:T(8,128)(2,1)}, u32[]{:S(2)}) copy-start(bf16[32,32768]{1,0:T(8,128)(2,1)} %states_ref.1) | copy-start | bytes 6291460
  31.8 19.8 %collective-permute-start = (bf16[16,8,3200]{2,1,0:T(8,128)(2,1)S(1)}, bf16[16,8,3200]{2,1,0:T(8,128)(2,1)S(1)}, u32[]{:S(2)}, u32[]{:S(2)}) collective-permute-start(bf16[16,8,3200]{2,1,0:T(8,128)(2,1)S(1)} %all-to-all-done.refs_0_), channel_id=1, source_target_pairs={{0,16},{16,0},{1,17},{17,1},{2,18},{18,2},{3,19},{19,3},{4,20},{20... | collective-permute-start | bytes 2457608 | tf_op jit(solution)/shard_map/ppermute | solution.py:469
  33.3 30.1 %all-to-all-start.1 = ((bf16[16,32,1024]{2,1,0:T(8,128)(2,1)}), bf16[16,32,1024]{2,1,0:T(8,128)(2,1)S(1)}, u32[]{:S(2)}, u32[]{:S(2)}) async-start(bf16[16,32,1024]{2,1,0:T(8,128)(2,1)} %cut_share.1), calls=%async_computation.1 | async-start | bytes 2097152 | tf_op jit(solution)/shard_map/all_to_all | solution.py:463

commit v19 on v18

--- a/solution.py
+++ b/solution.py
@@ -351,7 +351,7 @@
         scratch_shapes=chain * groups,
         compiler_params=pltpu.CompilerParams(vmem_limit_bytes=(8 + 10 * groups) * MEBI),
         cost_estimate=pl.CostEstimate(
-            flops=80 * groups * members * members * members,
+            flops=8 * groups * members * members * members,
             bytes_accessed=8 * members * members,
             transcendentals=0,
         ),
@@ -359,18 +359,22 @@
     )(*own, *other_rows)
 
 
-def update_kernel(order, blended_ref, background_ref, analysis_ref):
+def update_kernel(order, blended_ref, *refs):
+    piece_refs, analysis_ref, members_ref = refs[:-2], refs[-2], refs[-1]
     groups = blended_ref.shape[0]
-    members, points = background_ref.shape
-    rows = members // len(order)
-    places = [order.index(holder) for holder in range(len(order))]
+    near, rows, points = piece_refs[0].shape
+    slabs = len(piece_refs)
+    members = slabs * near * rows
+    slab, place = lax.axis_index(SPACE[:2]), lax.axis_index(SPACE[2])
+    for far, piece_ref in enumerate(piece_refs):
+        for step in range(near):
+            holder = lax.rem(slab + slabs - far, slabs) * near + lax.rem(place + near - step, near)
+            begin = pl.multiple_of(holder * rows, rows)
+            members_ref[pl.ds(begin, rows), :] = piece_ref[step].astype(members_ref.dtype)
     tile = min(points, 256)
     for begin in range(0, points, tile):
         columns = slice(begin, begin + tile)
-        background = background_ref[:, columns].astype(F32)
-        background = jnp.concatenate(
-            [background[place * rows : (place + 1) * rows, :] for place in places], axis=0
-        )
+        background = members_ref[:, columns].astype(F32)
         centre = jnp.sum(background, axis=0, keepdims=True) / members
         perturb = (background - centre).astype(BF16)
         for turn in range(groups):
@@ -384,14 +388,14 @@
             analysis_ref[:, group, :, columns] = update
 
 
-def update_points(blended, background, order):
-    groups = blended.shape[0]
-    members, points = background.shape
+def update_points(blended, pieces, order):
+    groups, members, _ = blended.shape
+    rows, points = pieces[0].shape[1:]
+    held = BF16 if rows % 16 == 0 else F32
     return pl.pallas_call(
         functools.partial(update_kernel, order),
-        out_shape=jax.ShapeDtypeStruct(
-            (len(order), groups, members // len(order), points), BF16
-        ),
+        out_shape=jax.ShapeDtypeStruct((len(order), groups, rows, points), BF16),
+        scratch_shapes=[pltpu.VMEM((members, points), held)],
         compiler_params=pltpu.CompilerParams(vmem_limit_bytes=16 * MEBI),
         cost_estimate=pl.CostEstimate(
             flops=2 * groups * members * members * points,
@@ -399,29 +403,65 @@
             transcendentals=0,
         ),
         name="update_points",
-    )(blended, background)
-
-
-def cut_kernel(order, states_ref, cut_ref):
-    patches, _, share = cut_ref.shape
-    region = states_ref.shape[1] // patches
+    )(blended, *pieces)
+
+
+def slab_sizes():
+    return lax.axis_size(SPACE[:2]), lax.axis_size(SPACE[2])
+
+
+def cut_kernel(slabs, states_ref, *cut_refs):
+    share = cut_refs[0].shape[2]
+    near = len(cut_refs)
+    region = states_ref.shape[1] // (slabs * near)
     offset = lax.axis_index("boot") * share
-    for place, patch in enumerate(order):
-        begin = pl.multiple_of(patch * region + offset, LANES)
-        cut_ref[place] = states_ref[:, pl.ds(begin, share)]
-
-
-def cut_share(states, order, share):
-    own_members, patches = states.shape[0], len(order)
-    return pl.pallas_call(
-        functools.partial(cut_kernel, order),
-        out_shape=jax.ShapeDtypeStruct((patches, own_members, share), BF16),
+    slab, place = lax.axis_index(SPACE[:2]), lax.axis_index(SPACE[2])
+    for step, cut_ref in enumerate(cut_refs):
+        for far in range(slabs):
+            patch = lax.rem(slab + far, slabs) * near + lax.rem(place + step, near)
+            begin = pl.multiple_of(patch * region + offset, LANES)
+            cut_ref[far] = states_ref[:, pl.ds(begin, share)]
+
+
+def cut_share(states, share):
+    slabs, near = slab_sizes()
+    own_members = states.shape[0]
+    return pl.pallas_call(
+        functools.partial(cut_kernel, slabs),
+        out_shape=[jax.ShapeDtypeStruct((slabs, own_members, share), BF16)] * near,
         compiler_params=pltpu.CompilerParams(vmem_limit_bytes=16 * MEBI),
         cost_estimate=pl.CostEstimate(
-            flops=0, bytes_accessed=4 * patches * own_members * share, transcendentals=0
+            flops=0, bytes_accessed=4 * slabs * near * own_members * share, transcendentals=0
         ),
         name="cut_share",
     )(states)
+
+
+def regroup_kernel(near, *refs):
+    for far, group_ref in enumerate(refs[near:]):
+        for step, cut_ref in enumerate(refs[:near]):
+            group_ref[step] = cut_ref[far]
+
+
+def regroup(cuts):
+    slabs, own_members, share = cuts[0].shape
+    return pl.pallas_call(
+        functools.partial(regroup_kernel, len(cuts)),
+        out_shape=[jax.ShapeDtypeStruct((len(cuts), own_members, share), BF16)] * slabs,
+        compiler_params=pltpu.CompilerParams(vmem_limit_bytes=16 * MEBI),
+        cost_estimate=pl.CostEstimate(
+            flops=0, bytes_accessed=4 * len(cuts) * slabs * own_members * share, transcendentals=0
+        ),
+        name="regroup",
+    )(*cuts)
+
+
+def shift_all(pieces, axes):
+    count = len(pieces)
+    return [pieces[0]] + [
+        lax.ppermute(pieces[step], axes, [(d, (d + step) % count) for d in range(count)])
+        for step in range(1, count)
+    ]
 
 
 def place_kernel(order, pieces_ref, whole_ref, held_ref, sems):
@@ -501,14 +541,16 @@
         slot_share,
         groups,
     )
-    own_points = cut_share(background_states, order, share)
-    own_rows, own_points = lax.optimization_barrier((exchange(slots), own_points))
+    slots, background_states = lax.optimization_barrier((slots, background_states))
+    cuts = shift_all(cut_share(background_states, share), SPACE[2])
+    own_rows, cuts[1] = lax.optimization_barrier((exchange(slots), cuts[1]))
+    by_slab = regroup(cuts)
     other_rows = swap_shares(own_rows)
-    own_points = exchange(own_points).reshape(-1, share)
+    points_by_slab = shift_all(by_slab, SPACE[:2])
 
     own = own_gram(own_rows, measurement_anomaly_matrix.shape[1], groups)
     blended = patch_weights(own, other_rows)
-    analysis = update_points(blended, own_points, order)
+    analysis = update_points(blended, points_by_slab, order)
     analysis = exchange(analysis.reshape(-1, own_members, share), PARTNERS + ("boot",))
     return place_pieces(analysis.reshape(device_count, groups, own_members, share), order)
 

time: 119 us -> 124 us (1.042)
  blocking collectives: 51.8 us -> 56.4 us
  starting transfers between devices: 12.5 us -> 14.7 us
    ppermute x0 -> x6, waiting for transfers between devices: none -> 20.6 us  [shift_all(): lax.ppermute(pieces[step], axes, [(d, (d + step) % count) for d in range(...]
    all_to_all x2 -> x1, waiting for transfers between devices: 19.8 us -> 8.25 us  [exchange(): return lax.all_to_all(blocks, axes, split_axis=0, concat_axis=0, tiled=True)]
    ppermute x1, waiting for transfers between devices: 13.7 us -> 4.09 us  [swap_shares(): lax.ppermute(own, 'boot', [(g, (g - turn) % groups) for g in range(groups)])]
    ppermute x0 -> x6, starting transfers between devices: none -> 5.81 us  [shift_all(): lax.ppermute(pieces[step], axes, [(d, (d + step) % count) for d in range(...]
    all_to_all x1, blocking collectives: 51.8 us -> 56.4 us  [exchange(): return lax.all_to_all(blocks, axes, split_axis=0, concat_axis=0, tiled=True)]
    all_to_all x2 -> x1, starting transfers between devices: 11.1 us -> 7.4 us  [exchange(): return lax.all_to_all(blocks, axes, split_axis=0, concat_axis=0, tiled=True)]
  transfers between devices with their start and end apart: 3 -> 8, of which waited for: 3 -> 6; matrix products, arithmetic and copies ran while one was open for 0% -> 0% of each run, Pallas kernels for 11% -> 10%
where the time goes in v19:
time: 124 us; the launch traced here: 123 us
  blocking collectives  56.4 us (45%)
  waiting for transfers between devices  32.9 us (27%)
  Pallas kernels  17.8 us (14%)
  starting transfers between devices  14.7 us (12%)
  local copies, waits for them, and re-layouts  1.59 us (1%)
    all_to_all x1, blocking collectives, exchange(): return lax.all_to_all(blocks, axes, split_axis=0, concat_axis=0, tiled=True)  56.4 us
    ppermute x6, waiting for transfers between devices, shift_all(): lax.ppermute(pieces[step], axes, [(d, (d + step) % count) for d in range(...  20.6 us
    pallas_call x1, Pallas kernels, patch_weights(): pl.pallas_call(weights_kernel, out_shape=jax.ShapeDtypeStruct((groups, me...  10.9 us
    all_to_all x1, waiting for transfers between devices, exchange(): return lax.all_to_all(blocks, axes, split_axis=0, concat_axis=0, tiled=True)  8.25 us
    all_to_all x1, starting transfers between devices, exchange(): return lax.all_to_all(blocks, axes, split_axis=0, concat_axis=0, tiled=True)  7.4 us
    ppermute x6, starting transfers between devices, shift_all(): lax.ppermute(pieces[step], axes, [(d, (d + step) % count) for d in range(...  5.81 us
    ppermute x1, waiting for transfers between devices, swap_shares(): lax.ppermute(own, 'boot', [(g, (g - turn) % groups) for g in range(groups)])  4.09 us
    pallas_call x1, Pallas kernels, pack(): pl.pallas_call(functools.partial(pack_kernel, groups, order), out_shape=j...  2.82 us
  transfers between devices with their start and end apart: 8, of which 6 were waited for; matrix products, arithmetic and copies ran while one was open for 0% of the time, Pallas kernels for 10%

profile of v19, /device:TPU:0, one launch (start us, length us, event | category | flops | bytes accessed | tf_op | source)
XLA Modules:
  0.0 123.4 jit_solution(13019878223852303385)
XLA Ops:
  0.0 2.8 %pack_rows.1 = bf16[16,8,3200]{2,1,0:T(8,128)(2,1)} custom-call(s32[2,384]{1,0:T(2,128)} %bitcast.6, s32[2,384]{1,0:T(2,128)} %bitcast.7, s32[384]{0:T(512)} %refs_2_.1, f32[384]{0:T(512)} %refs_3_.1, bf16[384]{0:T(512)(128)(2,1)} %refs_4_.1, bf16[384,512]{1,0:T(8,128)(2,1)} %refs_5_.1), custom_call_target="tpu_custom_call" | custom-call | flops 301989888 | bytes 1179648 | tf_op jit(solution)/shard_map/pack_rows/pallas_call | solution.py:104
  2.8 7.4 %all-to-all-start = ((bf16[16,8,3200]{2,1,0:T(8,128)(2,1)}), bf16[16,8,3200]{2,1,0:T(8,128)(2,1)S(1)}, u32[]{:S(2)}, u32[]{:S(2)}) async-start(bf16[16,8,3200]{2,1,0:T(8,128)(2,1)} %pack_rows.1), calls=%async_computation | async-start | bytes 1638400 | tf_op jit(solution)/shard_map/all_to_all | solution.py:503
  10.2 0.0 copy-start
  10.2 1.6 %copy-done = bf16[32,32768]{1,0:T(8,128)(2,1)S(1)} copy-done((bf16[32,32768]{1,0:T(8,128)(2,1)S(1)}, bf16[32,32768]{1,0:T(8,128)(2,1)}, u32[]{:S(2)}) %copy-start) | copy-done | bytes 2097176
  11.8 0.1 cut_share.1
  11.9 0.5 collective-permute-start
  12.4 11.2 %collective-permute-done.refs_1_ = bf16[4,32,1024]{2,1,0:T(8,128)(2,1)S(1)} collective-permute-done((bf16[4,32,1024]{2,1,0:T(8,128)(2,1)S(1)}, bf16[4,32,1024]{2,1,0:T(8,128)(2,1)S(1)}, u32[]{:S(2)}, u32[]{:S(2)}) %collective-permute-start) | collective-permute-done | bytes 262176 | tf_op jit(solution)/shard_map/ppermute | solution.py:462
  23.6 8.2 %all-to-all-done.refs_0_ = bf16[16,8,3200]{2,1,0:T(8,128)(2,1)S(1)} async-done(((bf16[16,8,3200]{2,1,0:T(8,128)(2,1)}), bf16[16,8,3200]{2,1,0:T(8,128)(2,1)S(1)}, u32[]{:S(2)}, u32[]{:S(2)}) %all-to-all-start) | async-done | bytes 819232 | tf_op jit(solution)/shard_map/all_to_all | solution.py:503
  31.8 1.5 %collective-permute-start.1 = (bf16[16,8,3200]{2,1,0:T(8,128)(2,1)S(1)}, bf16[16,8,3200]{2,1,0:T(8,128)(2,1)S(1)}, u32[]{:S(2)}, u32[]{:S(2)}) collective-permute-start(bf16[16,8,3200]{2,1,0:T(8,128)(2,1)S(1)} %all-to-all-done.refs_0_), channel_id=1, source_target_pairs={{0,16},{16,0},{1,17},{17,1},{2,18},{18,2},{3,19},{19,3},{4,20},{20... | collective-permute-start | bytes 2457608 | tf_op jit(solution)/shard_map/ppermute | solution.py:509
  33.3 1.5 %collective-permute-start.2 = (bf16[4,32,1024]{2,1,0:T(8,128)(2,1)S(1)}, bf16[4,32,1024]{2,1,0:T(8,128)(2,1)S(1)}, u32[]{:S(2)}, u32[]{:S(2)}) collective-permute-start(bf16[4,32,1024]{2,1,0:T(8,128)(2,1)S(1)} %get-tuple-element.35), channel_id=1, source_target_pairs={{0,2},{1,3},{2,0},{3,1},{4,6},{5,7},{6,4},{7,5},{8,10},{9,11},{10,... | collective-permute-start | bytes 786440 | tf_op jit(solution)/shard_map/ppermute | solution.py:462
  34.8 0.0 collective-permute-start.3
  34.8 6.1 %collective-permute-done.2.refs_2_ = bf16[4,32,1024]{2,1,0:T(8,128)(2,1)S(1)} collective-permute-done((bf16[4,32,1024]{2,1,0:T(8,128)(2,1)S(1)}, bf16[4,32,1024]{2,1,0:T(8,128)(2,1)S(1)}, u32[]{:S(2)}, u32[]{:S(2)}) %collective-permute-start.2) | collective-permute-done | bytes 262176 | tf_op jit(solution)/shard_map/ppermute | solution.py:462
  40.9 1.8 %collective-permute-done.3.refs_3_ = bf16[4,32,1024]{2,1,0:T(8,128)(2,1)S(1)} collective-permute-done((bf16[4,32,1024]{2,1,0:T(8,128)(2,1)S(1)}, bf16[4,32,1024]{2,1,0:T(8,128)(2,1)S(1)}, u32[]{:S(2)}, u32[]{:S(2)}) %collective-permute-start.3) | collective-permute-done | bytes 262176 | tf_op jit(solution)/shard_map/ppermute | solution.py:462
  42.7 0.1 regroup.1
  42.7 0.2 collective-permute-start.4
  42.9 1.5 %collective-permute-start.5 = (bf16[4,32,1024]{2,1,0:T(8,128)(2,1)S(1)}, bf16[4,32,1024]{2,1,0:T(8,128)(2,1)S(1)}, u32[]{:S(2)}, u32[]{:S(2)}) collective-permute-start(bf16[4,32,1024]{2,1,0:T(8,128)(2,1)S(1)} %get-tuple-element.39), channel_id=1, source_target_pairs={{0,8},{4,12},{8,0},{12,4},{1,9},{5,13},{9,1},{13,5},{2,10},{6,14},... | collective-permute-start | bytes 786440 | tf_op jit(solution)/shard_map/ppermute | solution.py:462
  44.4 2.2 %collective-permute-start.6 = (bf16[4,32,1024]{2,1,0:T(8,128)(2,1)S(1)}, bf16[4,32,1024]{2,1,0:T(8,128)(2,1)S(1)}, u32[]{:S(2)}, u32[]{:S(2)}) collective-permute-start(bf16[4,32,1024]{2,1,0:T(8,128)(2,1)S(1)} %get-tuple-element.40), channel_id=1, source_target_pairs={{0,12},{4,0},{8,4},{12,8},{1,13},{5,1},{9,5},{13,9},{2,14},{6,2},{... | collective-permute-start | bytes 786440 | tf_op jit(solution)/shard_map/ppermute | solution.py:462
  46.6 0.9 own_gram.1
  47.5 4.1 %collective-permute-done.1.refs_6_ = bf16[16,8,3200]{2,1,0:T(8,128)(2,1)S(1)} collective-permute-done((bf16[16,8,3200]{2,1,0:T(8,128)(2,1)S(1)}, bf16[16,8,3200]{2,1,0:T(8,128)(2,1)S(1)}, u32[]{:S(2)}, u32[]{:S(2)}) %collective-permute-start.1) | collective-permute-done | bytes 819232 | tf_op jit(solution)/shard_map/ppermute | solution.py:509
  51.6 10.9 %patch_weights.1.blended_ref = bf16[2,512,512]{2,1,0:T(8,128)(2,1)S(1)} custom-call(f32[512,256]{1,0:T(8,128)S(1)} %get-tuple-element.27.refs_0_, f32[256,256]{1,0:T(8,128)S(1)} %get-tuple-element.28.refs_1_, f32[1,512]{1,0:T(1,128)S(1)} %get-tuple-element.29.refs_2_, f32[16,8,128]{2,1,0:T(8,128)S(1)} %get-tuple-element.30.refs_3_, ...), custom_call_target="tpu_custom_call" | custom-call | flops 2147483648 | bytes 2097152 | tf_op jit(solution)/shard_map/patch_weights/pallas_call | solution.py:348
  62.5 0.0 collective-permute-done.4.refs_1_
  62.5 1.5 %collective-permute-done.5.refs_2_ = bf16[4,32,1024]{2,1,0:T(8,128)(2,1)S(1)} collective-permute-done((bf16[4,32,1024]{2,1,0:T(8,128)(2,1)S(1)}, bf16[4,32,1024]{2,1,0:T(8,128)(2,1)S(1)}, u32[]{:S(2)}, u32[]{:S(2)}) %collective-permute-start.5) | collective-permute-done | bytes 262176 | tf_op jit(solution)/shard_map/ppermute | solution.py:462
  64.0 0.0 collective-permute-done.6.refs_3_
  64.0 1.6 %update_points.1 = bf16[16,2,32,1024]{3,2,1,0:T(8,128)(2,1)S(1)} custom-call(bf16[2,512,512]{2,1,0:T(8,128)(2,1)S(1)} %patch_weights.1.blended_ref, bf16[4,32,1024]{2,1,0:T(8,128)(2,1)S(1)} %get-tuple-element.37.refs_0_, bf16[4,32,1024]{2,1,0:T(8,128)(2,1)S(1)} %collective-permute-done.4.refs_1_, bf16[4,32,1024]{2,1,0:T(8,128)(2,1)S(1)} %collective-permute-done.5.refs_2_, ...), custom_call_target="tpu_custom_call" | custom-call | flops 1073741824 | bytes 3145728 | tf_op jit(solution)/shard_map/update_points/pallas_call | solution.py:395
  65.7 56.4 %all_to_all.10 = bf16[32,32,1024]{2,1,0:T(8,128)(2,1)S(1)} all-to-all(bf16[32,32,1024]{2,1,0:T(8,128)(2,1)S(1)} %bitcast.4), channel_id=1, replica_groups=mesh['boot'=2,'za'=2,'zb'=2,'near'=4] {'near','zb','za','boot'}, dimensions={0} | all-to-all | bytes 4194304 | tf_op jit(solution)/shard_map/all_to_all | solution.py:503
  122.0 1.4 %place_pieces.1 = bf16[32,32768]{1,0:T(8,128)(2,1)} custom-call(bf16[16,2,32,1024]{3,2,1,0:T(8,128)(2,1)S(1)} %bitcast.5), custom_call_target="tpu_custom_call" | custom-call | bytes 4194304 | tf_op jit(solution)/shard_map/place_pieces/pallas_call | solution.py:489
Async XLA Ops:
  2.8 29.0 %all-to-all-start = ((bf16[16,8,3200]{2,1,0:T(8,128)(2,1)}), bf16[16,8,3200]{2,1,0:T(8,128)(2,1)S(1)}, u32[]{:S(2)}, u32[]{:S(2)}) async-start(bf16[16,8,3200]{2,1,0:T(8,128)(2,1)} %pack_rows.1), calls=%async_computation | async-start | bytes 1638400 | tf_op jit(solution)/shard_map/all_to_all | solution.py:503
  10.2 1.6 %copy-start = (bf16[32,32768]{1,0:T(8,128)(2,1)S(1)}, bf16[32,32768]{1,0:T(8,128)(2,1)}, u32[]{:S(2)}) copy-start(bf16[32,32768]{1,0:T(8,128)(2,1)} %states_ref) | copy-start | bytes 6291460
  11.9 11.7 %collective-permute-start = (bf16[4,32,1024]{2,1,0:T(8,128)(2,1)S(1)}, bf16[4,32,1024]{2,1,0:T(8,128)(2,1)S(1)}, u32[]{:S(2)}, u32[]{:S(2)}) collective-permute-start(bf16[4,32,1024]{2,1,0:T(8,128)(2,1)S(1)} %get-tuple-element.25), channel_id=1, source_target_pairs={{0,1},{1,2},{2,3},{3,0},{4,5},{5,6},{6,7},{7,4},{8,9},{9,10},{10,1... | collective-permute-start | bytes 786440 | tf_op jit(solution)/shard_map/ppermute | solution.py:462
  31.8 19.8 %collective-permute-start.1 = (bf16[16,8,3200]{2,1,0:T(8,128)(2,1)S(1)}, bf16[16,8,3200]{2,1,0:T(8,128)(2,1)S(1)}, u32[]{:S(2)}, u32[]{:S(2)}) collective-permute-start(bf16[16,8,3200]{2,1,0:T(8,128)(2,1)S(1)} %all-to-all-done.refs_0_), channel_id=1, source_target_pairs={{0,16},{16,0},{1,17},{17,1},{2,18},{18,2},{3,19},{19,3},{4,20},{20... | collective-permute-start | bytes 2457608 | tf_op jit(solution)/shard_map/ppermute | solution.py:509
  33.3 7.6 %collective-permute-start.2 = (bf16[4,32,1024]{2,1,0:T(8,128)(2,1)S(1)}, bf16[4,32,1024]{2,1,0:T(8,128)(2,1)S(1)}, u32[]{:S(2)}, u32[]{:S(2)}) collective-permute-start(bf16[4,32,1024]{2,1,0:T(8,128)(2,1)S(1)} %get-tuple-element.35), channel_id=1, source_target_pairs={{0,2},{1,3},{2,0},{3,1},{4,6},{5,7},{6,4},{7,5},{8,10},{9,11},{10,... | collective-permute-start | bytes 786440 | tf_op jit(solution)/shard_map/ppermute | solution.py:462
  34.8 7.9 %collective-permute-start.3 = (bf16[4,32,1024]{2,1,0:T(8,128)(2,1)S(1)}, bf16[4,32,1024]{2,1,0:T(8,128)(2,1)S(1)}, u32[]{:S(2)}, u32[]{:S(2)}) collective-permute-start(bf16[4,32,1024]{2,1,0:T(8,128)(2,1)S(1)} %get-tuple-element.36), channel_id=1, source_target_pairs={{0,3},{1,0},{2,1},{3,2},{4,7},{5,4},{6,5},{7,6},{8,11},{9,8},{10,9... | collective-permute-start | bytes 786440 | tf_op jit(solution)/shard_map/ppermute | solution.py:462
  42.7 19.8 %collective-permute-start.4 = (bf16[4,32,1024]{2,1,0:T(8,128)(2,1)S(1)}, bf16[4,32,1024]{2,1,0:T(8,128)(2,1)S(1)}, u32[]{:S(2)}, u32[]{:S(2)}) collective-permute-start(bf16[4,32,1024]{2,1,0:T(8,128)(2,1)S(1)} %get-tuple-element.38), channel_id=1, source_target_pairs={{0,4},{4,8},{8,12},{12,0},{1,5},{5,9},{9,13},{13,1},{2,6},{6,10},{... | collective-permute-start | bytes 786440 | tf_op jit(solution)/shard_map/ppermute | solution.py:462
  42.9 21.1 %collective-permute-start.5 = (bf16[4,32,1024]{2,1,0:T(8,128)(2,1)S(1)}, bf16[4,32,1024]{2,1,0:T(8,128)(2,1)S(1)}, u32[]{:S(2)}, u32[]{:S(2)}) collective-permute-start(bf16[4,32,1024]{2,1,0:T(8,128)(2,1)S(1)} %get-tuple-element.39), channel_id=1, source_target_pairs={{0,8},{4,12},{8,0},{12,4},{1,9},{5,13},{9,1},{13,5},{2,10},{6,14},... | collective-permute-start | bytes 786440 | tf_op jit(solution)/shard_map/ppermute | solution.py:462
  44.4 19.6 %collective-permute-start.6 = (bf16[4,32,1024]{2,1,0:T(8,128)(2,1)S(1)}, bf16[4,32,1024]{2,1,0:T(8,128)(2,1)S(1)}, u32[]{:S(2)}, u32[]{:S(2)}) collective-permute-start(bf16[4,32,1024]{2,1,0:T(8,128)(2,1)S(1)} %get-tuple-element.40), channel_id=1, source_target_pairs={{0,12},{4,0},{8,4},{12,8},{1,13},{5,1},{9,5},{13,9},{2,14},{6,2},{... | collective-permute-start | bytes 786440 | tf_op jit(solution)/shard_map/ppermute | solution.py:462

commit v20 on v18

--- a/solution.py
+++ b/solution.py
@@ -221,10 +221,14 @@
 
 def weights_kernel(*refs):
     right_ref, corner_ref, drive_ref, tails_ref, ordered_ref, turned_ref = refs[:6]
-    groups = (len(refs) - 6) // 9
+    groups = (len(refs) - 6) // 8
     rows_refs, blended_ref = refs[6 : 5 + groups], refs[5 + groups]
-    chains = [refs[6 + groups + 8 * c : 14 + groups + 8 * c] for c in range(groups)]
+    scratch = [refs[6 + groups + 7 * c : 13 + groups + 7 * c] for c in range(groups)]
     members, half = right_ref.shape
+    chains = [
+        (*state, both.at[0:members], both.at[members : 2 * members], z_off, w_high)
+        for *state, both, z_off, w_high in scratch
+    ]
     row_id = lax.broadcasted_iota(jnp.int32, (members, members), 0)
     col_id = lax.broadcasted_iota(jnp.int32, (members, members), 1)
     identity = jnp.where(row_id == col_id, 1.0, 0.0)
@@ -304,12 +308,15 @@
         factors = [
             split(chain[7], *symmetric_product(chain[5], chain[4])) for chain in chains
         ]
-        for factor, chain in zip(factors, chains):
-            for right, corner, high in (
-                (chain[0], chain[1], chain[4]),
-                (chain[2], chain[3], chain[5]),
+        for factor, chain, (*_, both, _, w_high) in zip(factors, chains, scratch):
+            changes = dot(both[...], w_high[:, half:])
+            for first, right, corner, high in (
+                (0, chain[0], chain[1], chain[4]),
+                (members, chain[2], chain[3], chain[5]),
             ):
-                new_right, new_corner = advance(factor, chain[7], right[...], corner[...], high)
+                change = dot(high[0:half, :], w_high[:, 0:half])
+                new_right = factor[:, half:] * right[...] + changes[first : first + members, :]
+                new_corner = factor[:, 0:half] * corner[...] + change
                 right[...], corner[...] = new_right, new_corner
                 put_symmetric(high, new_right, new_corner)
         return carry
@@ -344,7 +351,8 @@
     groups, members = len(other_rows) + 1, own[0].shape[0]
     half = members // 2
     right, corner = pltpu.VMEM((members, half), F32), pltpu.VMEM((half, half), F32)
-    chain = [right, corner] * 2 + [pltpu.VMEM((members, members), BF16)] * 4
+    chain = [right, corner] * 2 + [pltpu.VMEM((2 * members, members), BF16)]
+    chain += [pltpu.VMEM((members, members), BF16)] * 2
     return pl.pallas_call(
         weights_kernel,
         out_shape=jax.ShapeDtypeStruct((groups, members, members), BF16),
@@ -373,8 +381,10 @@
         )
         centre = jnp.sum(background, axis=0, keepdims=True) / members
         perturb = (background - centre).astype(BF16)
+        blended = blended_ref[...].reshape(groups * members, members)
+        updates = jnp.dot(blended, perturb, preferred_element_type=F32)
         for turn in range(groups):
-            update = jnp.dot(blended_ref[turn], perturb, preferred_element_type=F32)
+            update = updates[turn * members : (turn + 1) * members, :]
             group = lax.rem(lax.axis_index("boot") + turn, groups)
             update = centre + update
             update = jnp.concatenate(

time: 119 us -> 119 us (level)
  no operation moved by 1% of the time
where the time goes in v20:
time: 119 us; the launch traced here: 118 us
  blocking collectives  51.8 us (44%)
  waiting for transfers between devices  33.5 us (28%)
  Pallas kernels  18.5 us (16%)
  starting transfers between devices  12.5 us (11%)
  local copies, waits for them, and re-layouts  1.59 us (1%)
    all_to_all x1, blocking collectives, exchange(): return lax.all_to_all(blocks, axes, split_axis=0, concat_axis=0, tiled=True)  51.8 us
    all_to_all x2, waiting for transfers between devices, exchange(): return lax.all_to_all(blocks, axes, split_axis=0, concat_axis=0, tiled=True)  19.8 us
    ppermute x1, waiting for transfers between devices, swap_shares(): lax.ppermute(own, 'boot', [(g, (g - turn) % groups) for g in range(groups)])  13.7 us
    all_to_all x2, starting transfers between devices, exchange(): return lax.all_to_all(blocks, axes, split_axis=0, concat_axis=0, tiled=True)  11.1 us
    pallas_call x1, Pallas kernels, patch_weights(): pl.pallas_call(weights_kernel, out_shape=jax.ShapeDtypeStruct((groups, me...  10.9 us
    pallas_call x1, Pallas kernels, pack(): pl.pallas_call(functools.partial(pack_kernel, groups, order), out_shape=j...  2.8 us
  transfers between devices with their start and end apart: 3, of which 3 were waited for; matrix products, arithmetic and copies ran while one was open for 0% of the time, Pallas kernels for 11%

profile of v20, /device:TPU:0, one launch (start us, length us, event | category | flops | bytes accessed | tf_op | source)
XLA Modules:
  0.0 118.0 jit_solution(5574904663622349742)
XLA Ops:
  0.0 2.8 %pack_rows.1 = bf16[16,8,3200]{2,1,0:T(8,128)(2,1)} custom-call(s32[2,384]{1,0:T(2,128)} %bitcast.8, s32[2,384]{1,0:T(2,128)} %bitcast.9, s32[384]{0:T(512)} %refs_2_.1, f32[384]{0:T(512)} %refs_3_.1, bf16[384]{0:T(512)(128)(2,1)} %refs_4_.1, bf16[384,512]{1,0:T(8,128)(2,1)} %refs_5_.1), custom_call_target="tpu_custom_call" | custom-call | flops 301989888 | bytes 1179648 | tf_op jit(solution)/shard_map/pack_rows/pallas_call | solution.py:104
  2.8 7.4 %all-to-all-start = ((bf16[16,8,3200]{2,1,0:T(8,128)(2,1)}), bf16[16,8,3200]{2,1,0:T(8,128)(2,1)S(1)}, u32[]{:S(2)}, u32[]{:S(2)}) async-start(bf16[16,8,3200]{2,1,0:T(8,128)(2,1)} %pack_rows.1), calls=%async_computation | async-start | bytes 1638400 | tf_op jit(solution)/shard_map/all_to_all | solution.py:473
  10.2 0.0 copy-start
  10.2 1.6 %copy-done = bf16[32,32768]{1,0:T(8,128)(2,1)S(1)} copy-done((bf16[32,32768]{1,0:T(8,128)(2,1)S(1)}, bf16[32,32768]{1,0:T(8,128)(2,1)}, u32[]{:S(2)}) %copy-start) | copy-done | bytes 2097176
  11.8 1.0 cut_share.1
  12.8 18.9 %all-to-all-done.refs_0_ = bf16[16,8,3200]{2,1,0:T(8,128)(2,1)S(1)} async-done(((bf16[16,8,3200]{2,1,0:T(8,128)(2,1)}), bf16[16,8,3200]{2,1,0:T(8,128)(2,1)S(1)}, u32[]{:S(2)}, u32[]{:S(2)}) %all-to-all-start) | async-done | bytes 819232 | tf_op jit(solution)/shard_map/all_to_all | solution.py:473
  31.8 1.5 %collective-permute-start = (bf16[16,8,3200]{2,1,0:T(8,128)(2,1)S(1)}, bf16[16,8,3200]{2,1,0:T(8,128)(2,1)S(1)}, u32[]{:S(2)}, u32[]{:S(2)}) collective-permute-start(bf16[16,8,3200]{2,1,0:T(8,128)(2,1)S(1)} %all-to-all-done.refs_0_), channel_id=1, source_target_pairs={{0,16},{16,0},{1,17},{17,1},{2,18},{18,2},{3,19},{19,3},{4,20},{20... | collective-permute-start | bytes 2457608 | tf_op jit(solution)/shard_map/ppermute | solution.py:479
  33.3 3.7 %all-to-all-start.1 = ((bf16[16,32,1024]{2,1,0:T(8,128)(2,1)}), bf16[16,32,1024]{2,1,0:T(8,128)(2,1)S(1)}, u32[]{:S(2)}, u32[]{:S(2)}) async-start(bf16[16,32,1024]{2,1,0:T(8,128)(2,1)} %cut_share.1), calls=%async_computation.1 | async-start | bytes 2097152 | tf_op jit(solution)/shard_map/all_to_all | solution.py:473
  37.0 0.9 own_gram.1
  37.8 13.7 %collective-permute-done.refs_6_ = bf16[16,8,3200]{2,1,0:T(8,128)(2,1)S(1)} collective-permute-done((bf16[16,8,3200]{2,1,0:T(8,128)(2,1)S(1)}, bf16[16,8,3200]{2,1,0:T(8,128)(2,1)S(1)}, u32[]{:S(2)}, u32[]{:S(2)}) %collective-permute-start) | collective-permute-done | bytes 819232 | tf_op jit(solution)/shard_map/ppermute | solution.py:479
  51.6 10.9 %patch_weights.1.blended_ref = bf16[2,512,512]{2,1,0:T(8,128)(2,1)S(1)} custom-call(f32[512,256]{1,0:T(8,128)S(1)} %get-tuple-element.14.refs_0_, f32[256,256]{1,0:T(8,128)S(1)} %get-tuple-element.15.refs_1_, f32[1,512]{1,0:T(1,128)S(1)} %get-tuple-element.16.refs_2_, f32[16,8,128]{2,1,0:T(8,128)S(1)} %get-tuple-element.17.refs_3_, ...), custom_call_target="tpu_custom_call" | custom-call | flops 21474836480 | bytes 2097152 | tf_op jit(solution)/shard_map/patch_weights/pallas_call | solution.py:356
  62.5 0.8 all-to-all-done.1
  63.4 1.4 %update_points.1 = bf16[16,2,32,1024]{3,2,1,0:T(8,128)(2,1)S(1)} custom-call(bf16[2,512,512]{2,1,0:T(8,128)(2,1)S(1)} %patch_weights.1.blended_ref, bf16[512,1024]{1,0:T(8,128)(2,1)S(1)} %bitcast.7), custom_call_target="tpu_custom_call" | custom-call | flops 1073741824 | bytes 3145728 | tf_op jit(solution)/shard_map/update_points/pallas_call | solution.py:400
  64.8 51.8 %all_to_all.15 = bf16[32,32,1024]{2,1,0:T(8,128)(2,1)S(1)} all-to-all(bf16[32,32,1024]{2,1,0:T(8,128)(2,1)S(1)} %bitcast.5), channel_id=1, replica_groups=mesh['boot'=2,'za'=2,'zb'=2,'near'=4] {'near','zb','za','boot'}, dimensions={0} | all-to-all | bytes 4194304 | tf_op jit(solution)/shard_map/all_to_all | solution.py:473
  116.6 1.4 %place_pieces.1 = bf16[32,32768]{1,0:T(8,128)(2,1)} custom-call(bf16[16,2,32,1024]{3,2,1,0:T(8,128)(2,1)S(1)} %bitcast.6), custom_call_target="tpu_custom_call" | custom-call | bytes 4194304 | tf_op jit(solution)/shard_map/place_pieces/pallas_call | solution.py:459
Async XLA Ops:
  2.8 29.0 %all-to-all-start = ((bf16[16,8,3200]{2,1,0:T(8,128)(2,1)}), bf16[16,8,3200]{2,1,0:T(8,128)(2,1)S(1)}, u32[]{:S(2)}, u32[]{:S(2)}) async-start(bf16[16,8,3200]{2,1,0:T(8,128)(2,1)} %pack_rows.1), calls=%async_computation | async-start | bytes 1638400 | tf_op jit(solution)/shard_map/all_to_all | solution.py:473
  10.2 1.6 %copy-start = (bf16[32,32768]{1,0:T(8,128)(2,1)S(1)}, bf16[32,32768]{1,0:T(8,128)(2,1)}, u32[]{:S(2)}) copy-start(bf16[32,32768]{1,0:T(8,128)(2,1)} %states_ref.1) | copy-start | bytes 6291460
  31.8 19.8 %collective-permute-start = (bf16[16,8,3200]{2,1,0:T(8,128)(2,1)S(1)}, bf16[16,8,3200]{2,1,0:T(8,128)(2,1)S(1)}, u32[]{:S(2)}, u32[]{:S(2)}) collective-permute-start(bf16[16,8,3200]{2,1,0:T(8,128)(2,1)S(1)} %all-to-all-done.refs_0_), channel_id=1, source_target_pairs={{0,16},{16,0},{1,17},{17,1},{2,18},{18,2},{3,19},{19,3},{4,20},{20... | collective-permute-start | bytes 2457608 | tf_op jit(solution)/shard_map/ppermute | solution.py:479
  33.3 30.1 %all-to-all-start.1 = ((bf16[16,32,1024]{2,1,0:T(8,128)(2,1)}), bf16[16,32,1024]{2,1,0:T(8,128)(2,1)S(1)}, u32[]{:S(2)}, u32[]{:S(2)}) async-start(bf16[16,32,1024]{2,1,0:T(8,128)(2,1)} %cut_share.1), calls=%async_computation.1 | async-start | bytes 2097152 | tf_op jit(solution)/shard_map/all_to_all | solution.py:473

commit v21 on v20

--- a/solution.py
+++ b/solution.py
@@ -10,7 +10,7 @@
 
 NS_STEPS = 6
 SPACE = ("za", "zb", "near")
-PARTNERS = ("near", "zb", "za")
+PARTNERS = ("zb", "near", "za")
 LANES = 128
 ROWS = 8
 MEBI = 1024 * 1024
@@ -20,7 +20,7 @@
 
 def partner_order(sizes):
     za, zb, near = sizes
-    return [(a * zb + b) * near + c for c in range(near) for b in range(zb) for a in range(za)]
+    return [(a * zb + b) * near + c for b in range(zb) for c in range(near) for a in range(za)]
 
 
 def pack_kernel(groups, order, *refs):

time: 119 us -> 120 us (level)
  blocking collectives: 51.8 us -> 53.3 us
    all_to_all x1, blocking collectives: 51.8 us -> 53.3 us  [exchange(): return lax.all_to_all(blocks, axes, split_axis=0, concat_axis=0, tiled=True)]
where the time goes in v21:
time: 120 us
  blocking collectives  53.3 us (44%)
  waiting for transfers between devices  33.6 us (28%)
  Pallas kernels  18.4 us (15%)
  starting transfers between devices  12.5 us (10%)
  local copies, waits for them, and re-layouts  1.59 us (1%)
    all_to_all x1, blocking collectives, exchange(): return lax.all_to_all(blocks, axes, split_axis=0, concat_axis=0, tiled=True)  53.3 us
    all_to_all x2, waiting for transfers between devices, exchange(): return lax.all_to_all(blocks, axes, split_axis=0, concat_axis=0, tiled=True)  19.4 us
    ppermute x1, waiting for transfers between devices, swap_shares(): lax.ppermute(own, 'boot', [(g, (g - turn) % groups) for g in range(groups)])  14.1 us
    all_to_all x2, starting transfers between devices, exchange(): return lax.all_to_all(blocks, axes, split_axis=0, concat_axis=0, tiled=True)  11.1 us
    pallas_call x1, Pallas kernels, patch_weights(): pl.pallas_call(weights_kernel, out_shape=jax.ShapeDtypeStruct((groups, me...  10.9 us
    pallas_call x1, Pallas kernels, pack(): pl.pallas_call(functools.partial(pack_kernel, groups, order), out_shape=j...  2.8 us
  transfers between devices with their start and end apart: 3, of which 3 were waited for; matrix products, arithmetic and copies ran while one was open for 0% of the time, Pallas kernels for 11%

profile of v21, /device:TPU:0, one launch (start us, length us, event | category | flops | bytes accessed | tf_op | source)
XLA Modules:
  0.0 119.5 jit_solution(18047457108959291082)
XLA Ops:
  0.0 2.8 %pack_rows.1 = bf16[16,8,3200]{2,1,0:T(8,128)(2,1)} custom-call(s32[2,384]{1,0:T(2,128)} %bitcast.8, s32[2,384]{1,0:T(2,128)} %bitcast.9, s32[384]{0:T(512)} %refs_2_.1, f32[384]{0:T(512)} %refs_3_.1, bf16[384]{0:T(512)(128)(2,1)} %refs_4_.1, bf16[384,512]{1,0:T(8,128)(2,1)} %refs_5_.1), custom_call_target="tpu_custom_call" | custom-call | flops 301989888 | bytes 1179648 | tf_op jit(solution)/shard_map/pack_rows/pallas_call | solution.py:104
  2.8 7.4 %all-to-all-start = ((bf16[16,8,3200]{2,1,0:T(8,128)(2,1)}), bf16[16,8,3200]{2,1,0:T(8,128)(2,1)S(1)}, u32[]{:S(2)}, u32[]{:S(2)}) async-start(bf16[16,8,3200]{2,1,0:T(8,128)(2,1)} %pack_rows.1), calls=%async_computation | async-start | bytes 1638400 | tf_op jit(solution)/shard_map/all_to_all | solution.py:473
  10.2 0.0 copy-start
  10.2 1.6 %copy-done = bf16[32,32768]{1,0:T(8,128)(2,1)S(1)} copy-done((bf16[32,32768]{1,0:T(8,128)(2,1)S(1)}, bf16[32,32768]{1,0:T(8,128)(2,1)}, u32[]{:S(2)}) %copy-start) | copy-done | bytes 2097176
  11.8 1.0 cut_share.1
  12.8 19.0 %all-to-all-done.refs_0_ = bf16[16,8,3200]{2,1,0:T(8,128)(2,1)S(1)} async-done(((bf16[16,8,3200]{2,1,0:T(8,128)(2,1)}), bf16[16,8,3200]{2,1,0:T(8,128)(2,1)S(1)}, u32[]{:S(2)}, u32[]{:S(2)}) %all-to-all-start) | async-done | bytes 819232 | tf_op jit(solution)/shard_map/all_to_all | solution.py:473
  31.8 1.5 %collective-permute-start = (bf16[16,8,3200]{2,1,0:T(8,128)(2,1)S(1)}, bf16[16,8,3200]{2,1,0:T(8,128)(2,1)S(1)}, u32[]{:S(2)}, u32[]{:S(2)}) collective-permute-start(bf16[16,8,3200]{2,1,0:T(8,128)(2,1)S(1)} %all-to-all-done.refs_0_), channel_id=1, source_target_pairs={{0,16},{16,0},{1,17},{17,1},{2,18},{18,2},{3,19},{19,3},{4,20},{20... | collective-permute-start | bytes 2457608 | tf_op jit(solution)/shard_map/ppermute | solution.py:479
  33.3 3.7 %all-to-all-start.1 = ((bf16[16,32,1024]{2,1,0:T(8,128)(2,1)}), bf16[16,32,1024]{2,1,0:T(8,128)(2,1)S(1)}, u32[]{:S(2)}, u32[]{:S(2)}) async-start(bf16[16,32,1024]{2,1,0:T(8,128)(2,1)} %cut_share.1), calls=%async_computation.1 | async-start | bytes 2097152 | tf_op jit(solution)/shard_map/all_to_all | solution.py:473
  37.0 0.9 own_gram.1
  37.9 14.1 %collective-permute-done.refs_6_ = bf16[16,8,3200]{2,1,0:T(8,128)(2,1)S(1)} collective-permute-done((bf16[16,8,3200]{2,1,0:T(8,128)(2,1)S(1)}, bf16[16,8,3200]{2,1,0:T(8,128)(2,1)S(1)}, u32[]{:S(2)}, u32[]{:S(2)}) %collective-permute-start) | collective-permute-done | bytes 819232 | tf_op jit(solution)/shard_map/ppermute | solution.py:479
  52.0 10.9 %patch_weights.1.blended_ref = bf16[2,512,512]{2,1,0:T(8,128)(2,1)S(1)} custom-call(f32[512,256]{1,0:T(8,128)S(1)} %get-tuple-element.14.refs_0_, f32[256,256]{1,0:T(8,128)S(1)} %get-tuple-element.15.refs_1_, f32[1,512]{1,0:T(1,128)S(1)} %get-tuple-element.16.refs_2_, f32[16,8,128]{2,1,0:T(8,128)S(1)} %get-tuple-element.17.refs_3_, ...), custom_call_target="tpu_custom_call" | custom-call | flops 21474836480 | bytes 2097152 | tf_op jit(solution)/shard_map/patch_weights/pallas_call | solution.py:356
  63.0 0.4 all-to-all-done.1
  63.4 1.4 %update_points.1 = bf16[16,2,32,1024]{3,2,1,0:T(8,128)(2,1)S(1)} custom-call(bf16[2,512,512]{2,1,0:T(8,128)(2,1)S(1)} %patch_weights.1.blended_ref, bf16[512,1024]{1,0:T(8,128)(2,1)S(1)} %bitcast.7), custom_call_target="tpu_custom_call" | custom-call | flops 1073741824 | bytes 3145728 | tf_op jit(solution)/shard_map/update_points/pallas_call | solution.py:400
  64.8 53.3 %all_to_all.15 = bf16[32,32,1024]{2,1,0:T(8,128)(2,1)S(1)} all-to-all(bf16[32,32,1024]{2,1,0:T(8,128)(2,1)S(1)} %bitcast.5), channel_id=1, replica_groups=mesh['boot'=2,'za'=2,'zb'=2,'near'=4] {'zb','near','za','boot'}, dimensions={0} | all-to-all | bytes 4194304 | tf_op jit(solution)/shard_map/all_to_all | solution.py:473
  118.1 1.4 %place_pieces.1 = bf16[32,32768]{1,0:T(8,128)(2,1)} custom-call(bf16[16,2,32,1024]{3,2,1,0:T(8,128)(2,1)S(1)} %bitcast.6), custom_call_target="tpu_custom_call" | custom-call | bytes 4194304 | tf_op jit(solution)/shard_map/place_pieces/pallas_call | solution.py:459
Async XLA Ops:
  2.8 29.0 %all-to-all-start = ((bf16[16,8,3200]{2,1,0:T(8,128)(2,1)}), bf16[16,8,3200]{2,1,0:T(8,128)(2,1)S(1)}, u32[]{:S(2)}, u32[]{:S(2)}) async-start(bf16[16,8,3200]{2,1,0:T(8,128)(2,1)} %pack_rows.1), calls=%async_computation | async-start | bytes 1638400 | tf_op jit(solution)/shard_map/all_to_all | solution.py:473
  10.2 1.6 %copy-start = (bf16[32,32768]{1,0:T(8,128)(2,1)S(1)}, bf16[32,32768]{1,0:T(8,128)(2,1)}, u32[]{:S(2)}) copy-start(bf16[32,32768]{1,0:T(8,128)(2,1)} %states_ref.1) | copy-start | bytes 6291460
  31.8 20.2 %collective-permute-start = (bf16[16,8,3200]{2,1,0:T(8,128)(2,1)S(1)}, bf16[16,8,3200]{2,1,0:T(8,128)(2,1)S(1)}, u32[]{:S(2)}, u32[]{:S(2)}) collective-permute-start(bf16[16,8,3200]{2,1,0:T(8,128)(2,1)S(1)} %all-to-all-done.refs_0_), channel_id=1, source_target_pairs={{0,16},{16,0},{1,17},{17,1},{2,18},{18,2},{3,19},{19,3},{4,20},{20... | collective-permute-start | bytes 2457608 | tf_op jit(solution)/shard_map/ppermute | solution.py:479
  33.3 30.1 %all-to-all-start.1 = ((bf16[16,32,1024]{2,1,0:T(8,128)(2,1)}), bf16[16,32,1024]{2,1,0:T(8,128)(2,1)S(1)}, u32[]{:S(2)}, u32[]{:S(2)}) async-start(bf16[16,32,1024]{2,1,0:T(8,128)(2,1)} %cut_share.1), calls=%async_computation.1 | async-start | bytes 2097152 | tf_op jit(solution)/shard_map/all_to_all | solution.py:473

commit v22 on v18

--- a/solution.py
+++ b/solution.py
@@ -502,7 +502,7 @@
         groups,
     )
     own_points = cut_share(background_states, order, share)
-    own_rows, own_points = lax.optimization_barrier((exchange(slots), own_points))
+    own_rows = exchange(slots)
     other_rows = swap_shares(own_rows)
     own_points = exchange(own_points).reshape(-1, share)
 

time: 119 us -> 121 us (1.017)
  blocking collectives: 51.8 us -> 80.3 us
  waiting for transfers between devices: 33.5 us -> 14.6 us
  starting transfers between devices: 12.5 us -> 5.15 us
    all_to_all x1 -> x2, blocking collectives: 51.8 us -> 80.3 us  [exchange(): return lax.all_to_all(blocks, axes, split_axis=0, concat_axis=0, tiled=True)]
    all_to_all x2 -> x1, waiting for transfers between devices: 19.8 us -> 2.79 us  [exchange(): return lax.all_to_all(blocks, axes, split_axis=0, concat_axis=0, tiled=True)]
    all_to_all x2 -> x1, starting transfers between devices: 11.1 us -> 3.66 us  [exchange(): return lax.all_to_all(blocks, axes, split_axis=0, concat_axis=0, tiled=True)]
    ppermute x1, waiting for transfers between devices: 13.7 us -> 11.8 us  [swap_shares(): lax.ppermute(own, 'boot', [(g, (g - turn) % groups) for g in range(groups)])]
  transfers between devices with their start and end apart: 3 -> 2, of which waited for: 3 -> 2; matrix products, arithmetic and copies ran while one was open for 0% -> 0% of each run, Pallas kernels for 11% -> 11%
where the time goes in v22:
time: 121 us; the launch traced here: 120 us
  blocking collectives  80.3 us (66%)
  Pallas kernels  18.6 us (15%)
  waiting for transfers between devices  14.6 us (12%)
  starting transfers between devices  5.15 us (4%)
  local copies, waits for them, and re-layouts  1.59 us (1%)
    all_to_all x2, blocking collectives, exchange(): return lax.all_to_all(blocks, axes, split_axis=0, concat_axis=0, tiled=True)  80.3 us
    ppermute x1, waiting for transfers between devices, swap_shares(): lax.ppermute(own, 'boot', [(g, (g - turn) % groups) for g in range(groups)])  11.8 us
    pallas_call x1, Pallas kernels, patch_weights(): pl.pallas_call(weights_kernel, out_shape=jax.ShapeDtypeStruct((groups, me...  10.9 us
    all_to_all x1, starting transfers between devices, exchange(): return lax.all_to_all(blocks, axes, split_axis=0, concat_axis=0, tiled=True)  3.66 us
    pallas_call x1, Pallas kernels, pack(): pl.pallas_call(functools.partial(pack_kernel, groups, order), out_shape=j...  2.82 us
    all_to_all x1, waiting for transfers between devices, exchange(): return lax.all_to_all(blocks, axes, split_axis=0, concat_axis=0, tiled=True)  2.79 us
  transfers between devices with their start and end apart: 2, of which 2 were waited for; matrix products, arithmetic and copies ran while one was open for 0% of the time, Pallas kernels for 11%

profile of v22, /device:TPU:0, one launch (start us, length us, event | category | flops | bytes accessed | tf_op | source)
XLA Modules:
  0.0 120.2 jit_solution(1556323028734381831)
XLA Ops:
  0.0 2.8 %pack_rows.1 = bf16[16,8,3200]{2,1,0:T(8,128)(2,1)} custom-call(s32[2,384]{1,0:T(2,128)} %bitcast.8, s32[2,384]{1,0:T(2,128)} %bitcast.9, s32[384]{0:T(512)} %refs_2_.1, f32[384]{0:T(512)} %refs_3_.1, bf16[384]{0:T(512)(128)(2,1)} %refs_4_.1, bf16[384,512]{1,0:T(8,128)(2,1)} %refs_5_.1), custom_call_target="tpu_custom_call" | custom-call | flops 301989888 | bytes 1179648 | tf_op jit(solution)/shard_map/pack_rows/pallas_call | solution.py:104
  2.8 29.0 %all_to_all.15.refs_0_ = bf16[16,8,3200]{2,1,0:T(8,128)(2,1)S(1)} all-to-all(bf16[16,8,3200]{2,1,0:T(8,128)(2,1)} %pack_rows.1), channel_id=1, replica_groups=mesh['boot'=2,'za'=2,'zb'=2,'near'=4] {'near','zb','za'}, dimensions={0} | all-to-all | bytes 1638400 | tf_op jit(solution)/shard_map/all_to_all | solution.py:463
  31.8 1.5 %collective-permute-start = (bf16[16,8,3200]{2,1,0:T(8,128)(2,1)S(1)}, bf16[16,8,3200]{2,1,0:T(8,128)(2,1)S(1)}, u32[]{:S(2)}, u32[]{:S(2)}) collective-permute-start(bf16[16,8,3200]{2,1,0:T(8,128)(2,1)S(1)} %all_to_all.15.refs_0_), channel_id=1, source_target_pairs={{0,16},{16,0},{1,17},{17,1},{2,18},{18,2},{3,19},{19,3},{4,20},{20... | collective-permute-start | bytes 2457608 | tf_op jit(solution)/shard_map/ppermute | solution.py:469
  33.3 0.0 copy-start
  33.3 1.6 %copy-done = bf16[32,32768]{1,0:T(8,128)(2,1)S(1)} copy-done((bf16[32,32768]{1,0:T(8,128)(2,1)S(1)}, bf16[32,32768]{1,0:T(8,128)(2,1)}, u32[]{:S(2)}) %copy-start) | copy-done | bytes 2097176
  34.9 1.0 cut_share.1
  35.9 3.7 %all-to-all-start.1 = ((bf16[16,32,1024]{2,1,0:T(8,128)(2,1)}), bf16[16,32,1024]{2,1,0:T(8,128)(2,1)S(1)}, u32[]{:S(2)}, u32[]{:S(2)}) async-start(bf16[16,32,1024]{2,1,0:T(8,128)(2,1)} %cut_share.1), calls=%async_computation.1 | async-start | bytes 2097152 | tf_op jit(solution)/shard_map/all_to_all | solution.py:463
  39.6 0.9 own_gram.1
  40.5 11.8 %collective-permute-done.refs_6_ = bf16[16,8,3200]{2,1,0:T(8,128)(2,1)S(1)} collective-permute-done((bf16[16,8,3200]{2,1,0:T(8,128)(2,1)S(1)}, bf16[16,8,3200]{2,1,0:T(8,128)(2,1)S(1)}, u32[]{:S(2)}, u32[]{:S(2)}) %collective-permute-start) | collective-permute-done | bytes 819232 | tf_op jit(solution)/shard_map/ppermute | solution.py:469
  52.3 10.9 %patch_weights.1.blended_ref = bf16[2,512,512]{2,1,0:T(8,128)(2,1)S(1)} custom-call(f32[512,256]{1,0:T(8,128)S(1)} %get-tuple-element.11.refs_0_, f32[256,256]{1,0:T(8,128)S(1)} %get-tuple-element.12.refs_1_, f32[1,512]{1,0:T(1,128)S(1)} %get-tuple-element.13.refs_2_, f32[16,8,128]{2,1,0:T(8,128)S(1)} %get-tuple-element.14.refs_3_, ...), custom_call_target="tpu_custom_call" | custom-call | flops 21474836480 | bytes 2097152 | tf_op jit(solution)/shard_map/patch_weights/pallas_call | solution.py:348
  63.2 2.8 %all-to-all-done.1 = bf16[16,32,1024]{2,1,0:T(8,128)(2,1)S(1)} async-done(((bf16[16,32,1024]{2,1,0:T(8,128)(2,1)}), bf16[16,32,1024]{2,1,0:T(8,128)(2,1)S(1)}, u32[]{:S(2)}, u32[]{:S(2)}) %all-to-all-start.1) | async-done | bytes 1048608 | tf_op jit(solution)/shard_map/all_to_all | solution.py:463
  66.0 1.5 %update_points.1 = bf16[16,2,32,1024]{3,2,1,0:T(8,128)(2,1)S(1)} custom-call(bf16[2,512,512]{2,1,0:T(8,128)(2,1)S(1)} %patch_weights.1.blended_ref, bf16[512,1024]{1,0:T(8,128)(2,1)S(1)} %bitcast.7), custom_call_target="tpu_custom_call" | custom-call | flops 1073741824 | bytes 3145728 | tf_op jit(solution)/shard_map/update_points/pallas_call | solution.py:390
  67.5 51.3 %all_to_all.16 = bf16[32,32,1024]{2,1,0:T(8,128)(2,1)S(1)} all-to-all(bf16[32,32,1024]{2,1,0:T(8,128)(2,1)S(1)} %bitcast.5), channel_id=1, replica_groups=mesh['boot'=2,'za'=2,'zb'=2,'near'=4] {'near','zb','za','boot'}, dimensions={0} | all-to-all | bytes 4194304 | tf_op jit(solution)/shard_map/all_to_all | solution.py:463
  118.9 1.4 %place_pieces.1 = bf16[32,32768]{1,0:T(8,128)(2,1)} custom-call(bf16[16,2,32,1024]{3,2,1,0:T(8,128)(2,1)S(1)} %bitcast.6), custom_call_target="tpu_custom_call" | custom-call | bytes 4194304 | tf_op jit(solution)/shard_map/place_pieces/pallas_call | solution.py:449
Async XLA Ops:
  31.8 20.5 %collective-permute-start = (bf16[16,8,3200]{2,1,0:T(8,128)(2,1)S(1)}, bf16[16,8,3200]{2,1,0:T(8,128)(2,1)S(1)}, u32[]{:S(2)}, u32[]{:S(2)}) collective-permute-start(bf16[16,8,3200]{2,1,0:T(8,128)(2,1)S(1)} %all_to_all.15.refs_0_), channel_id=1, source_target_pairs={{0,16},{16,0},{1,17},{17,1},{2,18},{18,2},{3,19},{19,3},{4,20},{20... | collective-permute-start | bytes 2457608 | tf_op jit(solution)/shard_map/ppermute | solution.py:469
  33.3 1.6 %copy-start = (bf16[32,32768]{1,0:T(8,128)(2,1)S(1)}, bf16[32,32768]{1,0:T(8,128)(2,1)}, u32[]{:S(2)}) copy-start(bf16[32,32768]{1,0:T(8,128)(2,1)} %states_ref.1) | copy-start | bytes 6291460
  35.9 30.1 %all-to-all-start.1 = ((bf16[16,32,1024]{2,1,0:T(8,128)(2,1)}), bf16[16,32,1024]{2,1,0:T(8,128)(2,1)S(1)}, u32[]{:S(2)}, u32[]{:S(2)}) async-start(bf16[16,32,1024]{2,1,0:T(8,128)(2,1)} %cut_share.1), calls=%async_computation.1 | async-start | bytes 2097152 | tf_op jit(solution)/shard_map/all_to_all | solution.py:463

commit v23 on v18

--- a/solution.py
+++ b/solution.py
@@ -373,8 +373,10 @@
         )
         centre = jnp.sum(background, axis=0, keepdims=True) / members
         perturb = (background - centre).astype(BF16)
+        blended = blended_ref[...].reshape(groups * members, members)
+        updates = jnp.dot(blended, perturb, preferred_element_type=F32)
         for turn in range(groups):
-            update = jnp.dot(blended_ref[turn], perturb, preferred_element_type=F32)
+            update = updates[turn * members : (turn + 1) * members, :]
             group = lax.rem(lax.axis_index("boot") + turn, groups)
             update = centre + update
             update = jnp.concatenate(

time: 119 us -> 119 us (level)
  no operation moved by 1% of the time
where the time goes in v23:
time: 119 us; the launch traced here: 118 us
  blocking collectives  51.8 us (44%)
  waiting for transfers between devices  33.5 us (28%)
  Pallas kernels  18.4 us (15%)
  starting transfers between devices  12.5 us (11%)
  local copies, waits for them, and re-layouts  1.59 us (1%)
    all_to_all x1, blocking collectives, exchange(): return lax.all_to_all(blocks, axes, split_axis=0, concat_axis=0, tiled=True)  51.8 us
    all_to_all x2, waiting for transfers between devices, exchange(): return lax.all_to_all(blocks, axes, split_axis=0, concat_axis=0, tiled=True)  19.8 us
    ppermute x1, waiting for transfers between devices, swap_shares(): lax.ppermute(own, 'boot', [(g, (g - turn) % groups) for g in range(groups)])  13.7 us
    all_to_all x2, starting transfers between devices, exchange(): return lax.all_to_all(blocks, axes, split_axis=0, concat_axis=0, tiled=True)  11.1 us
    pallas_call x1, Pallas kernels, patch_weights(): pl.pallas_call(weights_kernel, out_shape=jax.ShapeDtypeStruct((groups, me...  10.9 us
    pallas_call x1, Pallas kernels, pack(): pl.pallas_call(functools.partial(pack_kernel, groups, order), out_shape=j...  2.8 us
  transfers between devices with their start and end apart: 3, of which 3 were waited for; matrix products, arithmetic and copies ran while one was open for 0% of the time, Pallas kernels for 11%

profile of v23, /device:TPU:0, one launch (start us, length us, event | category | flops | bytes accessed | tf_op | source)
XLA Modules:
  0.0 117.9 jit_solution(2957062797569981833)
XLA Ops:
  0.0 2.8 %pack_rows.1 = bf16[16,8,3200]{2,1,0:T(8,128)(2,1)} custom-call(s32[2,384]{1,0:T(2,128)} %bitcast.8, s32[2,384]{1,0:T(2,128)} %bitcast.9, s32[384]{0:T(512)} %refs_2_.1, f32[384]{0:T(512)} %refs_3_.1, bf16[384]{0:T(512)(128)(2,1)} %refs_4_.1, bf16[384,512]{1,0:T(8,128)(2,1)} %refs_5_.1), custom_call_target="tpu_custom_call" | custom-call | flops 301989888 | bytes 1179648 | tf_op jit(solution)/shard_map/pack_rows/pallas_call | solution.py:104
  2.8 7.4 %all-to-all-start = ((bf16[16,8,3200]{2,1,0:T(8,128)(2,1)}), bf16[16,8,3200]{2,1,0:T(8,128)(2,1)S(1)}, u32[]{:S(2)}, u32[]{:S(2)}) async-start(bf16[16,8,3200]{2,1,0:T(8,128)(2,1)} %pack_rows.1), calls=%async_computation | async-start | bytes 1638400 | tf_op jit(solution)/shard_map/all_to_all | solution.py:465
  10.2 0.0 copy-start
  10.2 1.6 %copy-done = bf16[32,32768]{1,0:T(8,128)(2,1)S(1)} copy-done((bf16[32,32768]{1,0:T(8,128)(2,1)S(1)}, bf16[32,32768]{1,0:T(8,128)(2,1)}, u32[]{:S(2)}) %copy-start) | copy-done | bytes 2097176
  11.8 1.0 cut_share.1
  12.8 18.9 %all-to-all-done.refs_0_ = bf16[16,8,3200]{2,1,0:T(8,128)(2,1)S(1)} async-done(((bf16[16,8,3200]{2,1,0:T(8,128)(2,1)}), bf16[16,8,3200]{2,1,0:T(8,128)(2,1)S(1)}, u32[]{:S(2)}, u32[]{:S(2)}) %all-to-all-start) | async-done | bytes 819232 | tf_op jit(solution)/shard_map/all_to_all | solution.py:465
  31.8 1.5 %collective-permute-start = (bf16[16,8,3200]{2,1,0:T(8,128)(2,1)S(1)}, bf16[16,8,3200]{2,1,0:T(8,128)(2,1)S(1)}, u32[]{:S(2)}, u32[]{:S(2)}) collective-permute-start(bf16[16,8,3200]{2,1,0:T(8,128)(2,1)S(1)} %all-to-all-done.refs_0_), channel_id=1, source_target_pairs={{0,16},{16,0},{1,17},{17,1},{2,18},{18,2},{3,19},{19,3},{4,20},{20... | collective-permute-start | bytes 2457608 | tf_op jit(solution)/shard_map/ppermute | solution.py:471
  33.3 3.7 %all-to-all-start.1 = ((bf16[16,32,1024]{2,1,0:T(8,128)(2,1)}), bf16[16,32,1024]{2,1,0:T(8,128)(2,1)S(1)}, u32[]{:S(2)}, u32[]{:S(2)}) async-start(bf16[16,32,1024]{2,1,0:T(8,128)(2,1)} %cut_share.1), calls=%async_computation.1 | async-start | bytes 2097152 | tf_op jit(solution)/shard_map/all_to_all | solution.py:465
  37.0 0.9 own_gram.1
  37.8 13.7 %collective-permute-done.refs_6_ = bf16[16,8,3200]{2,1,0:T(8,128)(2,1)S(1)} collective-permute-done((bf16[16,8,3200]{2,1,0:T(8,128)(2,1)S(1)}, bf16[16,8,3200]{2,1,0:T(8,128)(2,1)S(1)}, u32[]{:S(2)}, u32[]{:S(2)}) %collective-permute-start) | collective-permute-done | bytes 819232 | tf_op jit(solution)/shard_map/ppermute | solution.py:471
  51.6 10.9 %patch_weights.1.blended_ref = bf16[2,512,512]{2,1,0:T(8,128)(2,1)S(1)} custom-call(f32[512,256]{1,0:T(8,128)S(1)} %get-tuple-element.14.refs_0_, f32[256,256]{1,0:T(8,128)S(1)} %get-tuple-element.15.refs_1_, f32[1,512]{1,0:T(1,128)S(1)} %get-tuple-element.16.refs_2_, f32[16,8,128]{2,1,0:T(8,128)S(1)} %get-tuple-element.17.refs_3_, ...), custom_call_target="tpu_custom_call" | custom-call | flops 21474836480 | bytes 2097152 | tf_op jit(solution)/shard_map/patch_weights/pallas_call | solution.py:348
  62.5 0.9 all-to-all-done.1
  63.4 1.4 %update_points.1 = bf16[16,2,32,1024]{3,2,1,0:T(8,128)(2,1)S(1)} custom-call(bf16[2,512,512]{2,1,0:T(8,128)(2,1)S(1)} %patch_weights.1.blended_ref, bf16[512,1024]{1,0:T(8,128)(2,1)S(1)} %bitcast.7), custom_call_target="tpu_custom_call" | custom-call | flops 1073741824 | bytes 3145728 | tf_op jit(solution)/shard_map/update_points/pallas_call | solution.py:392
  64.8 51.8 %all_to_all.15 = bf16[32,32,1024]{2,1,0:T(8,128)(2,1)S(1)} all-to-all(bf16[32,32,1024]{2,1,0:T(8,128)(2,1)S(1)} %bitcast.5), channel_id=1, replica_groups=mesh['boot'=2,'za'=2,'zb'=2,'near'=4] {'near','zb','za','boot'}, dimensions={0} | all-to-all | bytes 4194304 | tf_op jit(solution)/shard_map/all_to_all | solution.py:465
  116.6 1.4 %place_pieces.1 = bf16[32,32768]{1,0:T(8,128)(2,1)} custom-call(bf16[16,2,32,1024]{3,2,1,0:T(8,128)(2,1)S(1)} %bitcast.6), custom_call_target="tpu_custom_call" | custom-call | bytes 4194304 | tf_op jit(solution)/shard_map/place_pieces/pallas_call | solution.py:451
Async XLA Ops:
  2.8 29.0 %all-to-all-start = ((bf16[16,8,3200]{2,1,0:T(8,128)(2,1)}), bf16[16,8,3200]{2,1,0:T(8,128)(2,1)S(1)}, u32[]{:S(2)}, u32[]{:S(2)}) async-start(bf16[16,8,3200]{2,1,0:T(8,128)(2,1)} %pack_rows.1), calls=%async_computation | async-start | bytes 1638400 | tf_op jit(solution)/shard_map/all_to_all | solution.py:465
  10.2 1.6 %copy-start = (bf16[32,32768]{1,0:T(8,128)(2,1)S(1)}, bf16[32,32768]{1,0:T(8,128)(2,1)}, u32[]{:S(2)}) copy-start(bf16[32,32768]{1,0:T(8,128)(2,1)} %states_ref.1) | copy-start | bytes 6291460
  31.8 19.8 %collective-permute-start = (bf16[16,8,3200]{2,1,0:T(8,128)(2,1)S(1)}, bf16[16,8,3200]{2,1,0:T(8,128)(2,1)S(1)}, u32[]{:S(2)}, u32[]{:S(2)}) collective-permute-start(bf16[16,8,3200]{2,1,0:T(8,128)(2,1)S(1)} %all-to-all-done.refs_0_), channel_id=1, source_target_pairs={{0,16},{16,0},{1,17},{17,1},{2,18},{18,2},{3,19},{19,3},{4,20},{20... | collective-permute-start | bytes 2457608 | tf_op jit(solution)/shard_map/ppermute | solution.py:471
  33.3 30.1 %all-to-all-start.1 = ((bf16[16,32,1024]{2,1,0:T(8,128)(2,1)}), bf16[16,32,1024]{2,1,0:T(8,128)(2,1)S(1)}, u32[]{:S(2)}, u32[]{:S(2)}) async-start(bf16[16,32,1024]{2,1,0:T(8,128)(2,1)} %cut_share.1), calls=%async_computation.1 | async-start | bytes 2097152 | tf_op jit(solution)/shard_map/all_to_all | solution.py:465
